TPU v7x, 32 devices: a whole 2x2x4 slice. The times are simulated.
32 devices in a mesh: replica: 8 (over y, x, core), shard: 4 (over z).
Axes of the slice: x: 2, y: 2, z: 4, core: 2. Of those that a mesh axis runs over, the one named last changes fastest.
Arguments:
- frames: bfloat16 [16, 1536, 1536], P('replica', 'shard'), may hold values from -6 to 6
- text_states: bfloat16 [16, 64, 1536], P('replica'), may hold values from -6 to 6
- text_mask: int32 [16, 64], P('replica'), may hold values from 0 to 1, as said below
- clip_lengths: int32 [16], P('replica'), may hold values from 384 to 1536, as said below
- slot_used: int32 [16], P('replica'), may hold values from 0 to 1, as said below
- teacher: bfloat16 [16, 1536, 1536], P('replica', 'shard'), may hold values from -16 to 16
- self_norm_gain: bfloat16 [1536], P('shard'), may hold values from 0.5 to 1.5
- self_norm_bias: bfloat16 [1536], P('shard'), may hold values from -1.1953125 to 1.1953125
- self_query_weight: bfloat16 [1536, 1536], P('shard'), may hold values from -0.15625 to 0.15625
- self_key_weight: bfloat16 [1536, 1536], P('shard'), may hold values from -0.15625 to 0.15625
- self_value_weight: bfloat16 [1536, 1536], P('shard'), may hold values from -0.15625 to 0.15625
- self_output_weight: bfloat16 [1536, 1536], P('shard'), may hold values from -1.25 to 1.25
- cross_norm_gain: bfloat16 [1536], P('shard'), may hold values from 0.5 to 1.5
- cross_norm_bias: bfloat16 [1536], P('shard'), may hold values from -1.1953125 to 1.1953125
- cross_query_weight: bfloat16 [1536, 1536], P('shard'), may hold values from -0.15625 to 0.15625
- cross_key_weight: bfloat16 [1536, 1536], P('shard'), may hold values from -0.15625 to 0.15625
- cross_value_weight: bfloat16 [1536, 1536], P('shard'), may hold values from -0.15625 to 0.15625
- cross_output_weight: bfloat16 [1536, 1536], P('shard'), may hold values from -0.625 to 0.625
- feed_norm_gain: bfloat16 [1536], P('shard'), may hold values from 0.5 to 1.5
- feed_norm_bias: bfloat16 [1536], P('shard'), may hold values from -1.1953125 to 1.1953125
- feed_up_weight: bfloat16 [1536, 6144], P('shard'), may hold values from -0.15625 to 0.15625
- feed_down_weight: bfloat16 [6144, 1536], P('shard'), may hold values from -0.078125 to 0.078125
Outputs:
- output: bfloat16 [16, 1536, 1536], P('replica', 'shard')
- loss: float32 [], replicated
- frames_grad: float32 [16, 1536, 1536], P('replica', 'shard')
- text_grad: float32 [16, 64, 1536], P('replica')
- self_norm_gain_grad: float32 [1536], P('shard')
- self_norm_bias_grad: float32 [1536], P('shard')
- self_query_weight_grad: float32 [1536, 1536], P('shard')
- self_key_weight_grad: float32 [1536, 1536], P('shard')
- self_value_weight_grad: float32 [1536, 1536], P('shard')
- self_output_weight_grad: float32 [1536, 1536], P('shard')
- cross_norm_gain_grad: float32 [1536], P('shard')
- cross_norm_bias_grad: float32 [1536], P('shard')
- cross_query_weight_grad: float32 [1536, 1536], P('shard')
- cross_key_weight_grad: float32 [1536, 1536], P('shard')
- cross_value_weight_grad: float32 [1536, 1536], P('shard')
- cross_output_weight_grad: float32 [1536, 1536], P('shard')
- feed_norm_gain_grad: float32 [1536], P('shard')
- feed_norm_bias_grad: float32 [1536], P('shard')
- feed_up_weight_grad: float32 [1536, 6144], P('shard')
- feed_down_weight_grad: float32 [6144, 1536], P('shard')
Inputs may be any that keep to these rules, and one draw needn't show every extreme that they name: `clip_lengths`: the first slot of every replica holds more than 1152 frames, slot 0 exactly 1536. `slot_used`: the first of the 2 slots of every replica is used. `text_mask`: each row is ones followed by zeros, with 8 or more ones; row 0 is all ones.
All inputs are finite; a program needn't handle non-finite values.
Results may differ from a plain program's by a relative error of at most 0.015.
Values may be sent and summed in bfloat16 or wider, within the bound.
No kernel may reach another device: no remote copies, remote signals or barrier semaphores. Data moves between devices by JAX's collectives and lax.ppermute only.
A program may use at most 512 MiB of HBM per device.

v0:
```python
import jax
import jax.numpy as jnp
from jax import lax
from jax.sharding import PartitionSpec as P

HEADS = 24
HEAD_DIM = 64


epsilon = 1e-05
masked_score = -1e30


def layer_norm(values, gain, shift):
    center = values - jnp.mean(values, axis=-1, keepdims=True)
    variance = jnp.mean(center * center, axis=-1, keepdims=True)
    return center * lax.rsqrt(variance + epsilon) * gain + shift


def exact_gelu(values):
    return jax.nn.gelu(values, approximate=False)


def project(left, right):
    return jnp.dot(left, right, preferred_element_type=jnp.float32)


def outer_sum(left, right):
    return jnp.einsum("rd,re->de", left, right, preferred_element_type=jnp.float32)


def back_project(grads, matrix):
    return jnp.einsum("re,de->rd", grads, matrix, preferred_element_type=jnp.float32)


def split_heads(values):
    return values.reshape(values.shape[:-1] + (HEADS, HEAD_DIM))


def self_forward(operands):
    queries, keys_all, values_all, allowed = operands
    scale = HEAD_DIM ** (-0.5)
    scores = (
        jnp.einsum("qhd,khd->hqk", queries, keys_all, preferred_element_type=jnp.float32) * scale
    )
    scores = jnp.where(allowed[None], scores, masked_score)
    peak = jnp.max(scores, axis=-1, keepdims=True)
    weights = jnp.exp(scores - peak)
    totals = jnp.sum(weights, axis=-1, keepdims=True)
    probs = (weights / totals).astype(jnp.bfloat16)
    mixed = jnp.einsum("hqk,khd->qhd", probs, values_all, preferred_element_type=jnp.float32)
    return (mixed.astype(jnp.bfloat16), (peak + jnp.log(totals))[..., 0])


def self_backward(operands):
    queries, keys_all, values_all, allowed, log_totals, grad_mixed = operands
    scale = HEAD_DIM ** (-0.5)
    scores = (
        jnp.einsum("qhd,khd->hqk", queries, keys_all, preferred_element_type=jnp.float32) * scale
    )
    scores = jnp.where(allowed[None], scores, masked_score)
    probs = jnp.exp(scores - log_totals[..., None])
    grad_probs = jnp.einsum(
        "qhd,khd->hqk", grad_mixed, values_all, preferred_element_type=jnp.float32
    )
    grad_values = jnp.einsum(
        "hqk,qhd->khd", probs.astype(jnp.bfloat16), grad_mixed, preferred_element_type=jnp.float32
    )
    inner = jnp.sum(probs * grad_probs, axis=-1, keepdims=True)
    grad_scores = (probs * (grad_probs - inner)).astype(jnp.bfloat16)
    grad_queries = (
        jnp.einsum("hqk,khd->qhd", grad_scores, keys_all, preferred_element_type=jnp.float32)
        * scale
    ).astype(jnp.bfloat16)
    grad_keys = (
        jnp.einsum("hqk,qhd->khd", grad_scores, queries, preferred_element_type=jnp.float32) * scale
    )
    return (grad_queries, grad_keys, grad_values)


def body(
    frames,
    text_states,
    text_mask,
    clip_lengths,
    slot_used,
    teacher,
    self_norm_gain,
    self_norm_bias,
    self_query_weight,
    self_key_weight,
    self_value_weight,
    self_output_weight,
    cross_norm_gain,
    cross_norm_bias,
    cross_query_weight,
    cross_key_weight,
    cross_value_weight,
    cross_output_weight,
    feed_norm_gain,
    feed_norm_bias,
    feed_up_weight,
    feed_down_weight,
):
    gathered = (
        lax.all_gather(self_norm_gain, "shard", axis=0, tiled=True),
        lax.all_gather(self_norm_bias, "shard", axis=0, tiled=True),
        lax.all_gather(self_query_weight, "shard", axis=0, tiled=True),
        lax.all_gather(self_key_weight, "shard", axis=0, tiled=True),
        lax.all_gather(self_value_weight, "shard", axis=0, tiled=True),
        lax.all_gather(self_output_weight, "shard", axis=0, tiled=True),
        lax.all_gather(cross_norm_gain, "shard", axis=0, tiled=True),
        lax.all_gather(cross_norm_bias, "shard", axis=0, tiled=True),
        lax.all_gather(cross_query_weight, "shard", axis=0, tiled=True),
        lax.all_gather(cross_key_weight, "shard", axis=0, tiled=True),
        lax.all_gather(cross_value_weight, "shard", axis=0, tiled=True),
        lax.all_gather(cross_output_weight, "shard", axis=0, tiled=True),
        lax.all_gather(feed_norm_gain, "shard", axis=0, tiled=True),
        lax.all_gather(feed_norm_bias, "shard", axis=0, tiled=True),
        lax.all_gather(feed_up_weight, "shard", axis=0, tiled=True),
        lax.all_gather(feed_down_weight, "shard", axis=0, tiled=True),
    )
    (
        gain_attend,
        bias_attend,
        query_matrix,
        key_matrix,
        value_matrix,
        output_matrix,
        gain_cross,
        bias_cross,
        probe_matrix,
        lookup_matrix,
        content_matrix,
        merge_matrix,
        gain_feed,
        bias_feed,
        expand_matrix,
        reduce_matrix,
    ) = gathered
    slots = frames.shape[0]
    frame_count = frames.shape[1]
    width = frames.shape[2]
    text_len = text_states.shape[1]
    shards = lax.axis_size("shard")
    replicas = lax.axis_size("replica")
    clip_total = frame_count * shards
    row_count = slots * frame_count
    scale = HEAD_DIM ** (-0.5)
    shard_rank = lax.axis_index("shard")
    positions = shard_rank * frame_count + jnp.arange(frame_count, dtype=jnp.int32)
    key_positions = jnp.arange(clip_total, dtype=jnp.int32)
    allowed = (key_positions[None, None, :] <= positions[None, :, None]) & (
        key_positions[None, None, :] < clip_lengths[:, None, None]
    )
    valid_rows = ((positions[None, :] < clip_lengths[:, None]) & (slot_used[:, None] > 0)).astype(
        jnp.float32
    )
    text_allowed = text_mask > 0
    inputs = frames.astype(jnp.float32)
    normed_one, pull_one = jax.vjp(
        layer_norm, inputs, gain_attend.astype(jnp.float32), bias_attend.astype(jnp.float32)
    )
    hidden_one = normed_one.astype(jnp.bfloat16).reshape(row_count, width)
    queries = (
        project(hidden_one, query_matrix).astype(jnp.bfloat16).reshape(slots, frame_count, width)
    )
    keys_local = (
        project(hidden_one, key_matrix).astype(jnp.bfloat16).reshape(slots, frame_count, width)
    )
    values_local = (
        project(hidden_one, value_matrix).astype(jnp.bfloat16).reshape(slots, frame_count, width)
    )
    keys_all, values_all = (
        lax.all_gather(keys_local, "shard", axis=1, tiled=True),
        lax.all_gather(values_local, "shard", axis=1, tiled=True),
    )
    head_queries = split_heads(queries)
    head_keys = split_heads(keys_all)
    head_values = split_heads(values_all)
    mixed_self, log_totals = lax.map(self_forward, (head_queries, head_keys, head_values, allowed))
    mixed_rows = mixed_self.reshape(row_count, width)
    after_self = inputs + project(mixed_rows, output_matrix).reshape(slots, frame_count, width)
    normed_two, pull_two = jax.vjp(
        layer_norm, after_self, gain_cross.astype(jnp.float32), bias_cross.astype(jnp.float32)
    )
    hidden_two = normed_two.astype(jnp.bfloat16).reshape(row_count, width)
    probes = split_heads(
        project(hidden_two, probe_matrix).astype(jnp.bfloat16).reshape(slots, frame_count, width)
    )
    text_rows = text_states.reshape(slots * text_len, width)
    lookups = split_heads(
        project(text_rows, lookup_matrix).astype(jnp.bfloat16).reshape(slots, text_len, width)
    )
    contents = split_heads(
        project(text_rows, content_matrix).astype(jnp.bfloat16).reshape(slots, text_len, width)
    )
    cross_scores = (
        jnp.einsum("sqhd,skhd->shqk", probes, lookups, preferred_element_type=jnp.float32) * scale
    )
    cross_scores = jnp.where(text_allowed[:, None, None, :], cross_scores, masked_score)
    cross_peak = jnp.max(cross_scores, axis=-1, keepdims=True)
    cross_weights = jnp.exp(cross_scores - cross_peak)
    cross_probs = cross_weights / jnp.sum(cross_weights, axis=-1, keepdims=True)
    cross_probs_low = cross_probs.astype(jnp.bfloat16)
    cross_mixed = jnp.einsum(
        "shqk,skhd->sqhd", cross_probs_low, contents, preferred_element_type=jnp.float32
    )
    cross_mixed = cross_mixed.astype(jnp.bfloat16).reshape(row_count, width)
    after_cross = after_self + project(cross_mixed, merge_matrix).reshape(slots, frame_count, width)
    normed_three, pull_three = jax.vjp(
        layer_norm, after_cross, gain_feed.astype(jnp.float32), bias_feed.astype(jnp.float32)
    )
    hidden_three = normed_three.astype(jnp.bfloat16).reshape(row_count, width)
    upward = project(hidden_three, expand_matrix)
    activated, gelu_pull = jax.vjp(exact_gelu, upward)
    activated_low = activated.astype(jnp.bfloat16)
    result = after_cross + project(activated_low, reduce_matrix).reshape(slots, frame_count, width)
    output = result.astype(jnp.bfloat16)
    errors = (result - teacher.astype(jnp.float32)) * valid_rows[..., None]
    squares_total, count_total = lax.psum(
        (jnp.sum(errors * errors), jnp.sum(valid_rows)), ("replica", "shard")
    )
    loss = squares_total / (width * count_total)
    grad_result = errors * (slots * replicas * clip_total / count_total)
    grad_feed_low = grad_result.reshape(row_count, width).astype(jnp.bfloat16)
    grad_activated = back_project(grad_feed_low, reduce_matrix)
    grad_upward = gelu_pull(grad_activated)[0].astype(jnp.bfloat16)
    grad_hidden_three = back_project(grad_upward, expand_matrix).reshape(slots, frame_count, width)
    grad_cross_norm, gain_feed_part, bias_feed_part = pull_three(grad_hidden_three)
    grad_after_cross = grad_result + grad_cross_norm
    feed_owned = (
        lax.psum_scatter(
            outer_sum(hidden_three, grad_upward).astype(jnp.bfloat16),
            "shard",
            scatter_dimension=0,
            tiled=True,
        ).astype(jnp.float32),
        lax.psum_scatter(
            outer_sum(activated_low, grad_feed_low).astype(jnp.bfloat16),
            "shard",
            scatter_dimension=0,
            tiled=True,
        ).astype(jnp.float32),
        lax.psum_scatter(
            gain_feed_part.astype(jnp.bfloat16), "shard", scatter_dimension=0, tiled=True
        ).astype(jnp.float32),
        lax.psum_scatter(
            bias_feed_part.astype(jnp.bfloat16), "shard", scatter_dimension=0, tiled=True
        ).astype(jnp.float32),
    )
    grad_cross_low = grad_after_cross.reshape(row_count, width).astype(jnp.bfloat16)
    grad_cross_mixed = split_heads(
        back_project(grad_cross_low, merge_matrix)
        .astype(jnp.bfloat16)
        .reshape(slots, frame_count, width)
    )
    grad_cross_probs = jnp.einsum(
        "sqhd,skhd->shqk", grad_cross_mixed, contents, preferred_element_type=jnp.float32
    )
    content_grads = jnp.einsum(
        "shqk,sqhd->skhd", cross_probs_low, grad_cross_mixed, preferred_element_type=jnp.float32
    )
    cross_inner = jnp.sum(cross_probs * grad_cross_probs, axis=-1, keepdims=True)
    grad_cross_scores = (cross_probs * (grad_cross_probs - cross_inner)).astype(jnp.bfloat16)
    probe_grads = (
        jnp.einsum(
            "shqk,skhd->sqhd", grad_cross_scores, lookups, preferred_element_type=jnp.float32
        )
        * scale
    )
    probe_grads = probe_grads.astype(jnp.bfloat16).reshape(row_count, width)
    lookup_grads = (
        jnp.einsum("shqk,sqhd->skhd", grad_cross_scores, probes, preferred_element_type=jnp.float32)
        * scale
    )
    lookup_sum, content_sum = (
        lax.psum(lookup_grads.astype(jnp.bfloat16), "shard").astype(jnp.float32),
        lax.psum(content_grads.astype(jnp.bfloat16), "shard").astype(jnp.float32),
    )
    lookup_low = lookup_sum.astype(jnp.bfloat16).reshape(slots * text_len, width)
    content_low = content_sum.astype(jnp.bfloat16).reshape(slots * text_len, width)
    own_width = width // shards
    own_text = lax.dynamic_slice_in_dim(text_rows, shard_rank * own_width, own_width, 1)
    lookup_own = outer_sum(own_text, lookup_low)
    content_own = outer_sum(own_text, content_low)
    text_grad = (
        back_project(lookup_low, lookup_matrix) + back_project(content_low, content_matrix)
    ).reshape(slots, text_len, width)
    grad_hidden_two = back_project(probe_grads, probe_matrix).reshape(slots, frame_count, width)
    grad_self_norm, gain_cross_part, bias_cross_part = pull_two(grad_hidden_two)
    grad_after_self = grad_after_cross + grad_self_norm
    grad_self_low = grad_after_self.reshape(row_count, width).astype(jnp.bfloat16)
    grad_mixed = split_heads(
        back_project(grad_self_low, output_matrix)
        .astype(jnp.bfloat16)
        .reshape(slots, frame_count, width)
    )
    grad_queries, grad_keys, grad_values = lax.map(
        self_backward, (head_queries, head_keys, head_values, allowed, log_totals, grad_mixed)
    )
    key_sum, value_sum = (
        lax.psum_scatter(
            grad_keys.reshape(slots, clip_total, width).astype(jnp.bfloat16),
            "shard",
            scatter_dimension=1,
            tiled=True,
        ).astype(jnp.float32),
        lax.psum_scatter(
            grad_values.reshape(slots, clip_total, width).astype(jnp.bfloat16),
            "shard",
            scatter_dimension=1,
            tiled=True,
        ).astype(jnp.float32),
    )
    key_low = key_sum.astype(jnp.bfloat16).reshape(row_count, width)
    value_low = value_sum.astype(jnp.bfloat16).reshape(row_count, width)
    query_low = grad_queries.reshape(row_count, width)
    grad_hidden_one = (
        back_project(query_low, query_matrix)
        + back_project(key_low, key_matrix)
        + back_project(value_low, value_matrix)
    )
    grad_inputs, gain_attend_part, bias_attend_part = pull_one(
        grad_hidden_one.reshape(slots, frame_count, width)
    )
    frames_grad = grad_after_self + grad_inputs
    attend_owned = (
        lax.psum_scatter(
            outer_sum(hidden_one, query_low).astype(jnp.bfloat16),
            "shard",
            scatter_dimension=0,
            tiled=True,
        ).astype(jnp.float32),
        lax.psum_scatter(
            outer_sum(hidden_one, key_low).astype(jnp.bfloat16),
            "shard",
            scatter_dimension=0,
            tiled=True,
        ).astype(jnp.float32),
        lax.psum_scatter(
            outer_sum(hidden_one, value_low).astype(jnp.bfloat16),
            "shard",
            scatter_dimension=0,
            tiled=True,
        ).astype(jnp.float32),
        lax.psum_scatter(
            outer_sum(mixed_rows, grad_self_low).astype(jnp.bfloat16),
            "shard",
            scatter_dimension=0,
            tiled=True,
        ).astype(jnp.float32),
        lax.psum_scatter(
            outer_sum(hidden_two, probe_grads).astype(jnp.bfloat16),
            "shard",
            scatter_dimension=0,
            tiled=True,
        ).astype(jnp.float32),
        lax.psum_scatter(
            outer_sum(cross_mixed, grad_cross_low).astype(jnp.bfloat16),
            "shard",
            scatter_dimension=0,
            tiled=True,
        ).astype(jnp.float32),
        lax.psum_scatter(
            gain_attend_part.astype(jnp.bfloat16), "shard", scatter_dimension=0, tiled=True
        ).astype(jnp.float32),
        lax.psum_scatter(
            bias_attend_part.astype(jnp.bfloat16), "shard", scatter_dimension=0, tiled=True
        ).astype(jnp.float32),
        lax.psum_scatter(
            gain_cross_part.astype(jnp.bfloat16), "shard", scatter_dimension=0, tiled=True
        ).astype(jnp.float32),
        lax.psum_scatter(
            bias_cross_part.astype(jnp.bfloat16), "shard", scatter_dimension=0, tiled=True
        ).astype(jnp.float32),
    )
    summed = (
        lax.psum(attend_owned[6].astype(jnp.bfloat16), "replica").astype(jnp.float32),
        lax.psum(attend_owned[7].astype(jnp.bfloat16), "replica").astype(jnp.float32),
        lax.psum(attend_owned[0].astype(jnp.bfloat16), "replica").astype(jnp.float32),
        lax.psum(attend_owned[1].astype(jnp.bfloat16), "replica").astype(jnp.float32),
        lax.psum(attend_owned[2].astype(jnp.bfloat16), "replica").astype(jnp.float32),
        lax.psum(attend_owned[3].astype(jnp.bfloat16), "replica").astype(jnp.float32),
        lax.psum(attend_owned[8].astype(jnp.bfloat16), "replica").astype(jnp.float32),
        lax.psum(attend_owned[9].astype(jnp.bfloat16), "replica").astype(jnp.float32),
        lax.psum(attend_owned[4].astype(jnp.bfloat16), "replica").astype(jnp.float32),
        lax.psum(lookup_own.astype(jnp.bfloat16), "replica").astype(jnp.float32),
        lax.psum(content_own.astype(jnp.bfloat16), "replica").astype(jnp.float32),
        lax.psum(attend_owned[5].astype(jnp.bfloat16), "replica").astype(jnp.float32),
        lax.psum(feed_owned[2].astype(jnp.bfloat16), "replica").astype(jnp.float32),
        lax.psum(feed_owned[3].astype(jnp.bfloat16), "replica").astype(jnp.float32),
        lax.psum(feed_owned[0].astype(jnp.bfloat16), "replica").astype(jnp.float32),
        lax.psum(feed_owned[1].astype(jnp.bfloat16), "replica").astype(jnp.float32),
    )
    return (
        output,
        loss,
        frames_grad,
        text_grad,
        summed[0],
        summed[1],
        summed[2],
        summed[3],
        summed[4],
        summed[5],
        summed[6],
        summed[7],
        summed[8],
        summed[9],
        summed[10],
        summed[11],
        summed[12],
        summed[13],
        summed[14],
        summed[15],
    )


def solution(mesh):
    placed = (
        P("replica", "shard", None),
        P("replica", None, None),
        P("replica", None),
        P("replica"),
        P("replica"),
        P("replica", "shard", None),
        P("shard"),
        P("shard"),
        P("shard", None),
        P("shard", None),
        P("shard", None),
        P("shard", None),
        P("shard"),
        P("shard"),
        P("shard", None),
        P("shard", None),
        P("shard", None),
        P("shard", None),
        P("shard"),
        P("shard"),
        P("shard", None),
        P("shard", None),
    )
    return jax.shard_map(
        body,
        mesh=mesh,
        in_specs=placed,
        out_specs=(
            P("replica", "shard", None),
            P(),
            P("replica", "shard", None),
            P("replica", None, None),
            P("shard"),
            P("shard"),
            P("shard", None),
            P("shard", None),
            P("shard", None),
            P("shard", None),
            P("shard"),
            P("shard"),
            P("shard", None),
            P("shard", None),
            P("shard", None),
            P("shard", None),
            P("shard"),
            P("shard"),
            P("shard", None),
            P("shard", None),
        ),
        check_vma=False,
    )
```

profile of v0, /device:TPU:0, one launch (start us, length us, event | category | flops | bytes accessed | tf_op | source)
XLA Modules:
  0.0 4060.2 jit_solution(1770479921453920131)
XLA Ops:
  41.5 60.3 %all-gather.19.cloned.1.call-done = bf16[1536,1536]{1,0:T(8,128)(2,1)} async-done(((bf16[384,1536]{1,0:T(8,128)(2,1)}), bf16[1536,1536]{1,0:T(8,128)(2,1)}) %all-gather.19.cloned.1.call-update) | async-done | bytes 4718608 | tf_op jit(solution)/shard_map/all_gather | solution.py:110
  110.4 81.0 %all-gather.25.cloned.1.call-done = bf16[1536,1536]{1,0:T(8,128)(2,1)} async-done(((bf16[384,1536]{1,0:T(8,128)(2,1)}), bf16[1536,1536]{1,0:T(8,128)(2,1)}) %all-gather.25.cloned.1.call-update) | async-done | bytes 4718608 | tf_op jit(solution)/shard_map/all_gather | solution.py:109
  257.2 24.1 all-gather.23.cloned.1.call-done
  298.1 72.5 %all-gather.35.cloned.1.call-done = bf16[1536,1536]{1,0:T(8,128)(2,1)} async-done(((bf16[384,1536]{1,0:T(8,128)(2,1)}), bf16[1536,1536]{1,0:T(8,128)(2,1)}) %all-gather.35.cloned.1.call-update) | async-done | bytes 4718608 | tf_op jit(solution)/shard_map/all_gather | solution.py:115
  377.5 82.4 %all-gather.31.cloned.1.call-done = bf16[1536,1536]{1,0:T(8,128)(2,1)} async-done(((bf16[384,1536]{1,0:T(8,128)(2,1)}), bf16[1536,1536]{1,0:T(8,128)(2,1)}) %all-gather.31.cloned.1.call-update) | async-done | bytes 4718608 | tf_op jit(solution)/shard_map/all_gather | solution.py:116
  464.4 162.8 %all-gather.21.cloned.1.call-done = bf16[2,1536,1536]{2,1,0:T(8,128)(2,1)} async-done(((bf16[2,384,1536]{2,1,0:T(8,128)(2,1)}), bf16[2,1536,1536]{2,1,0:T(8,128)(2,1)}) %all-gather.21.cloned.1.call-update) | async-done | bytes 9437200 | tf_op jit(solution)/shard_map/all_gather | solution.py:176
  640.0 154.3 %all-gather.27.cloned.1.call-done = bf16[2,1536,1536]{2,1,0:T(8,128)(2,1)} async-done(((bf16[2,384,1536]{2,1,0:T(8,128)(2,1)}), bf16[2,1536,1536]{2,1,0:T(8,128)(2,1)}) %all-gather.27.cloned.1.call-update) | async-done | bytes 9437200 | tf_op jit(solution)/shard_map/all_gather | solution.py:175
  808.8 139.2 %while.26 = (s32[]{:T(128)}, bf16[2,384,24,64]{1,3,2,0:T(8,128)(2,1)}, f32[2,24,384]{2,1,0:T(8,128)S(1)}, bf16[2,1536,24,64]{1,3,2,0:T(8,128)(2,1)}, pred[2,384,...) while((s32[]{:T(128)}, ...), condition=%wide.region_5.6_spmd, body=%wide.region_2.5_spmd.sunk | while | flops 3794328576 | bytes 184911968 | solution.py:181
  809.9 23.4 fusion.210
  833.3 19.3 fusion.211
  852.7 25.0 fusion.212
  878.8 24.3 fusion.210
  903.1 19.3 fusion.211
  922.5 25.1 fusion.212
  1001.2 61.1 %all-gather.37.cloned.1.call-done = bf16[1536,1536]{1,0:T(8,128)(2,1)} async-done(((bf16[384,1536]{1,0:T(8,128)(2,1)}), bf16[1536,1536]{1,0:T(8,128)(2,1)}) %all-gather.37.cloned.1.call-update) | async-done | bytes 4718608 | tf_op jit(solution)/shard_map/all_gather | solution.py:117
  1074.0 311.0 %all-gather.39.cloned.1.call-done = bf16[1536,6144]{1,0:T(8,128)(2,1)} async-done(((bf16[384,6144]{1,0:T(8,128)(2,1)}), bf16[1536,6144]{1,0:T(8,128)(2,1)}) %all-gather.39.cloned.1.call-update) | async-done | bytes 18874384 | tf_op jit(solution)/shard_map/all_gather | solution.py:120
  1385.0 56.5 %multiply_convert_fusion.2 = (bf16[768,6144]{1,0:T(8,128)(2,1)}, f32[768,6144]{1,0:T(8,128)}, f32[768,6144]{1,0:T(8,128)}) fusion(bf16[768,1536]{1,0:T(8,128)(2,1)S(1)} %bitcast.300, bf16[1536,6144]{1,0:T(8,128)(2,1)} %all-gather.39.cloned.1.call-done), kind=kOutput, calls=%fused_computation.65 | convolution fusion | flops 14802223104 | bytes 68419584 | tf_op jit(solution)/shard_map/dot_general | solution.py:25
  1441.5 266.4 %all-gather.41.cloned.1.call-done = bf16[6144,1536]{1,0:T(8,128)(2,1)} async-done(((bf16[1536,1536]{1,0:T(8,128)(2,1)}), bf16[6144,1536]{1,0:T(8,128)(2,1)}) %all-gather.41.cloned.1.call-update) | async-done | bytes 18874384 | tf_op jit(solution)/shard_map/all_gather | solution.py:121
  1707.9 19.2 fusion.124
  1732.5 39.5 all-reduce.6
  1777.2 29.6 add_convert_fusion
  1806.8 20.2 fusion.123
  1890.6 332.9 %while.27 = (s32[]{:T(128)}, bf16[2,384,24,64]{1,3,2,0:T(8,128)(2,1)}, bf16[2,1536,24,64]{1,3,2,0:T(8,128)(2,1)}, bf16[2,1536,24,64]{1,3,2,0:T(8,128)(2,1)}, bf1...) while((s32[]{:T(128)}, ...), condition=%wide.region_23.24_spmd, body=%wide.region_21.23_spmd.sunk | while | flops 9275563008 | bytes 480969888 | solution.py:299
  1890.7 23.0 fusion.221
  1913.8 42.0 %multiply_reduce_fusion.10 = (f32[24,384]{1,0:T(8,128)S(1)}, f32[24,384,1536]{2,1,0:T(8,128)}) fusion(f32[24,384,1536]{2,1,0:T(8,128)} %fusion.221, f32[24,384]{1,0:T(8,128)S(1)} %dynamic-slice_bitcast_fusion.7, pred[384,1536]{1,0:T(8,128)(4,1)S(1)} %dynamic-slice_bitcast_fusion.8, bf16[2,1536,24,64]{1,3,2,0:T(8,128)(2,1)} %get-tuple-element.431, ...), kind=kOutput, calls=%fused_computation.23.clone.1 | convolution fusion | flops 1882708992 | bytes 119809024 | tf_op jit(solution)/shard_map/while/body/eval_jaxpr/qhd,khd->hqk/dot_general | solution.py:63
  1955.8 45.2 %multiply_convert_fusion.8 = bf16[24,384,1536]{2,1,0:T(8,128)(2,1)} fusion(f32[24,384,1536]{2,1,0:T(8,128)} %get-tuple-element.374, f32[24,384,1536]{2,1,0:T(8,128)} %fusion.221, f32[24,384]{1,0:T(8,128)S(1)} %get-tuple-element.375, f32[24,384]{1,0:T(8,128)S(1)} %dynamic-slice_bitcast_fusion.7, pred[384,1536]{1,0:T(8,128)(4,1)S(1)} %dynamic-slice_bitcast_fusion.8), kind=kLoop, calls=%fused_computation.22.clone.1 | loop fusion | flops 84934656 | bytes 142221312 | tf_op jit(solution)/shard_map/while/body/eval_jaxpr/convert_element_type | solution.py:70
  2015.0 15.5 fusion.222
  2030.5 26.5 bitcast_dynamic-update-slice_fusion.8
  2057.0 23.0 fusion.221
  2080.0 42.0 %multiply_reduce_fusion.10 = (f32[24,384]{1,0:T(8,128)S(1)}, f32[24,384,1536]{2,1,0:T(8,128)}) fusion(f32[24,384,1536]{2,1,0:T(8,128)} %fusion.221, f32[24,384]{1,0:T(8,128)S(1)} %dynamic-slice_bitcast_fusion.7, pred[384,1536]{1,0:T(8,128)(4,1)S(1)} %dynamic-slice_bitcast_fusion.8, bf16[2,1536,24,64]{1,3,2,0:T(8,128)(2,1)} %get-tuple-element.431, ...), kind=kOutput, calls=%fused_computation.23.clone.1 | convolution fusion | flops 1882708992 | bytes 119809024 | tf_op jit(solution)/shard_map/while/body/eval_jaxpr/qhd,khd->hqk/dot_general | solution.py:63
  2122.0 45.2 %multiply_convert_fusion.8 = bf16[24,384,1536]{2,1,0:T(8,128)(2,1)} fusion(f32[24,384,1536]{2,1,0:T(8,128)} %get-tuple-element.374, f32[24,384,1536]{2,1,0:T(8,128)} %fusion.221, f32[24,384]{1,0:T(8,128)S(1)} %get-tuple-element.375, f32[24,384]{1,0:T(8,128)S(1)} %dynamic-slice_bitcast_fusion.7, pred[384,1536]{1,0:T(8,128)(4,1)S(1)} %dynamic-slice_bitcast_fusion.8), kind=kLoop, calls=%fused_computation.22.clone.1 | loop fusion | flops 84934656 | bytes 142221312 | tf_op jit(solution)/shard_map/while/body/eval_jaxpr/convert_element_type | solution.py:70
  2167.2 13.9 bitcast_dynamic-update-slice_fusion.7
  2181.2 15.5 fusion.222
  2196.7 26.6 bitcast_dynamic-update-slice_fusion.8
  2307.2 90.3 %reduce-scatter.11.cloned.1.call-done = bf16[2,384,1536]{2,1,0:T(8,128)(2,1)} async-done(((bf16[2,1536,1536]{2,1,0:T(8,128)(2,1)}), bf16[2,384,1536]{2,1,0:T(8,128)(2,1)}) %reduce-scatter.11.cloned.1.call-update) | async-done | bytes 2359312 | tf_op jit(solution)/shard_map/reduce_scatter | solution.py:303
  2404.8 157.7 %reduce-scatter.13.cloned.1.call-done = bf16[2,384,1536]{2,1,0:T(8,128)(2,1)} async-done(((bf16[2,1536,1536]{2,1,0:T(8,128)(2,1)}), bf16[2,384,1536]{2,1,0:T(8,128)(2,1)}) %reduce-scatter.13.cloned.1.call-update) | async-done | bytes 2359312 | tf_op jit(solution)/shard_map/reduce_scatter | solution.py:309
  2571.3 21.9 convolution_convert_fusion
  2594.9 21.6 convolution_convert_fusion.1
  2621.9 75.6 %reduce-scatter.21.cloned.1.call-done = bf16[384,1536]{1,0:T(8,128)(2,1)} async-done(((bf16[1536,1536]{1,0:T(8,128)(2,1)}), bf16[384,1536]{1,0:T(8,128)(2,1)}) %reduce-scatter.21.cloned.1.call-update) | async-done | bytes 1179664 | tf_op jit(solution)/shard_map/reduce_scatter | solution.py:347
  2697.5 88.0 %reduce-scatter.23.cloned.1.call-done = bf16[384,1536]{1,0:T(8,128)(2,1)} async-done(((bf16[1536,1536]{1,0:T(8,128)(2,1)}), bf16[384,1536]{1,0:T(8,128)(2,1)}) %reduce-scatter.23.cloned.1.call-update) | async-done | bytes 1179664 | tf_op jit(solution)/shard_map/reduce_scatter | solution.py:353
  2785.4 88.0 %reduce-scatter.25.cloned.1.call-done = bf16[384,1536]{1,0:T(8,128)(2,1)} async-done(((bf16[1536,1536]{1,0:T(8,128)(2,1)}), bf16[384,1536]{1,0:T(8,128)(2,1)}) %reduce-scatter.25.cloned.1.call-update) | async-done | bytes 1179664 | tf_op jit(solution)/shard_map/reduce_scatter | solution.py:359
  2873.4 88.7 %reduce-scatter.15.cloned.1.call-done = bf16[384,1536]{1,0:T(8,128)(2,1)} async-done(((bf16[1536,1536]{1,0:T(8,128)(2,1)}), bf16[384,1536]{1,0:T(8,128)(2,1)}) %reduce-scatter.15.cloned.1.call-update) | async-done | bytes 1179664 | tf_op jit(solution)/shard_map/reduce_scatter | solution.py:329
  2962.1 88.5 %reduce-scatter.17.cloned.1.call-done = bf16[384,1536]{1,0:T(8,128)(2,1)} async-done(((bf16[1536,1536]{1,0:T(8,128)(2,1)}), bf16[384,1536]{1,0:T(8,128)(2,1)}) %reduce-scatter.17.cloned.1.call-update) | async-done | bytes 1179664 | tf_op jit(solution)/shard_map/reduce_scatter | solution.py:335
  3050.6 88.7 %reduce-scatter.19.cloned.1.call-done = bf16[384,1536]{1,0:T(8,128)(2,1)} async-done(((bf16[1536,1536]{1,0:T(8,128)(2,1)}), bf16[384,1536]{1,0:T(8,128)(2,1)}) %reduce-scatter.19.cloned.1.call-update) | async-done | bytes 1179664 | tf_op jit(solution)/shard_map/reduce_scatter | solution.py:341
  3139.3 316.7 %reduce-scatter.29.cloned.1.call-done = bf16[1536,1536]{1,0:T(8,128)(2,1)} async-done(((bf16[6144,1536]{1,0:T(8,128)(2,1)}), bf16[1536,1536]{1,0:T(8,128)(2,1)}) %reduce-scatter.29.cloned.1.call-update) | async-done | bytes 4718608 | tf_op jit(solution)/shard_map/reduce_scatter | solution.py:239
  3456.0 317.4 %reduce-scatter.27.cloned.1.call-done = bf16[384,6144]{1,0:T(8,128)(2,1)} async-done(((bf16[1536,6144]{1,0:T(8,128)(2,1)}), bf16[384,6144]{1,0:T(8,128)(2,1)}) %reduce-scatter.27.cloned.1.call-update) | async-done | bytes 4718608 | tf_op jit(solution)/shard_map/reduce_scatter | solution.py:233
  3802.8 18.2 all-reduce.9
  3847.9 177.8 %all-reduce.14.cloned.1.call-done = (bf16[384,1536]{1,0:T(8,128)(2,1)}, bf16[384,1536]{1,0:T(8,128)(2,1)}, bf16[384,1536]{1,0:T(8,128)(2,1)}, bf16[384,1536]{1,0...) async-done(((bf16[384,1536]{1,0:T(8,128)(2,1)}, ...) | async-done | bytes 18874384 | tf_op jit(solution)/shard_map/psum | solution.py:381
  (447 shorter events, 504.3 us)
Async XLA Ops:
  7.2 363.4 %copy-start = (bf16[2,64,1536]{2,1,0:T(8,128)(2,1)S(1)}, bf16[2,64,1536]{2,1,0:T(8,128)(2,1)}, u32[]{:S(2)}) copy-start(bf16[2,64,1536]{2,1,0:T(8,128)(2,1)} %param.27) | copy-start | bytes 1179652
  7.2 29.6 copy-start.6
  7.2 94.7 %all-gather.19.cloned.1.call-start = ((), (), s32[]{:S(2)}) async-start(), calls=%async_computation.10 | async-start | bytes 5898240 | tf_op jit(solution)/shard_map/all_gather | solution.py:110
  8.0 183.4 %all-gather.25.cloned.1.call-start = ((), (), s32[]{:S(2)}) async-start(), calls=%async_computation.13 | async-start | bytes 5898240 | tf_op jit(solution)/shard_map/all_gather | solution.py:109
  8.7 272.5 %all-gather.23.cloned.1.call-start = ((), (), s32[]{:S(2)}) async-start(), calls=%async_computation.12 | async-start | bytes 5898240 | tf_op jit(solution)/shard_map/all_gather | solution.py:108
  9.5 361.1 %all-gather.35.cloned.1.call-start = ((), (), s32[]{:S(2)}) async-start(), calls=%async_computation.18 | async-start | bytes 5898240 | tf_op jit(solution)/shard_map/all_gather | solution.py:115
  10.0 449.9 %all-gather.31.cloned.1.call-start = ((), (), s32[]{:S(2)}) async-start(), calls=%async_computation.16 | async-start | bytes 5898240 | tf_op jit(solution)/shard_map/all_gather | solution.py:116
  10.6 616.6 %all-gather.21.cloned.1.call-start = ((), (), s32[]{:S(2)}) async-start(), calls=%async_computation.11 | async-start | bytes 11796480 | tf_op jit(solution)/shard_map/all_gather | solution.py:176
  101.9 89.5 %copy-start.34 = (bf16[2,384,1536]{2,1,0:T(8,128)(2,1)S(1)}, bf16[2,384,1536]{2,1,0:T(8,128)(2,1)}, u32[]{:S(2)}) copy-start(bf16[2,384,1536]{2,1,0:T(8,128)(2,1)} %fusion.75) | copy-start | bytes 7077892
  110.3 684.0 %all-gather.27.cloned.1.call-start = ((), (), s32[]{:S(2)}) async-start(), calls=%async_computation.14 | async-start | bytes 11796480 | tf_op jit(solution)/shard_map/all_gather | solution.py:175
  198.7 749.3 %all-gather.29.cloned.1.call-start = ((), (), s32[]{:S(2)}) async-start(), calls=%async_computation.15 | async-start | bytes 5898240 | tf_op jit(solution)/shard_map/all_gather | solution.py:111
  199.5 773.5 %all-gather.33.cloned.1.call-start = ((), (), s32[]{:S(2)}) async-start(), calls=%async_computation.17 | async-start | bytes 5898240 | tf_op jit(solution)/shard_map/all_gather | solution.py:114
  200.2 862.1 %all-gather.37.cloned.1.call-start = ((), (), s32[]{:S(2)}) async-start(), calls=%async_computation.19 | async-start | bytes 5898240 | tf_op jit(solution)/shard_map/all_gather | solution.py:117
  200.8 27.5 copy-start.94
  200.9 28.0 copy-start.90
  200.9 40.7 %copy-start.91 = (bf16[384]{0:T(512)(128)(2,1)S(1)}, bf16[384]{0:T(512)(128)(2,1)}, u32[]{:S(2)}) copy-start(bf16[384]{0:T(512)(128)(2,1)} %param.45) | copy-start | bytes 2308
  200.9 53.5 %copy-start.95 = (s32[2]{0:T(128)S(1)}, s32[2]{0:T(128)}, u32[]{:S(2)}) copy-start(s32[2]{0:T(128)} %param.30) | copy-start | bytes 28
  200.9 1184.1 %all-gather.39.cloned.1.call-start = ((), (), s32[]{:S(2)}) async-start(), calls=%async_computation.20 | async-start | bytes 23592960 | tf_op jit(solution)/shard_map/all_gather | solution.py:120
  201.6 1506.3 %all-gather.41.cloned.1.call-start = ((), (), s32[]{:S(2)}) async-start(), calls=%async_computation.21 | async-start | bytes 23592960 | tf_op jit(solution)/shard_map/all_gather | solution.py:121
  202.2 2195.3 %reduce-scatter.11.cloned.1.call-start = ((), (), s32[]{:S(2)}) async-start(), calls=%async_computation.22 | async-start | bytes 11796480 | tf_op jit(solution)/shard_map/reduce_scatter | solution.py:303
  957.6 22.8 copy-start.72
  959.1 21.2 copy-start.70
  959.9 20.4 copy-start.29
  1001.2 68.7 %copy-start.15 = (bf16[2,24,64,384]{3,2,1,0:T(8,128)(2,1)}, bf16[2,24,64,384]{3,2,1,0:T(8,128)(2,1)S(1)}, u32[]{:S(2)}) copy-start(bf16[2,24,64,384]{3,2,1,0:T(8,128)(2,1)S(1)} %convolution_convert_fusion.16) | copy-start | bytes 7077892
  1074.0 367.5 %copy-start.26 = (bf16[2,384,1536]{2,1,0:T(8,128)(2,1)}, bf16[2,384,1536]{2,1,0:T(8,128)(2,1)S(1)}, u32[]{:S(2)}) copy-start(bf16[2,384,1536]{2,1,0:T(8,128)(2,1)S(1)} %add_convert_fusion.1) | copy-start | bytes 7077892
  1707.9 19.2 copy-start.2
  1707.9 19.2 copy-start.23
  1707.9 19.2 copy-start.81
  1772.8 54.3 %slice-start = ((s8[4718592]{0:T(1024)(128)(4,1)}), s8[4194304]{0:T(1024)(128)(4,1)S(1)}, s32[]{:S(2)}) async-start(s8[4718592]{0:T(1024)(128)(4,1)} %bitcast.265), calls=%async_computation.34 | async-start | bytes 8388608
  1777.2 49.8 %slice-start.1 = ((s8[4718592]{0:T(1024)(128)(4,1)}), s8[524288]{0:T(1024)(128)(4,1)S(1)}, s32[]{:S(2)}) async-start(s8[4718592]{0:T(1024)(128)(4,1)} %bitcast.265), calls=%async_computation.35 | async-start | bytes 1048576
  1806.8 20.2 copy-start.53
  1806.8 20.2 copy-start.55
  1890.7 23.0 copy-start.10
  1890.7 23.1 copy-start.11
  2057.0 23.0 copy-start.10
  2057.0 23.1 copy-start.11
  2236.1 326.3 %reduce-scatter.13.cloned.1.call-start = ((), (), s32[]{:S(2)}) async-start(), calls=%async_computation.23 | async-start | bytes 11796480 | tf_op jit(solution)/shard_map/reduce_scatter | solution.py:309
  2248.8 368.1 %all-reduce.16.cloned.1.call-start = ((), (), s32[]{:S(2)}) async-start(), calls=%async_computation.33 | async-start | bytes 1572864 | tf_op jit(solution)/shard_map/psum | solution.py:278
  2266.3 431.2 %reduce-scatter.21.cloned.1.call-start = ((), (), s32[]{:S(2)}) async-start(), calls=%async_computation.27 | async-start | bytes 5898240 | tf_op jit(solution)/shard_map/reduce_scatter | solution.py:347
  2274.8 510.6 %reduce-scatter.23.cloned.1.call-start = ((), (), s32[]{:S(2)}) async-start(), calls=%async_computation.28 | async-start | bytes 5898240 | tf_op jit(solution)/shard_map/reduce_scatter | solution.py:353
  2285.0 588.3 %reduce-scatter.25.cloned.1.call-start = ((), (), s32[]{:S(2)}) async-start(), calls=%async_computation.29 | async-start | bytes 5898240 | tf_op jit(solution)/shard_map/reduce_scatter | solution.py:359
  2295.2 666.9 %reduce-scatter.15.cloned.1.call-start = ((), (), s32[]{:S(2)}) async-start(), calls=%async_computation.24 | async-start | bytes 5898240 | tf_op jit(solution)/shard_map/reduce_scatter | solution.py:329
  2307.1 743.5 %reduce-scatter.17.cloned.1.call-start = ((), (), s32[]{:S(2)}) async-start(), calls=%async_computation.25 | async-start | bytes 5898240 | tf_op jit(solution)/shard_map/reduce_scatter | solution.py:335
  2404.7 734.6 %reduce-scatter.19.cloned.1.call-start = ((), (), s32[]{:S(2)}) async-start(), calls=%async_computation.26 | async-start | bytes 5898240 | tf_op jit(solution)/shard_map/reduce_scatter | solution.py:341
  2569.6 886.4 %reduce-scatter.29.cloned.1.call-start = ((), (), s32[]{:S(2)}) async-start(), calls=%async_computation.31 | async-start | bytes 23592960 | tf_op jit(solution)/shard_map/reduce_scatter | solution.py:239
  2593.2 1180.2 %reduce-scatter.27.cloned.1.call-start = ((), (), s32[]{:S(2)}) async-start(), calls=%async_computation.30 | async-start | bytes 23592960 | tf_op jit(solution)/shard_map/reduce_scatter | solution.py:233
  2616.6 1409.1 %all-reduce.14.cloned.1.call-start = ((), (), s32[]{:S(2)}) async-start(), calls=%async_computation.32 | async-start | bytes 37748736 | tf_op jit(solution)/shard_map/psum | solution.py:381
  3800.7 37.9 copy-start.79
  (92 other events, 461.6 us)
Sparse Core Ops, SparseCore 0:
  9.6 92.2 all-gather.18
  103.5 87.8 all-gather.24
  192.9 88.2 all-gather.22
  282.7 87.8 all-gather.34
  372.0 87.8 all-gather.30
  461.9 165.2 all-gather.20
  629.3 164.9 all-gather.26
  795.9 87.5 all-gather.28
  885.1 87.8 all-gather.32
  974.4 87.8 all-gather.36
  1063.9 321.0 all-gather.38
  1386.4 321.4 all-gather.40
  2236.3 161.2 reduce-scatter.10
  2400.3 162.1 reduce-scatter.12
  2565.9 44.8 all-reduce.15
  2612.9 84.4 reduce-scatter.20
  2699.6 85.7 reduce-scatter.22
  2787.6 85.7 reduce-scatter.24
  2876.3 85.7 reduce-scatter.14
  2964.8 85.7 reduce-scatter.16
  3053.5 85.7 reduce-scatter.18
  3141.7 314.2 reduce-scatter.28
  3458.5 314.8 reduce-scatter.26
  3779.6 246.0 all-reduce.13
where the time goes:
time: 4070 us; the launch traced here: 4060 us
  waiting for transfers between devices  2870 us (71%)
  matrix products  668 us (16%)
  other arithmetic  204 us (5%)
  local copies, waits for them, and re-layouts  147 us (4%)
  blocking collectives  146 us (4%)
    reduce_scatter x1, waiting for transfers between devices, body(): lax.psum_scatter(outer_sum(hidden_three, grad_upward).astype(jnp.bfloat16...  317 us
    reduce_scatter x1, waiting for transfers between devices, body(): lax.psum_scatter(outer_sum(activated_low, grad_feed_low).astype(jnp.bfloa...  317 us
    all_gather x1, waiting for transfers between devices, body(): lax.all_gather(feed_up_weight, 'shard', axis=0, tiled=True)  311 us
    all_gather x1, waiting for transfers between devices, body(): lax.all_gather(feed_down_weight, 'shard', axis=0, tiled=True)  266 us
    psum x1, waiting for transfers between devices, body(): lax.psum(attend_owned[0].astype(jnp.bfloat16), 'replica')  178 us
    all_gather x1, waiting for transfers between devices, body(): lax.all_gather(values_local, 'shard', axis=1, tiled=True)  163 us
    reduce_scatter x1, waiting for transfers between devices, body(): lax.psum_scatter(grad_values.reshape(slots, clip_total, width).astype(jnp...  158 us
    all_gather x1, waiting for transfers between devices, body(): lax.all_gather(keys_local, 'shard', axis=1, tiled=True)  154 us
  transfers between devices with their start and end apart: 24, of which 22 were waited for; matrix products, arithmetic and copies ran while one was open for 12% of the time, Pallas kernels for 0%

commit v1 on v0

--- a/solution.py
+++ b/solution.py
@@ -1,6 +1,9 @@
 import jax
 import jax.numpy as jnp
 from jax import lax
+from jax.experimental import pallas as pl
+from jax.experimental.pallas import tpu as pltpu
+from jax.sharding import Mesh
 from jax.sharding import PartitionSpec as P
 
 HEADS = 24
@@ -78,7 +81,7 @@
     return (grad_queries, grad_keys, grad_values)
 
 
-def body(
+def general_body(
     frames,
     text_states,
     text_mask,
@@ -417,56 +420,785 @@
     )
 
 
+PAIR = 2 * HEAD_DIM
+EVERY = ("shard", "y", "x", "core")
+REPLICAS = ("core", "y", "x")
+NT = (((1,), (1,)), ((), ()))
+TN = (((0,), (0,)), ((), ()))
+NN = (((1,), (0,)), ((), ()))
+
+
+def dot(left, right, dims):
+    return lax.dot_general(left, right, dims, preferred_element_type=jnp.float32)
+
+
+def half_mask(side, value):
+    lanes = lax.broadcasted_iota(jnp.int32, (1, PAIR), 1)
+    inside = (lanes >= HEAD_DIM) if side else (lanes < HEAD_DIM)
+    return jnp.where(inside, value, 0.0).astype(jnp.bfloat16)
+
+
+def self_forward_kernel(place, q_ref, k_ref, v_ref, mixed_ref, lse_ref, acc_ref):
+    block = q_ref.shape[0] // 2
+    length = place[2]
+    low = lax.broadcasted_iota(jnp.int32, (PAIR, 1), 0) < HEAD_DIM
+    for part in range(2):
+        first = place[part] * block
+        rows = slice(part * block, (part + 1) * block)
+        q = q_ref[rows, :]
+        q_half = [q * half_mask(side, HEAD_DIM ** (-0.5)) for side in range(2)]
+        limit = jnp.minimum(
+            first + lax.broadcasted_iota(jnp.int32, (1, block), 1) + 1, length
+        )
+        acc_ref[...] = jnp.zeros_like(acc_ref)
+
+        def step(j, peaks, q_half=q_half, limit=limit):
+            at = pl.multiple_of(j * block, block)
+            k = k_ref[pl.ds(at, block), :]
+            v = v_ref[pl.ds(at, block), :]
+            allowed = at + lax.broadcasted_iota(jnp.int32, (block, block), 0) < limit
+            out = []
+            for side in range(2):
+                scores = jnp.where(allowed, dot(k, q_half[side], NT), masked_score)
+                peak = jnp.maximum(peaks[side], jnp.max(scores, axis=0, keepdims=True))
+                weights = jnp.exp(scores - peak).astype(jnp.bfloat16)
+                v_ones = v * half_mask(side, 1.0) + half_mask(1 - side, 1.0)
+                acc_ref[side] = acc_ref[side] * jnp.exp(peaks[side] - peak) + dot(
+                    v_ones, weights, TN
+                )
+                out.append(peak)
+            return tuple(out)
+
+        peaks = lax.fori_loop(
+            0, place[part] + 1, step, (jnp.full((1, block), masked_score, jnp.float32),) * 2
+        )
+        top, bottom = acc_ref[0], acc_ref[1]
+        total = jnp.where(low, top[HEAD_DIM : HEAD_DIM + 1], bottom[0:1])
+        mixed = jnp.where(low, top, bottom) / total
+        mixed_ref[rows, :] = mixed.T.astype(jnp.bfloat16)
+        lse_ref[0:1, rows] = peaks[0] + jnp.log(top[HEAD_DIM : HEAD_DIM + 1])
+        lse_ref[1:2, rows] = peaks[1] + jnp.log(bottom[0:1])
+
+
+def self_backward_kernel(
+    place, q_ref, k_ref, v_ref, mixed_ref, grad_ref, lse_ref, dq_ref, dk_ref, dv_ref,
+    dq_acc, dk_acc, dv_acc,
+):
+    block = q_ref.shape[0] // 2
+    length = place[2]
+    scale = HEAD_DIM ** (-0.5)
+    dk_acc[...] = jnp.zeros_like(dk_acc)
+    dv_acc[...] = jnp.zeros_like(dv_acc)
+    for part in range(2):
+        first = place[part] * block
+        rows = slice(part * block, (part + 1) * block)
+        q = q_ref[rows, :]
+        grad = grad_ref[rows, :]
+        q_half = [q * half_mask(side, scale) for side in range(2)]
+        grad_half = [grad * half_mask(side, 1.0) for side in range(2)]
+        product = (grad.astype(jnp.float32) * mixed_ref[rows, :].astype(jnp.float32)).T
+        inner = [
+            jnp.sum(product[side * HEAD_DIM : (side + 1) * HEAD_DIM], axis=0, keepdims=True)
+            for side in range(2)
+        ]
+        lse = [lse_ref[side : side + 1, rows] for side in range(2)]
+        limit = jnp.minimum(
+            first + lax.broadcasted_iota(jnp.int32, (1, block), 1) + 1, length
+        )
+        dq_acc[...] = jnp.zeros_like(dq_acc)
+
+        def step(
+            j, carry, q_half=q_half, grad_half=grad_half, inner=inner, lse=lse, limit=limit
+        ):
+            at = pl.multiple_of(j * block, block)
+            k = k_ref[pl.ds(at, block), :]
+            v = v_ref[pl.ds(at, block), :]
+            allowed = at + lax.broadcasted_iota(jnp.int32, (block, block), 0) < limit
+            dq, dk, dv = 0.0, 0.0, 0.0
+            for side in range(2):
+                scores = jnp.where(allowed, dot(k, q_half[side], NT), masked_score)
+                probs = jnp.exp(scores - lse[side])
+                grad_probs = dot(v, grad_half[side], NT)
+                grad_scores = (probs * (grad_probs - inner[side])).astype(jnp.bfloat16)
+                dv += dot(probs.astype(jnp.bfloat16), grad_half[side], NN)
+                dk += dot(grad_scores, q_half[side], NN)
+                dq += dot(k * half_mask(side, scale), grad_scores, TN)
+            dk_acc[pl.ds(at, block), :] += dk
+            dv_acc[pl.ds(at, block), :] += dv
+            dq_acc[...] += dq
+            return carry
+
+        lax.fori_loop(0, place[part] + 1, step, 0)
+        dq_ref[rows, :] = dq_acc[...].T.astype(jnp.bfloat16)
+    dk_ref[...] = dk_acc[...].astype(jnp.bfloat16)
+    dv_ref[...] = dv_acc[...].astype(jnp.bfloat16)
+
+
+def pair_block(rows):
+    return pl.BlockSpec((rows, PAIR), lambda i, *_: (0, i))
+
+
+def self_attend(place, queries, keys, values):
+    rows, width = queries.shape
+    clip = keys.shape[0]
+    pairs = width // PAIR
+    return pl.pallas_call(
+        self_forward_kernel,
+        out_shape=(
+            jax.ShapeDtypeStruct((rows, width), jnp.bfloat16),
+            jax.ShapeDtypeStruct((pairs * 8, rows), jnp.float32),
+        ),
+        grid_spec=pltpu.PrefetchScalarGridSpec(
+            num_scalar_prefetch=1,
+            grid=(pairs,),
+            in_specs=[pair_block(rows), pair_block(clip), pair_block(clip)],
+            out_specs=(pair_block(rows), pl.BlockSpec((8, rows), lambda i, *_: (i, 0))),
+            scratch_shapes=[pltpu.VMEM((2, PAIR, rows // 2), jnp.float32)],
+        ),
+        compiler_params=pltpu.CompilerParams(vmem_limit_bytes=32 * 2**20),
+        cost_estimate=pl.CostEstimate(
+            flops=2 * 2 * rows * clip * width, bytes_accessed=8 * clip * width, transcendentals=0
+        ),
+        name="self_attend",
+    )(place, queries, keys, values)
+
+
+def self_attend_back(place, queries, keys, values, mixed, grads, lse):
+    rows, width = queries.shape
+    clip = keys.shape[0]
+    pairs = width // PAIR
+    return pl.pallas_call(
+        self_backward_kernel,
+        out_shape=(
+            jax.ShapeDtypeStruct((rows, width), jnp.bfloat16),
+            jax.ShapeDtypeStruct((clip, width), jnp.bfloat16),
+            jax.ShapeDtypeStruct((clip, width), jnp.bfloat16),
+        ),
+        grid_spec=pltpu.PrefetchScalarGridSpec(
+            num_scalar_prefetch=1,
+            grid=(pairs,),
+            in_specs=[
+                pair_block(rows),
+                pair_block(clip),
+                pair_block(clip),
+                pair_block(rows),
+                pair_block(rows),
+                pl.BlockSpec((8, rows), lambda i, *_: (i, 0)),
+            ],
+            out_specs=(pair_block(rows), pair_block(clip), pair_block(clip)),
+            scratch_shapes=[
+                pltpu.VMEM((PAIR, rows // 2), jnp.float32),
+                pltpu.VMEM((clip, PAIR), jnp.float32),
+                pltpu.VMEM((clip, PAIR), jnp.float32),
+            ],
+        ),
+        compiler_params=pltpu.CompilerParams(vmem_limit_bytes=32 * 2**20),
+        cost_estimate=pl.CostEstimate(
+            flops=5 * 2 * rows * clip * width, bytes_accessed=16 * clip * width, transcendentals=0
+        ),
+        name="self_attend_back",
+    )(place, queries, keys, values, mixed, grads, lse)
+
+
+def both_heads(rows, value):
+    return jnp.concatenate([rows * half_mask(side, value) for side in range(2)], axis=0)
+
+
+def cross_probs_of(lookup_two, probes, present):
+    text = present.shape[0]
+    scores = dot(lookup_two, probes, NT)
+    out = []
+    for side in range(2):
+        part = jnp.where(
+            present > 0, scores[side * text : (side + 1) * text], masked_score
+        )
+        weights = jnp.exp(part - jnp.max(part, axis=0, keepdims=True))
+        out.append(weights / jnp.sum(weights, axis=0, keepdims=True))
+    return out
+
+
+def cross_forward_kernel(probe_ref, lookup_ref, content_ref, present_ref, mixed_ref):
+    probs = cross_probs_of(
+        both_heads(lookup_ref[...], HEAD_DIM ** (-0.5)), probe_ref[...], present_ref[...]
+    )
+    probs = jnp.concatenate(probs, axis=0).astype(jnp.bfloat16)
+    mixed_ref[...] = dot(probs, both_heads(content_ref[...], 1.0), TN).astype(jnp.bfloat16)
+
+
+def cross_backward_kernel(
+    probe_ref, lookup_ref, content_ref, present_ref, grad_ref, dp_ref, dl_ref, dc_ref
+):
+    text = present_ref.shape[0]
+    scale = HEAD_DIM ** (-0.5)
+    probes = probe_ref[...]
+    grads = grad_ref[...]
+    lookup_two = both_heads(lookup_ref[...], scale)
+    probs = cross_probs_of(lookup_two, probes, present_ref[...])
+    grad_probs = dot(both_heads(content_ref[...], 1.0), grads, NT)
+    grad_scores = []
+    for side in range(2):
+        part = grad_probs[side * text : (side + 1) * text]
+        inner = jnp.sum(probs[side] * part, axis=0, keepdims=True)
+        grad_scores.append(probs[side] * (part - inner))
+    grad_scores = jnp.concatenate(grad_scores, axis=0).astype(jnp.bfloat16)
+    probs = jnp.concatenate(probs, axis=0).astype(jnp.bfloat16)
+    low = lax.broadcasted_iota(jnp.int32, (1, PAIR), 1) < HEAD_DIM
+    dp_ref[...] = dot(grad_scores, lookup_two, TN).astype(jnp.bfloat16)
+    dl = dot(grad_scores, probes, NN) * scale
+    dl_ref[...] = jnp.where(low, dl[:text], dl[text:]).astype(jnp.bfloat16)
+    dc = dot(probs, grads, NN)
+    dc_ref[...] = jnp.where(low, dc[:text], dc[text:]).astype(jnp.bfloat16)
+
+
+def cross_attend(probes, lookups, contents, present):
+    rows, width = probes.shape
+    text = lookups.shape[0]
+    return pl.pallas_call(
+        cross_forward_kernel,
+        out_shape=jax.ShapeDtypeStruct((rows, width), jnp.bfloat16),
+        grid=(width // PAIR,),
+        in_specs=[
+            pair_block(rows),
+            pair_block(text),
+            pair_block(text),
+            pl.BlockSpec((text, 1), lambda i: (0, 0)),
+        ],
+        out_specs=pair_block(rows),
+        compiler_params=pltpu.CompilerParams(vmem_limit_bytes=32 * 2**20),
+        cost_estimate=pl.CostEstimate(
+            flops=8 * rows * text * width, bytes_accessed=4 * rows * width, transcendentals=0
+        ),
+        name="cross_attend",
+    )(probes, lookups, contents, present)
+
+
+def cross_attend_back(probes, lookups, contents, present, grads):
+    rows, width = probes.shape
+    text = lookups.shape[0]
+    return pl.pallas_call(
+        cross_backward_kernel,
+        out_shape=(
+            jax.ShapeDtypeStruct((rows, width), jnp.bfloat16),
+            jax.ShapeDtypeStruct((text, width), jnp.bfloat16),
+            jax.ShapeDtypeStruct((text, width), jnp.bfloat16),
+        ),
+        grid=(width // PAIR,),
+        in_specs=[
+            pair_block(rows),
+            pair_block(text),
+            pair_block(text),
+            pl.BlockSpec((text, 1), lambda i: (0, 0)),
+            pair_block(rows),
+        ],
+        out_specs=(pair_block(rows), pair_block(text), pair_block(text)),
+        compiler_params=pltpu.CompilerParams(vmem_limit_bytes=32 * 2**20),
+        cost_estimate=pl.CostEstimate(
+            flops=20 * rows * text * width, bytes_accessed=6 * rows * width, transcendentals=0
+        ),
+        name="cross_attend_back",
+    )(probes, lookups, contents, present, grads)
+
+
+def unpack_kernel(in_ref, out_ref):
+    pieces = in_ref[...]
+    out_ref[...] = pieces.reshape(-1, pieces.shape[-1]).T.astype(jnp.float32)
+
+
+def unpack(full, rows, place, out_shape, out_at, together):
+    owners, _, features = full.shape
+    tall = out_shape[0] // features
+    wide = out_shape[1] // (together * rows)
+    return pl.pallas_call(
+        unpack_kernel,
+        out_shape=jax.ShapeDtypeStruct(out_shape, jnp.float32),
+        grid=(tall, wide),
+        in_specs=[
+            pl.BlockSpec((together, rows, features), lambda i, j: (j + out_at, place + i, 0))
+        ],
+        out_specs=pl.BlockSpec((features, together * rows), lambda i, j: (i, j)),
+        compiler_params=pltpu.CompilerParams(vmem_limit_bytes=32 * 2**20),
+        cost_estimate=pl.CostEstimate(
+            flops=0, bytes_accessed=6 * out_shape[0] * out_shape[1], transcendentals=0
+        ),
+        name="unpack",
+    )(full)
+
+
+def after(value, *others):
+    return lax.optimization_barrier((value, *others))[0]
+
+
+def norm_parts(values):
+    mean = jnp.mean(values, axis=-1, keepdims=True)
+    center = values - mean
+    return mean, lax.rsqrt(jnp.mean(center * center, axis=-1, keepdims=True) + epsilon)
+
+
+def norm_back(grads, values, parts, gain):
+    mean, inverse = parts
+    unit = (values - mean) * inverse
+    gain_grad = jnp.sum(grads * unit, axis=0)
+    bias_grad = jnp.sum(grads, axis=0)
+    scaled = grads * gain
+    back = inverse * (
+        scaled
+        - jnp.mean(scaled, axis=-1, keepdims=True)
+        - unit * jnp.mean(scaled * unit, axis=-1, keepdims=True)
+    )
+    return back, gain_grad, bias_grad
+
+
+def clip_body(
+    frames,
+    text_states,
+    text_mask,
+    clip_lengths,
+    slot_used,
+    teacher,
+    self_norm_gain,
+    self_norm_bias,
+    self_query_weight,
+    self_key_weight,
+    self_value_weight,
+    self_output_weight,
+    cross_norm_gain,
+    cross_norm_bias,
+    cross_query_weight,
+    cross_key_weight,
+    cross_value_weight,
+    cross_output_weight,
+    feed_norm_gain,
+    feed_norm_bias,
+    feed_up_weight,
+    feed_down_weight,
+):
+    block, width = frames.shape[1:]
+    text_len = text_states.shape[1]
+    shards, replicas, outers = 4, 8, 4
+    core = lax.axis_index("core")
+    shard = lax.axis_index("shard")
+    outer = 2 * lax.axis_index("y") + lax.axis_index("x")
+    replica = 2 * outer + core
+    clip = block * shards
+    hidden_units = feed_up_weight.shape[1]
+
+    holder = {0: 0, 1: 1, 2: 1, 3: 0}
+    there = ([], [])
+    for c in range(2):
+        for s in range(4):
+            for turn in range(2):
+                slot = turn if s < 2 else 1 - turn
+                there[turn].append((c * 4 + s, holder[s] * 4 + 2 * c + slot))
+    back = tuple([(b, a) for a, b in pairs] for pairs in there)
+    spot = ("core", "shard")
+    swap = [(0, 1), (1, 0)]
+    even = shard % 2 == 0
+    lower = shard < 2
+    first_core = core == 0
+
+    def hop(values, distance):
+        pairs = [(i, (i + distance) % shards) for i in range(shards)]
+        return lax.ppermute(values, "shard", pairs)
+
+    def to_chip(pair):
+        one = lax.ppermute(jnp.where(lower, pair[0], pair[1]), spot, there[0])
+        two = lax.ppermute(jnp.where(lower, pair[1], pair[0]), spot, there[1])
+        return jnp.concatenate([jnp.where(even, one, two), jnp.where(even, two, one)], axis=0)
+
+    def from_chip(values):
+        early, late = values[:block], values[block:]
+        one = lax.ppermute(jnp.where(even, early, late), spot, back[0])
+        two = lax.ppermute(jnp.where(even, late, early), spot, back[1])
+        return jnp.stack([jnp.where(lower, one, two), jnp.where(lower, two, one)])
+
+    def share_of(weight):
+        share = weight.shape[0] // replicas
+        return lax.dynamic_slice_in_dim(weight, replica * share, share, 0)
+
+    def whole(parts):
+        return lax.all_gather(jnp.concatenate(parts, axis=1), EVERY, axis=0, tiled=True)
+
+    share = block // replicas
+    facts = jnp.concatenate(
+        [(clip_lengths // 64)[:, None], (clip_lengths % 64)[:, None], slot_used[:, None], text_mask],
+        axis=1,
+    ).astype(jnp.bfloat16)
+    rider = jnp.zeros((share, PAIR), jnp.bfloat16)
+    for i, vector in enumerate(
+        (
+            self_norm_gain,
+            self_norm_bias,
+            cross_norm_gain,
+            cross_norm_bias,
+            feed_norm_gain,
+            feed_norm_bias,
+        )
+    ):
+        rider = rider.at[:, i].set(share_of(vector))
+    rider = rider.at[:2, 8 : 8 + facts.shape[1]].set(facts)
+    first = whole(
+        [
+            share_of(self_query_weight),
+            share_of(self_key_weight),
+            share_of(self_value_weight),
+            rider,
+        ]
+    )
+    x_low = to_chip(frames)
+    teacher_low = to_chip(teacher)
+    rest = whole(
+        [share_of(self_output_weight), share_of(cross_query_weight), share_of(cross_output_weight)]
+    )
+    expand_matrix = whole([share_of(feed_up_weight)])
+
+    quarter_rows = feed_down_weight.shape[0] // 4
+    quarter = 2 * lax.axis_index("x") + core
+    mine = lax.dynamic_slice_in_dim(feed_down_weight, quarter * quarter_rows, quarter_rows, 0)
+    reduce_matrix = jnp.zeros((hidden_units, width), jnp.bfloat16)
+    reduce_matrix = lax.dynamic_update_slice_in_dim(
+        reduce_matrix, feed_down_weight, shard * 4 * quarter_rows, 0
+    )
+    for distance in (1, 2, 3):
+        came = hop(mine, distance)
+        across = lax.ppermute(came, "x", swap)
+        owner = lax.rem(shard + shards - distance, shards)
+        for values, which in (
+            (came, quarter),
+            (across, lax.rem(quarter + 2, 4)),
+            (lax.ppermute(came, "core", swap), quarter + 1 - 2 * core),
+            (lax.ppermute(across, "core", swap), lax.rem(quarter + 3 - 2 * core, 4)),
+        ):
+            reduce_matrix = lax.dynamic_update_slice_in_dim(
+                reduce_matrix, values, (owner * 4 + which) * quarter_rows, 0
+            )
+
+    text_other = lax.ppermute(text_states, "core", swap)
+    text_all = jnp.concatenate(
+        [
+            jnp.where(first_core, text_states, text_other),
+            jnp.where(first_core, text_other, text_states),
+        ],
+        axis=0,
+    ).reshape(4 * text_len, width)
+    text_all = lax.dynamic_slice_in_dim(text_all, shard * block, block, 1)
+    text_matrix = jnp.where(first_core, cross_key_weight, cross_value_weight)
+    text_part = project(text_all, text_matrix).astype(jnp.bfloat16).reshape(4, text_len, width)
+    text_half = lax.dynamic_index_in_dim(text_part, shard, 0, keepdims=False).astype(jnp.float32)
+    for distance in (1, 2, 3):
+        away = lax.dynamic_index_in_dim(
+            text_part, lax.rem(shard + distance, shards), 0, keepdims=False
+        )
+        text_half += hop(away, distance).astype(jnp.float32)
+    text_half = text_half.astype(jnp.bfloat16)
+    text_swap = lax.ppermute(text_half, "core", swap)
+    lookups = jnp.where(first_core, text_half, text_swap)
+    contents = jnp.where(first_core, text_swap, text_half)
+
+    qkv_matrix = first[:, : 3 * width]
+    norms = first[:, 3 * width : 3 * width + 8].astype(jnp.float32).T
+    facts = (
+        first[: replicas * share, 3 * width + 8 : 3 * width + 11 + text_len]
+        .reshape(replicas, share, 3 + text_len)[:, :2]
+        .astype(jnp.int32)
+        .reshape(2 * replicas, 3 + text_len)
+    )
+    lengths = facts[:, 0] * 64 + facts[:, 1]
+    slot = outer * 4 + shard
+    length = lengths[slot]
+    used = facts[slot, 2]
+    present = facts[slot, 3:].reshape(text_len, 1)
+    count = jnp.sum(jnp.where(facts[:, 2] > 0, jnp.minimum(lengths, clip), 0)).astype(jnp.float32)
+    places = jnp.stack([core, 3 - core, length]).astype(jnp.int32)
+    positions = jnp.concatenate(
+        [core * block + jnp.arange(block), (3 - core) * block + jnp.arange(block)]
+    )
+    valid_rows = ((positions < length) & (used > 0)).astype(jnp.float32)[:, None]
+    output_matrix = rest[:, :width]
+    probe_matrix = rest[:, width : 2 * width]
+    merge_matrix = rest[:, 2 * width :]
+
+    inputs = x_low.astype(jnp.float32)
+    parts_one = norm_parts(inputs)
+    hidden_one = ((inputs - parts_one[0]) * parts_one[1] * norms[0] + norms[1]).astype(
+        jnp.bfloat16
+    )
+    kv = project(hidden_one, qkv_matrix[:, width:]).astype(jnp.bfloat16)
+    kv_other = lax.ppermute(kv, "core", swap)
+    queries = project(after(hidden_one, kv), qkv_matrix[:, :width]).astype(jnp.bfloat16)
+
+    def in_order(mine, other):
+        return jnp.concatenate(
+            [
+                jnp.where(first_core, mine[:block], other[:block]),
+                jnp.where(first_core, other[:block], mine[:block]),
+                jnp.where(first_core, other[block:], mine[block:]),
+                jnp.where(first_core, mine[block:], other[block:]),
+            ],
+            axis=0,
+        )
+
+    keys = in_order(kv[:, :width], kv_other[:, :width])
+    values = in_order(kv[:, width:], kv_other[:, width:])
+    mixed_self, lse = self_attend(places, queries, keys, values)
+    after_self = inputs + project(mixed_self, output_matrix)
+    parts_two = norm_parts(after_self)
+    hidden_two = ((after_self - parts_two[0]) * parts_two[1] * norms[2] + norms[3]).astype(
+        jnp.bfloat16
+    )
+    probes = project(hidden_two, probe_matrix).astype(jnp.bfloat16)
+    cross_mixed = cross_attend(probes, lookups, contents, present)
+    after_cross = after_self + project(cross_mixed, merge_matrix)
+    parts_three = norm_parts(after_cross)
+    hidden_three = (
+        (after_cross - parts_three[0]) * parts_three[1] * norms[4] + norms[5]
+    ).astype(jnp.bfloat16)
+    upward = project(hidden_three, expand_matrix)
+    activated, gelu_pull = jax.vjp(exact_gelu, upward)
+    activated_low = activated.astype(jnp.bfloat16)
+    result = after_cross + project(activated_low, reduce_matrix)
+    errors = (result - teacher_low.astype(jnp.float32)) * valid_rows
+    squares = jnp.sum(errors * errors)
+    grad_result = errors * (4 * outers * clip / count)
+    grad_feed_low = grad_result.astype(jnp.bfloat16)
+
+    def theirs_of(right, left):
+        columns = right.shape[1] // 2
+        part = lax.dynamic_slice_in_dim(right, (1 - core) * columns, columns, 1)
+        return outer_sum(part, left).astype(jnp.bfloat16)
+
+    def ours_of(right, left, theirs):
+        columns = right.shape[1] // 2
+        sent = lax.ppermute(theirs, "core", swap)
+        part = lax.dynamic_slice_in_dim(right, core * columns, columns, 1)
+        return (outer_sum(part, left) + sent.astype(jnp.float32)).astype(jnp.bfloat16)
+
+    def over_outer(values):
+        return lax.psum_scatter(values, ("y", "x"), scatter_dimension=0, tiled=True)
+
+    def over_shard(values):
+        columns = values.shape[1] // shards
+        total = lax.dynamic_slice_in_dim(values, shard * columns, columns, 1).astype(jnp.float32)
+        for distance in (1, 2, 3):
+            away = lax.dynamic_slice_in_dim(
+                values, lax.rem(shard + distance, shards) * columns, columns, 1
+            )
+            total += hop(away, distance).astype(jnp.float32)
+        return total.astype(jnp.bfloat16)
+
+    down_theirs = theirs_of(grad_feed_low, activated_low)
+    grad_activated = back_project(after(grad_feed_low, down_theirs), reduce_matrix)
+    grad_upward = gelu_pull(grad_activated)[0].astype(jnp.bfloat16)
+    down_ours = ours_of(after(grad_feed_low, grad_upward), activated_low, down_theirs)
+    down_sum = over_outer(down_ours)
+    up_theirs = theirs_of(after(grad_upward, down_ours), hidden_three)
+    grad_hidden_three = back_project(after(grad_upward, up_theirs), expand_matrix)
+    up_ours = ours_of(after(grad_upward, grad_hidden_three), hidden_three, up_theirs)
+    up_sum = over_outer(up_ours)
+    output = from_chip(after(result.astype(jnp.bfloat16), up_ours))
+    grad_norm, gain_feed, bias_feed = norm_back(
+        after(grad_hidden_three, up_ours), after_cross, parts_three, norms[4]
+    )
+    grad_after_cross = grad_result + grad_norm
+    grad_cross_low = grad_after_cross.astype(jnp.bfloat16)
+    merge_theirs = theirs_of(grad_cross_low, cross_mixed)
+    grad_cross_mixed = back_project(after(grad_cross_low, merge_theirs), merge_matrix).astype(
+        jnp.bfloat16
+    )
+    probe_grads, lookup_grads, content_grads = cross_attend_back(
+        probes, lookups, contents, present, grad_cross_mixed
+    )
+    text_mine = jnp.where(first_core, lookup_grads, content_grads)
+    text_sent = lax.ppermute(
+        jnp.where(first_core, content_grads, lookup_grads), "core", swap
+    )
+    text_mine = (text_mine.astype(jnp.float32) + text_sent.astype(jnp.float32)).astype(
+        jnp.bfloat16
+    )
+    merge_ours = ours_of(after(grad_cross_low, probe_grads), cross_mixed, merge_theirs)
+    probe_theirs = theirs_of(after(probe_grads, merge_ours), hidden_two)
+    grad_hidden_two = back_project(after(probe_grads, probe_theirs), probe_matrix)
+    text_four = jnp.zeros((4, text_len, width), jnp.bfloat16)
+    text_four = lax.dynamic_update_index_in_dim(text_four, text_mine, shard, 0)
+    for distance in (1, 2, 3):
+        text_four = lax.dynamic_update_index_in_dim(
+            text_four,
+            hop(text_mine, distance),
+            lax.rem(shard + shards - distance, shards),
+            0,
+        )
+    text_four = text_four.reshape(4 * text_len, width)
+    grad_norm, gain_cross, bias_cross = norm_back(
+        grad_hidden_two, after_self, parts_two, norms[2]
+    )
+    grad_after_self = grad_after_cross + grad_norm
+    grad_self_low = grad_after_self.astype(jnp.bfloat16)
+    output_theirs = theirs_of(grad_self_low, mixed_self)
+    grad_mixed = back_project(after(grad_self_low, output_theirs), output_matrix).astype(
+        jnp.bfloat16
+    )
+    probe_ours = ours_of(after(probe_grads, grad_mixed), hidden_two, probe_theirs)
+    text_weights = outer_sum(text_four, text_all).astype(jnp.bfloat16)
+    text_back = back_project(text_four, text_matrix).astype(jnp.bfloat16)
+    output_ours = ours_of(after(grad_self_low, probe_ours), mixed_self, output_theirs)
+    text_rows = width // outers
+    middle = jnp.concatenate(
+        [
+            values.reshape(outers, -1, width)
+            for values in (
+                output_ours,
+                probe_ours,
+                merge_ours,
+                text_weights.reshape(outers, shards, text_rows // shards, block)
+                .transpose(0, 2, 1, 3)
+                .reshape(outers, text_rows // shards, width),
+            )
+        ],
+        axis=1,
+    )
+    middle_rows = middle.shape[1]
+    middle = middle.reshape(outers * middle_rows, width)
+    middle_sum = over_outer(middle)
+    text_split = text_rows // shards
+    text_piece = (
+        middle_sum[middle_rows - text_split :]
+        .reshape(text_split, shards, block)
+        .transpose(1, 0, 2)
+        .reshape(text_rows, block)
+    )
+    grad_queries, grad_keys, grad_values = self_attend_back(
+        places, queries, keys, values, mixed_self, after(grad_mixed, middle), lse
+    )
+
+    text_back = text_back.reshape(2, 2, text_len, block)
+    text_kept = lax.dynamic_index_in_dim(text_back, core, 0, keepdims=False)
+    text_gone = lax.dynamic_index_in_dim(text_back, 1 - core, 0, keepdims=False)
+    text_own = text_kept.astype(jnp.float32) + lax.ppermute(text_gone, "core", swap).astype(
+        jnp.float32
+    )
+    text_own = text_own.astype(jnp.bfloat16)
+    text_grad = jnp.zeros(text_states.shape, jnp.float32)
+    text_grad = lax.dynamic_update_slice_in_dim(
+        text_grad, text_own.astype(jnp.float32), shard * block, 2
+    )
+    for distance in (1, 2, 3):
+        text_grad = lax.dynamic_update_slice_in_dim(
+            text_grad,
+            hop(text_own, distance).astype(jnp.float32),
+            lax.rem(shard + shards - distance, shards) * block,
+            2,
+        )
+
+    def gather_sum(grads):
+        quarters = [grads[i * block : (i + 1) * block] for i in range(4)]
+        outside = jnp.concatenate([quarters[0], quarters[3]], axis=0)
+        inside = jnp.concatenate([quarters[1], quarters[2]], axis=0)
+        mine = jnp.where(first_core, outside, inside)
+        other = lax.ppermute(jnp.where(first_core, inside, outside), "core", swap)
+        return (mine.astype(jnp.float32) + other.astype(jnp.float32)).astype(jnp.bfloat16)
+
+    qkv_grads = jnp.concatenate(
+        [grad_queries, gather_sum(grad_keys), gather_sum(grad_values)], axis=1
+    )
+    qkv_theirs = theirs_of(qkv_grads, hidden_one)
+    grad_hidden_one = back_project(after(qkv_grads, qkv_theirs), qkv_matrix)
+    qkv_ours = ours_of(after(qkv_grads, grad_hidden_one), hidden_one, qkv_theirs)
+    qkv_sum = over_outer(qkv_ours)
+    grad_norm, gain_self, bias_self = norm_back(
+        after(grad_hidden_one, qkv_ours), inputs, parts_one, norms[0]
+    )
+    frames_grad = from_chip((grad_after_self + grad_norm).astype(jnp.bfloat16)).astype(
+        jnp.float32
+    )
+
+    small = jnp.stack(
+        [
+            gain_self,
+            bias_self,
+            gain_cross,
+            bias_cross,
+            gain_feed,
+            bias_feed,
+            jnp.full((width,), squares),
+            jnp.zeros((width,), jnp.float32),
+        ]
+    )
+    for axis, pairs in (
+        ("core", swap),
+        ("x", swap),
+        ("y", swap),
+        ("shard", [(0, 1), (1, 0), (2, 3), (3, 2)]),
+        ("shard", [(0, 2), (2, 0), (1, 3), (3, 1)]),
+    ):
+        small += lax.ppermute(small, axis, pairs)
+    loss = small[6, 0] / (width * count)
+    small_own = lax.dynamic_slice_in_dim(small, shard * block, block, 1)
+
+    down_piece = over_shard(down_sum)
+    middle_piece = over_shard(middle_sum[: middle_rows - text_split])
+    early = jnp.concatenate(
+        [over_shard(up_sum)]
+        + [down_piece[:, i * block : (i + 1) * block] for i in range(4)]
+        + [text_piece, middle_piece],
+        axis=0,
+    )
+    early = lax.all_gather(early, REPLICAS, axis=0)
+    piece = width // replicas
+    square = (block, width)
+    up_grad = unpack(early, hidden_units // replicas, 0, (block, hidden_units), 0, 1)
+    at = hidden_units // replicas // piece
+    down_grad = unpack(early, piece, at, (4 * block, width), 0, 2)
+    at += 4
+    key_grad = unpack(early, text_rows, at * piece // text_rows, square, 0, 1)
+    value_grad = unpack(early, text_rows, at * piece // text_rows, square, 4, 1)
+    at += text_rows // piece
+    output_grad = unpack(early, piece, at, square, 0, 2)
+    probe_grad = unpack(early, piece, at + 1, square, 0, 2)
+    merge_grad = unpack(early, piece, at + 2, square, 0, 2)
+    late = lax.all_gather(over_shard(qkv_sum), REPLICAS, axis=0, tiled=True)
+    late = late.reshape(3, width, block)
+    qkv_grad = [late[i].T.astype(jnp.float32) for i in range(3)]
+    return (
+        output,
+        loss,
+        frames_grad,
+        text_grad,
+        small_own[0],
+        small_own[1],
+        qkv_grad[0],
+        qkv_grad[1],
+        qkv_grad[2],
+        output_grad,
+        small_own[2],
+        small_own[3],
+        probe_grad,
+        key_grad,
+        value_grad,
+        merge_grad,
+        small_own[4],
+        small_own[5],
+        up_grad,
+        down_grad,
+    )
+
+
 def solution(mesh):
-    placed = (
-        P("replica", "shard", None),
-        P("replica", None, None),
-        P("replica", None),
-        P("replica"),
-        P("replica"),
-        P("replica", "shard", None),
-        P("shard"),
-        P("shard"),
-        P("shard", None),
-        P("shard", None),
-        P("shard", None),
-        P("shard", None),
-        P("shard"),
-        P("shard"),
-        P("shard", None),
-        P("shard", None),
-        P("shard", None),
-        P("shard", None),
-        P("shard"),
-        P("shard"),
-        P("shard", None),
-        P("shard", None),
-    )
+    by_chip = mesh.shape["shard"] == 4 and mesh.shape["replica"] == 8
+    replica = ("y", "x", "core") if by_chip else "replica"
+    row = P(replica)
+    clip = P(replica, "shard", None)
+    text = P(replica, None, None)
+    vector = P("shard")
+    matrix = P("shard", None)
+    weights = (
+        [vector, vector] + [matrix] * 4 + [vector, vector] + [matrix] * 4 + [vector, vector]
+        + [matrix] * 2
+    )
+    if by_chip:
+        mesh = Mesh(mesh.devices.reshape(2, 2, 2, 4), ("y", "x", "core", "shard"))
     return jax.shard_map(
-        body,
+        clip_body if by_chip else general_body,
         mesh=mesh,
-        in_specs=placed,
-        out_specs=(
-            P("replica", "shard", None),
-            P(),
-            P("replica", "shard", None),
-            P("replica", None, None),
-            P("shard"),
-            P("shard"),
-            P("shard", None),
-            P("shard", None),
-            P("shard", None),
-            P("shard", None),
-            P("shard"),
-            P("shard"),
-            P("shard", None),
-            P("shard", None),
-            P("shard", None),
-            P("shard", None),
-            P("shard"),
-            P("shard"),
-            P("shard", None),
-            P("shard", None),
-        ),
+        in_specs=(clip, text, P(replica, None), row, row, clip, *weights),
+        out_specs=(clip, P(), clip, text, *weights),
         check_vma=False,
     )

time: 4070 us -> 1550 us (0.38)
  waiting for transfers between devices: 2870 us -> 607 us
  matrix products: 668 us -> 302 us
  starting transfers between devices: 2 us -> 214 us
  Pallas kernels: 0 us -> 167 us
  blocking collectives: 146 us -> 0 us
  other arithmetic: 204 us -> 124 us
  local copies, waits for them, and re-layouts: 147 us -> 104 us
    all_gather x12 -> x5, waiting for transfers between devices: 1290 us -> 0.05 us  [the longest x3 0.04 us: whole(): lax.all_gather(jnp.concatenate(parts, axis=1), EVERY, axis=0, tiled=True)]
    reduce_scatter x10 -> x4, waiting for transfers between devices: 1400 us -> 276 us  [over_outer(): return lax.psum_scatter(values, ('y', 'x'), scatter_dimension=0, tiled=True)]
    dot_general x19 -> x0, matrix products: 355 us -> none  [the longest x2 84 us: self_backward(): jnp.einsum('qhd,khd->hqk', grad_mixed, values_all, preferred_element_type...]
    ppermute x0 -> x59, waiting for transfers between devices: none -> 330 us  [the longest x24 286 us: hop(): return lax.ppermute(values, 'shard', pairs)]
    ppermute x0 -> x59, starting transfers between devices: none -> 214 us  [the longest x1 70.7 us: clip_body(): kv_other = lax.ppermute(kv, 'core', swap)]
    psum x2 -> x0, waiting for transfers between devices: 178 us -> none  [the longest x1 178 us: body(): lax.psum(attend_owned[0].astype(jnp.bfloat16), 'replica')]
    pallas_call x0 -> x11, Pallas kernels: none -> 167 us  [the longest x1 68.9 us: self_attend_back(): pl.pallas_call(self_backward_kernel, out_shape=(jax.ShapeDtypeStruct((row...]
    convert_element_type x31 -> x13, other arithmetic: 136 us -> 43 us  [the longest x1 11.3 us: clip_body(): grad_cross_low = grad_after_cross.astype(jnp.bfloat16)]
  transfers between devices with their start and end apart: 24 -> 68, of which waited for: 22 -> 24; matrix products, arithmetic and copies ran while one was open for 12% -> 19% of each run, Pallas kernels for 0% -> 5%
where the time goes in v1:
time: 1550 us; the launch traced here: 1540 us
  waiting for transfers between devices  607 us (39%)
  matrix products  302 us (19%)
  starting transfers between devices  214 us (14%)
  Pallas kernels  167 us (11%)
  other arithmetic  124 us (8%)
  local copies, waits for them, and re-layouts  104 us (7%)
  between operations  18.3 us (1%)
    ppermute x24, waiting for transfers between devices, hop(): return lax.ppermute(values, 'shard', pairs)  286 us
    reduce_scatter x4, waiting for transfers between devices, over_outer(): return lax.psum_scatter(values, ('y', 'x'), scatter_dimension=0, tiled=True)  276 us
    dot_general x8, matrix products, project(): return jnp.dot(left, right, preferred_element_type=jnp.float32)  122 us
    dot_general x7, matrix products, back_project(): jnp.einsum('re,de->rd', grads, matrix, preferred_element_type=jnp.float32)  92.3 us
    dot_general x13, matrix products, outer_sum(): jnp.einsum('rd,re->de', left, right, preferred_element_type=jnp.float32)  88.3 us
    ppermute x1, starting transfers between devices, clip_body(): kv_other = lax.ppermute(kv, 'core', swap)  70.7 us
    pallas_call x1, Pallas kernels, self_attend_back(): pl.pallas_call(self_backward_kernel, out_shape=(jax.ShapeDtypeStruct((row...  68.9 us
    pallas_call x1, Pallas kernels, self_attend(): pl.pallas_call(self_forward_kernel, out_shape=(jax.ShapeDtypeStruct((rows...  57.8 us
  transfers between devices with their start and end apart: 68, of which 24 were waited for; matrix products, arithmetic and copies ran while one was open for 19% of the time, Pallas kernels for 5%

profile of v1, /device:TPU:0, one launch (start us, length us, event | category | flops | bytes accessed | tf_op | source)
XLA Modules:
  0.0 1537.4 jit_solution(13774749187123523172)
XLA Ops:
  64.6 6.7 broadcast_in_dim.53
  76.5 84.5 %collective-permute-done.4 = bf16[64,1536]{1,0:T(8,128)(2,1)S(1)} collective-permute-done((bf16[64,1536]{1,0:T(8,128)(2,1)S(1)}, bf16[64,1536]{1,0:T(8,128)(2,1)S(1)}, u32[]{:S(2)}, u32[]{:S(2)}) %collective-permute-start.4) | collective-permute-done | bytes 196640 | tf_op jit(solution)/shard_map/ppermute | solution.py:801
  162.6 61.6 %collective-permute-done.5 = bf16[64,1536]{1,0:T(8,128)(2,1)} collective-permute-done((bf16[64,1536]{1,0:T(8,128)(2,1)}, bf16[64,1536]{1,0:T(8,128)(2,1)}, u32[]{:S(2)}, u32[]{:S(2)}) %collective-permute-start.5) | collective-permute-done | bytes 196640 | tf_op jit(solution)/shard_map/ppermute | solution.py:801
  230.4 8.8 collective-permute-start.16
  239.2 10.3 collective-permute-start.20
  262.8 18.7 %collective-permute-done.12 = bf16[384,1536]{1,0:T(8,128)(2,1)} collective-permute-done((bf16[384,1536]{1,0:T(8,128)(2,1)}, bf16[384,1536]{1,0:T(8,128)(2,1)}, u32[]{:S(2)}, u32[]{:S(2)}) %collective-permute-start.12) | collective-permute-done | bytes 1179680 | tf_op jit(solution)/shard_map/ppermute | solution.py:801
  292.6 13.6 fusion.16
  306.5 24.8 %collective-permute-start.11 = (bf16[384,1536]{1,0:T(8,128)(2,1)}, bf16[384,1536]{1,0:T(8,128)(2,1)S(1)}, u32[]{:S(2)}, u32[]{:S(2)}) collective-permute-start(bf16[384,1536]{1,0:T(8,128)(2,1)} %collective-permute-done.9), channel_id=1, source_target_pairs={{0,4},{4,0},{1,5},{5,1},{2,6},{6,2},{3,7},{7,3},{8,12},{12,8},{9,1... | collective-permute-start | bytes 3538952 | tf_op jit(solution)/shard_map/ppermute | solution.py:869
  331.2 7.9 collective-permute-done.21
  339.2 70.7 %collective-permute-start.2 = (bf16[768,3072]{1,0:T(8,128)(2,1)}, bf16[768,3072]{1,0:T(8,128)(2,1)}, u32[]{:S(2)}, u32[]{:S(2)}) collective-permute-start(bf16[768,3072]{1,0:T(8,128)(2,1)} %fusion.16), channel_id=1, source_target_pairs={{0,4},{4,0},{1,5},{5,1},{2,6},{6,2},{3,7},{7,3},{8,12},{12,8},{9,1... | collective-permute-start | bytes 14155784 | tf_op jit(solution)/shard_map/ppermute | solution.py:926
  439.2 6.3 fusion.66.q_ref
  452.9 57.8 %self_attend.1 = (bf16[768,1536]{1,0:T(8,128)(2,1)S(1)}, f32[96,768]{1,0:T(8,128)S(1)}) custom-call(s32[3]{0:T(128)S(1)} %pad_add_fusion.place, bf16[768,1536]{1,0:T(8,128)(2,1)S(1)} %fusion.66.q_ref, bf16[1536,1536]{1,0:T(8,128)(2,1)S(1)} %pad_maximum_fusion.2.k_ref, bf16[1536,1536]{1,0:T(8,128)(2,1)S(1)} %pad_maximum_fusion.3.v_ref), custom_call_target="tpu_custom_call" | custom-call | flops 7247757312 | bytes 18874368 | tf_op jit(solution)/shard_map/self_attend/pallas_call | solution.py:545
  512.8 7.8 fusion.122
  527.3 6.8 cross_attend.1
  540.9 60.8 %multiply_convert_fusion = (bf16[768,6144]{1,0:T(8,128)(2,1)S(1)}, f32[768,6144]{1,0:T(8,128)}, f32[768,6144]{1,0:T(8,128)}) fusion(bf16[1536,6144]{1,0:T(8,128)(2,1)} %all-gather.11.cloned.1.call-done, f32[768,1536]{1,0:T(8,128)} %copy-done.27, f32[1536]{0:T(1024)S(1)} %get-tuple-element.251, f32[1536]{0:T(1024)S(1)} %get-tuple-element.250, ...), kind=kOutput, calls=%fused_computation.5 | convolution fusion | flops 14808121344 | bytes 70797312 | tf_op jit(solution)/shard_map/dot_general | solution.py:28
  601.8 23.0 %multiply_convert_fusion.1 = (bf16[768,1536]{1,0:T(8,128)(2,1)}, f32[768,1536]{1,0:T(8,128)}) fusion(f32[]{:T(128)S(6)} %div.64, f32[768]{0:T(1024)S(1)} %copy-done.70, bf16[384,1536]{1,0:T(8,128)(2,1)S(1)} %copy-done.42, bf16[384,1536]{1,0:T(8,128)(2,1)S(1)} %copy-done.41, f32[768,1536]{1,0:T(8,128)S(1)} %copy-done.28, ...), kind=kOutput, calls=%fused_computation.72 | convolution fusion | flops 14506131456 | bytes 42470404 | tf_op jit(solution)/shard_map/dot_general | solution.py:28
  624.8 11.3 convolution_convert_fusion.2
  636.2 29.6 %add_convert_fusion.2 = bf16[768,6144]{1,0:T(8,128)(2,1)} fusion(f32[768,6144]{1,0:T(8,128)} %get-tuple-element.273, f32[768,6144]{1,0:T(8,128)} %get-tuple-element.334, bf16[768,1536]{1,0:T(8,128)(2,1)} %get-tuple-element.134, bf16[6144,1536]{1,0:T(8,128)(2,1)} %constant_dynamic-update-slice_fusion), kind=kOutput, calls=%fused_computation.4 | convolution fusion | flops 14561574912 | bytes 68419584 | tf_op jit(solution)/shard_map/re,de->rd/dot_general | solution.py:36
  665.9 14.8 add_convert_fusion.1
  680.6 13.9 convolution_convert_fusion.1
  694.9 21.3 %fusion.125 = f32[768,1536]{1,0:T(8,128)} fusion(bf16[768,6144]{1,0:T(8,128)(2,1)} %add_convert_fusion.2, bf16[1536,6144]{1,0:T(8,128)(2,1)} %all-gather.11.cloned.1.call-done), kind=kOutput, calls=%fused_computation.312 | convolution fusion | flops 14495514624 | bytes 33030144 | tf_op jit(solution)/shard_map/re,de->rd/dot_general | solution.py:36
  716.2 13.6 add_convert_fusion
  735.6 11.3 fusion.117
  749.2 6.6 fusion.63.grad_ref
  755.9 9.5 cross_attend_back.1
  782.7 7.6 multiply_reduce_fusion.2
  798.5 7.5 fusion.57.grad_ref
  818.8 68.9 %self_attend_back.1 = (bf16[768,1536]{1,0:T(8,128)(2,1)S(1)}, bf16[1536,1536]{1,0:T(8,128)(2,1)S(1)}, bf16[1536,1536]{1,0:T(8,128)(2,1)S(1)}) custom-call(s32[3]{0:T(128)S(1)} %copy-done.20, bf16[768,1536]{1,0:T(8,128)(2,1)S(1)} %copy-done.24, bf16[1536,1536]{1,0:T(8,128)(2,1)} %copy-done.6, bf16[1536,1536]{1,0:T(8,128)(2,1)} %copy-done.5, ...), custom_call_target="tpu_custom_call" | custom-call | flops 18119393280 | bytes 37748736 | tf_op jit(solution)/shard_map/self_attend_back/pallas_call | solution.py:570
  904.6 7.7 convolution_convert_fusion
  912.3 17.4 %fusion.6 = f32[768,1536]{1,0:T(8,128)} fusion(bf16[768,4608]{1,0:T(8,128)(2,1)} %copy-done.39, bf16[1536,4736]{1,0:T(8,128)(2,1)} %all-gather.7.cloned.1.call-done), kind=kOutput, calls=%fused_computation.19 | convolution fusion | flops 10871635968 | bytes 25952256 | tf_op jit(solution)/shard_map/re,de->rd/dot_general | solution.py:36
  929.8 9.7 add_convert_fusion.3
  941.5 80.9 %reduce-scatter.5.cloned.1.call-done = bf16[576,1536]{1,0:T(8,128)(2,1)} async-done(((bf16[2304,1536]{1,0:T(8,128)(2,1)}), bf16[576,1536]{1,0:T(8,128)(2,1)}) %reduce-scatter.5.cloned.1.call-update) | async-done | bytes 1769488 | tf_op jit(solution)/shard_map/reduce_scatter | solution.py:976
  1029.4 9.4 collective-permute-done.47
  1038.8 17.8 %collective-permute-done.48 = bf16[576,384]{1,0:T(8,128)(2,1)S(1)} collective-permute-done((bf16[576,384]{1,0:T(8,128)(2,1)S(1)}, bf16[576,384]{1,0:T(8,128)(2,1)S(1)}, u32[]{:S(2)}, u32[]{:S(2)}) %collective-permute-start.48) | collective-permute-done | bytes 442400 | tf_op jit(solution)/shard_map/ppermute | solution.py:801
  1058.7 61.6 %reduce-scatter.9.cloned.1.call-done = bf16[192,6144]{1,0:T(8,128)(2,1)} async-done(((bf16[768,6144]{1,0:T(8,128)(2,1)}), bf16[192,6144]{1,0:T(8,128)(2,1)}) %reduce-scatter.9.cloned.1.call-update) | async-done | bytes 2359312 | tf_op jit(solution)/shard_map/reduce_scatter | solution.py:976
  1127.3 91.7 %reduce-scatter.7.cloned.1.call-done = bf16[768,1536]{1,0:T(8,128)(2,1)} async-done(((bf16[3072,1536]{1,0:T(8,128)(2,1)}), bf16[768,1536]{1,0:T(8,128)(2,1)}) %reduce-scatter.7.cloned.1.call-update) | async-done | bytes 2359312 | tf_op jit(solution)/shard_map/reduce_scatter | solution.py:976
  1227.3 11.5 collective-permute-done.50
  1238.8 24.1 %collective-permute-done.51 = bf16[768,384]{1,0:T(8,128)(2,1)S(1)} collective-permute-done((bf16[768,384]{1,0:T(8,128)(2,1)S(1)}, bf16[768,384]{1,0:T(8,128)(2,1)S(1)}, u32[]{:S(2)}, u32[]{:S(2)}) %collective-permute-start.51) | collective-permute-done | bytes 589856 | tf_op jit(solution)/shard_map/ppermute | solution.py:801
  1266.6 41.5 %reduce-scatter.11.cloned.1.call-done = bf16[672,1536]{1,0:T(8,128)(2,1)} async-done(((bf16[2688,1536]{1,0:T(8,128)(2,1)}), bf16[672,1536]{1,0:T(8,128)(2,1)}) %reduce-scatter.11.cloned.1.call-update) | async-done | bytes 2064400 | tf_op jit(solution)/shard_map/reduce_scatter | solution.py:976
  1318.4 7.7 collective-permute-done.56
  1326.1 17.9 %collective-permute-done.57 = bf16[576,384]{1,0:T(8,128)(2,1)} collective-permute-done((bf16[576,384]{1,0:T(8,128)(2,1)}, bf16[576,384]{1,0:T(8,128)(2,1)}, u32[]{:S(2)}, u32[]{:S(2)}) %collective-permute-start.57) | collective-permute-done | bytes 442400 | tf_op jit(solution)/shard_map/ppermute | solution.py:801
  1351.5 9.9 collective-permute-start.44
  1367.2 10.3 collective-permute-start.24
  1406.2 21.3 %collective-permute-done.45 = bf16[2,64,384]{2,1,0:T(8,128)(2,1)} collective-permute-done((bf16[2,64,384]{2,1,0:T(8,128)(2,1)}, bf16[2,64,384]{2,1,0:T(8,128)(2,1)}, u32[]{:S(2)}, u32[]{:S(2)}) %collective-permute-start.45) | collective-permute-done | bytes 98336 | tf_op jit(solution)/shard_map/ppermute | solution.py:801
  1427.5 10.3 collective-permute-start.41
  1449.6 20.3 %collective-permute-done.39 = f32[8,1536]{1,0:T(8,128)S(1)} collective-permute-done((f32[8,1536]{1,0:T(8,128)S(1)}, f32[8,1536]{1,0:T(8,128)S(1)}, u32[]{:S(2)}, u32[]{:S(2)}) %collective-permute-start.39) | collective-permute-done | bytes 49184 | tf_op jit(solution)/shard_map/ppermute | solution.py:1132
  1471.6 9.5 collective-permute-done.40
  1510.5 8.1 unpack.13
  (469 shorter events, 344.5 us)
Async XLA Ops:
  7.2 250.0 %all-gather.7.cloned.1.call-start = ((), (), s32[]{:S(2)}) async-start(), calls=%async_computation.4 | async-start | bytes 15003648 | tf_op jit(solution)/shard_map/all_gather | solution.py:819
  41.5 471.2 %all-gather.9.cloned.1.call-start = ((), (), s32[]{:S(2)}) async-start(), calls=%async_computation.5 | async-start | bytes 14598144 | tf_op jit(solution)/shard_map/all_gather | solution.py:819
  44.3 496.5 %all-gather.11.cloned.1.call-start = ((), (), s32[]{:S(2)}) async-start(), calls=%async_computation.6 | async-start | bytes 19464192 | tf_op jit(solution)/shard_map/all_gather | solution.py:819
  46.3 976.0 %reduce-scatter.5.cloned.1.call-start = ((), (), s32[]{:S(2)}) async-start(), calls=%async_computation.7 | async-start | bytes 8847360 | tf_op jit(solution)/shard_map/reduce_scatter | solution.py:976
  48.8 190.4 %collective-permute-start.8 = (bf16[384,1536]{1,0:T(8,128)(2,1)}, bf16[384,1536]{1,0:T(8,128)(2,1)}, u32[]{:S(2)}, u32[]{:S(2)}) collective-permute-start(bf16[384,1536]{1,0:T(8,128)(2,1)} %constant_dynamic-slice_fusion.13), channel_id=1, source_target_pairs={{0,1},{1,2},{2,3},{3,0},{4,5},{5,6},{6,7},{7,4},{8,9},{9,10},{10,1... | collective-permute-start | bytes 3538952 | tf_op jit(solution)/shard_map/ppermute | solution.py:801
  53.4 196.2 %collective-permute-start = (bf16[384,1536]{1,0:T(8,128)(2,1)}, bf16[384,1536]{1,0:T(8,128)(2,1)S(1)}, u32[]{:S(2)}, u32[]{:S(2)}) collective-permute-start(bf16[384,1536]{1,0:T(8,128)(2,1)} %get-tuple-element.311), channel_id=1, source_target_pairs={{0,0},{1,4},{2,5},{3,1},{4,2},{5,6},{6,7},{7,3},{8,8},{9,12},{10,1... | collective-permute-start | bytes 3538952 | tf_op jit(solution)/shard_map/ppermute | solution.py:804
  55.3 196.2 %collective-permute-start.1 = (bf16[384,1536]{1,0:T(8,128)(2,1)}, bf16[384,1536]{1,0:T(8,128)(2,1)S(1)}, u32[]{:S(2)}, u32[]{:S(2)}) collective-permute-start(bf16[384,1536]{1,0:T(8,128)(2,1)} %get-tuple-element.312), channel_id=1, source_target_pairs={{0,1},{1,5},{2,4},{3,0},{4,3},{5,7},{6,6},{7,2},{8,9},{9,13},{10,1... | collective-permute-start | bytes 3538952 | tf_op jit(solution)/shard_map/ppermute | solution.py:805
  63.4 97.6 %collective-permute-start.4 = (bf16[64,1536]{1,0:T(8,128)(2,1)S(1)}, bf16[64,1536]{1,0:T(8,128)(2,1)S(1)}, u32[]{:S(2)}, u32[]{:S(2)}) collective-permute-start(bf16[64,1536]{1,0:T(8,128)(2,1)S(1)} %get-tuple-element.319), channel_id=1, source_target_pairs={{0,1},{1,2},{2,3},{3,0},{4,5},{5,6},{6,7},{7,4},{8,9},{9,10},{10,1... | collective-permute-start | bytes 589832 | tf_op jit(solution)/shard_map/ppermute | solution.py:801
  73.7 150.4 %collective-permute-start.5 = (bf16[64,1536]{1,0:T(8,128)(2,1)}, bf16[64,1536]{1,0:T(8,128)(2,1)}, u32[]{:S(2)}, u32[]{:S(2)}) collective-permute-start(bf16[64,1536]{1,0:T(8,128)(2,1)} %get-tuple-element.321), channel_id=1, source_target_pairs={{0,2},{1,3},{2,0},{3,1},{4,6},{5,7},{6,4},{7,5},{8,10},{9,11},{10,... | collective-permute-start | bytes 589832 | tf_op jit(solution)/shard_map/ppermute | solution.py:801
  161.0 63.2 %collective-permute-start.6 = (bf16[64,1536]{1,0:T(8,128)(2,1)S(1)}, bf16[64,1536]{1,0:T(8,128)(2,1)}, u32[]{:S(2)}, u32[]{:S(2)}) collective-permute-start(bf16[64,1536]{1,0:T(8,128)(2,1)S(1)} %get-tuple-element.320), channel_id=1, source_target_pairs={{0,3},{1,0},{2,1},{3,2},{4,7},{5,4},{6,5},{7,6},{8,11},{9,8},{10,9... | collective-permute-start | bytes 589832 | tf_op jit(solution)/shard_map/ppermute | solution.py:801
  224.2 57.3 %collective-permute-start.12 = (bf16[384,1536]{1,0:T(8,128)(2,1)}, bf16[384,1536]{1,0:T(8,128)(2,1)}, u32[]{:S(2)}, u32[]{:S(2)}) collective-permute-start(bf16[384,1536]{1,0:T(8,128)(2,1)} %constant_dynamic-slice_fusion.13), channel_id=1, source_target_pairs={{0,2},{1,3},{2,0},{3,1},{4,6},{5,7},{6,4},{7,5},{8,10},{9,11},{10,... | collective-permute-start | bytes 3538952 | tf_op jit(solution)/shard_map/ppermute | solution.py:801
  230.4 60.5 %collective-permute-start.16 = (bf16[384,1536]{1,0:T(8,128)(2,1)}, bf16[384,1536]{1,0:T(8,128)(2,1)}, u32[]{:S(2)}, u32[]{:S(2)}) collective-permute-start(bf16[384,1536]{1,0:T(8,128)(2,1)} %constant_dynamic-slice_fusion.13), channel_id=1, source_target_pairs={{0,3},{1,0},{2,1},{3,2},{4,7},{5,4},{6,5},{7,6},{8,11},{9,8},{10,9... | collective-permute-start | bytes 3538952 | tf_op jit(solution)/shard_map/ppermute | solution.py:801
  239.2 66.9 %collective-permute-start.20 = (bf16[384,1536]{1,0:T(8,128)(2,1)}, bf16[384,1536]{1,0:T(8,128)(2,1)}, u32[]{:S(2)}, u32[]{:S(2)}) collective-permute-start(bf16[384,1536]{1,0:T(8,128)(2,1)} %get-tuple-element.307), channel_id=1, source_target_pairs={{0,0},{1,4},{2,5},{3,1},{4,2},{5,6},{6,7},{7,3},{8,8},{9,12},{10,1... | collective-permute-start | bytes 3538952 | tf_op jit(solution)/shard_map/ppermute | solution.py:804
  249.6 89.6 %collective-permute-start.21 = (bf16[384,1536]{1,0:T(8,128)(2,1)}, bf16[384,1536]{1,0:T(8,128)(2,1)}, u32[]{:S(2)}, u32[]{:S(2)}) collective-permute-start(bf16[384,1536]{1,0:T(8,128)(2,1)} %get-tuple-element.308), channel_id=1, source_target_pairs={{0,1},{1,5},{2,4},{3,0},{4,3},{5,7},{6,6},{7,2},{8,9},{9,13},{10,1... | collective-permute-start | bytes 3538952 | tf_op jit(solution)/shard_map/ppermute | solution.py:805
  252.5 53.9 %collective-permute-start.9 = (bf16[384,1536]{1,0:T(8,128)(2,1)}, bf16[384,1536]{1,0:T(8,128)(2,1)}, u32[]{:S(2)}, u32[]{:S(2)}) collective-permute-start(bf16[384,1536]{1,0:T(8,128)(2,1)} %collective-permute-done.8), channel_id=1, source_target_pairs={{0,8},{8,0},{1,9},{9,1},{2,10},{10,2},{3,11},{11,3},{4,12},{12,4},... | collective-permute-start | bytes 3538952 | tf_op jit(solution)/shard_map/ppermute | solution.py:863
  281.4 134.1 %collective-permute-start.10 = (bf16[384,1536]{1,0:T(8,128)(2,1)}, bf16[384,1536]{1,0:T(8,128)(2,1)S(1)}, u32[]{:S(2)}, u32[]{:S(2)}) collective-permute-start(bf16[384,1536]{1,0:T(8,128)(2,1)} %collective-permute-done.8), channel_id=1, source_target_pairs={{0,4},{4,0},{1,5},{5,1},{2,6},{6,2},{3,7},{7,3},{8,12},{12,8},{9,1... | collective-permute-start | bytes 3538952 | tf_op jit(solution)/shard_map/ppermute | solution.py:868
  290.9 127.1 %collective-permute-start.13 = (bf16[384,1536]{1,0:T(8,128)(2,1)}, bf16[384,1536]{1,0:T(8,128)(2,1)S(1)}, u32[]{:S(2)}, u32[]{:S(2)}) collective-permute-start(bf16[384,1536]{1,0:T(8,128)(2,1)} %collective-permute-done.12), channel_id=1, source_target_pairs={{0,8},{8,0},{1,9},{9,1},{2,10},{10,2},{3,11},{11,3},{4,12},{12,4},... | collective-permute-start | bytes 3538952 | tf_op jit(solution)/shard_map/ppermute | solution.py:863
  306.2 113.5 %collective-permute-start.17 = (bf16[384,1536]{1,0:T(8,128)(2,1)}, bf16[384,1536]{1,0:T(8,128)(2,1)S(1)}, u32[]{:S(2)}, u32[]{:S(2)}) collective-permute-start(bf16[384,1536]{1,0:T(8,128)(2,1)} %collective-permute-done.16), channel_id=1, source_target_pairs={{0,8},{8,0},{1,9},{9,1},{2,10},{10,2},{3,11},{11,3},{4,12},{12,4},... | collective-permute-start | bytes 3538952 | tf_op jit(solution)/shard_map/ppermute | solution.py:863
  306.5 113.3 %collective-permute-start.11 = (bf16[384,1536]{1,0:T(8,128)(2,1)}, bf16[384,1536]{1,0:T(8,128)(2,1)S(1)}, u32[]{:S(2)}, u32[]{:S(2)}) collective-permute-start(bf16[384,1536]{1,0:T(8,128)(2,1)} %collective-permute-done.9), channel_id=1, source_target_pairs={{0,4},{4,0},{1,5},{5,1},{2,6},{6,2},{3,7},{7,3},{8,12},{12,8},{9,1... | collective-permute-start | bytes 3538952 | tf_op jit(solution)/shard_map/ppermute | solution.py:869
  339.2 106.4 %collective-permute-start.2 = (bf16[768,3072]{1,0:T(8,128)(2,1)}, bf16[768,3072]{1,0:T(8,128)(2,1)}, u32[]{:S(2)}, u32[]{:S(2)}) collective-permute-start(bf16[768,3072]{1,0:T(8,128)(2,1)} %fusion.16), channel_id=1, source_target_pairs={{0,4},{4,0},{1,5},{5,1},{2,6},{6,2},{3,7},{7,3},{8,12},{12,8},{9,1... | collective-permute-start | bytes 14155784 | tf_op jit(solution)/shard_map/ppermute | solution.py:926
  636.1 29.8 %collective-permute-start.22 = (bf16[768,6144]{1,0:T(8,128)(2,1)}, bf16[768,6144]{1,0:T(8,128)(2,1)}, u32[]{:S(2)}, u32[]{:S(2)}) collective-permute-start(bf16[768,6144]{1,0:T(8,128)(2,1)} %convolution_convert_fusion.2), channel_id=1, source_target_pairs={{0,4},{4,0},{1,5},{5,1},{2,6},{6,2},{3,7},{7,3},{8,12},{12,8},{9,1... | collective-permute-start | bytes 28311560 | tf_op jit(solution)/shard_map/ppermute | solution.py:971
  749.0 28.0 %collective-permute-start.26 = (bf16[768,1536]{1,0:T(8,128)(2,1)S(1)}, bf16[768,1536]{1,0:T(8,128)(2,1)S(1)}, u32[]{:S(2)}, u32[]{:S(2)}) collective-permute-start(bf16[768,1536]{1,0:T(8,128)(2,1)S(1)} %convolution_convert_fusion.5), channel_id=1, source_target_pairs={{0,4},{4,0},{1,5},{5,1},{2,6},{6,2},{3,7},{7,3},{8,12},{12,8},{9,1... | collective-permute-start | bytes 7077896 | tf_op jit(solution)/shard_map/ppermute | solution.py:971
  767.6 28.8 %collective-permute-start.31 = (bf16[64,1536]{1,0:T(8,128)(2,1)S(1)}, bf16[64,1536]{1,0:T(8,128)(2,1)S(1)}, u32[]{:S(2)}, u32[]{:S(2)}) collective-permute-start(bf16[64,1536]{1,0:T(8,128)(2,1)S(1)} %get-tuple-element.265), channel_id=1, source_target_pairs={{0,2},{1,3},{2,0},{3,1},{4,6},{5,7},{6,4},{7,5},{8,10},{9,11},{10,... | collective-permute-start | bytes 589832 | tf_op jit(solution)/shard_map/ppermute | solution.py:801
  770.3 26.1 %collective-permute-start.32 = (bf16[64,1536]{1,0:T(8,128)(2,1)S(1)}, bf16[64,1536]{1,0:T(8,128)(2,1)S(1)}, u32[]{:S(2)}, u32[]{:S(2)}) collective-permute-start(bf16[64,1536]{1,0:T(8,128)(2,1)S(1)} %get-tuple-element.265), channel_id=1, source_target_pairs={{0,3},{1,0},{2,1},{3,2},{4,7},{5,4},{6,5},{7,6},{8,11},{9,8},{10,9... | collective-permute-start | bytes 589832 | tf_op jit(solution)/shard_map/ppermute | solution.py:801
  782.6 23.4 %collective-permute-start.27 = (bf16[768,1536]{1,0:T(8,128)(2,1)}, bf16[768,1536]{1,0:T(8,128)(2,1)}, u32[]{:S(2)}, u32[]{:S(2)}) collective-permute-start(bf16[768,1536]{1,0:T(8,128)(2,1)} %convolution_convert_fusion.4), channel_id=1, source_target_pairs={{0,4},{4,0},{1,5},{5,1},{2,6},{6,2},{3,7},{7,3},{8,12},{12,8},{9,1... | collective-permute-start | bytes 7077896 | tf_op jit(solution)/shard_map/ppermute | solution.py:971
  939.5 180.8 %reduce-scatter.9.cloned.1.call-start = ((), (), s32[]{:S(2)}) async-start(), calls=%async_computation.10 | async-start | bytes 11796480 | tf_op jit(solution)/shard_map/reduce_scatter | solution.py:976
  940.1 278.9 %reduce-scatter.7.cloned.1.call-start = ((), (), s32[]{:S(2)}) async-start(), calls=%async_computation.9 | async-start | bytes 11796480 | tf_op jit(solution)/shard_map/reduce_scatter | solution.py:976
  940.7 367.4 %reduce-scatter.11.cloned.1.call-start = ((), (), s32[]{:S(2)}) async-start(), calls=%async_computation.11 | async-start | bytes 10321920 | tf_op jit(solution)/shard_map/reduce_scatter | solution.py:976
  941.4 545.8 %all-gather.13.cloned.1.call-start = ((), (), s32[]{:S(2)}) async-start(), calls=%async_computation.8 | async-start | bytes 3981312 | tf_op jit(solution)/shard_map/all_gather | solution.py:1157
  1025.3 31.3 %collective-permute-start.48 = (bf16[576,384]{1,0:T(8,128)(2,1)S(1)}, bf16[576,384]{1,0:T(8,128)(2,1)S(1)}, u32[]{:S(2)}, u32[]{:S(2)}) collective-permute-start(bf16[576,384]{1,0:T(8,128)(2,1)S(1)} %get-tuple-element.318), channel_id=1, source_target_pairs={{0,2},{1,3},{2,0},{3,1},{4,6},{5,7},{6,4},{7,5},{8,10},{9,11},{10,... | collective-permute-start | bytes 1327112 | tf_op jit(solution)/shard_map/ppermute | solution.py:801
  1027.7 28.9 %collective-permute-start.49 = (bf16[576,384]{1,0:T(8,128)(2,1)S(1)}, bf16[576,384]{1,0:T(8,128)(2,1)S(1)}, u32[]{:S(2)}, u32[]{:S(2)}) collective-permute-start(bf16[576,384]{1,0:T(8,128)(2,1)S(1)} %get-tuple-element.317), channel_id=1, source_target_pairs={{0,3},{1,0},{2,1},{3,2},{4,7},{5,4},{6,5},{7,6},{8,11},{9,8},{10,9... | collective-permute-start | bytes 1327112 | tf_op jit(solution)/shard_map/ppermute | solution.py:801
  1058.7 441.3 %all-gather.15.cloned.1.call-start = ((), (), s32[]{:S(2)}) async-start(), calls=%async_computation.12 | async-start | bytes 17252352 | tf_op jit(solution)/shard_map/all_gather | solution.py:1144
  1121.9 102.6 %collective-permute-start.53 = (bf16[192,1536]{1,0:T(8,128)(2,1)S(1)}, bf16[192,1536]{1,0:T(8,128)(2,1)S(1)}, u32[]{:S(2)}, u32[]{:S(2)}) collective-permute-start(bf16[192,1536]{1,0:T(8,128)(2,1)S(1)} %get-tuple-element.291), channel_id=1, source_target_pairs={{0,1},{1,2},{2,3},{3,0},{4,5},{5,6},{6,7},{7,4},{8,9},{9,10},{10,1... | collective-permute-start | bytes 1769480 | tf_op jit(solution)/shard_map/ppermute | solution.py:801
  1123.5 102.5 %collective-permute-start.54 = (bf16[192,1536]{1,0:T(8,128)(2,1)S(1)}, bf16[192,1536]{1,0:T(8,128)(2,1)S(1)}, u32[]{:S(2)}, u32[]{:S(2)}) collective-permute-start(bf16[192,1536]{1,0:T(8,128)(2,1)S(1)} %get-tuple-element.293), channel_id=1, source_target_pairs={{0,2},{1,3},{2,0},{3,1},{4,6},{5,7},{6,4},{7,5},{8,10},{9,11},{10,... | collective-permute-start | bytes 1769480 | tf_op jit(solution)/shard_map/ppermute | solution.py:801
  1125.9 100.1 %collective-permute-start.55 = (bf16[192,1536]{1,0:T(8,128)(2,1)S(1)}, bf16[192,1536]{1,0:T(8,128)(2,1)S(1)}, u32[]{:S(2)}, u32[]{:S(2)}) collective-permute-start(bf16[192,1536]{1,0:T(8,128)(2,1)S(1)} %get-tuple-element.292), channel_id=1, source_target_pairs={{0,3},{1,0},{2,1},{3,2},{4,7},{5,4},{6,5},{7,6},{8,11},{9,8},{10,9... | collective-permute-start | bytes 1769480 | tf_op jit(solution)/shard_map/ppermute | solution.py:801
  1222.1 40.8 %collective-permute-start.51 = (bf16[768,384]{1,0:T(8,128)(2,1)S(1)}, bf16[768,384]{1,0:T(8,128)(2,1)S(1)}, u32[]{:S(2)}, u32[]{:S(2)}) collective-permute-start(bf16[768,384]{1,0:T(8,128)(2,1)S(1)} %get-tuple-element.296), channel_id=1, source_target_pairs={{0,2},{1,3},{2,0},{3,1},{4,6},{5,7},{6,4},{7,5},{8,10},{9,11},{10,... | collective-permute-start | bytes 1769480 | tf_op jit(solution)/shard_map/ppermute | solution.py:801
  1224.5 38.4 %collective-permute-start.52 = (bf16[768,384]{1,0:T(8,128)(2,1)S(1)}, bf16[768,384]{1,0:T(8,128)(2,1)S(1)}, u32[]{:S(2)}, u32[]{:S(2)}) collective-permute-start(bf16[768,384]{1,0:T(8,128)(2,1)S(1)} %get-tuple-element.295), channel_id=1, source_target_pairs={{0,3},{1,0},{2,1},{3,2},{4,7},{5,4},{6,5},{7,6},{8,11},{9,8},{10,9... | collective-permute-start | bytes 1769480 | tf_op jit(solution)/shard_map/ppermute | solution.py:801
  1312.3 31.6 %collective-permute-start.57 = (bf16[576,384]{1,0:T(8,128)(2,1)}, bf16[576,384]{1,0:T(8,128)(2,1)}, u32[]{:S(2)}, u32[]{:S(2)}) collective-permute-start(bf16[576,384]{1,0:T(8,128)(2,1)} %get-tuple-element.315), channel_id=1, source_target_pairs={{0,2},{1,3},{2,0},{3,1},{4,6},{5,7},{6,4},{7,5},{8,10},{9,11},{10,... | collective-permute-start | bytes 1327112 | tf_op jit(solution)/shard_map/ppermute | solution.py:801
  1314.8 29.2 %collective-permute-start.58 = (bf16[576,384]{1,0:T(8,128)(2,1)}, bf16[576,384]{1,0:T(8,128)(2,1)}, u32[]{:S(2)}, u32[]{:S(2)}) collective-permute-start(bf16[576,384]{1,0:T(8,128)(2,1)} %get-tuple-element.314), channel_id=1, source_target_pairs={{0,3},{1,0},{2,1},{3,2},{4,7},{5,4},{6,5},{7,6},{8,11},{9,8},{10,9... | collective-permute-start | bytes 1327112 | tf_op jit(solution)/shard_map/ppermute | solution.py:801
  1351.5 32.4 %collective-permute-start.44 = (bf16[2,64,384]{2,1,0:T(8,128)(2,1)}, bf16[2,64,384]{2,1,0:T(8,128)(2,1)S(1)}, u32[]{:S(2)}, u32[]{:S(2)}) collective-permute-start(bf16[2,64,384]{2,1,0:T(8,128)(2,1)} %get-tuple-element.263), channel_id=1, source_target_pairs={{0,1},{1,2},{2,3},{3,0},{4,5},{5,6},{6,7},{7,4},{8,9},{9,10},{10,1... | collective-permute-start | bytes 294920 | tf_op jit(solution)/shard_map/ppermute | solution.py:801
  1367.2 80.6 %collective-permute-start.24 = (bf16[384,1536]{1,0:T(8,128)(2,1)}, bf16[384,1536]{1,0:T(8,128)(2,1)}, u32[]{:S(2)}, u32[]{:S(2)}) collective-permute-start(bf16[384,1536]{1,0:T(8,128)(2,1)} %get-tuple-element.303), channel_id=1, source_target_pairs={{0,0},{4,1},{5,2},{1,3},{2,4},{6,5},{7,6},{3,7},{8,8},{12,9},{13,1... | collective-permute-start | bytes 3538952 | tf_op jit(solution)/shard_map/ppermute | solution.py:810
  1377.6 70.3 %collective-permute-start.25 = (bf16[384,1536]{1,0:T(8,128)(2,1)S(1)}, bf16[384,1536]{1,0:T(8,128)(2,1)}, u32[]{:S(2)}, u32[]{:S(2)}) collective-permute-start(bf16[384,1536]{1,0:T(8,128)(2,1)S(1)} %get-tuple-element.304), channel_id=1, source_target_pairs={{1,0},{5,1},{4,2},{0,3},{3,4},{7,5},{6,6},{2,7},{9,8},{13,9},{12,1... | collective-permute-start | bytes 3538952 | tf_op jit(solution)/shard_map/ppermute | solution.py:811
  1379.5 48.0 %collective-permute-start.45 = (bf16[2,64,384]{2,1,0:T(8,128)(2,1)}, bf16[2,64,384]{2,1,0:T(8,128)(2,1)}, u32[]{:S(2)}, u32[]{:S(2)}) collective-permute-start(bf16[2,64,384]{2,1,0:T(8,128)(2,1)} %get-tuple-element.263), channel_id=1, source_target_pairs={{0,2},{1,3},{2,0},{3,1},{4,6},{5,7},{6,4},{7,5},{8,10},{9,11},{10,... | collective-permute-start | bytes 294920 | tf_op jit(solution)/shard_map/ppermute | solution.py:801
  1379.5 62.0 %collective-permute-start.46 = (bf16[2,64,384]{2,1,0:T(8,128)(2,1)}, bf16[2,64,384]{2,1,0:T(8,128)(2,1)}, u32[]{:S(2)}, u32[]{:S(2)}) collective-permute-start(bf16[2,64,384]{2,1,0:T(8,128)(2,1)} %get-tuple-element.263), channel_id=1, source_target_pairs={{0,3},{1,0},{2,1},{3,2},{4,7},{5,4},{6,5},{7,6},{8,11},{9,8},{10,9... | collective-permute-start | bytes 294920 | tf_op jit(solution)/shard_map/ppermute | solution.py:801
  1403.5 34.3 %collective-permute-start.37 = (f32[8,1536]{1,0:T(8,128)S(1)}, f32[8,1536]{1,0:T(8,128)S(1)}, u32[]{:S(2)}, u32[]{:S(2)}) collective-permute-start(f32[8,1536]{1,0:T(8,128)S(1)} %add.550), channel_id=1, source_target_pairs={{0,8},{8,0},{1,9},{9,1},{2,10},{10,2},{3,11},{11,3},{4,12},{12,4},... | collective-permute-start | bytes 147464 | tf_op jit(solution)/shard_map/ppermute | solution.py:1132
  1427.5 55.5 %collective-permute-start.41 = (bf16[384,1536]{1,0:T(8,128)(2,1)}, bf16[384,1536]{1,0:T(8,128)(2,1)}, u32[]{:S(2)}, u32[]{:S(2)}) collective-permute-start(bf16[384,1536]{1,0:T(8,128)(2,1)} %get-tuple-element.299), channel_id=1, source_target_pairs={{0,0},{4,1},{5,2},{1,3},{2,4},{6,5},{7,6},{3,7},{8,8},{12,9},{13,1... | collective-permute-start | bytes 3538952 | tf_op jit(solution)/shard_map/ppermute | solution.py:810
  1437.8 45.2 %collective-permute-start.42 = (bf16[384,1536]{1,0:T(8,128)(2,1)S(1)}, bf16[384,1536]{1,0:T(8,128)(2,1)}, u32[]{:S(2)}, u32[]{:S(2)}) collective-permute-start(bf16[384,1536]{1,0:T(8,128)(2,1)S(1)} %get-tuple-element.300), channel_id=1, source_target_pairs={{1,0},{5,1},{4,2},{0,3},{3,4},{7,5},{6,6},{2,7},{9,8},{13,9},{12,1... | collective-permute-start | bytes 3538952 | tf_op jit(solution)/shard_map/ppermute | solution.py:811
  1445.8 24.1 %collective-permute-start.39 = (f32[8,1536]{1,0:T(8,128)S(1)}, f32[8,1536]{1,0:T(8,128)S(1)}, u32[]{:S(2)}, u32[]{:S(2)}) collective-permute-start(f32[8,1536]{1,0:T(8,128)S(1)} %add.552), channel_id=1, source_target_pairs={{0,1},{1,0},{2,3},{3,2},{4,5},{5,4},{6,7},{7,6},{8,9},{9,8},{10,11... | collective-permute-start | bytes 147464 | tf_op jit(solution)/shard_map/ppermute | solution.py:1132
  (104 other events, 2320.6 us)
Sparse Core Ops, SparseCore 0:
  41.7 177.8 all-gather.6
  223.0 176.7 all-gather.8
  403.3 129.2 all-gather.10
  939.6 82.6 reduce-scatter.4
  1025.3 94.9 reduce-scatter.8
  1123.9 95.0 reduce-scatter.6
  1222.7 85.3 reduce-scatter.10
  1310.6 33.9 all-gather.12
  1347.0 90.8 all-gather.14

commit v2 on v1

--- a/solution.py
+++ b/solution.py
@@ -699,6 +699,55 @@
     )(probes, lookups, contents, present, grads)
 
 
+def assemble_kernel(spot, own_ref, *refs):
+    *pieces, out_ref, sems = refs
+    shard, y, x, core = spot[0], spot[1], spot[2], spot[3]
+    rows = own_ref.shape[0]
+    share = rows // 8
+    copies = [(own_ref, shard * rows, rows)]
+    for flip in range(2):
+        z_ref, x_ref, y_ref, first_ref, second_ref = pieces[5 * flip : 5 * flip + 5]
+        c = core if flip == 0 else 1 - core
+        split = first_ref.shape[0] // share
+        for k in range(3):
+            owner = lax.rem(shard + 3 - k, 4) * rows
+            part = pl.ds(k * share, share)
+            copies.append((z_ref.at[part], owner + (4 * y + 2 * x + c) * share, share))
+            copies.append((x_ref.at[part], owner + (4 * y + 2 * (1 - x) + c) * share, share))
+            copies.append((y_ref.at[part], owner + (4 * (1 - y) + 2 * x + c) * share, share))
+            at = owner + (4 * (1 - y) + 2 * (1 - x) + c) * share
+            if k < split:
+                copies.append((first_ref.at[part], at, share))
+            else:
+                copies.append((second_ref.at[pl.ds((k - split) * share, share)], at, share))
+    started = []
+    for i, (source, at, size) in enumerate(copies):
+        copy = pltpu.make_async_copy(
+            source, out_ref.at[pl.ds(pl.multiple_of(at, 16), size)], sems.at[i]
+        )
+        copy.start()
+        started.append(copy)
+    for copy in started:
+        copy.wait()
+
+
+def assemble(spot, own, pieces):
+    rows, columns = own.shape
+    return pl.pallas_call(
+        assemble_kernel,
+        out_shape=jax.ShapeDtypeStruct((4 * rows, columns), own.dtype),
+        in_specs=[pl.BlockSpec(memory_space=pltpu.SMEM)]
+        + [pl.BlockSpec(memory_space=pl.ANY)] * (1 + len(pieces)),
+        out_specs=pl.BlockSpec(memory_space=pl.ANY),
+        scratch_shapes=[pltpu.SemaphoreType.DMA((25,))],
+        compiler_params=pltpu.CompilerParams(vmem_limit_bytes=4 * 2**20),
+        cost_estimate=pl.CostEstimate(
+            flops=0, bytes_accessed=16 * rows * columns, transcendentals=0
+        ),
+        name="assemble",
+    )(spot, own, *pieces)
+
+
 def unpack_kernel(in_ref, out_ref):
     pieces = in_ref[...]
     out_ref[...] = pieces.reshape(-1, pieces.shape[-1]).T.astype(jnp.float32)
@@ -845,32 +894,31 @@
         ]
     )
     x_low = to_chip(frames)
-    teacher_low = to_chip(teacher)
     rest = whole(
         [share_of(self_output_weight), share_of(cross_query_weight), share_of(cross_output_weight)]
     )
-    expand_matrix = whole([share_of(feed_up_weight)])
-
-    quarter_rows = feed_down_weight.shape[0] // 4
-    quarter = 2 * lax.axis_index("x") + core
-    mine = lax.dynamic_slice_in_dim(feed_down_weight, quarter * quarter_rows, quarter_rows, 0)
-    reduce_matrix = jnp.zeros((hidden_units, width), jnp.bfloat16)
-    reduce_matrix = lax.dynamic_update_slice_in_dim(
-        reduce_matrix, feed_down_weight, shard * 4 * quarter_rows, 0
-    )
-    for distance in (1, 2, 3):
-        came = hop(mine, distance)
-        across = lax.ppermute(came, "x", swap)
-        owner = lax.rem(shard + shards - distance, shards)
-        for values, which in (
-            (came, quarter),
-            (across, lax.rem(quarter + 2, 4)),
-            (lax.ppermute(came, "core", swap), quarter + 1 - 2 * core),
-            (lax.ppermute(across, "core", swap), lax.rem(quarter + 3 - 2 * core, 4)),
-        ):
-            reduce_matrix = lax.dynamic_update_slice_in_dim(
-                reduce_matrix, values, (owner * 4 + which) * quarter_rows, 0
-            )
+
+    def along_line(mine):
+        return jnp.concatenate([hop(mine, distance) for distance in (1, 2, 3)], axis=0)
+
+    def over_sides(line):
+        return [line, lax.ppermute(line, "x", swap), lax.ppermute(line, "y", swap)]
+
+    def over_corner(pieces, split):
+        _, over_x, over_y = pieces
+        return pieces + [
+            lax.ppermute(over_x[:split], "y", swap),
+            lax.ppermute(over_y[split:], "x", swap),
+        ]
+
+    def over_core(pieces):
+        return pieces + [lax.ppermute(values, "core", swap) for values in pieces]
+
+    seat = jnp.stack([shard, lax.axis_index("y"), lax.axis_index("x"), core]).astype(jnp.int32)
+    expand_share = share_of(feed_up_weight)
+    reduce_share = share_of(feed_down_weight)
+    expand_pieces = over_sides(along_line(after(expand_share, x_low)))
+    reduce_line = along_line(after(reduce_share, expand_pieces[0]))
 
     text_other = lax.ppermute(text_states, "core", swap)
     text_all = jnp.concatenate(
@@ -922,9 +970,14 @@
     hidden_one = ((inputs - parts_one[0]) * parts_one[1] * norms[0] + norms[1]).astype(
         jnp.bfloat16
     )
-    kv = project(hidden_one, qkv_matrix[:, width:]).astype(jnp.bfloat16)
+    kv = project(after(hidden_one, expand_pieces[0]), qkv_matrix[:, width:]).astype(jnp.bfloat16)
     kv_other = lax.ppermute(kv, "core", swap)
-    queries = project(after(hidden_one, kv), qkv_matrix[:, :width]).astype(jnp.bfloat16)
+    queries = project(after(hidden_one, kv, *expand_pieces), qkv_matrix[:, :width])
+    queries = after(queries.astype(jnp.bfloat16), reduce_line)
+    expand_pieces = over_corner(
+        list(lax.optimization_barrier((*expand_pieces, queries))[:3]), expand_share.shape[0]
+    )
+    reduce_pieces = over_sides(after(reduce_line, queries))
 
     def in_order(mine, other):
         return jnp.concatenate(
@@ -940,21 +993,30 @@
     keys = in_order(kv[:, :width], kv_other[:, :width])
     values = in_order(kv[:, width:], kv_other[:, width:])
     mixed_self, lse = self_attend(places, queries, keys, values)
+    expand_pieces = over_core(list(lax.optimization_barrier((*expand_pieces, mixed_self))[:5]))
+    reduce_pieces = over_corner(
+        list(lax.optimization_barrier((*reduce_pieces, mixed_self))[:3]),
+        2 * reduce_share.shape[0],
+    )
+    teacher_low = to_chip(after(teacher, mixed_self))
     after_self = inputs + project(mixed_self, output_matrix)
     parts_two = norm_parts(after_self)
     hidden_two = ((after_self - parts_two[0]) * parts_two[1] * norms[2] + norms[3]).astype(
         jnp.bfloat16
     )
     probes = project(hidden_two, probe_matrix).astype(jnp.bfloat16)
+    reduce_pieces = over_core(list(lax.optimization_barrier((*reduce_pieces, probes))[:5]))
     cross_mixed = cross_attend(probes, lookups, contents, present)
     after_cross = after_self + project(cross_mixed, merge_matrix)
     parts_three = norm_parts(after_cross)
     hidden_three = (
         (after_cross - parts_three[0]) * parts_three[1] * norms[4] + norms[5]
     ).astype(jnp.bfloat16)
+    expand_matrix = assemble(seat, feed_up_weight, expand_pieces)
     upward = project(hidden_three, expand_matrix)
     activated, gelu_pull = jax.vjp(exact_gelu, upward)
     activated_low = activated.astype(jnp.bfloat16)
+    reduce_matrix = assemble(seat, feed_down_weight, reduce_pieces)
     result = after_cross + project(activated_low, reduce_matrix)
     errors = (result - teacher_low.astype(jnp.float32)) * valid_rows
     squares = jnp.sum(errors * errors)
@@ -993,7 +1055,6 @@
     up_theirs = theirs_of(after(grad_upward, down_ours), hidden_three)
     grad_hidden_three = back_project(after(grad_upward, up_theirs), expand_matrix)
     up_ours = ours_of(after(grad_upward, grad_hidden_three), hidden_three, up_theirs)
-    up_sum = over_outer(up_ours)
     output = from_chip(after(result.astype(jnp.bfloat16), up_ours))
     grad_norm, gain_feed, bias_feed = norm_back(
         after(grad_hidden_three, up_ours), after_cross, parts_three, norms[4]
@@ -1007,6 +1068,7 @@
     probe_grads, lookup_grads, content_grads = cross_attend_back(
         probes, lookups, contents, present, grad_cross_mixed
     )
+    up_sum = over_outer(after(up_ours, down_sum, probe_grads))
     text_mine = jnp.where(first_core, lookup_grads, content_grads)
     text_sent = lax.ppermute(
         jnp.where(first_core, content_grads, lookup_grads), "core", swap
@@ -1057,7 +1119,7 @@
     )
     middle_rows = middle.shape[1]
     middle = middle.reshape(outers * middle_rows, width)
-    middle_sum = over_outer(middle)
+    middle_sum = over_outer(after(middle, up_sum))
     text_split = text_rows // shards
     text_piece = (
         middle_sum[middle_rows - text_split :]
@@ -1102,7 +1164,7 @@
     qkv_theirs = theirs_of(qkv_grads, hidden_one)
     grad_hidden_one = back_project(after(qkv_grads, qkv_theirs), qkv_matrix)
     qkv_ours = ours_of(after(qkv_grads, grad_hidden_one), hidden_one, qkv_theirs)
-    qkv_sum = over_outer(qkv_ours)
+    qkv_sum = over_outer(after(qkv_ours, middle_sum))
     grad_norm, gain_self, bias_self = norm_back(
         after(grad_hidden_one, qkv_ours), inputs, parts_one, norms[0]
     )
@@ -1141,7 +1203,7 @@
         + [text_piece, middle_piece],
         axis=0,
     )
-    early = lax.all_gather(early, REPLICAS, axis=0)
+    early = lax.all_gather(after(early, qkv_sum), REPLICAS, axis=0)
     piece = width // replicas
     square = (block, width)
     up_grad = unpack(early, hidden_units // replicas, 0, (block, hidden_units), 0, 1)
@@ -1154,7 +1216,7 @@
     output_grad = unpack(early, piece, at, square, 0, 2)
     probe_grad = unpack(early, piece, at + 1, square, 0, 2)
     merge_grad = unpack(early, piece, at + 2, square, 0, 2)
-    late = lax.all_gather(over_shard(qkv_sum), REPLICAS, axis=0, tiled=True)
+    late = lax.all_gather(after(over_shard(qkv_sum), early), REPLICAS, axis=0, tiled=True)
     late = late.reshape(3, width, block)
     qkv_grad = [late[i].T.astype(jnp.float32) for i in range(3)]
     return (

time: 1550 us -> 1450 us (0.935)
  starting transfers between devices: 214 us -> 141 us
  waiting for transfers between devices: 607 us -> 564 us
    reduce_scatter x4, waiting for transfers between devices: 276 us -> 39.5 us  [over_outer(): return lax.psum_scatter(values, ('y', 'x'), scatter_dimension=0, tiled=True)]
    ppermute x1, starting transfers between devices: 70.7 us -> 6.06 us  [clip_body(): kv_other = lax.ppermute(kv, 'core', swap)]
    ppermute x2, waiting for transfers between devices: 7.93 us -> 72.2 us  [to_chip(): two = lax.ppermute(jnp.where(lower, pair[1], pair[0]), spot, there[1])]
    all_gather x3 -> x2, waiting for transfers between devices: 0.04 us -> 58 us  [whole(): lax.all_gather(jnp.concatenate(parts, axis=1), EVERY, axis=0, tiled=True)]
    all_gather x2, waiting for transfers between devices: 0.01 us -> 48.1 us  [the longest x1 48.1 us: clip_body(): early = lax.all_gather(after(early, qkv_sum), REPLICAS, axis=0)]
    unnamed x174 -> x210, local copies, waits for them, and re-layouts: 32 us -> 53.7 us
    dynamic_update_slice x13 -> x0, local copies, waits for them, and re-layouts: 21.1 us -> none  [the longest x12 18.7 us: clip_body(): lax.dynamic_update_slice_in_dim(reduce_matrix, values, (owner * 4 + which...]
    ppermute x24 -> x27, waiting for transfers between devices: 286 us -> 301 us  [hop(): return lax.ppermute(values, 'shard', pairs)]
  transfers between devices with their start and end apart: 68 -> 79, of which waited for: 24 -> 30; matrix products, arithmetic and copies ran while one was open for 19% -> 29% of each run, Pallas kernels for 5% -> 12%
where the time goes in v2:
time: 1450 us; the launch traced here: 1440 us
  waiting for transfers between devices  564 us (39%)
  matrix products  314 us (22%)
  Pallas kernels  177 us (12%)
  starting transfers between devices  141 us (10%)
  other arithmetic  121 us (8%)
  local copies, waits for them, and re-layouts  106 us (7%)
  between operations  18.6 us (1%)
    ppermute x27, waiting for transfers between devices, hop(): return lax.ppermute(values, 'shard', pairs)  301 us
    dot_general x8, matrix products, project(): return jnp.dot(left, right, preferred_element_type=jnp.float32)  127 us
    dot_general x7, matrix products, back_project(): jnp.einsum('re,de->rd', grads, matrix, preferred_element_type=jnp.float32)  95.2 us
    dot_general x13, matrix products, outer_sum(): jnp.einsum('rd,re->de', left, right, preferred_element_type=jnp.float32)  92.4 us
    ppermute x2, waiting for transfers between devices, to_chip(): two = lax.ppermute(jnp.where(lower, pair[1], pair[0]), spot, there[1])  72.2 us
    ppermute x27, starting transfers between devices, hop(): return lax.ppermute(values, 'shard', pairs)  70.3 us
    pallas_call x1, Pallas kernels, self_attend_back(): pl.pallas_call(self_backward_kernel, out_shape=(jax.ShapeDtypeStruct((row...  68.7 us
    all_gather x2, waiting for transfers between devices, whole(): lax.all_gather(jnp.concatenate(parts, axis=1), EVERY, axis=0, tiled=True)  58 us
  transfers between devices with their start and end apart: 79, of which 30 were waited for; matrix products, arithmetic and copies ran while one was open for 29% of the time, Pallas kernels for 12%

profile of v2, /device:TPU:0, one launch (start us, length us, event | category | flops | bytes accessed | tf_op | source)
XLA Modules:
  0.0 1441.1 jit_solution(17051969180257579962)
XLA Ops:
  59.0 14.7 %collective-permute-done.2 = bf16[48,6144]{1,0:T(8,128)(2,1)} collective-permute-done((bf16[48,6144]{1,0:T(8,128)(2,1)}, bf16[48,6144]{1,0:T(8,128)(2,1)}, u32[]{:S(2)}, u32[]{:S(2)}) %collective-permute-start.2) | collective-permute-done | bytes 589856 | tf_op jit(solution)/shard_map/ppermute | solution.py:850
  75.6 24.5 %collective-permute-done.3 = bf16[48,6144]{1,0:T(8,128)(2,1)} collective-permute-done((bf16[48,6144]{1,0:T(8,128)(2,1)}, bf16[48,6144]{1,0:T(8,128)(2,1)}, u32[]{:S(2)}, u32[]{:S(2)}) %collective-permute-start.3) | collective-permute-done | bytes 589856 | tf_op jit(solution)/shard_map/ppermute | solution.py:850
  104.0 53.5 %collective-permute-done.1 = bf16[384,1536]{1,0:T(8,128)(2,1)} collective-permute-done((bf16[384,1536]{1,0:T(8,128)(2,1)S(1)}, bf16[384,1536]{1,0:T(8,128)(2,1)}, u32[]{:S(2)}, u32[]{:S(2)}) %collective-permute-start.1) | collective-permute-done | bytes 1179680 | tf_op jit(solution)/shard_map/ppermute | solution.py:854
  160.1 58.0 %all-gather.6.cloned.1.call-done = bf16[1536,4736]{1,0:T(8,128)(2,1)} async-done(((bf16[48,4736]{1,0:T(8,128)(2,1)}), bf16[1536,4736]{1,0:T(8,128)(2,1)}) %all-gather.6.cloned.1.call-update) | async-done | bytes 14549008 | tf_op jit(solution)/shard_map/all_gather | solution.py:868
  224.4 14.2 fusion.16
  261.2 12.2 collective-permute-done.13
  286.0 13.8 collective-permute-done.7
  301.1 36.2 %collective-permute-done.8 = bf16[192,1536]{1,0:T(8,128)(2,1)S(1)} collective-permute-done((bf16[192,1536]{1,0:T(8,128)(2,1)S(1)}, bf16[192,1536]{1,0:T(8,128)(2,1)S(1)}, u32[]{:S(2)}, u32[]{:S(2)}) %collective-permute-start.8) | collective-permute-done | bytes 589856 | tf_op jit(solution)/shard_map/ppermute | solution.py:850
  338.1 33.2 %collective-permute-done.9 = bf16[192,1536]{1,0:T(8,128)(2,1)S(1)} collective-permute-done((bf16[192,1536]{1,0:T(8,128)(2,1)S(1)}, bf16[192,1536]{1,0:T(8,128)(2,1)S(1)}, u32[]{:S(2)}, u32[]{:S(2)}) %collective-permute-start.9) | collective-permute-done | bytes 589856 | tf_op jit(solution)/shard_map/ppermute | solution.py:850
  372.2 8.2 fusion.66.q_ref
  401.6 57.4 %self_attend.1 = (bf16[768,1536]{1,0:T(8,128)(2,1)S(1)}, f32[96,768]{1,0:T(8,128)S(1)}) custom-call(s32[3]{0:T(128)S(1)} %pad_add_fusion.place, bf16[768,1536]{1,0:T(8,128)(2,1)S(1)} %copy-done.31, bf16[1536,1536]{1,0:T(8,128)(2,1)S(1)} %pad_maximum_fusion.2.k_ref, bf16[1536,1536]{1,0:T(8,128)(2,1)S(1)} %pad_maximum_fusion.3.v_ref), custom_call_target="tpu_custom_call" | custom-call | flops 7247757312 | bytes 18874368 | tf_op jit(solution)/shard_map/self_attend/pallas_call | solution.py:545
  466.3 7.6 fusion.122
  512.3 18.8 %collective-permute-done.33 = bf16[384,1536]{1,0:T(8,128)(2,1)S(1)} collective-permute-done((bf16[384,1536]{1,0:T(8,128)(2,1)S(1)}, bf16[384,1536]{1,0:T(8,128)(2,1)S(1)}, u32[]{:S(2)}, u32[]{:S(2)}) %collective-permute-start.33) | collective-permute-done | bytes 1179680 | tf_op jit(solution)/shard_map/ppermute | solution.py:854
  542.8 63.0 %multiply_convert_fusion = (bf16[768,6144]{1,0:T(8,128)(2,1)}, f32[768,6144]{1,0:T(8,128)}, f32[768,6144]{1,0:T(8,128)}) fusion(bf16[1536,6144]{1,0:T(8,128)(2,1)S(1)} %assemble.2, f32[768,1536]{1,0:T(8,128)} %copy-done.37, f32[1536]{0:T(1024)} %get-tuple-element.305, f32[1536]{0:T(1024)S(1)} %copy-done.77, f32[768]{0:T(1024)} %add_rsqrt_fusion, ...), kind=kOutput, calls=%fused_computation.5 | convolution fusion | flops 14808121344 | bytes 70797312 | tf_op jit(solution)/shard_map/dot_general | solution.py:28
  614.8 9.0 copy-done.4
  623.8 19.8 %multiply_convert_fusion.1 = (bf16[768,1536]{1,0:T(8,128)(2,1)}, f32[768,1536]{1,0:T(8,128)}) fusion(f32[]{:T(128)S(6)} %div.64, f32[768]{0:T(1024)S(1)} %copy-done.86, bf16[384,1536]{1,0:T(8,128)(2,1)S(1)} %copy-done.53, bf16[384,1536]{1,0:T(8,128)(2,1)S(1)} %copy-done.51, f32[768,1536]{1,0:T(8,128)S(1)} %copy-done.38, ...), kind=kOutput, calls=%fused_computation.72 | convolution fusion | flops 14506131456 | bytes 42470404 | tf_op jit(solution)/shard_map/dot_general | solution.py:28
  643.6 11.2 convolution_convert_fusion.2
  655.1 29.4 %add_convert_fusion.2 = bf16[768,6144]{1,0:T(8,128)(2,1)} fusion(f32[768,6144]{1,0:T(8,128)} %get-tuple-element.327, f32[768,6144]{1,0:T(8,128)} %get-tuple-element.388, bf16[768,1536]{1,0:T(8,128)(2,1)S(1)} %copy-done.68, bf16[6144,1536]{1,0:T(8,128)(2,1)} %copy-done.4), kind=kOutput, calls=%fused_computation.4 | convolution fusion | flops 14561574912 | bytes 68419584 | tf_op jit(solution)/shard_map/re,de->rd/dot_general | solution.py:36
  684.5 14.8 %add_convert_fusion.1 = bf16[768,6144]{1,0:T(8,128)(2,1)} fusion(bf16[768,6144]{1,0:T(8,128)(2,1)} %collective-permute-done.34, bf16[768,6144]{1,0:T(8,128)(2,1)} %get-tuple-element.326, bf16[768,1536]{1,0:T(8,128)(2,1)S(1)} %copy-done.68, s32[]{:T(128)S(6)} %select_n.351), kind=kOutput, calls=%fused_computation.3 | convolution fusion | flops 7261913088 | bytes 29491204 | tf_op jit(solution)/shard_map/rd,re->de/dot_general | solution.py:32
  700.0 14.7 %convolution_convert_fusion.1 = bf16[3072,1536]{1,0:T(8,128)(2,1)} fusion(bf16[768,6144]{1,0:T(8,128)(2,1)} %add_convert_fusion.2, s32[]{:T(128)S(6)} %select_n.352, f32[768,1536]{1,0:T(8,128)} %copy-done.37, f32[1536]{0:T(1024)S(1)} %copy-done.88, f32[1536]{0:T(1024)S(1)} %copy-done.77, f32[768]{0:T(1024)S(1)} %copy-done.82, ...), kind=kOutput, calls=%fused_computation.23 | convolution fusion | flops 7258374144 | bytes 18892804 | tf_op jit(solution)/shard_map/rd,re->de/dot_general | solution.py:32
  715.0 21.6 %fusion.125 = f32[768,1536]{1,0:T(8,128)} fusion(bf16[768,6144]{1,0:T(8,128)(2,1)} %add_convert_fusion.2, bf16[1536,6144]{1,0:T(8,128)(2,1)} %copy-done.3), kind=kOutput, calls=%fused_computation.306 | convolution fusion | flops 14495514624 | bytes 33030144 | tf_op jit(solution)/shard_map/re,de->rd/dot_general | solution.py:36
  736.6 14.0 add_convert_fusion
  756.5 11.6 fusion.117
  778.4 9.5 cross_attend_back.1
  812.5 9.4 multiply_reduce_fusion.2
  830.0 7.6 fusion.57.grad_ref
  850.4 68.7 %self_attend_back.1 = (bf16[768,1536]{1,0:T(8,128)(2,1)S(1)}, bf16[1536,1536]{1,0:T(8,128)(2,1)S(1)}, bf16[1536,1536]{1,0:T(8,128)(2,1)S(1)}) custom-call(s32[3]{0:T(128)S(1)} %copy-done.26, bf16[768,1536]{1,0:T(8,128)(2,1)S(1)} %copy-done.32, bf16[1536,1536]{1,0:T(8,128)(2,1)} %copy-done.12, bf16[1536,1536]{1,0:T(8,128)(2,1)} %copy-done.11, ...), custom_call_target="tpu_custom_call" | custom-call | flops 18119393280 | bytes 37748736 | tf_op jit(solution)/shard_map/self_attend_back/pallas_call | solution.py:570
  942.0 7.8 convolution_convert_fusion
  950.0 18.4 %fusion.6 = f32[768,1536]{1,0:T(8,128)} fusion(bf16[768,4608]{1,0:T(8,128)(2,1)} %copy-done.49, bf16[1536,4736]{1,0:T(8,128)(2,1)} %all-gather.6.cloned.1.call-done), kind=kOutput, calls=%fused_computation.19 | convolution fusion | flops 10871635968 | bytes 25952256 | tf_op jit(solution)/shard_map/re,de->rd/dot_general | solution.py:36
  968.4 9.9 add_convert_fusion.3
  978.3 37.9 %reduce-scatter.9.cloned.1.call-done = bf16[672,1536]{1,0:T(8,128)(2,1)} async-done(((bf16[2688,1536]{1,0:T(8,128)(2,1)}), bf16[672,1536]{1,0:T(8,128)(2,1)}) %reduce-scatter.9.cloned.1.call-update) | async-done | bytes 2064400 | tf_op jit(solution)/shard_map/reduce_scatter | solution.py:1038
  1026.7 9.0 collective-permute-done.65
  1037.8 23.4 %collective-permute-done.66 = bf16[192,1536]{1,0:T(8,128)(2,1)} collective-permute-done((bf16[192,1536]{1,0:T(8,128)(2,1)}, bf16[192,1536]{1,0:T(8,128)(2,1)}, u32[]{:S(2)}, u32[]{:S(2)}) %collective-permute-start.66) | collective-permute-done | bytes 589856 | tf_op jit(solution)/shard_map/ppermute | solution.py:850
  1062.7 11.1 collective-permute-done.62
  1073.8 36.7 %collective-permute-done.63 = bf16[768,384]{1,0:T(8,128)(2,1)} collective-permute-done((bf16[768,384]{1,0:T(8,128)(2,1)}, bf16[768,384]{1,0:T(8,128)(2,1)}, u32[]{:S(2)}, u32[]{:S(2)}) %collective-permute-start.63) | collective-permute-done | bytes 589856 | tf_op jit(solution)/shard_map/ppermute | solution.py:850
  1115.8 13.2 collective-permute-start.68
  1133.7 7.6 collective-permute-done.68
  1141.3 17.2 %collective-permute-done.69 = bf16[576,384]{1,0:T(8,128)(2,1)} collective-permute-done((bf16[576,384]{1,0:T(8,128)(2,1)}, bf16[576,384]{1,0:T(8,128)(2,1)}, u32[]{:S(2)}, u32[]{:S(2)}) %collective-permute-start.69) | collective-permute-done | bytes 442400 | tf_op jit(solution)/shard_map/ppermute | solution.py:850
  1162.2 10.0 collective-permute-start.59
  1174.8 10.6 collective-permute-done.59
  1185.5 17.7 %collective-permute-done.60 = bf16[576,384]{1,0:T(8,128)(2,1)S(1)} collective-permute-done((bf16[576,384]{1,0:T(8,128)(2,1)S(1)}, bf16[576,384]{1,0:T(8,128)(2,1)S(1)}, u32[]{:S(2)}, u32[]{:S(2)}) %collective-permute-start.60) | collective-permute-done | bytes 442400 | tf_op jit(solution)/shard_map/ppermute | solution.py:850
  1205.2 48.1 %all-gather.12.cloned.1.call-done = bf16[19968,384]{1,0:T(8,128)(2,1)} async-done(((bf16[2496,384]{1,0:T(8,128)(2,1)}), bf16[19968,384]{1,0:T(8,128)(2,1)}) %all-gather.12.cloned.1.call-update) | async-done | bytes 15335440 | tf_op jit(solution)/shard_map/all_gather | solution.py:1206
  1265.6 10.3 collective-permute-start.36
  1304.5 22.1 %collective-permute-done.57 = bf16[2,64,384]{2,1,0:T(8,128)(2,1)} collective-permute-done((bf16[2,64,384]{2,1,0:T(8,128)(2,1)}, bf16[2,64,384]{2,1,0:T(8,128)(2,1)}, u32[]{:S(2)}, u32[]{:S(2)}) %collective-permute-start.57) | collective-permute-done | bytes 98336 | tf_op jit(solution)/shard_map/ppermute | solution.py:850
  1326.6 10.3 collective-permute-start.53
  1348.5 21.0 %collective-permute-done.51 = f32[8,1536]{1,0:T(8,128)S(1)} collective-permute-done((f32[8,1536]{1,0:T(8,128)S(1)}, f32[8,1536]{1,0:T(8,128)S(1)}, u32[]{:S(2)}, u32[]{:S(2)}) %collective-permute-start.51) | collective-permute-done | bytes 49184 | tf_op jit(solution)/shard_map/ppermute | solution.py:1194
  1371.2 13.3 collective-permute-done.52
  1401.2 8.1 unpack.13
  (520 shorter events, 402.1 us)
Async XLA Ops:
  7.2 210.9 %all-gather.6.cloned.1.call-start = ((), (), s32[]{:S(2)}) async-start(), calls=%async_computation.4 | async-start | bytes 15003648 | tf_op jit(solution)/shard_map/all_gather | solution.py:868
  41.5 424.8 %all-gather.8.cloned.1.call-start = ((), (), s32[]{:S(2)}) async-start(), calls=%async_computation.5 | async-start | bytes 14598144 | tf_op jit(solution)/shard_map/all_gather | solution.py:868
  44.3 746.6 %reduce-scatter.5.cloned.1.call-start = ((), (), s32[]{:S(2)}) async-start(), calls=%async_computation.6 | async-start | bytes 11796480 | tf_op jit(solution)/shard_map/reduce_scatter | solution.py:1038
  49.3 50.9 %collective-permute-start.3 = (bf16[48,6144]{1,0:T(8,128)(2,1)}, bf16[48,6144]{1,0:T(8,128)(2,1)}, u32[]{:S(2)}, u32[]{:S(2)}) collective-permute-start(bf16[48,6144]{1,0:T(8,128)(2,1)} %constant_dynamic-slice_fusion.17), channel_id=1, source_target_pairs={{0,2},{1,3},{2,0},{3,1},{4,6},{5,7},{6,4},{7,5},{8,10},{9,11},{10,... | collective-permute-start | bytes 1769480 | tf_op jit(solution)/shard_map/ppermute | solution.py:850
  51.9 50.2 %collective-permute-start.4 = (bf16[48,6144]{1,0:T(8,128)(2,1)}, bf16[48,6144]{1,0:T(8,128)(2,1)}, u32[]{:S(2)}, u32[]{:S(2)}) collective-permute-start(bf16[48,6144]{1,0:T(8,128)(2,1)} %constant_dynamic-slice_fusion.17), channel_id=1, source_target_pairs={{0,3},{1,0},{2,1},{3,2},{4,7},{5,4},{6,5},{7,6},{8,11},{9,8},{10,9... | collective-permute-start | bytes 1769480 | tf_op jit(solution)/shard_map/ppermute | solution.py:850
  54.4 49.6 %collective-permute-start = (bf16[384,1536]{1,0:T(8,128)(2,1)}, bf16[384,1536]{1,0:T(8,128)(2,1)S(1)}, u32[]{:S(2)}, u32[]{:S(2)}) collective-permute-start(bf16[384,1536]{1,0:T(8,128)(2,1)} %get-tuple-element.365), channel_id=1, source_target_pairs={{0,0},{1,4},{2,5},{3,1},{4,2},{5,6},{6,7},{7,3},{8,8},{9,12},{10,1... | collective-permute-start | bytes 3538952 | tf_op jit(solution)/shard_map/ppermute | solution.py:853
  56.3 101.2 %collective-permute-start.1 = (bf16[384,1536]{1,0:T(8,128)(2,1)S(1)}, bf16[384,1536]{1,0:T(8,128)(2,1)}, u32[]{:S(2)}, u32[]{:S(2)}) collective-permute-start(bf16[384,1536]{1,0:T(8,128)(2,1)S(1)} %get-tuple-element.366), channel_id=1, source_target_pairs={{0,1},{1,5},{2,4},{3,0},{4,3},{5,7},{6,6},{7,2},{8,9},{9,13},{10,1... | collective-permute-start | bytes 3538952 | tf_op jit(solution)/shard_map/ppermute | solution.py:854
  73.7 170.9 %collective-permute-start.11 = (bf16[2,64,1536]{2,1,0:T(8,128)(2,1)}, bf16[2,64,1536]{2,1,0:T(8,128)(2,1)}, u32[]{:S(2)}, u32[]{:S(2)}) collective-permute-start(bf16[2,64,1536]{2,1,0:T(8,128)(2,1)} %param.37), channel_id=1, source_target_pairs={{0,4},{4,0},{1,5},{5,1},{2,6},{6,2},{3,7},{7,3},{8,12},{12,8},{9,1... | collective-permute-start | bytes 1179656 | tf_op jit(solution)/shard_map/ppermute | solution.py:923
  238.6 155.3 %collective-permute-start.10 = (bf16[768,3072]{1,0:T(8,128)(2,1)}, bf16[768,3072]{1,0:T(8,128)(2,1)}, u32[]{:S(2)}, u32[]{:S(2)}) collective-permute-start(bf16[768,3072]{1,0:T(8,128)(2,1)} %fusion.16), channel_id=1, source_target_pairs={{0,4},{4,0},{1,5},{5,1},{2,6},{6,2},{3,7},{7,3},{8,12},{12,8},{9,1... | collective-permute-start | bytes 14155784 | tf_op jit(solution)/shard_map/ppermute | solution.py:974
  251.5 120.8 %collective-permute-start.5 = (bf16[144,6144]{1,0:T(8,128)(2,1)}, bf16[144,6144]{1,0:T(8,128)(2,1)}, u32[]{:S(2)}, u32[]{:S(2)}) collective-permute-start(bf16[144,6144]{1,0:T(8,128)(2,1)} %constant_dynamic-update-slice_fusion.refs_0_), channel_id=1, source_target_pairs={{0,8},{8,0},{1,9},{9,1},{2,10},{10,2},{3,11},{11,3},{4,12},{12,4},... | collective-permute-start | bytes 5308424 | tf_op jit(solution)/shard_map/ppermute | solution.py:905
  259.8 112.5 %collective-permute-start.6 = (bf16[144,6144]{1,0:T(8,128)(2,1)}, bf16[144,6144]{1,0:T(8,128)(2,1)S(1)}, u32[]{:S(2)}, u32[]{:S(2)}) collective-permute-start(bf16[144,6144]{1,0:T(8,128)(2,1)} %constant_dynamic-update-slice_fusion.refs_0_), channel_id=1, source_target_pairs={{0,16},{16,0},{1,17},{17,1},{2,18},{18,2},{3,19},{19,3},{4,20},{20... | collective-permute-start | bytes 5308424 | tf_op jit(solution)/shard_map/ppermute | solution.py:905
  279.9 57.4 %collective-permute-start.8 = (bf16[192,1536]{1,0:T(8,128)(2,1)S(1)}, bf16[192,1536]{1,0:T(8,128)(2,1)S(1)}, u32[]{:S(2)}, u32[]{:S(2)}) collective-permute-start(bf16[192,1536]{1,0:T(8,128)(2,1)S(1)} %constant_dynamic-slice_fusion.16), channel_id=1, source_target_pairs={{0,2},{1,3},{2,0},{3,1},{4,6},{5,7},{6,4},{7,5},{8,10},{9,11},{10,... | collective-permute-start | bytes 1769480 | tf_op jit(solution)/shard_map/ppermute | solution.py:850
  299.9 71.5 %collective-permute-start.9 = (bf16[192,1536]{1,0:T(8,128)(2,1)S(1)}, bf16[192,1536]{1,0:T(8,128)(2,1)S(1)}, u32[]{:S(2)}, u32[]{:S(2)}) collective-permute-start(bf16[192,1536]{1,0:T(8,128)(2,1)S(1)} %constant_dynamic-slice_fusion.16), channel_id=1, source_target_pairs={{0,3},{1,0},{2,1},{3,2},{4,7},{5,4},{6,5},{7,6},{8,11},{9,8},{10,9... | collective-permute-start | bytes 1769480 | tf_op jit(solution)/shard_map/ppermute | solution.py:850
  380.4 80.0 %collective-permute-start.23 = (bf16[576,1536]{1,0:T(8,128)(2,1)}, bf16[576,1536]{1,0:T(8,128)(2,1)}, u32[]{:S(2)}, u32[]{:S(2)}) collective-permute-start(bf16[576,1536]{1,0:T(8,128)(2,1)} %constant_dynamic-update-slice_fusion.3.refs_0_), channel_id=1, source_target_pairs={{0,8},{8,0},{1,9},{9,1},{2,10},{10,2},{3,11},{11,3},{4,12},{12,4},... | collective-permute-start | bytes 5308424 | tf_op jit(solution)/shard_map/ppermute | solution.py:905
  380.4 80.0 %collective-permute-start.24 = (bf16[576,1536]{1,0:T(8,128)(2,1)}, bf16[576,1536]{1,0:T(8,128)(2,1)}, u32[]{:S(2)}, u32[]{:S(2)}) collective-permute-start(bf16[576,1536]{1,0:T(8,128)(2,1)} %constant_dynamic-update-slice_fusion.3.refs_0_), channel_id=1, source_target_pairs={{0,16},{16,0},{1,17},{17,1},{2,18},{18,2},{3,19},{19,3},{4,20},{20... | collective-permute-start | bytes 5308424 | tf_op jit(solution)/shard_map/ppermute | solution.py:905
  386.1 88.5 %collective-permute-start.17 = (bf16[96,6144]{1,0:T(8,128)(2,1)}, bf16[96,6144]{1,0:T(8,128)(2,1)}, u32[]{:S(2)}, u32[]{:S(2)}) collective-permute-start(bf16[96,6144]{1,0:T(8,128)(2,1)} %slice.368), channel_id=1, source_target_pairs={{0,8},{8,0},{1,9},{9,1},{2,10},{10,2},{3,11},{11,3},{4,12},{12,4},... | collective-permute-start | bytes 3538952 | tf_op jit(solution)/shard_map/ppermute | solution.py:911
  390.0 84.6 %collective-permute-start.16 = (bf16[48,6144]{1,0:T(8,128)(2,1)}, bf16[48,6144]{1,0:T(8,128)(2,1)S(1)}, u32[]{:S(2)}, u32[]{:S(2)}) collective-permute-start(bf16[48,6144]{1,0:T(8,128)(2,1)} %slice.367), channel_id=1, source_target_pairs={{0,16},{16,0},{1,17},{17,1},{2,18},{18,2},{3,19},{19,3},{4,20},{20... | collective-permute-start | bytes 1769480 | tf_op jit(solution)/shard_map/ppermute | solution.py:910
  462.9 36.6 %collective-permute-start.25 = (bf16[384,1536]{1,0:T(8,128)(2,1)}, bf16[384,1536]{1,0:T(8,128)(2,1)}, u32[]{:S(2)}, u32[]{:S(2)}) collective-permute-start(bf16[384,1536]{1,0:T(8,128)(2,1)} %slice.369), channel_id=1, source_target_pairs={{0,16},{16,0},{1,17},{17,1},{2,18},{18,2},{3,19},{19,3},{4,20},{20... | collective-permute-start | bytes 3538952 | tf_op jit(solution)/shard_map/ppermute | solution.py:910
  474.6 63.8 %collective-permute-start.18 = (bf16[144,6144]{1,0:T(8,128)(2,1)}, bf16[144,6144]{1,0:T(8,128)(2,1)S(1)}, u32[]{:S(2)}, u32[]{:S(2)}) collective-permute-start(bf16[144,6144]{1,0:T(8,128)(2,1)} %constant_dynamic-update-slice_fusion.refs_0_), channel_id=1, source_target_pairs={{0,4},{4,0},{1,5},{5,1},{2,6},{6,2},{3,7},{7,3},{8,12},{12,8},{9,1... | collective-permute-start | bytes 5308424 | tf_op jit(solution)/shard_map/ppermute | solution.py:915
  474.7 64.1 %collective-permute-start.19 = (bf16[144,6144]{1,0:T(8,128)(2,1)}, bf16[144,6144]{1,0:T(8,128)(2,1)S(1)}, u32[]{:S(2)}, u32[]{:S(2)}) collective-permute-start(bf16[144,6144]{1,0:T(8,128)(2,1)} %collective-permute-done.5.refs_1_), channel_id=1, source_target_pairs={{0,4},{4,0},{1,5},{5,1},{2,6},{6,2},{3,7},{7,3},{8,12},{12,8},{9,1... | collective-permute-start | bytes 5308424 | tf_op jit(solution)/shard_map/ppermute | solution.py:915
  477.4 31.1 %collective-permute-start.32 = (bf16[384,1536]{1,0:T(8,128)(2,1)S(1)}, bf16[384,1536]{1,0:T(8,128)(2,1)S(1)}, u32[]{:S(2)}, u32[]{:S(2)}) collective-permute-start(bf16[384,1536]{1,0:T(8,128)(2,1)S(1)} %get-tuple-element.361), channel_id=1, source_target_pairs={{0,0},{1,4},{2,5},{3,1},{4,2},{5,6},{6,7},{7,3},{8,8},{9,12},{10,1... | collective-permute-start | bytes 3538952 | tf_op jit(solution)/shard_map/ppermute | solution.py:853
  493.2 45.8 %collective-permute-start.20 = (bf16[144,6144]{1,0:T(8,128)(2,1)S(1)}, bf16[144,6144]{1,0:T(8,128)(2,1)S(1)}, u32[]{:S(2)}, u32[]{:S(2)}) collective-permute-start(bf16[144,6144]{1,0:T(8,128)(2,1)S(1)} %collective-permute-done.6.refs_2_), channel_id=1, source_target_pairs={{0,4},{4,0},{1,5},{5,1},{2,6},{6,2},{3,7},{7,3},{8,12},{12,8},{9,1... | collective-permute-start | bytes 5308424 | tf_op jit(solution)/shard_map/ppermute | solution.py:915
  499.5 31.6 %collective-permute-start.33 = (bf16[384,1536]{1,0:T(8,128)(2,1)S(1)}, bf16[384,1536]{1,0:T(8,128)(2,1)S(1)}, u32[]{:S(2)}, u32[]{:S(2)}) collective-permute-start(bf16[384,1536]{1,0:T(8,128)(2,1)S(1)} %get-tuple-element.362), channel_id=1, source_target_pairs={{0,1},{1,5},{2,4},{3,0},{4,3},{5,7},{6,6},{7,2},{8,9},{9,13},{10,1... | collective-permute-start | bytes 3538952 | tf_op jit(solution)/shard_map/ppermute | solution.py:854
  508.5 29.7 %collective-permute-start.22 = (bf16[96,6144]{1,0:T(8,128)(2,1)}, bf16[96,6144]{1,0:T(8,128)(2,1)S(1)}, u32[]{:S(2)}, u32[]{:S(2)}) collective-permute-start(bf16[96,6144]{1,0:T(8,128)(2,1)} %collective-permute-done.17.refs_4_), channel_id=1, source_target_pairs={{0,4},{4,0},{1,5},{5,1},{2,6},{6,2},{3,7},{7,3},{8,12},{12,8},{9,1... | collective-permute-start | bytes 3538952 | tf_op jit(solution)/shard_map/ppermute | solution.py:915
  537.8 68.0 %collective-permute-start.27 = (bf16[576,1536]{1,0:T(8,128)(2,1)}, bf16[576,1536]{1,0:T(8,128)(2,1)}, u32[]{:S(2)}, u32[]{:S(2)}) collective-permute-start(bf16[576,1536]{1,0:T(8,128)(2,1)} %constant_dynamic-update-slice_fusion.3.refs_0_), channel_id=1, source_target_pairs={{0,4},{4,0},{1,5},{5,1},{2,6},{6,2},{3,7},{7,3},{8,12},{12,8},{9,1... | collective-permute-start | bytes 5308424 | tf_op jit(solution)/shard_map/ppermute | solution.py:915
  538.2 67.6 %collective-permute-start.28 = (bf16[576,1536]{1,0:T(8,128)(2,1)}, bf16[576,1536]{1,0:T(8,128)(2,1)}, u32[]{:S(2)}, u32[]{:S(2)}) collective-permute-start(bf16[576,1536]{1,0:T(8,128)(2,1)} %collective-permute-done.23.refs_1_), channel_id=1, source_target_pairs={{0,4},{4,0},{1,5},{5,1},{2,6},{6,2},{3,7},{7,3},{8,12},{12,8},{9,1... | collective-permute-start | bytes 5308424 | tf_op jit(solution)/shard_map/ppermute | solution.py:915
  538.4 67.5 %collective-permute-start.29 = (bf16[576,1536]{1,0:T(8,128)(2,1)}, bf16[576,1536]{1,0:T(8,128)(2,1)}, u32[]{:S(2)}, u32[]{:S(2)}) collective-permute-start(bf16[576,1536]{1,0:T(8,128)(2,1)} %collective-permute-done.24.refs_2_), channel_id=1, source_target_pairs={{0,4},{4,0},{1,5},{5,1},{2,6},{6,2},{3,7},{7,3},{8,12},{12,8},{9,1... | collective-permute-start | bytes 5308424 | tf_op jit(solution)/shard_map/ppermute | solution.py:915
  538.7 67.1 %collective-permute-start.30 = (bf16[384,1536]{1,0:T(8,128)(2,1)}, bf16[384,1536]{1,0:T(8,128)(2,1)}, u32[]{:S(2)}, u32[]{:S(2)}) collective-permute-start(bf16[384,1536]{1,0:T(8,128)(2,1)} %collective-permute-done.25.refs_3_), channel_id=1, source_target_pairs={{0,4},{4,0},{1,5},{5,1},{2,6},{6,2},{3,7},{7,3},{8,12},{12,8},{9,1... | collective-permute-start | bytes 3538952 | tf_op jit(solution)/shard_map/ppermute | solution.py:915
  538.9 66.9 %collective-permute-start.31 = (bf16[192,1536]{1,0:T(8,128)(2,1)}, bf16[192,1536]{1,0:T(8,128)(2,1)}, u32[]{:S(2)}, u32[]{:S(2)}) collective-permute-start(bf16[192,1536]{1,0:T(8,128)(2,1)} %collective-permute-done.26.refs_4_), channel_id=1, source_target_pairs={{0,4},{4,0},{1,5},{5,1},{2,6},{6,2},{3,7},{7,3},{8,12},{12,8},{9,1... | collective-permute-start | bytes 1769480 | tf_op jit(solution)/shard_map/ppermute | solution.py:915
  699.3 225.8 %reduce-scatter.7.cloned.1.call-start = ((), (), s32[]{:S(2)}) async-start(), calls=%async_computation.7 | async-start | bytes 11796480 | tf_op jit(solution)/shard_map/reduce_scatter | solution.py:1038
  790.9 225.3 %reduce-scatter.9.cloned.1.call-start = ((), (), s32[]{:S(2)}) async-start(), calls=%async_computation.8 | async-start | bytes 10321920 | tf_op jit(solution)/shard_map/reduce_scatter | solution.py:1038
  797.2 30.9 %collective-permute-start.43 = (bf16[64,1536]{1,0:T(8,128)(2,1)S(1)}, bf16[64,1536]{1,0:T(8,128)(2,1)S(1)}, u32[]{:S(2)}, u32[]{:S(2)}) collective-permute-start(bf16[64,1536]{1,0:T(8,128)(2,1)S(1)} %get-tuple-element.319), channel_id=1, source_target_pairs={{0,2},{1,3},{2,0},{3,1},{4,6},{5,7},{6,4},{7,5},{8,10},{9,11},{10,... | collective-permute-start | bytes 589832 | tf_op jit(solution)/shard_map/ppermute | solution.py:850
  925.2 235.5 %reduce-scatter.11.cloned.1.call-start = ((), (), s32[]{:S(2)}) async-start(), calls=%async_computation.9 | async-start | bytes 8847360 | tf_op jit(solution)/shard_map/reduce_scatter | solution.py:1038
  1016.2 237.2 %all-gather.12.cloned.1.call-start = ((), (), s32[]{:S(2)}) async-start(), calls=%async_computation.11 | async-start | bytes 17252352 | tf_op jit(solution)/shard_map/all_gather | solution.py:1206
  1018.9 42.3 %collective-permute-start.66 = (bf16[192,1536]{1,0:T(8,128)(2,1)}, bf16[192,1536]{1,0:T(8,128)(2,1)}, u32[]{:S(2)}, u32[]{:S(2)}) collective-permute-start(bf16[192,1536]{1,0:T(8,128)(2,1)} %get-tuple-element.347), channel_id=1, source_target_pairs={{0,2},{1,3},{2,0},{3,1},{4,6},{5,7},{6,4},{7,5},{8,10},{9,11},{10,... | collective-permute-start | bytes 1769480 | tf_op jit(solution)/shard_map/ppermute | solution.py:850
  1021.3 39.9 %collective-permute-start.67 = (bf16[192,1536]{1,0:T(8,128)(2,1)S(1)}, bf16[192,1536]{1,0:T(8,128)(2,1)}, u32[]{:S(2)}, u32[]{:S(2)}) collective-permute-start(bf16[192,1536]{1,0:T(8,128)(2,1)S(1)} %get-tuple-element.346), channel_id=1, source_target_pairs={{0,3},{1,0},{2,1},{3,2},{4,7},{5,4},{6,5},{7,6},{8,11},{9,8},{10,9... | collective-permute-start | bytes 1769480 | tf_op jit(solution)/shard_map/ppermute | solution.py:850
  1025.4 48.4 %collective-permute-start.62 = (bf16[768,384]{1,0:T(8,128)(2,1)}, bf16[768,384]{1,0:T(8,128)(2,1)}, u32[]{:S(2)}, u32[]{:S(2)}) collective-permute-start(bf16[768,384]{1,0:T(8,128)(2,1)} %get-tuple-element.348), channel_id=1, source_target_pairs={{0,1},{1,2},{2,3},{3,0},{4,5},{5,6},{6,7},{7,4},{8,9},{9,10},{10,1... | collective-permute-start | bytes 1769480 | tf_op jit(solution)/shard_map/ppermute | solution.py:850
  1026.2 84.3 %collective-permute-start.63 = (bf16[768,384]{1,0:T(8,128)(2,1)}, bf16[768,384]{1,0:T(8,128)(2,1)}, u32[]{:S(2)}, u32[]{:S(2)}) collective-permute-start(bf16[768,384]{1,0:T(8,128)(2,1)} %get-tuple-element.350), channel_id=1, source_target_pairs={{0,2},{1,3},{2,0},{3,1},{4,6},{5,7},{6,4},{7,5},{8,10},{9,11},{10,... | collective-permute-start | bytes 1769480 | tf_op jit(solution)/shard_map/ppermute | solution.py:850
  1035.8 74.8 %collective-permute-start.64 = (bf16[768,384]{1,0:T(8,128)(2,1)}, bf16[768,384]{1,0:T(8,128)(2,1)}, u32[]{:S(2)}, u32[]{:S(2)}) collective-permute-start(bf16[768,384]{1,0:T(8,128)(2,1)} %get-tuple-element.349), channel_id=1, source_target_pairs={{0,3},{1,0},{2,1},{3,2},{4,7},{5,4},{6,5},{7,6},{8,11},{9,8},{10,9... | collective-permute-start | bytes 1769480 | tf_op jit(solution)/shard_map/ppermute | solution.py:850
  1160.7 259.5 %all-gather.10.cloned.1.call-start = ((), (), s32[]{:S(2)}) async-start(), calls=%async_computation.10 | async-start | bytes 3981312 | tf_op jit(solution)/shard_map/all_gather | solution.py:1219
  1172.2 31.0 %collective-permute-start.60 = (bf16[576,384]{1,0:T(8,128)(2,1)S(1)}, bf16[576,384]{1,0:T(8,128)(2,1)S(1)}, u32[]{:S(2)}, u32[]{:S(2)}) collective-permute-start(bf16[576,384]{1,0:T(8,128)(2,1)S(1)} %get-tuple-element.372), channel_id=1, source_target_pairs={{0,2},{1,3},{2,0},{3,1},{4,6},{5,7},{6,4},{7,5},{8,10},{9,11},{10,... | collective-permute-start | bytes 1327112 | tf_op jit(solution)/shard_map/ppermute | solution.py:850
  1265.6 81.1 %collective-permute-start.36 = (bf16[384,1536]{1,0:T(8,128)(2,1)}, bf16[384,1536]{1,0:T(8,128)(2,1)}, u32[]{:S(2)}, u32[]{:S(2)}) collective-permute-start(bf16[384,1536]{1,0:T(8,128)(2,1)} %get-tuple-element.357), channel_id=1, source_target_pairs={{0,0},{4,1},{5,2},{1,3},{2,4},{6,5},{7,6},{3,7},{8,8},{12,9},{13,1... | collective-permute-start | bytes 3538952 | tf_op jit(solution)/shard_map/ppermute | solution.py:859
  1275.9 70.7 %collective-permute-start.37 = (bf16[384,1536]{1,0:T(8,128)(2,1)S(1)}, bf16[384,1536]{1,0:T(8,128)(2,1)}, u32[]{:S(2)}, u32[]{:S(2)}) collective-permute-start(bf16[384,1536]{1,0:T(8,128)(2,1)S(1)} %get-tuple-element.358), channel_id=1, source_target_pairs={{1,0},{5,1},{4,2},{0,3},{3,4},{7,5},{6,6},{2,7},{9,8},{13,9},{12,1... | collective-permute-start | bytes 3538952 | tf_op jit(solution)/shard_map/ppermute | solution.py:860
  1277.9 48.7 %collective-permute-start.57 = (bf16[2,64,384]{2,1,0:T(8,128)(2,1)}, bf16[2,64,384]{2,1,0:T(8,128)(2,1)}, u32[]{:S(2)}, u32[]{:S(2)}) collective-permute-start(bf16[2,64,384]{2,1,0:T(8,128)(2,1)} %get-tuple-element.317), channel_id=1, source_target_pairs={{0,2},{1,3},{2,0},{3,1},{4,6},{5,7},{6,4},{7,5},{8,10},{9,11},{10,... | collective-permute-start | bytes 294920 | tf_op jit(solution)/shard_map/ppermute | solution.py:850
  1277.9 62.5 %collective-permute-start.58 = (bf16[2,64,384]{2,1,0:T(8,128)(2,1)}, bf16[2,64,384]{2,1,0:T(8,128)(2,1)}, u32[]{:S(2)}, u32[]{:S(2)}) collective-permute-start(bf16[2,64,384]{2,1,0:T(8,128)(2,1)} %get-tuple-element.317), channel_id=1, source_target_pairs={{0,3},{1,0},{2,1},{3,2},{4,7},{5,4},{6,5},{7,6},{8,11},{9,8},{10,9... | collective-permute-start | bytes 294920 | tf_op jit(solution)/shard_map/ppermute | solution.py:850
  1301.8 35.1 %collective-permute-start.49 = (f32[8,1536]{1,0:T(8,128)S(1)}, f32[8,1536]{1,0:T(8,128)S(1)}, u32[]{:S(2)}, u32[]{:S(2)}) collective-permute-start(f32[8,1536]{1,0:T(8,128)S(1)} %add.427), channel_id=1, source_target_pairs={{0,8},{8,0},{1,9},{9,1},{2,10},{10,2},{3,11},{11,3},{4,12},{12,4},... | collective-permute-start | bytes 147464 | tf_op jit(solution)/shard_map/ppermute | solution.py:1194
  1326.6 59.8 %collective-permute-start.53 = (bf16[384,1536]{1,0:T(8,128)(2,1)}, bf16[384,1536]{1,0:T(8,128)(2,1)}, u32[]{:S(2)}, u32[]{:S(2)}) collective-permute-start(bf16[384,1536]{1,0:T(8,128)(2,1)} %get-tuple-element.353), channel_id=1, source_target_pairs={{0,0},{4,1},{5,2},{1,3},{2,4},{6,5},{7,6},{3,7},{8,8},{12,9},{13,1... | collective-permute-start | bytes 3538952 | tf_op jit(solution)/shard_map/ppermute | solution.py:859
  1336.9 49.4 %collective-permute-start.54 = (bf16[384,1536]{1,0:T(8,128)(2,1)S(1)}, bf16[384,1536]{1,0:T(8,128)(2,1)}, u32[]{:S(2)}, u32[]{:S(2)}) collective-permute-start(bf16[384,1536]{1,0:T(8,128)(2,1)S(1)} %get-tuple-element.354), channel_id=1, source_target_pairs={{1,0},{5,1},{4,2},{0,3},{3,4},{7,5},{6,6},{2,7},{9,8},{13,9},{12,1... | collective-permute-start | bytes 3538952 | tf_op jit(solution)/shard_map/ppermute | solution.py:860
  (131 other events, 3099.8 us)
Sparse Core Ops, SparseCore 0:
  41.6 176.4 all-gather.5
  221.6 155.4 all-gather.7
  699.5 91.3 reduce-scatter.4
  794.4 95.0 reduce-scatter.6
  925.3 90.7 reduce-scatter.8
  1019.6 76.7 reduce-scatter.10
  1160.8 92.4 all-gather.11
  1255.8 33.9 all-gather.9

commit v3 on v2

--- a/solution.py
+++ b/solution.py
@@ -852,6 +852,9 @@
     def to_chip(pair):
         one = lax.ppermute(jnp.where(lower, pair[0], pair[1]), spot, there[0])
         two = lax.ppermute(jnp.where(lower, pair[1], pair[0]), spot, there[1])
+        return one, two
+
+    def by_time(one, two):
         return jnp.concatenate([jnp.where(even, one, two), jnp.where(even, two, one)], axis=0)
 
     def from_chip(values):
@@ -864,42 +867,18 @@
         share = weight.shape[0] // replicas
         return lax.dynamic_slice_in_dim(weight, replica * share, share, 0)
 
-    def whole(parts):
-        return lax.all_gather(jnp.concatenate(parts, axis=1), EVERY, axis=0, tiled=True)
-
-    share = block // replicas
-    facts = jnp.concatenate(
-        [(clip_lengths // 64)[:, None], (clip_lengths % 64)[:, None], slot_used[:, None], text_mask],
-        axis=1,
-    ).astype(jnp.bfloat16)
-    rider = jnp.zeros((share, PAIR), jnp.bfloat16)
-    for i, vector in enumerate(
-        (
-            self_norm_gain,
-            self_norm_bias,
-            cross_norm_gain,
-            cross_norm_bias,
-            feed_norm_gain,
-            feed_norm_bias,
-        )
-    ):
-        rider = rider.at[:, i].set(share_of(vector))
-    rider = rider.at[:2, 8 : 8 + facts.shape[1]].set(facts)
-    first = whole(
-        [
-            share_of(self_query_weight),
-            share_of(self_key_weight),
-            share_of(self_value_weight),
-            rider,
-        ]
-    )
-    x_low = to_chip(frames)
-    rest = whole(
-        [share_of(self_output_weight), share_of(cross_query_weight), share_of(cross_output_weight)]
-    )
-
-    def along_line(mine):
-        return jnp.concatenate([hop(mine, distance) for distance in (1, 2, 3)], axis=0)
+    def from_shards(mine, hops=None):
+        hops = hops or [hop(mine, distance) for distance in (1, 2, 3)]
+        out = jnp.zeros((shards,) + mine.shape, mine.dtype)
+        out = lax.dynamic_update_index_in_dim(out, mine, shard, 0)
+        for distance in (1, 2, 3):
+            owner = lax.rem(shard + shards - distance, shards)
+            out = lax.dynamic_update_index_in_dim(out, hops[distance - 1], owner, 0)
+        return out
+
+    def from_replicas(line):
+        full = lax.all_gather(line, ("y", "x", "core"), axis=1, tiled=True)
+        return full.reshape(-1, line.shape[-1])
 
     def over_sides(line):
         return [line, lax.ppermute(line, "x", swap), lax.ppermute(line, "y", swap)]
@@ -914,11 +893,35 @@
     def over_core(pieces):
         return pieces + [lax.ppermute(values, "core", swap) for values in pieces]
 
+    qkv_line = from_shards(
+        jnp.concatenate(
+            [share_of(self_query_weight), share_of(self_key_weight), share_of(self_value_weight)],
+            axis=1,
+        )
+    )
+    rest_own = jnp.concatenate([self_output_weight, cross_query_weight, cross_output_weight], axis=1)
+    rest_share = share_of(rest_own)
+    rest_mine = after(rest_share, qkv_line)
+    rest_line = jnp.concatenate([hop(rest_mine, distance) for distance in (1, 2, 3)], axis=0)
+    norms = from_shards(
+        jnp.stack(
+            [
+                self_norm_gain,
+                self_norm_bias,
+                cross_norm_gain,
+                cross_norm_bias,
+                feed_norm_gain,
+                feed_norm_bias,
+            ]
+        )
+    )
+    norms = norms.transpose(1, 0, 2).reshape(6, width).astype(jnp.float32)
+    came = to_chip(after(frames, rest_line))
+    x_low = by_time(*came)
+    expand_line = from_shards(after(share_of(feed_up_weight), *came))
+    qkv_matrix = from_replicas(qkv_line)
+    expand_matrix = from_replicas(expand_line)
     seat = jnp.stack([shard, lax.axis_index("y"), lax.axis_index("x"), core]).astype(jnp.int32)
-    expand_share = share_of(feed_up_weight)
-    reduce_share = share_of(feed_down_weight)
-    expand_pieces = over_sides(along_line(after(expand_share, x_low)))
-    reduce_line = along_line(after(reduce_share, expand_pieces[0]))
 
     text_other = lax.ppermute(text_states, "core", swap)
     text_all = jnp.concatenate(
@@ -942,43 +945,35 @@
     lookups = jnp.where(first_core, text_half, text_swap)
     contents = jnp.where(first_core, text_swap, text_half)
 
-    qkv_matrix = first[:, : 3 * width]
-    norms = first[:, 3 * width : 3 * width + 8].astype(jnp.float32).T
-    facts = (
-        first[: replicas * share, 3 * width + 8 : 3 * width + 11 + text_len]
-        .reshape(replicas, share, 3 + text_len)[:, :2]
-        .astype(jnp.int32)
-        .reshape(2 * replicas, 3 + text_len)
-    )
-    lengths = facts[:, 0] * 64 + facts[:, 1]
-    slot = outer * 4 + shard
-    length = lengths[slot]
-    used = facts[slot, 2]
-    present = facts[slot, 3:].reshape(text_len, 1)
-    count = jnp.sum(jnp.where(facts[:, 2] > 0, jnp.minimum(lengths, clip), 0)).astype(jnp.float32)
+    facts = jnp.concatenate([clip_lengths[:, None], slot_used[:, None], text_mask], axis=1)
+    facts_other = lax.ppermute(facts, "core", swap)
+    fact = lax.dynamic_index_in_dim(
+        jnp.where(shard // 2 == core, facts, facts_other), shard % 2, 0, keepdims=False
+    )
+    length, used = fact[0], fact[1]
+    present = fact[2:].reshape(text_len, 1)
+    both = jnp.stack([facts, facts_other])
+    count = jnp.sum(
+        jnp.where(both[:, :, 1] > 0, jnp.minimum(both[:, :, 0], clip), 0).astype(jnp.float32)
+    )
+    count = jnp.full((8, 128), count)
+    for axis in ("x", "y"):
+        count += lax.ppermute(count, axis, swap)
+    count = count[0, 0]
     places = jnp.stack([core, 3 - core, length]).astype(jnp.int32)
     positions = jnp.concatenate(
         [core * block + jnp.arange(block), (3 - core) * block + jnp.arange(block)]
     )
     valid_rows = ((positions < length) & (used > 0)).astype(jnp.float32)[:, None]
-    output_matrix = rest[:, :width]
-    probe_matrix = rest[:, width : 2 * width]
-    merge_matrix = rest[:, 2 * width :]
-
     inputs = x_low.astype(jnp.float32)
     parts_one = norm_parts(inputs)
     hidden_one = ((inputs - parts_one[0]) * parts_one[1] * norms[0] + norms[1]).astype(
         jnp.bfloat16
     )
-    kv = project(after(hidden_one, expand_pieces[0]), qkv_matrix[:, width:]).astype(jnp.bfloat16)
+    kv = project(hidden_one, qkv_matrix[:, width:]).astype(jnp.bfloat16)
     kv_other = lax.ppermute(kv, "core", swap)
-    queries = project(after(hidden_one, kv, *expand_pieces), qkv_matrix[:, :width])
-    queries = after(queries.astype(jnp.bfloat16), reduce_line)
-    expand_pieces = over_corner(
-        list(lax.optimization_barrier((*expand_pieces, queries))[:3]), expand_share.shape[0]
-    )
-    reduce_pieces = over_sides(after(reduce_line, queries))
-
+    rest_pieces = over_sides(after(rest_line, qkv_matrix))
+    queries = project(after(hidden_one, kv), qkv_matrix[:, :width]).astype(jnp.bfloat16)
     def in_order(mine, other):
         return jnp.concatenate(
             [
@@ -992,31 +987,39 @@
 
     keys = in_order(kv[:, :width], kv_other[:, :width])
     values = in_order(kv[:, width:], kv_other[:, width:])
-    mixed_self, lse = self_attend(places, queries, keys, values)
-    expand_pieces = over_core(list(lax.optimization_barrier((*expand_pieces, mixed_self))[:5]))
-    reduce_pieces = over_corner(
-        list(lax.optimization_barrier((*reduce_pieces, mixed_self))[:3]),
-        2 * reduce_share.shape[0],
-    )
-    teacher_low = to_chip(after(teacher, mixed_self))
+    rest_pieces = over_corner(
+        list(lax.optimization_barrier((*rest_pieces, values))[:3]), 2 * rest_share.shape[0]
+    )
+    reduce_share = after(share_of(feed_down_weight), expand_line, keys)
+    reduce_hops = [hop(reduce_share, distance) for distance in (1, 2, 3)]
+    mixed_self, lse = self_attend(
+        after(places, expand_line, text_part, *rest_pieces), queries, keys, values
+    )
+    rest_pieces = over_core(list(lax.optimization_barrier((*rest_pieces, mixed_self))[:5]))
+    rest = assemble(seat, rest_own, rest_pieces)
+    reduce_line = from_shards(
+        reduce_share, list(lax.optimization_barrier((*reduce_hops, mixed_self))[:3])
+    )
+    reduce_matrix = from_replicas(reduce_line)
+    output_matrix = rest[:, :width]
+    probe_matrix = rest[:, width : 2 * width]
+    merge_matrix = rest[:, 2 * width :]
     after_self = inputs + project(mixed_self, output_matrix)
     parts_two = norm_parts(after_self)
     hidden_two = ((after_self - parts_two[0]) * parts_two[1] * norms[2] + norms[3]).astype(
         jnp.bfloat16
     )
     probes = project(hidden_two, probe_matrix).astype(jnp.bfloat16)
-    reduce_pieces = over_core(list(lax.optimization_barrier((*reduce_pieces, probes))[:5]))
+    teacher_low = by_time(*to_chip(after(teacher, reduce_line, probes)))
     cross_mixed = cross_attend(probes, lookups, contents, present)
     after_cross = after_self + project(cross_mixed, merge_matrix)
     parts_three = norm_parts(after_cross)
     hidden_three = (
         (after_cross - parts_three[0]) * parts_three[1] * norms[4] + norms[5]
     ).astype(jnp.bfloat16)
-    expand_matrix = assemble(seat, feed_up_weight, expand_pieces)
     upward = project(hidden_three, expand_matrix)
     activated, gelu_pull = jax.vjp(exact_gelu, upward)
     activated_low = activated.astype(jnp.bfloat16)
-    reduce_matrix = assemble(seat, feed_down_weight, reduce_pieces)
     result = after_cross + project(activated_low, reduce_matrix)
     errors = (result - teacher_low.astype(jnp.float32)) * valid_rows
     squares = jnp.sum(errors * errors)
@@ -1068,7 +1071,8 @@
     probe_grads, lookup_grads, content_grads = cross_attend_back(
         probes, lookups, contents, present, grad_cross_mixed
     )
-    up_sum = over_outer(after(up_ours, down_sum, probe_grads))
+    up_sum = over_outer(up_ours)
+    down_piece = over_shard(down_sum)
     text_mine = jnp.where(first_core, lookup_grads, content_grads)
     text_sent = lax.ppermute(
         jnp.where(first_core, content_grads, lookup_grads), "core", swap
@@ -1119,7 +1123,7 @@
     )
     middle_rows = middle.shape[1]
     middle = middle.reshape(outers * middle_rows, width)
-    middle_sum = over_outer(after(middle, up_sum))
+    middle_sum = over_outer(middle)
     text_split = text_rows // shards
     text_piece = (
         middle_sum[middle_rows - text_split :]
@@ -1128,8 +1132,9 @@
         .reshape(text_rows, block)
     )
     grad_queries, grad_keys, grad_values = self_attend_back(
-        places, queries, keys, values, mixed_self, after(grad_mixed, middle), lse
-    )
+        places, queries, keys, values, mixed_self, after(grad_mixed, middle, down_piece, output), lse
+    )
+    up_piece = over_shard(after(up_sum, down_piece, grad_queries))
 
     text_back = text_back.reshape(2, 2, text_len, block)
     text_kept = lax.dynamic_index_in_dim(text_back, core, 0, keepdims=False)
@@ -1161,10 +1166,10 @@
     qkv_grads = jnp.concatenate(
         [grad_queries, gather_sum(grad_keys), gather_sum(grad_values)], axis=1
     )
-    qkv_theirs = theirs_of(qkv_grads, hidden_one)
+    qkv_theirs = theirs_of(after(qkv_grads, text_grad), hidden_one)
     grad_hidden_one = back_project(after(qkv_grads, qkv_theirs), qkv_matrix)
-    qkv_ours = ours_of(after(qkv_grads, grad_hidden_one), hidden_one, qkv_theirs)
-    qkv_sum = over_outer(after(qkv_ours, middle_sum))
+    qkv_ours = ours_of(after(qkv_grads, grad_hidden_one, up_piece), hidden_one, qkv_theirs)
+    qkv_sum = over_outer(qkv_ours)
     grad_norm, gain_self, bias_self = norm_back(
         after(grad_hidden_one, qkv_ours), inputs, parts_one, norms[0]
     )
@@ -1195,15 +1200,15 @@
     loss = small[6, 0] / (width * count)
     small_own = lax.dynamic_slice_in_dim(small, shard * block, block, 1)
 
-    down_piece = over_shard(down_sum)
+    middle_sum = after(middle_sum, up_piece, frames_grad)
     middle_piece = over_shard(middle_sum[: middle_rows - text_split])
     early = jnp.concatenate(
-        [over_shard(up_sum)]
+        [up_piece]
         + [down_piece[:, i * block : (i + 1) * block] for i in range(4)]
         + [text_piece, middle_piece],
         axis=0,
     )
-    early = lax.all_gather(after(early, qkv_sum), REPLICAS, axis=0)
+    early = lax.all_gather(early, REPLICAS, axis=0)
     piece = width // replicas
     square = (block, width)
     up_grad = unpack(early, hidden_units // replicas, 0, (block, hidden_units), 0, 1)
@@ -1216,7 +1221,8 @@
     output_grad = unpack(early, piece, at, square, 0, 2)
     probe_grad = unpack(early, piece, at + 1, square, 0, 2)
     merge_grad = unpack(early, piece, at + 2, square, 0, 2)
-    late = lax.all_gather(after(over_shard(qkv_sum), early), REPLICAS, axis=0, tiled=True)
+    late = over_shard(after(qkv_sum, middle_piece))
+    late = lax.all_gather(after(late, small, early), REPLICAS, axis=0, tiled=True)
     late = late.reshape(3, width, block)
     qkv_grad = [late[i].T.astype(jnp.float32) for i in range(3)]
     return (

time: 1450 us -> 1370 us (0.945)
  waiting for transfers between devices: 564 us -> 481 us
  starting transfers between devices: 141 us -> 201 us
  local copies, waits for them, and re-layouts: 106 us -> 80.6 us
  other arithmetic: 121 us -> 101 us
    ppermute x27 -> x36, waiting for transfers between devices: 301 us -> 222 us  [hop(): return lax.ppermute(values, 'shard', pairs)]
    all_gather x4 -> x5, waiting for transfers between devices: 106 us -> 41.6 us  [the longest x1 37.4 us: clip_body(): early = lax.all_gather(early, REPLICAS, axis=0)]
    ppermute x27 -> x36, starting transfers between devices: 70.3 us -> 128 us  [hop(): return lax.ppermute(values, 'shard', pairs)]
    ppermute x4 -> x2, waiting for transfers between devices: 0.01 us -> 45.1 us  [over_sides(): return [line, lax.ppermute(line, 'x', swap), lax.ppermute(line, 'y', swap)]]
    reduce_scatter x4, waiting for transfers between devices: 39.5 us -> 0.02 us  [over_outer(): return lax.psum_scatter(values, ('y', 'x'), scatter_dimension=0, tiled=True)]
    ppermute x2, waiting for transfers between devices: 0.01 us -> 31 us  [from_chip(): two = lax.ppermute(jnp.where(even, late, early), spot, back[1])]
    another operation x15 -> x1, other arithmetic: 19.1 us -> 0.07 us  [clip_body(): both = jnp.stack([facts, facts_other])]
    ppermute x2 -> x1, waiting for transfers between devices: 0.01 us -> 17.9 us  [over_corner(): lax.ppermute(over_y[split:], 'x', swap)]
  transfers between devices with their start and end apart: 79 -> 83, of which waited for: 30 -> 37; matrix products, arithmetic and copies ran while one was open for 29% -> 29% of each run, Pallas kernels for 12% -> 13%
where the time goes in v3:
time: 1370 us; the launch traced here: 1360 us
  waiting for transfers between devices  481 us (35%)
  matrix products  305 us (22%)
  starting transfers between devices  201 us (15%)
  Pallas kernels  175 us (13%)
  other arithmetic  101 us (7%)
  local copies, waits for them, and re-layouts  80.6 us (6%)
  between operations  19.9 us (1%)
    ppermute x36, waiting for transfers between devices, hop(): return lax.ppermute(values, 'shard', pairs)  222 us
    ppermute x36, starting transfers between devices, hop(): return lax.ppermute(values, 'shard', pairs)  128 us
    dot_general x8, matrix products, project(): return jnp.dot(left, right, preferred_element_type=jnp.float32)  121 us
    dot_general x13, matrix products, outer_sum(): jnp.einsum('rd,re->de', left, right, preferred_element_type=jnp.float32)  93.4 us
    dot_general x7, matrix products, back_project(): jnp.einsum('re,de->rd', grads, matrix, preferred_element_type=jnp.float32)  91.2 us
    pallas_call x1, Pallas kernels, self_attend_back(): pl.pallas_call(self_backward_kernel, out_shape=(jax.ShapeDtypeStruct((row...  69.2 us
    ppermute x2, waiting for transfers between devices, to_chip(): two = lax.ppermute(jnp.where(lower, pair[1], pair[0]), spot, there[1])  65.3 us
    pallas_call x1, Pallas kernels, self_attend(): pl.pallas_call(self_forward_kernel, out_shape=(jax.ShapeDtypeStruct((rows...  57.4 us
  transfers between devices with their start and end apart: 83, of which 37 were waited for; matrix products, arithmetic and copies ran while one was open for 29% of the time, Pallas kernels for 13%

profile of v3, /device:TPU:0, one launch (start us, length us, event | category | flops | bytes accessed | tf_op | source)
XLA Modules:
  0.0 1363.0 jit_solution(8090768458942685929)
XLA Ops:
  16.7 9.1 collective-permute-done
  26.9 17.1 %collective-permute-done.1 = bf16[48,4608]{1,0:T(8,128)(2,1)} collective-permute-done((bf16[48,4608]{1,0:T(8,128)(2,1)S(1)}, bf16[48,4608]{1,0:T(8,128)(2,1)}, u32[]{:S(2)}, u32[]{:S(2)}) %collective-permute-start.1) | collective-permute-done | bytes 442400 | tf_op jit(solution)/shard_map/ppermute | solution.py:850
  51.0 8.9 collective-permute-start.3
  62.5 10.8 collective-permute-done.3
  75.1 15.3 %collective-permute-done.4 = bf16[48,4608]{1,0:T(8,128)(2,1)S(1)} collective-permute-done((bf16[48,4608]{1,0:T(8,128)(2,1)S(1)}, bf16[48,4608]{1,0:T(8,128)(2,1)S(1)}, u32[]{:S(2)}, u32[]{:S(2)}) %collective-permute-start.4) | collective-permute-done | bytes 442400 | tf_op jit(solution)/shard_map/ppermute | solution.py:850
  92.8 12.2 collective-permute-start.7
  106.3 38.7 %collective-permute-done.7 = bf16[384,1536]{1,0:T(8,128)(2,1)S(1)} collective-permute-done((bf16[384,1536]{1,0:T(8,128)(2,1)S(1)}, bf16[384,1536]{1,0:T(8,128)(2,1)S(1)}, u32[]{:S(2)}, u32[]{:S(2)}) %collective-permute-start.7) | collective-permute-done | bytes 1179680 | tf_op jit(solution)/shard_map/ppermute | solution.py:854
  145.0 17.3 %collective-permute-start.10 = (bf16[48,6144]{1,0:T(8,128)(2,1)S(1)}, bf16[48,6144]{1,0:T(8,128)(2,1)S(1)}, u32[]{:S(2)}, u32[]{:S(2)}) collective-permute-start(bf16[48,6144]{1,0:T(8,128)(2,1)S(1)} %constant_dynamic-slice_fusion.14), channel_id=1, source_target_pairs={{0,2},{1,3},{2,0},{3,1},{4,6},{5,7},{6,4},{7,5},{8,10},{9,11},{10,... | collective-permute-start | bytes 1769480 | tf_op jit(solution)/shard_map/ppermute | solution.py:850
  165.6 27.5 %collective-permute-done.10 = bf16[48,6144]{1,0:T(8,128)(2,1)S(1)} collective-permute-done((bf16[48,6144]{1,0:T(8,128)(2,1)S(1)}, bf16[48,6144]{1,0:T(8,128)(2,1)S(1)}, u32[]{:S(2)}, u32[]{:S(2)}) %collective-permute-start.10) | collective-permute-done | bytes 589856 | tf_op jit(solution)/shard_map/ppermute | solution.py:850
  196.2 15.1 %collective-permute-start.15 = (bf16[6,384]{1,0:T(8,128)(2,1)S(1)}, bf16[6,384]{1,0:T(8,128)(2,1)S(1)}, u32[]{:S(2)}, u32[]{:S(2)}) collective-permute-start(bf16[6,384]{1,0:T(8,128)(2,1)S(1)} %stack.100), channel_id=1, source_target_pairs={{0,1},{1,2},{2,3},{3,0},{4,5},{5,6},{6,7},{7,4},{8,9},{9,10},{10,1... | collective-permute-start | bytes 13832 | tf_op jit(solution)/shard_map/ppermute | solution.py:850
  224.9 13.5 fusion.14
  253.6 7.8 fusion.64.q_ref
  266.8 42.8 %collective-permute-done.13.refs_1_ = bf16[144,4608]{1,0:T(8,128)(2,1)S(1)} collective-permute-done((bf16[144,4608]{1,0:T(8,128)(2,1)}, bf16[144,4608]{1,0:T(8,128)(2,1)S(1)}, u32[]{:S(2)}, u32[]{:S(2)}) %collective-permute-start.13) | collective-permute-done | bytes 1327136 | tf_op jit(solution)/shard_map/ppermute | solution.py:884
  322.2 17.9 %collective-permute-done.20.refs_4_ = bf16[48,4608]{1,0:T(8,128)(2,1)S(1)} collective-permute-done((bf16[48,4608]{1,0:T(8,128)(2,1)S(1)}, bf16[48,4608]{1,0:T(8,128)(2,1)S(1)}, u32[]{:S(2)}, u32[]{:S(2)}) %collective-permute-start.20) | collective-permute-done | bytes 442400 | tf_op jit(solution)/shard_map/ppermute | solution.py:890
  340.1 12.8 collective-permute-done.19.refs_3_
  352.9 57.4 %self_attend.1 = (bf16[768,1536]{1,0:T(8,128)(2,1)S(1)}, f32[96,768]{1,0:T(8,128)S(1)}) custom-call(s32[3]{0:T(128)S(1)} %pad_add_fusion.2.place, bf16[768,1536]{1,0:T(8,128)(2,1)S(1)} %fusion.64.q_ref, bf16[1536,1536]{1,0:T(8,128)(2,1)S(1)} %pad_maximum_fusion.3.k_ref, bf16[1536,1536]{1,0:T(8,128)(2,1)S(1)} %pad_maximum_fusion.2.v_ref), custom_call_target="tpu_custom_call" | custom-call | flops 7247757312 | bytes 18874368 | tf_op jit(solution)/shard_map/self_attend/pallas_call | solution.py:545
  442.7 7.3 assemble.1
  480.8 26.6 %collective-permute-done.34 = bf16[384,1536]{1,0:T(8,128)(2,1)S(1)} collective-permute-done((bf16[384,1536]{1,0:T(8,128)(2,1)S(1)}, bf16[384,1536]{1,0:T(8,128)(2,1)S(1)}, u32[]{:S(2)}, u32[]{:S(2)}) %collective-permute-start.34) | collective-permute-done | bytes 1179680 | tf_op jit(solution)/shard_map/ppermute | solution.py:854
  508.9 61.6 %multiply_convert_fusion = (bf16[768,6144]{1,0:T(8,128)(2,1)}, f32[768,6144]{1,0:T(8,128)}, f32[768,6144]{1,0:T(8,128)}) fusion(bf16[1536,6144]{1,0:T(8,128)(2,1)} %bitcast.181, f32[768,1536]{1,0:T(8,128)} %copy-done.32, f32[1536]{0:T(1024)S(1)} %add.390, f32[1536]{0:T(1024)S(1)} %mul.307, f32[768]{0:T(1024)S(1)} %add_rsqrt_fusion, ...), kind=kOutput, calls=%fused_computation.5 | convolution fusion | flops 14808121344 | bytes 70797312 | tf_op jit(solution)/shard_map/dot_general | solution.py:28
  570.6 22.7 %multiply_convert_fusion.1 = (bf16[768,1536]{1,0:T(8,128)(2,1)S(1)}, f32[768,1536]{1,0:T(8,128)}) fusion(f32[]{:T(128)} %bitcast.43, f32[768]{0:T(1024)S(1)} %copy-done.95, bf16[384,1536]{1,0:T(8,128)(2,1)S(1)} %copy-done.50, bf16[384,1536]{1,0:T(8,128)(2,1)S(1)} %copy-done.48, f32[768,1536]{1,0:T(8,128)} %copy-done.32, ...), kind=kOutput, calls=%fused_computation.70 | convolution fusion | flops 14506131456 | bytes 42470404 | tf_op jit(solution)/shard_map/dot_general | solution.py:28
  593.3 10.2 convolution_convert_fusion.2
  603.5 10.9 collective-permute-start.37
  614.4 29.6 %add_convert_fusion.2 = bf16[768,6144]{1,0:T(8,128)(2,1)} fusion(f32[768,6144]{1,0:T(8,128)} %get-tuple-element.177, f32[768,6144]{1,0:T(8,128)} %get-tuple-element.236, bf16[768,1536]{1,0:T(8,128)(2,1)} %copy-done.73, bf16[6144,1536]{1,0:T(8,128)(2,1)} %bitcast.184), kind=kOutput, calls=%fused_computation.4 | convolution fusion | flops 14561574912 | bytes 68419584 | tf_op jit(solution)/shard_map/re,de->rd/dot_general | solution.py:36
  644.0 14.9 %add_convert_fusion.1 = bf16[768,6144]{1,0:T(8,128)(2,1)} fusion(bf16[768,6144]{1,0:T(8,128)(2,1)} %collective-permute-done.37, bf16[768,6144]{1,0:T(8,128)(2,1)} %get-tuple-element.176, bf16[768,1536]{1,0:T(8,128)(2,1)S(1)} %copy-done.74, s32[]{:T(128)S(6)} %select_n.366), kind=kOutput, calls=%fused_computation.3 | convolution fusion | flops 7261913088 | bytes 29491204 | tf_op jit(solution)/shard_map/rd,re->de/dot_general | solution.py:32
  659.0 13.9 %convolution_convert_fusion.1 = bf16[3072,1536]{1,0:T(8,128)(2,1)} fusion(bf16[768,6144]{1,0:T(8,128)(2,1)} %add_convert_fusion.2, s32[]{:T(128)S(6)} %select_n.367, f32[768,1536]{1,0:T(8,128)} %copy-done.32, f32[1536]{0:T(1024)S(1)} %add.390, f32[1536]{0:T(1024)S(1)} %mul.307, f32[768]{0:T(1024)S(1)} %add_rsqrt_fusion, f32[768]{0:T(1024)S(1)} %broadcast_multiply_fusion.6), kind=kOutput, calls=%fused_computation.21 | convolution fusion | flops 7258374144 | bytes 18892804 | tf_op jit(solution)/shard_map/rd,re->de/dot_general | solution.py:32
  673.0 21.6 %fusion.119 = f32[768,1536]{1,0:T(8,128)} fusion(bf16[768,6144]{1,0:T(8,128)(2,1)} %add_convert_fusion.2, bf16[1536,6144]{1,0:T(8,128)(2,1)} %bitcast.182), kind=kOutput, calls=%fused_computation.292 | convolution fusion | flops 14495514624 | bytes 33030144 | tf_op jit(solution)/shard_map/re,de->rd/dot_general | solution.py:36
  694.5 13.9 %add_convert_fusion = bf16[3072,1536]{1,0:T(8,128)(2,1)} fusion(bf16[3072,1536]{1,0:T(8,128)(2,1)} %collective-permute-done.38, bf16[768,6144]{1,0:T(8,128)(2,1)} %add_convert_fusion.2, s32[]{:T(128)S(6)} %select_n.368, f32[768,1536]{1,0:T(8,128)S(1)} %bitcast.159, f32[1536]{0:T(1024)S(1)} %add.390, f32[1536]{0:T(1024)S(1)} %mul.307, ...), kind=kOutput, calls=%fused_computation.2 | convolution fusion | flops 7267811328 | bytes 28329988 | tf_op jit(solution)/shard_map/rd,re->de/dot_general | solution.py:32
  714.4 13.1 fusion.112
  737.8 9.5 cross_attend_back.1
  754.0 10.5 collective-permute-start.39
  771.2 48.5 %collective-permute-done.46 = bf16[64,1536]{1,0:T(8,128)(2,1)S(1)} collective-permute-done((bf16[64,1536]{1,0:T(8,128)(2,1)S(1)}, bf16[64,1536]{1,0:T(8,128)(2,1)S(1)}, u32[]{:S(2)}, u32[]{:S(2)}) %collective-permute-start.46) | collective-permute-done | bytes 196640 | tf_op jit(solution)/shard_map/ppermute | solution.py:850
  883.5 24.7 %collective-permute-done.49 = bf16[192,1536]{1,0:T(8,128)(2,1)} collective-permute-done((bf16[192,1536]{1,0:T(8,128)(2,1)}, bf16[192,1536]{1,0:T(8,128)(2,1)}, u32[]{:S(2)}, u32[]{:S(2)}) %collective-permute-start.49) | collective-permute-done | bytes 589856 | tf_op jit(solution)/shard_map/ppermute | solution.py:850
  916.2 69.2 %self_attend_back.1 = (bf16[768,1536]{1,0:T(8,128)(2,1)S(1)}, bf16[1536,1536]{1,0:T(8,128)(2,1)S(1)}, bf16[1536,1536]{1,0:T(8,128)(2,1)S(1)}) custom-call(s32[3]{0:T(128)S(1)} %copy-done.19, bf16[768,1536]{1,0:T(8,128)(2,1)S(1)} %copy-done.27, bf16[1536,1536]{1,0:T(8,128)(2,1)} %copy-done.9, bf16[1536,1536]{1,0:T(8,128)(2,1)} %copy-done.8, ...), custom_call_target="tpu_custom_call" | custom-call | flops 18119393280 | bytes 37748736 | tf_op jit(solution)/shard_map/self_attend_back/pallas_call | solution.py:570
  1000.4 13.1 collective-permute-start.54
  1031.9 7.8 convolution_convert_fusion
  1045.9 18.9 %fusion.120 = f32[768,1536]{1,0:T(8,128)} fusion(bf16[768,4608]{1,0:T(8,128)(2,1)} %copy-done.46, bf16[1536,4608]{1,0:T(8,128)(2,1)} %bitcast.187), kind=kOutput, calls=%fused_computation.293 | convolution fusion | flops 10871635968 | bytes 25952256 | tf_op jit(solution)/shard_map/re,de->rd/dot_general | solution.py:36
  1064.7 19.9 %collective-permute-done.58 = bf16[768,384]{1,0:T(8,128)(2,1)S(1)} collective-permute-done((bf16[768,384]{1,0:T(8,128)(2,1)S(1)}, bf16[768,384]{1,0:T(8,128)(2,1)S(1)}, u32[]{:S(2)}, u32[]{:S(2)}) %collective-permute-start.58) | collective-permute-done | bytes 589856 | tf_op jit(solution)/shard_map/ppermute | solution.py:850
  1086.9 9.8 add_convert_fusion.3
  1108.3 16.7 %collective-permute-start.67 = (bf16[384,1536]{1,0:T(8,128)(2,1)S(1)}, bf16[384,1536]{1,0:T(8,128)(2,1)S(1)}, u32[]{:S(2)}, u32[]{:S(2)}) collective-permute-start(bf16[384,1536]{1,0:T(8,128)(2,1)S(1)} %get-tuple-element.198), channel_id=1, source_target_pairs={{1,0},{5,1},{4,2},{0,3},{3,4},{7,5},{6,6},{2,7},{9,8},{13,9},{12,1... | collective-permute-start | bytes 3538952 | tf_op jit(solution)/shard_map/ppermute | solution.py:863
  1126.4 31.0 %collective-permute-done.67 = bf16[384,1536]{1,0:T(8,128)(2,1)S(1)} collective-permute-done((bf16[384,1536]{1,0:T(8,128)(2,1)S(1)}, bf16[384,1536]{1,0:T(8,128)(2,1)S(1)}, u32[]{:S(2)}, u32[]{:S(2)}) %collective-permute-start.67) | collective-permute-done | bytes 1179680 | tf_op jit(solution)/shard_map/ppermute | solution.py:863
  1163.3 16.0 %collective-permute-start.68 = (bf16[576,384]{1,0:T(8,128)(2,1)}, bf16[576,384]{1,0:T(8,128)(2,1)S(1)}, u32[]{:S(2)}, u32[]{:S(2)}) collective-permute-start(bf16[576,384]{1,0:T(8,128)(2,1)} %get-tuple-element.220), channel_id=1, source_target_pairs={{0,1},{1,2},{2,3},{3,0},{4,5},{5,6},{6,7},{7,4},{8,9},{9,10},{10,1... | collective-permute-start | bytes 1327112 | tf_op jit(solution)/shard_map/ppermute | solution.py:850
  1185.0 8.4 collective-permute-done.68
  1193.5 18.6 %collective-permute-done.69 = bf16[576,384]{1,0:T(8,128)(2,1)} collective-permute-done((bf16[576,384]{1,0:T(8,128)(2,1)}, bf16[576,384]{1,0:T(8,128)(2,1)}, u32[]{:S(2)}, u32[]{:S(2)}) %collective-permute-start.69) | collective-permute-done | bytes 442400 | tf_op jit(solution)/shard_map/ppermute | solution.py:850
  1215.7 10.1 collective-permute-start.71
  1240.9 14.9 %collective-permute-done.64 = f32[8,1536]{1,0:T(8,128)S(1)} collective-permute-done((f32[8,1536]{1,0:T(8,128)S(1)}, f32[8,1536]{1,0:T(8,128)S(1)}, u32[]{:S(2)}, u32[]{:S(2)}) %collective-permute-start.64) | collective-permute-done | bytes 49184 | tf_op jit(solution)/shard_map/ppermute | solution.py:1199
  1256.6 9.9 collective-permute-done.65
  1268.5 37.4 %all-gather.15.cloned.1.call-done = bf16[19968,384]{1,0:T(8,128)(2,1)} async-done(((bf16[2496,384]{1,0:T(8,128)(2,1)}), bf16[19968,384]{1,0:T(8,128)(2,1)}) %all-gather.15.cloned.1.call-update) | async-done | bytes 15335440 | tf_op jit(solution)/shard_map/all_gather | solution.py:1211
  1319.3 8.1 unpack.13
  (578 shorter events, 369.6 us)
Async XLA Ops:
  7.2 217.6 %all-gather.7.cloned.1.call-start = ((), (), s32[]{:S(2)}) async-start(), calls=%async_computation.4 | async-start | bytes 15925248 | tf_op jit(solution)/shard_map/all_gather | solution.py:880
  12.6 31.4 %collective-permute-start.1 = (bf16[48,4608]{1,0:T(8,128)(2,1)S(1)}, bf16[48,4608]{1,0:T(8,128)(2,1)}, u32[]{:S(2)}, u32[]{:S(2)}) collective-permute-start(bf16[48,4608]{1,0:T(8,128)(2,1)S(1)} %pad_maximum_fusion.9), channel_id=1, source_target_pairs={{0,2},{1,3},{2,0},{3,1},{4,6},{5,7},{6,4},{7,5},{8,10},{9,11},{10,... | collective-permute-start | bytes 1327112 | tf_op jit(solution)/shard_map/ppermute | solution.py:850
  15.2 29.9 %collective-permute-start.2 = (bf16[48,4608]{1,0:T(8,128)(2,1)S(1)}, bf16[48,4608]{1,0:T(8,128)(2,1)}, u32[]{:S(2)}, u32[]{:S(2)}) collective-permute-start(bf16[48,4608]{1,0:T(8,128)(2,1)S(1)} %pad_maximum_fusion.9), channel_id=1, source_target_pairs={{0,3},{1,0},{2,1},{3,2},{4,7},{5,4},{6,5},{7,6},{8,11},{9,8},{10,9... | collective-permute-start | bytes 1327112 | tf_op jit(solution)/shard_map/ppermute | solution.py:850
  47.4 461.5 %all-gather.9.cloned.1.call-start = ((), (), s32[]{:S(2)}) async-start(), calls=%async_computation.5 | async-start | bytes 21233664 | tf_op jit(solution)/shard_map/all_gather | solution.py:880
  51.0 22.3 %collective-permute-start.3 = (bf16[48,4608]{1,0:T(8,128)(2,1)S(1)}, bf16[48,4608]{1,0:T(8,128)(2,1)}, u32[]{:S(2)}, u32[]{:S(2)}) collective-permute-start(bf16[48,4608]{1,0:T(8,128)(2,1)S(1)} %constant_dynamic-slice_fusion.19), channel_id=1, source_target_pairs={{0,1},{1,2},{2,3},{3,0},{4,5},{5,6},{6,7},{7,4},{8,9},{9,10},{10,1... | collective-permute-start | bytes 1327112 | tf_op jit(solution)/shard_map/ppermute | solution.py:850
  59.8 30.5 %collective-permute-start.4 = (bf16[48,4608]{1,0:T(8,128)(2,1)S(1)}, bf16[48,4608]{1,0:T(8,128)(2,1)S(1)}, u32[]{:S(2)}, u32[]{:S(2)}) collective-permute-start(bf16[48,4608]{1,0:T(8,128)(2,1)S(1)} %constant_dynamic-slice_fusion.19), channel_id=1, source_target_pairs={{0,2},{1,3},{2,0},{3,1},{4,6},{5,7},{6,4},{7,5},{8,10},{9,11},{10,... | collective-permute-start | bytes 1327112 | tf_op jit(solution)/shard_map/ppermute | solution.py:850
  62.5 28.6 %collective-permute-start.5 = (bf16[48,4608]{1,0:T(8,128)(2,1)S(1)}, bf16[48,4608]{1,0:T(8,128)(2,1)S(1)}, u32[]{:S(2)}, u32[]{:S(2)}) collective-permute-start(bf16[48,4608]{1,0:T(8,128)(2,1)S(1)} %constant_dynamic-slice_fusion.19), channel_id=1, source_target_pairs={{0,3},{1,0},{2,1},{3,2},{4,7},{5,4},{6,5},{7,6},{8,11},{9,8},{10,9... | collective-permute-start | bytes 1327112 | tf_op jit(solution)/shard_map/ppermute | solution.py:850
  92.8 52.2 %collective-permute-start.7 = (bf16[384,1536]{1,0:T(8,128)(2,1)S(1)}, bf16[384,1536]{1,0:T(8,128)(2,1)S(1)}, u32[]{:S(2)}, u32[]{:S(2)}) collective-permute-start(bf16[384,1536]{1,0:T(8,128)(2,1)S(1)} %get-tuple-element.215), channel_id=1, source_target_pairs={{0,1},{1,5},{2,4},{3,0},{4,3},{5,7},{6,6},{7,2},{8,9},{9,13},{10,1... | collective-permute-start | bytes 3538952 | tf_op jit(solution)/shard_map/ppermute | solution.py:854
  145.0 48.1 %collective-permute-start.10 = (bf16[48,6144]{1,0:T(8,128)(2,1)S(1)}, bf16[48,6144]{1,0:T(8,128)(2,1)S(1)}, u32[]{:S(2)}, u32[]{:S(2)}) collective-permute-start(bf16[48,6144]{1,0:T(8,128)(2,1)S(1)} %constant_dynamic-slice_fusion.14), channel_id=1, source_target_pairs={{0,2},{1,3},{2,0},{3,1},{4,6},{5,7},{6,4},{7,5},{8,10},{9,11},{10,... | collective-permute-start | bytes 1769480 | tf_op jit(solution)/shard_map/ppermute | solution.py:850
  162.3 30.9 %collective-permute-start.11 = (bf16[48,6144]{1,0:T(8,128)(2,1)S(1)}, bf16[48,6144]{1,0:T(8,128)(2,1)S(1)}, u32[]{:S(2)}, u32[]{:S(2)}) collective-permute-start(bf16[48,6144]{1,0:T(8,128)(2,1)S(1)} %constant_dynamic-slice_fusion.14), channel_id=1, source_target_pairs={{0,3},{1,0},{2,1},{3,2},{4,7},{5,4},{6,5},{7,6},{8,11},{9,8},{10,9... | collective-permute-start | bytes 1769480 | tf_op jit(solution)/shard_map/ppermute | solution.py:850
  194.7 375.9 %all-gather.11.cloned.1.call-start = ((), (), s32[]{:S(2)}) async-start(), calls=%async_computation.6 | async-start | bytes 21233664 | tf_op jit(solution)/shard_map/all_gather | solution.py:880
  238.4 23.0 %collective-permute-start.18 = (bf16[768,3072]{1,0:T(8,128)(2,1)}, bf16[768,3072]{1,0:T(8,128)(2,1)}, u32[]{:S(2)}, u32[]{:S(2)}) collective-permute-start(bf16[768,3072]{1,0:T(8,128)(2,1)} %fusion.14), channel_id=1, source_target_pairs={{0,4},{4,0},{1,5},{5,1},{2,6},{6,2},{3,7},{7,3},{8,12},{12,8},{9,1... | collective-permute-start | bytes 14155784 | tf_op jit(solution)/shard_map/ppermute | solution.py:974
  250.6 59.0 %collective-permute-start.13 = (bf16[144,4608]{1,0:T(8,128)(2,1)}, bf16[144,4608]{1,0:T(8,128)(2,1)S(1)}, u32[]{:S(2)}, u32[]{:S(2)}) collective-permute-start(bf16[144,4608]{1,0:T(8,128)(2,1)} %constant_dynamic-update-slice_fusion.3.refs_0_), channel_id=1, source_target_pairs={{0,8},{8,0},{1,9},{9,1},{2,10},{10,2},{3,11},{11,3},{4,12},{12,4},... | collective-permute-start | bytes 3981320 | tf_op jit(solution)/shard_map/ppermute | solution.py:884
  252.1 59.7 %collective-permute-start.14 = (bf16[144,4608]{1,0:T(8,128)(2,1)}, bf16[144,4608]{1,0:T(8,128)(2,1)S(1)}, u32[]{:S(2)}, u32[]{:S(2)}) collective-permute-start(bf16[144,4608]{1,0:T(8,128)(2,1)} %constant_dynamic-update-slice_fusion.3.refs_0_), channel_id=1, source_target_pairs={{0,16},{16,0},{1,17},{17,1},{2,18},{18,2},{3,19},{19,3},{4,20},{20... | collective-permute-start | bytes 3981320 | tf_op jit(solution)/shard_map/ppermute | solution.py:884
  311.9 41.0 %collective-permute-start.19 = (bf16[96,4608]{1,0:T(8,128)(2,1)S(1)}, bf16[96,4608]{1,0:T(8,128)(2,1)S(1)}, u32[]{:S(2)}, u32[]{:S(2)}) collective-permute-start(bf16[96,4608]{1,0:T(8,128)(2,1)S(1)} %slice.223), channel_id=1, source_target_pairs={{0,16},{16,0},{1,17},{17,1},{2,18},{18,2},{3,19},{19,3},{4,20},{20... | collective-permute-start | bytes 2654216 | tf_op jit(solution)/shard_map/ppermute | solution.py:889
  314.2 97.6 %collective-permute-start.30 = (bf16[192,1536]{1,0:T(8,128)(2,1)}, bf16[192,1536]{1,0:T(8,128)(2,1)S(1)}, u32[]{:S(2)}, u32[]{:S(2)}) collective-permute-start(bf16[192,1536]{1,0:T(8,128)(2,1)} %constant_dynamic-slice_fusion.13), channel_id=1, source_target_pairs={{0,1},{1,2},{2,3},{3,0},{4,5},{5,6},{6,7},{7,4},{8,9},{9,10},{10,1... | collective-permute-start | bytes 1769480 | tf_op jit(solution)/shard_map/ppermute | solution.py:850
  314.2 97.5 %collective-permute-start.31 = (bf16[192,1536]{1,0:T(8,128)(2,1)}, bf16[192,1536]{1,0:T(8,128)(2,1)S(1)}, u32[]{:S(2)}, u32[]{:S(2)}) collective-permute-start(bf16[192,1536]{1,0:T(8,128)(2,1)} %constant_dynamic-slice_fusion.13), channel_id=1, source_target_pairs={{0,2},{1,3},{2,0},{3,1},{4,6},{5,7},{6,4},{7,5},{8,10},{9,11},{10,... | collective-permute-start | bytes 1769480 | tf_op jit(solution)/shard_map/ppermute | solution.py:850
  316.2 95.5 %collective-permute-start.32 = (bf16[192,1536]{1,0:T(8,128)(2,1)}, bf16[192,1536]{1,0:T(8,128)(2,1)S(1)}, u32[]{:S(2)}, u32[]{:S(2)}) collective-permute-start(bf16[192,1536]{1,0:T(8,128)(2,1)} %constant_dynamic-slice_fusion.13), channel_id=1, source_target_pairs={{0,3},{1,0},{2,1},{3,2},{4,7},{5,4},{6,5},{7,6},{8,11},{9,8},{10,9... | collective-permute-start | bytes 1769480 | tf_op jit(solution)/shard_map/ppermute | solution.py:850
  318.4 21.7 %collective-permute-start.20 = (bf16[48,4608]{1,0:T(8,128)(2,1)S(1)}, bf16[48,4608]{1,0:T(8,128)(2,1)S(1)}, u32[]{:S(2)}, u32[]{:S(2)}) collective-permute-start(bf16[48,4608]{1,0:T(8,128)(2,1)S(1)} %slice.224), channel_id=1, source_target_pairs={{0,8},{8,0},{1,9},{9,1},{2,10},{10,2},{3,11},{11,3},{4,12},{12,4},... | collective-permute-start | bytes 1327112 | tf_op jit(solution)/shard_map/ppermute | solution.py:890
  414.3 447.1 %reduce-scatter.5.cloned.1.call-start = ((), (), s32[]{:S(2)}) async-start(), calls=%async_computation.7 | async-start | bytes 11796480 | tf_op jit(solution)/shard_map/reduce_scatter | solution.py:1041
  462.8 44.5 %collective-permute-start.34 = (bf16[384,1536]{1,0:T(8,128)(2,1)S(1)}, bf16[384,1536]{1,0:T(8,128)(2,1)S(1)}, u32[]{:S(2)}, u32[]{:S(2)}) collective-permute-start(bf16[384,1536]{1,0:T(8,128)(2,1)S(1)} %get-tuple-element.212), channel_id=1, source_target_pairs={{0,1},{1,5},{2,4},{3,0},{4,3},{5,7},{6,6},{7,2},{8,9},{9,13},{10,1... | collective-permute-start | bytes 3538952 | tf_op jit(solution)/shard_map/ppermute | solution.py:854
  603.5 40.5 %collective-permute-start.37 = (bf16[768,6144]{1,0:T(8,128)(2,1)}, bf16[768,6144]{1,0:T(8,128)(2,1)}, u32[]{:S(2)}, u32[]{:S(2)}) collective-permute-start(bf16[768,6144]{1,0:T(8,128)(2,1)} %convolution_convert_fusion.2), channel_id=1, source_target_pairs={{0,4},{4,0},{1,5},{5,1},{2,6},{6,2},{3,7},{7,3},{8,12},{12,8},{9,1... | collective-permute-start | bytes 28311560 | tf_op jit(solution)/shard_map/ppermute | solution.py:1036
  658.9 380.8 %reduce-scatter.7.cloned.1.call-start = ((), (), s32[]{:S(2)}) async-start(), calls=%async_computation.8 | async-start | bytes 11796480 | tf_op jit(solution)/shard_map/reduce_scatter | solution.py:1041
  708.5 451.6 %reduce-scatter.11.cloned.1.call-start = ((), (), s32[]{:S(2)}) async-start(), calls=%async_computation.10 | async-start | bytes 10321920 | tf_op jit(solution)/shard_map/reduce_scatter | solution.py:1041
  749.2 72.6 %collective-permute-start.41 = (bf16[768,1536]{1,0:T(8,128)(2,1)}, bf16[768,1536]{1,0:T(8,128)(2,1)S(1)}, u32[]{:S(2)}, u32[]{:S(2)}) collective-permute-start(bf16[768,1536]{1,0:T(8,128)(2,1)} %convolution_convert_fusion.5), channel_id=1, source_target_pairs={{0,4},{4,0},{1,5},{5,1},{2,6},{6,2},{3,7},{7,3},{8,12},{12,8},{9,1... | collective-permute-start | bytes 7077896 | tf_op jit(solution)/shard_map/ppermute | solution.py:1036
  754.0 90.1 %collective-permute-start.39 = (bf16[384,1536]{1,0:T(8,128)(2,1)}, bf16[384,1536]{1,0:T(8,128)(2,1)}, u32[]{:S(2)}, u32[]{:S(2)}) collective-permute-start(bf16[384,1536]{1,0:T(8,128)(2,1)} %get-tuple-element.207), channel_id=1, source_target_pairs={{0,0},{4,1},{5,2},{1,3},{2,4},{6,5},{7,6},{3,7},{8,8},{12,9},{13,1... | collective-permute-start | bytes 3538952 | tf_op jit(solution)/shard_map/ppermute | solution.py:862
  764.6 79.6 %collective-permute-start.40 = (bf16[384,1536]{1,0:T(8,128)(2,1)}, bf16[384,1536]{1,0:T(8,128)(2,1)}, u32[]{:S(2)}, u32[]{:S(2)}) collective-permute-start(bf16[384,1536]{1,0:T(8,128)(2,1)} %get-tuple-element.208), channel_id=1, source_target_pairs={{1,0},{5,1},{4,2},{0,3},{3,4},{7,5},{6,6},{2,7},{9,8},{13,9},{12,1... | collective-permute-start | bytes 3538952 | tf_op jit(solution)/shard_map/ppermute | solution.py:863
  766.5 53.1 %collective-permute-start.46 = (bf16[64,1536]{1,0:T(8,128)(2,1)S(1)}, bf16[64,1536]{1,0:T(8,128)(2,1)S(1)}, u32[]{:S(2)}, u32[]{:S(2)}) collective-permute-start(bf16[64,1536]{1,0:T(8,128)(2,1)S(1)} %get-tuple-element.171), channel_id=1, source_target_pairs={{0,2},{1,3},{2,0},{3,1},{4,6},{5,7},{6,4},{7,5},{8,10},{9,11},{10,... | collective-permute-start | bytes 589832 | tf_op jit(solution)/shard_map/ppermute | solution.py:850
  766.6 53.1 %collective-permute-start.47 = (bf16[64,1536]{1,0:T(8,128)(2,1)S(1)}, bf16[64,1536]{1,0:T(8,128)(2,1)S(1)}, u32[]{:S(2)}, u32[]{:S(2)}) collective-permute-start(bf16[64,1536]{1,0:T(8,128)(2,1)S(1)} %get-tuple-element.171), channel_id=1, source_target_pairs={{0,3},{1,0},{2,1},{3,2},{4,7},{5,4},{6,5},{7,6},{8,11},{9,8},{10,9... | collective-permute-start | bytes 589832 | tf_op jit(solution)/shard_map/ppermute | solution.py:850
  828.8 24.0 %collective-permute-start.42 = (bf16[768,1536]{1,0:T(8,128)(2,1)}, bf16[768,1536]{1,0:T(8,128)(2,1)}, u32[]{:S(2)}, u32[]{:S(2)}) collective-permute-start(bf16[768,1536]{1,0:T(8,128)(2,1)} %convolution_convert_fusion.4), channel_id=1, source_target_pairs={{0,4},{4,0},{1,5},{5,1},{2,6},{6,2},{3,7},{7,3},{8,12},{12,8},{9,1... | collective-permute-start | bytes 7077896 | tf_op jit(solution)/shard_map/ppermute | solution.py:1036
  867.8 40.4 %collective-permute-start.49 = (bf16[192,1536]{1,0:T(8,128)(2,1)}, bf16[192,1536]{1,0:T(8,128)(2,1)}, u32[]{:S(2)}, u32[]{:S(2)}) collective-permute-start(bf16[192,1536]{1,0:T(8,128)(2,1)} %get-tuple-element.204), channel_id=1, source_target_pairs={{0,2},{1,3},{2,0},{3,1},{4,6},{5,7},{6,4},{7,5},{8,10},{9,11},{10,... | collective-permute-start | bytes 1769480 | tf_op jit(solution)/shard_map/ppermute | solution.py:850
  869.5 38.8 %collective-permute-start.50 = (bf16[192,1536]{1,0:T(8,128)(2,1)}, bf16[192,1536]{1,0:T(8,128)(2,1)}, u32[]{:S(2)}, u32[]{:S(2)}) collective-permute-start(bf16[192,1536]{1,0:T(8,128)(2,1)} %get-tuple-element.203), channel_id=1, source_target_pairs={{0,3},{1,0},{2,1},{3,2},{4,7},{5,4},{6,5},{7,6},{8,11},{9,8},{10,9... | collective-permute-start | bytes 1769480 | tf_op jit(solution)/shard_map/ppermute | solution.py:850
  876.2 338.1 %reduce-scatter.9.cloned.1.call-start = ((), (), s32[]{:S(2)}) async-start(), calls=%async_computation.9 | async-start | bytes 8847360 | tf_op jit(solution)/shard_map/reduce_scatter | solution.py:1041
  989.0 34.2 %collective-permute-start.51 = (bf16[768,1536]{1,0:T(8,128)(2,1)}, bf16[768,1536]{1,0:T(8,128)(2,1)}, u32[]{:S(2)}, u32[]{:S(2)}) collective-permute-start(bf16[768,1536]{1,0:T(8,128)(2,1)} %broadcast_select_fusion.1), channel_id=1, source_target_pairs={{0,4},{4,0},{1,5},{5,1},{2,6},{6,2},{3,7},{7,3},{8,12},{12,8},{9,1... | collective-permute-start | bytes 7077896 | tf_op jit(solution)/shard_map/ppermute | solution.py:1163
  992.6 35.0 %collective-permute-start.52 = (bf16[768,1536]{1,0:T(8,128)(2,1)}, bf16[768,1536]{1,0:T(8,128)(2,1)}, u32[]{:S(2)}, u32[]{:S(2)}) collective-permute-start(bf16[768,1536]{1,0:T(8,128)(2,1)} %broadcast_select_fusion), channel_id=1, source_target_pairs={{0,4},{4,0},{1,5},{5,1},{2,6},{6,2},{3,7},{7,3},{8,12},{12,8},{9,1... | collective-permute-start | bytes 7077896 | tf_op jit(solution)/shard_map/ppermute | solution.py:1163
  1039.7 47.1 %collective-permute-start.60 = (bf16[2304,1536]{1,0:T(8,128)(2,1)}, bf16[2304,1536]{1,0:T(8,128)(2,1)}, u32[]{:S(2)}, u32[]{:S(2)}) collective-permute-start(bf16[2304,1536]{1,0:T(8,128)(2,1)} %convolution_convert_fusion), channel_id=1, source_target_pairs={{0,4},{4,0},{1,5},{5,1},{2,6},{6,2},{3,7},{7,3},{8,12},{12,8},{9,1... | collective-permute-start | bytes 21233672 | tf_op jit(solution)/shard_map/ppermute | solution.py:1036
  1041.3 23.4 %collective-permute-start.57 = (bf16[768,384]{1,0:T(8,128)(2,1)S(1)}, bf16[768,384]{1,0:T(8,128)(2,1)S(1)}, u32[]{:S(2)}, u32[]{:S(2)}) collective-permute-start(bf16[768,384]{1,0:T(8,128)(2,1)S(1)} %get-tuple-element.199), channel_id=1, source_target_pairs={{0,1},{1,2},{2,3},{3,0},{4,5},{5,6},{6,7},{7,4},{8,9},{9,10},{10,1... | collective-permute-start | bytes 1769480 | tf_op jit(solution)/shard_map/ppermute | solution.py:850
  1043.3 41.4 %collective-permute-start.58 = (bf16[768,384]{1,0:T(8,128)(2,1)S(1)}, bf16[768,384]{1,0:T(8,128)(2,1)S(1)}, u32[]{:S(2)}, u32[]{:S(2)}) collective-permute-start(bf16[768,384]{1,0:T(8,128)(2,1)S(1)} %get-tuple-element.201), channel_id=1, source_target_pairs={{0,2},{1,3},{2,0},{3,1},{4,6},{5,7},{6,4},{7,5},{8,10},{9,11},{10,... | collective-permute-start | bytes 1769480 | tf_op jit(solution)/shard_map/ppermute | solution.py:850
  1045.9 38.8 %collective-permute-start.59 = (bf16[768,384]{1,0:T(8,128)(2,1)S(1)}, bf16[768,384]{1,0:T(8,128)(2,1)S(1)}, u32[]{:S(2)}, u32[]{:S(2)}) collective-permute-start(bf16[768,384]{1,0:T(8,128)(2,1)S(1)} %get-tuple-element.200), channel_id=1, source_target_pairs={{0,3},{1,0},{2,1},{3,2},{4,7},{5,4},{6,5},{7,6},{8,11},{9,8},{10,9... | collective-permute-start | bytes 1769480 | tf_op jit(solution)/shard_map/ppermute | solution.py:850
  1096.7 209.2 %all-gather.15.cloned.1.call-start = ((), (), s32[]{:S(2)}) async-start(), calls=%async_computation.12 | async-start | bytes 17252352 | tf_op jit(solution)/shard_map/all_gather | solution.py:1211
  1108.3 49.1 %collective-permute-start.67 = (bf16[384,1536]{1,0:T(8,128)(2,1)S(1)}, bf16[384,1536]{1,0:T(8,128)(2,1)S(1)}, u32[]{:S(2)}, u32[]{:S(2)}) collective-permute-start(bf16[384,1536]{1,0:T(8,128)(2,1)S(1)} %get-tuple-element.198), channel_id=1, source_target_pairs={{1,0},{5,1},{4,2},{0,3},{3,4},{7,5},{6,6},{2,7},{9,8},{13,9},{12,1... | collective-permute-start | bytes 3538952 | tf_op jit(solution)/shard_map/ppermute | solution.py:863
  1163.3 30.1 %collective-permute-start.68 = (bf16[576,384]{1,0:T(8,128)(2,1)}, bf16[576,384]{1,0:T(8,128)(2,1)S(1)}, u32[]{:S(2)}, u32[]{:S(2)}) collective-permute-start(bf16[576,384]{1,0:T(8,128)(2,1)} %get-tuple-element.220), channel_id=1, source_target_pairs={{0,1},{1,2},{2,3},{3,0},{4,5},{5,6},{6,7},{7,4},{8,9},{9,10},{10,1... | collective-permute-start | bytes 1327112 | tf_op jit(solution)/shard_map/ppermute | solution.py:850
  1179.3 32.7 %collective-permute-start.69 = (bf16[576,384]{1,0:T(8,128)(2,1)}, bf16[576,384]{1,0:T(8,128)(2,1)}, u32[]{:S(2)}, u32[]{:S(2)}) collective-permute-start(bf16[576,384]{1,0:T(8,128)(2,1)} %get-tuple-element.222), channel_id=1, source_target_pairs={{0,2},{1,3},{2,0},{3,1},{4,6},{5,7},{6,4},{7,5},{8,10},{9,11},{10,... | collective-permute-start | bytes 1327112 | tf_op jit(solution)/shard_map/ppermute | solution.py:850
  1182.7 29.3 %collective-permute-start.70 = (bf16[576,384]{1,0:T(8,128)(2,1)}, bf16[576,384]{1,0:T(8,128)(2,1)}, u32[]{:S(2)}, u32[]{:S(2)}) collective-permute-start(bf16[576,384]{1,0:T(8,128)(2,1)} %get-tuple-element.221), channel_id=1, source_target_pairs={{0,3},{1,0},{2,1},{3,2},{4,7},{5,4},{6,5},{7,6},{8,11},{9,8},{10,9... | collective-permute-start | bytes 1327112 | tf_op jit(solution)/shard_map/ppermute | solution.py:850
  1214.2 128.2 %all-gather.13.cloned.1.call-start = ((), (), s32[]{:S(2)}) async-start(), calls=%async_computation.11 | async-start | bytes 3981312 | tf_op jit(solution)/shard_map/all_gather | solution.py:1225
  1215.7 50.8 %collective-permute-start.71 = (bf16[576,384]{1,0:T(8,128)(2,1)S(1)}, bf16[576,384]{1,0:T(8,128)(2,1)S(1)}, u32[]{:S(2)}, u32[]{:S(2)}) collective-permute-start(bf16[576,384]{1,0:T(8,128)(2,1)S(1)} %get-tuple-element.217), channel_id=1, source_target_pairs={{0,1},{1,2},{2,3},{3,0},{4,5},{5,6},{6,7},{7,4},{8,9},{9,10},{10,1... | collective-permute-start | bytes 1327112 | tf_op jit(solution)/shard_map/ppermute | solution.py:850
  1225.8 40.7 %collective-permute-start.72 = (bf16[576,384]{1,0:T(8,128)(2,1)S(1)}, bf16[576,384]{1,0:T(8,128)(2,1)S(1)}, u32[]{:S(2)}, u32[]{:S(2)}) collective-permute-start(bf16[576,384]{1,0:T(8,128)(2,1)S(1)} %get-tuple-element.219), channel_id=1, source_target_pairs={{0,2},{1,3},{2,0},{3,1},{4,6},{5,7},{6,4},{7,5},{8,10},{9,11},{10,... | collective-permute-start | bytes 1327112 | tf_op jit(solution)/shard_map/ppermute | solution.py:850
  1226.4 40.1 %collective-permute-start.73 = (bf16[576,384]{1,0:T(8,128)(2,1)S(1)}, bf16[576,384]{1,0:T(8,128)(2,1)S(1)}, u32[]{:S(2)}, u32[]{:S(2)}) collective-permute-start(bf16[576,384]{1,0:T(8,128)(2,1)S(1)} %get-tuple-element.218), channel_id=1, source_target_pairs={{0,3},{1,0},{2,1},{3,2},{4,7},{5,4},{6,5},{7,6},{8,11},{9,8},{10,9... | collective-permute-start | bytes 1327112 | tf_op jit(solution)/shard_map/ppermute | solution.py:850
  (155 other events, 2734.5 us)
Sparse Core Ops, SparseCore 0:
  47.5 87.3 all-gather.6
  194.8 160.8 all-gather.8
  414.5 96.6 all-gather.10
  659.0 92.3 reduce-scatter.4
  755.0 95.0 reduce-scatter.6
  876.3 84.2 reduce-scatter.10
  1096.8 86.7 reduce-scatter.8
  1214.3 91.5 all-gather.14
  1308.4 33.9 all-gather.12

commit v4 on v1

--- a/solution.py
+++ b/solution.py
@@ -438,7 +438,19 @@
     return jnp.where(inside, value, 0.0).astype(jnp.bfloat16)
 
 
-def self_forward_kernel(place, q_ref, k_ref, v_ref, mixed_ref, lse_ref, acc_ref):
+def fill_clip(place, own_ref, other_ref, all_ref):
+    block = own_ref.shape[0] // 2
+    for part in range(2):
+        rows = slice(part * block, (part + 1) * block)
+        for at, ref in ((place[part], own_ref), (place[3 + part], other_ref)):
+            all_ref[pl.ds(pl.multiple_of(at * block, block), block), :] = ref[rows, :]
+
+
+def self_forward_kernel(
+    place, q_ref, own_k, own_v, other_k, other_v, mixed_ref, lse_ref, k_ref, v_ref, acc_ref
+):
+    fill_clip(place, own_k, other_k, k_ref)
+    fill_clip(place, own_v, other_v, v_ref)
     block = q_ref.shape[0] // 2
     length = place[2]
     low = lax.broadcasted_iota(jnp.int32, (PAIR, 1), 0) < HEAD_DIM
@@ -481,9 +493,11 @@
 
 
 def self_backward_kernel(
-    place, q_ref, k_ref, v_ref, mixed_ref, grad_ref, lse_ref, dq_ref, dk_ref, dv_ref,
-    dq_acc, dk_acc, dv_acc,
+    place, q_ref, own_k, own_v, other_k, other_v, mixed_ref, grad_ref, lse_ref,
+    dq_ref, own_dk, own_dv, other_dk, other_dv, k_ref, v_ref, dq_acc, dk_acc, dv_acc,
 ):
+    fill_clip(place, own_k, other_k, k_ref)
+    fill_clip(place, own_v, other_v, v_ref)
     block = q_ref.shape[0] // 2
     length = place[2]
     scale = HEAD_DIM ** (-0.5)
@@ -530,17 +544,27 @@
 
         lax.fori_loop(0, place[part] + 1, step, 0)
         dq_ref[rows, :] = dq_acc[...].T.astype(jnp.bfloat16)
-    dk_ref[...] = dk_acc[...].astype(jnp.bfloat16)
-    dv_ref[...] = dv_acc[...].astype(jnp.bfloat16)
+    for part in range(2):
+        rows = slice(part * block, (part + 1) * block)
+        own = pl.ds(pl.multiple_of(place[part] * block, block), block)
+        other = pl.ds(pl.multiple_of(place[3 + part] * block, block), block)
+        own_dk[rows, :] = dk_acc[own, :].astype(jnp.bfloat16)
+        own_dv[rows, :] = dv_acc[own, :].astype(jnp.bfloat16)
+        other_dk[rows, :] = dk_acc[other, :].astype(jnp.bfloat16)
+        other_dv[rows, :] = dv_acc[other, :].astype(jnp.bfloat16)
 
 
 def pair_block(rows):
     return pl.BlockSpec((rows, PAIR), lambda i, *_: (0, i))
 
 
-def self_attend(place, queries, keys, values):
+def value_block(rows, pairs):
+    return pl.BlockSpec((rows, PAIR), lambda i, *_: (0, pairs + i))
+
+
+def self_attend(place, queries, own, other):
     rows, width = queries.shape
-    clip = keys.shape[0]
+    clip = 2 * rows
     pairs = width // PAIR
     return pl.pallas_call(
         self_forward_kernel,
@@ -551,42 +575,43 @@
         grid_spec=pltpu.PrefetchScalarGridSpec(
             num_scalar_prefetch=1,
             grid=(pairs,),
-            in_specs=[pair_block(rows), pair_block(clip), pair_block(clip)],
+            in_specs=[pair_block(rows)] + [pair_block(rows), value_block(rows, pairs)] * 2,
             out_specs=(pair_block(rows), pl.BlockSpec((8, rows), lambda i, *_: (i, 0))),
-            scratch_shapes=[pltpu.VMEM((2, PAIR, rows // 2), jnp.float32)],
+            scratch_shapes=[
+                pltpu.VMEM((clip, PAIR), jnp.bfloat16),
+                pltpu.VMEM((clip, PAIR), jnp.bfloat16),
+                pltpu.VMEM((2, PAIR, rows // 2), jnp.float32),
+            ],
         ),
         compiler_params=pltpu.CompilerParams(vmem_limit_bytes=32 * 2**20),
         cost_estimate=pl.CostEstimate(
             flops=2 * 2 * rows * clip * width, bytes_accessed=8 * clip * width, transcendentals=0
         ),
         name="self_attend",
-    )(place, queries, keys, values)
-
-
-def self_attend_back(place, queries, keys, values, mixed, grads, lse):
+    )(place, queries, own, own, other, other)
+
+
+def self_attend_back(place, queries, own, other, mixed, grads, lse):
     rows, width = queries.shape
-    clip = keys.shape[0]
+    clip = 2 * rows
     pairs = width // PAIR
     return pl.pallas_call(
         self_backward_kernel,
-        out_shape=(
-            jax.ShapeDtypeStruct((rows, width), jnp.bfloat16),
-            jax.ShapeDtypeStruct((clip, width), jnp.bfloat16),
-            jax.ShapeDtypeStruct((clip, width), jnp.bfloat16),
-        ),
+        out_shape=(jax.ShapeDtypeStruct((rows, width), jnp.bfloat16),) * 5,
         grid_spec=pltpu.PrefetchScalarGridSpec(
             num_scalar_prefetch=1,
             grid=(pairs,),
-            in_specs=[
-                pair_block(rows),
-                pair_block(clip),
-                pair_block(clip),
+            in_specs=[pair_block(rows)]
+            + [pair_block(rows), value_block(rows, pairs)] * 2
+            + [
                 pair_block(rows),
                 pair_block(rows),
                 pl.BlockSpec((8, rows), lambda i, *_: (i, 0)),
             ],
-            out_specs=(pair_block(rows), pair_block(clip), pair_block(clip)),
+            out_specs=(pair_block(rows),) * 5,
             scratch_shapes=[
+                pltpu.VMEM((clip, PAIR), jnp.bfloat16),
+                pltpu.VMEM((clip, PAIR), jnp.bfloat16),
                 pltpu.VMEM((PAIR, rows // 2), jnp.float32),
                 pltpu.VMEM((clip, PAIR), jnp.float32),
                 pltpu.VMEM((clip, PAIR), jnp.float32),
@@ -597,7 +622,7 @@
             flops=5 * 2 * rows * clip * width, bytes_accessed=16 * clip * width, transcendentals=0
         ),
         name="self_attend_back",
-    )(place, queries, keys, values, mixed, grads, lse)
+    )(place, queries, own, own, other, other, mixed, grads, lse)
 
 
 def both_heads(rows, value):
@@ -722,6 +747,10 @@
         ),
         name="unpack",
     )(full)
+
+
+def held(values, *others):
+    return list(lax.optimization_barrier((*values, *others))[: len(values)])
 
 
 def after(value, *others):
@@ -800,79 +829,101 @@
         pairs = [(i, (i + distance) % shards) for i in range(shards)]
         return lax.ppermute(values, "shard", pairs)
 
+    def hops(values):
+        return [hop(values, distance) for distance in (1, 2, 3)]
+
+    def line_up(mine, came):
+        out = jnp.zeros((shards,) + mine.shape, mine.dtype)
+        out = lax.dynamic_update_index_in_dim(out, mine, shard, 0)
+        for distance, values in zip((1, 2, 3), came):
+            owner = lax.rem(shard + shards - distance, shards)
+            out = lax.dynamic_update_index_in_dim(out, values, owner, 0)
+        return out
+
     def to_chip(pair):
         one = lax.ppermute(jnp.where(lower, pair[0], pair[1]), spot, there[0])
         two = lax.ppermute(jnp.where(lower, pair[1], pair[0]), spot, there[1])
+        return one, two
+
+    def by_time(one, two):
         return jnp.concatenate([jnp.where(even, one, two), jnp.where(even, two, one)], axis=0)
 
     def from_chip(values):
         early, late = values[:block], values[block:]
         one = lax.ppermute(jnp.where(even, early, late), spot, back[0])
         two = lax.ppermute(jnp.where(even, late, early), spot, back[1])
+        return one, two
+
+    def by_slot(one, two):
         return jnp.stack([jnp.where(lower, one, two), jnp.where(lower, two, one)])
 
     def share_of(weight):
         share = weight.shape[0] // replicas
         return lax.dynamic_slice_in_dim(weight, replica * share, share, 0)
 
-    def whole(parts):
-        return lax.all_gather(jnp.concatenate(parts, axis=1), EVERY, axis=0, tiled=True)
-
-    share = block // replicas
-    facts = jnp.concatenate(
-        [(clip_lengths // 64)[:, None], (clip_lengths % 64)[:, None], slot_used[:, None], text_mask],
+    def from_replicas(line):
+        full = lax.all_gather(line, ("y", "x", "core"), axis=1, tiled=True)
+        return full.reshape(-1, line.shape[-1])
+
+    qkv_share = jnp.concatenate(
+        [share_of(self_query_weight), share_of(self_key_weight), share_of(self_value_weight)],
         axis=1,
-    ).astype(jnp.bfloat16)
-    rider = jnp.zeros((share, PAIR), jnp.bfloat16)
-    for i, vector in enumerate(
-        (
+    )
+    vectors = jnp.concatenate(
+        [
             self_norm_gain,
             self_norm_bias,
             cross_norm_gain,
             cross_norm_bias,
             feed_norm_gain,
             feed_norm_bias,
-        )
-    ):
-        rider = rider.at[:, i].set(share_of(vector))
-    rider = rider.at[:2, 8 : 8 + facts.shape[1]].set(facts)
-    first = whole(
-        [
-            share_of(self_query_weight),
-            share_of(self_key_weight),
-            share_of(self_value_weight),
-            rider,
         ]
     )
-    x_low = to_chip(frames)
-    teacher_low = to_chip(teacher)
-    rest = whole(
-        [share_of(self_output_weight), share_of(cross_query_weight), share_of(cross_output_weight)]
-    )
-    expand_matrix = whole([share_of(feed_up_weight)])
-
-    quarter_rows = feed_down_weight.shape[0] // 4
-    quarter = 2 * lax.axis_index("x") + core
-    mine = lax.dynamic_slice_in_dim(feed_down_weight, quarter * quarter_rows, quarter_rows, 0)
-    reduce_matrix = jnp.zeros((hidden_units, width), jnp.bfloat16)
-    reduce_matrix = lax.dynamic_update_slice_in_dim(
-        reduce_matrix, feed_down_weight, shard * 4 * quarter_rows, 0
-    )
-    for distance in (1, 2, 3):
-        came = hop(mine, distance)
-        across = lax.ppermute(came, "x", swap)
-        owner = lax.rem(shard + shards - distance, shards)
-        for values, which in (
-            (came, quarter),
-            (across, lax.rem(quarter + 2, 4)),
-            (lax.ppermute(came, "core", swap), quarter + 1 - 2 * core),
-            (lax.ppermute(across, "core", swap), lax.rem(quarter + 3 - 2 * core, 4)),
-        ):
-            reduce_matrix = lax.dynamic_update_slice_in_dim(
-                reduce_matrix, values, (owner * 4 + which) * quarter_rows, 0
-            )
-
-    text_other = lax.ppermute(text_states, "core", swap)
+    vectors = jnp.pad(vectors[None, :], ((0, 15), (0, 3 * width - 6 * block)))
+    qkv_mine = jnp.concatenate([qkv_share, vectors], axis=0)
+    qkv_came = hops(qkv_mine)
+    share = qkv_share.shape[0]
+    qkv_line = line_up(qkv_share, [values[:share] for values in qkv_came])
+    qkv_matrix = from_replicas(qkv_line)
+    norms = line_up(qkv_mine[share], [values[share] for values in qkv_came])
+    norms = norms[:, : 6 * block].reshape(shards, 6, block).transpose(1, 0, 2)
+    norms = norms.reshape(6, width).astype(jnp.float32)
+
+    came = to_chip(after(frames, *qkv_came))
+    x_low = by_time(*came)
+    rest_share = jnp.concatenate(
+        [share_of(self_output_weight), share_of(cross_query_weight), share_of(cross_output_weight)],
+        axis=1,
+    )
+    rest_came = hops(after(rest_share, *came))
+    rest = from_replicas(line_up(rest_share, rest_came))
+    output_matrix = rest[:, :width]
+    probe_matrix = rest[:, width : 2 * width]
+    merge_matrix = rest[:, 2 * width :]
+    expand_share = share_of(feed_up_weight)
+    expand_came = hops(after(expand_share, *rest_came))
+
+    facts = jnp.concatenate(
+        [(clip_lengths // 64)[:, None], (clip_lengths % 64)[:, None], slot_used[:, None], text_mask],
+        axis=1,
+    ).astype(jnp.bfloat16)
+    facts = jnp.pad(facts[:, None, :], ((0, 0), (0, 15), (0, width - facts.shape[1])))
+    text_sent = lax.ppermute(jnp.concatenate([text_states, facts], axis=1), "core", swap)
+    text_other = text_sent[:, :text_len]
+    both = jnp.stack([facts[:, 0], text_sent[:, text_len]])[:, :, : 3 + text_len].astype(jnp.int32)
+    lengths = 64 * both[:, :, 0] + both[:, :, 1]
+    fact = lax.dynamic_index_in_dim(
+        jnp.where(shard // 2 == core, both[0], both[1]), shard % 2, 0, keepdims=False
+    )
+    length, used = 64 * fact[0] + fact[1], fact[2]
+    present = fact[3:].reshape(text_len, 1)
+    count = jnp.sum(
+        jnp.where(both[:, :, 2] > 0, jnp.minimum(lengths, clip), 0).astype(jnp.float32)
+    )
+    count = jnp.full((8, 128), count)
+    for axis in ("x", "y"):
+        count += lax.ppermute(count, axis, swap)
+    count = count[0, 0]
     text_all = jnp.concatenate(
         [
             jnp.where(first_core, text_states, text_other),
@@ -883,70 +934,51 @@
     text_all = lax.dynamic_slice_in_dim(text_all, shard * block, block, 1)
     text_matrix = jnp.where(first_core, cross_key_weight, cross_value_weight)
     text_part = project(text_all, text_matrix).astype(jnp.bfloat16).reshape(4, text_len, width)
+    text_came = [
+        hop(
+            lax.dynamic_index_in_dim(
+                text_part, lax.rem(shard + distance, shards), 0, keepdims=False
+            ),
+            distance,
+        )
+        for distance in (1, 2, 3)
+    ]
+
+    places = jnp.stack([core, 3 - core, length, 1 - core, 2 + core]).astype(jnp.int32)
+    positions = jnp.concatenate(
+        [core * block + jnp.arange(block), (3 - core) * block + jnp.arange(block)]
+    )
+    valid_rows = ((positions < length) & (used > 0)).astype(jnp.float32)[:, None]
+    inputs = x_low.astype(jnp.float32)
+    parts_one = norm_parts(inputs)
+    hidden_one = ((inputs - parts_one[0]) * parts_one[1] * norms[0] + norms[1]).astype(
+        jnp.bfloat16
+    )
+    kv = project(hidden_one, qkv_matrix[:, width:]).astype(jnp.bfloat16)
+    kv_other = lax.ppermute(kv, "core", swap)
+    queries = project(after(hidden_one, kv), qkv_matrix[:, :width]).astype(jnp.bfloat16)
+    expand_line = line_up(expand_share, held(expand_came, queries, kv_other))
+    expand_matrix = from_replicas(expand_line)
+    reduce_share = share_of(feed_down_weight)
+    reduce_came = hops(after(reduce_share, *expand_came))
+    mixed_self, lse = self_attend(after(places, expand_line, text_part), queries, kv, kv_other)
+    reduce_matrix = from_replicas(line_up(reduce_share, held(reduce_came, mixed_self)))
+    text_came = held(text_came, mixed_self)
     text_half = lax.dynamic_index_in_dim(text_part, shard, 0, keepdims=False).astype(jnp.float32)
-    for distance in (1, 2, 3):
-        away = lax.dynamic_index_in_dim(
-            text_part, lax.rem(shard + distance, shards), 0, keepdims=False
-        )
-        text_half += hop(away, distance).astype(jnp.float32)
+    for values in text_came:
+        text_half += values.astype(jnp.float32)
     text_half = text_half.astype(jnp.bfloat16)
     text_swap = lax.ppermute(text_half, "core", swap)
     lookups = jnp.where(first_core, text_half, text_swap)
     contents = jnp.where(first_core, text_swap, text_half)
-
-    qkv_matrix = first[:, : 3 * width]
-    norms = first[:, 3 * width : 3 * width + 8].astype(jnp.float32).T
-    facts = (
-        first[: replicas * share, 3 * width + 8 : 3 * width + 11 + text_len]
-        .reshape(replicas, share, 3 + text_len)[:, :2]
-        .astype(jnp.int32)
-        .reshape(2 * replicas, 3 + text_len)
-    )
-    lengths = facts[:, 0] * 64 + facts[:, 1]
-    slot = outer * 4 + shard
-    length = lengths[slot]
-    used = facts[slot, 2]
-    present = facts[slot, 3:].reshape(text_len, 1)
-    count = jnp.sum(jnp.where(facts[:, 2] > 0, jnp.minimum(lengths, clip), 0)).astype(jnp.float32)
-    places = jnp.stack([core, 3 - core, length]).astype(jnp.int32)
-    positions = jnp.concatenate(
-        [core * block + jnp.arange(block), (3 - core) * block + jnp.arange(block)]
-    )
-    valid_rows = ((positions < length) & (used > 0)).astype(jnp.float32)[:, None]
-    output_matrix = rest[:, :width]
-    probe_matrix = rest[:, width : 2 * width]
-    merge_matrix = rest[:, 2 * width :]
-
-    inputs = x_low.astype(jnp.float32)
-    parts_one = norm_parts(inputs)
-    hidden_one = ((inputs - parts_one[0]) * parts_one[1] * norms[0] + norms[1]).astype(
-        jnp.bfloat16
-    )
-    kv = project(hidden_one, qkv_matrix[:, width:]).astype(jnp.bfloat16)
-    kv_other = lax.ppermute(kv, "core", swap)
-    queries = project(after(hidden_one, kv), qkv_matrix[:, :width]).astype(jnp.bfloat16)
-
-    def in_order(mine, other):
-        return jnp.concatenate(
-            [
-                jnp.where(first_core, mine[:block], other[:block]),
-                jnp.where(first_core, other[:block], mine[:block]),
-                jnp.where(first_core, other[block:], mine[block:]),
-                jnp.where(first_core, mine[block:], other[block:]),
-            ],
-            axis=0,
-        )
-
-    keys = in_order(kv[:, :width], kv_other[:, :width])
-    values = in_order(kv[:, width:], kv_other[:, width:])
-    mixed_self, lse = self_attend(places, queries, keys, values)
     after_self = inputs + project(mixed_self, output_matrix)
     parts_two = norm_parts(after_self)
     hidden_two = ((after_self - parts_two[0]) * parts_two[1] * norms[2] + norms[3]).astype(
         jnp.bfloat16
     )
     probes = project(hidden_two, probe_matrix).astype(jnp.bfloat16)
-    cross_mixed = cross_attend(probes, lookups, contents, present)
+    teacher_low = by_time(*to_chip(after(teacher, *reduce_came, probes)))
+    cross_mixed = cross_attend(probes, lookups, contents, after(present, count))
     after_cross = after_self + project(cross_mixed, merge_matrix)
     parts_three = norm_parts(after_cross)
     hidden_three = (
@@ -975,14 +1007,23 @@
     def over_outer(values):
         return lax.psum_scatter(values, ("y", "x"), scatter_dimension=0, tiled=True)
 
-    def over_shard(values):
+    def shard_hops(values):
+        columns = values.shape[1] // shards
+        return [
+            hop(
+                lax.dynamic_slice_in_dim(
+                    values, lax.rem(shard + distance, shards) * columns, columns, 1
+                ),
+                distance,
+            )
+            for distance in (1, 2, 3)
+        ]
+
+    def over_shard(values, came):
         columns = values.shape[1] // shards
         total = lax.dynamic_slice_in_dim(values, shard * columns, columns, 1).astype(jnp.float32)
-        for distance in (1, 2, 3):
-            away = lax.dynamic_slice_in_dim(
-                values, lax.rem(shard + distance, shards) * columns, columns, 1
-            )
-            total += hop(away, distance).astype(jnp.float32)
+        for part in came:
+            total += part.astype(jnp.float32)
         return total.astype(jnp.bfloat16)
 
     down_theirs = theirs_of(grad_feed_low, activated_low)
@@ -993,8 +1034,6 @@
     up_theirs = theirs_of(after(grad_upward, down_ours), hidden_three)
     grad_hidden_three = back_project(after(grad_upward, up_theirs), expand_matrix)
     up_ours = ours_of(after(grad_upward, grad_hidden_three), hidden_three, up_theirs)
-    up_sum = over_outer(up_ours)
-    output = from_chip(after(result.astype(jnp.bfloat16), up_ours))
     grad_norm, gain_feed, bias_feed = norm_back(
         after(grad_hidden_three, up_ours), after_cross, parts_three, norms[4]
     )
@@ -1007,6 +1046,7 @@
     probe_grads, lookup_grads, content_grads = cross_attend_back(
         probes, lookups, contents, present, grad_cross_mixed
     )
+    up_sum = over_outer(up_ours)
     text_mine = jnp.where(first_core, lookup_grads, content_grads)
     text_sent = lax.ppermute(
         jnp.where(first_core, content_grads, lookup_grads), "core", swap
@@ -1017,16 +1057,7 @@
     merge_ours = ours_of(after(grad_cross_low, probe_grads), cross_mixed, merge_theirs)
     probe_theirs = theirs_of(after(probe_grads, merge_ours), hidden_two)
     grad_hidden_two = back_project(after(probe_grads, probe_theirs), probe_matrix)
-    text_four = jnp.zeros((4, text_len, width), jnp.bfloat16)
-    text_four = lax.dynamic_update_index_in_dim(text_four, text_mine, shard, 0)
-    for distance in (1, 2, 3):
-        text_four = lax.dynamic_update_index_in_dim(
-            text_four,
-            hop(text_mine, distance),
-            lax.rem(shard + shards - distance, shards),
-            0,
-        )
-    text_four = text_four.reshape(4 * text_len, width)
+    text_four = line_up(text_mine, hops(text_mine)).reshape(4 * text_len, width)
     grad_norm, gain_cross, bias_cross = norm_back(
         grad_hidden_two, after_self, parts_two, norms[2]
     )
@@ -1065,10 +1096,6 @@
         .transpose(1, 0, 2)
         .reshape(text_rows, block)
     )
-    grad_queries, grad_keys, grad_values = self_attend_back(
-        places, queries, keys, values, mixed_self, after(grad_mixed, middle), lse
-    )
-
     text_back = text_back.reshape(2, 2, text_len, block)
     text_kept = lax.dynamic_index_in_dim(text_back, core, 0, keepdims=False)
     text_gone = lax.dynamic_index_in_dim(text_back, 1 - core, 0, keepdims=False)
@@ -1076,39 +1103,36 @@
         jnp.float32
     )
     text_own = text_own.astype(jnp.bfloat16)
-    text_grad = jnp.zeros(text_states.shape, jnp.float32)
-    text_grad = lax.dynamic_update_slice_in_dim(
-        text_grad, text_own.astype(jnp.float32), shard * block, 2
-    )
-    for distance in (1, 2, 3):
-        text_grad = lax.dynamic_update_slice_in_dim(
-            text_grad,
-            hop(text_own, distance).astype(jnp.float32),
-            lax.rem(shard + shards - distance, shards) * block,
-            2,
-        )
-
-    def gather_sum(grads):
-        quarters = [grads[i * block : (i + 1) * block] for i in range(4)]
-        outside = jnp.concatenate([quarters[0], quarters[3]], axis=0)
-        inside = jnp.concatenate([quarters[1], quarters[2]], axis=0)
-        mine = jnp.where(first_core, outside, inside)
-        other = lax.ppermute(jnp.where(first_core, inside, outside), "core", swap)
-        return (mine.astype(jnp.float32) + other.astype(jnp.float32)).astype(jnp.bfloat16)
-
-    qkv_grads = jnp.concatenate(
-        [grad_queries, gather_sum(grad_keys), gather_sum(grad_values)], axis=1
-    )
+    down_came = shard_hops(down_sum)
+    output_came = from_chip(after(result.astype(jnp.bfloat16), middle))
+    grad_queries, own_keys, own_values, other_keys, other_values = self_attend_back(
+        places, queries, kv, kv_other, mixed_self, after(grad_mixed, middle, text_own), lse
+    )
+    down_came = held(down_came, grad_queries)
+    output_came = held(output_came, grad_queries)
+    other_keys, other_values = held([other_keys, other_values], *down_came, *output_came)
+    own_keys += lax.ppermute(other_keys, "core", swap)
+    own_values += lax.ppermute(other_values, "core", swap)
+    down_piece = over_shard(down_sum, down_came)
+    output = by_slot(*output_came)
+    up_came = shard_hops(after(up_sum, down_piece))
+    text_came = hops(after(text_own, grad_queries))
+
+    qkv_grads = jnp.concatenate([grad_queries, own_keys, own_values], axis=1)
     qkv_theirs = theirs_of(qkv_grads, hidden_one)
     grad_hidden_one = back_project(after(qkv_grads, qkv_theirs), qkv_matrix)
-    qkv_ours = ours_of(after(qkv_grads, grad_hidden_one), hidden_one, qkv_theirs)
+    qkv_ours = ours_of(
+        after(qkv_grads, grad_hidden_one, *up_came, *text_came), hidden_one, qkv_theirs
+    )
+    up_piece = over_shard(up_sum, up_came)
+    text_grad = line_up(text_own, text_came).astype(jnp.float32)
+    text_grad = text_grad.transpose(1, 2, 0, 3).reshape(text_states.shape)
     qkv_sum = over_outer(qkv_ours)
     grad_norm, gain_self, bias_self = norm_back(
         after(grad_hidden_one, qkv_ours), inputs, parts_one, norms[0]
     )
-    frames_grad = from_chip((grad_after_self + grad_norm).astype(jnp.bfloat16)).astype(
-        jnp.float32
-    )
+    frames_came = from_chip((grad_after_self + grad_norm).astype(jnp.bfloat16))
+    frames_grad = by_slot(*frames_came).astype(jnp.float32)
 
     small = jnp.stack(
         [
@@ -1133,10 +1157,11 @@
     loss = small[6, 0] / (width * count)
     small_own = lax.dynamic_slice_in_dim(small, shard * block, block, 1)
 
-    down_piece = over_shard(down_sum)
-    middle_piece = over_shard(middle_sum[: middle_rows - text_split])
+    middle_sum = after(middle_sum, up_piece, *frames_came)
+    middle_kept = middle_sum[: middle_rows - text_split]
+    middle_piece = over_shard(middle_kept, shard_hops(middle_kept))
     early = jnp.concatenate(
-        [over_shard(up_sum)]
+        [up_piece]
         + [down_piece[:, i * block : (i + 1) * block] for i in range(4)]
         + [text_piece, middle_piece],
         axis=0,
@@ -1154,7 +1179,9 @@
     output_grad = unpack(early, piece, at, square, 0, 2)
     probe_grad = unpack(early, piece, at + 1, square, 0, 2)
     merge_grad = unpack(early, piece, at + 2, square, 0, 2)
-    late = lax.all_gather(over_shard(qkv_sum), REPLICAS, axis=0, tiled=True)
+    qkv_sum = after(qkv_sum, middle_piece, small)
+    late = over_shard(qkv_sum, shard_hops(qkv_sum))
+    late = lax.all_gather(after(late, early), REPLICAS, axis=0, tiled=True)
     late = late.reshape(3, width, block)
     qkv_grad = [late[i].T.astype(jnp.float32) for i in range(3)]
     return (

time: 1550 us -> 1210 us (0.78)
  waiting for transfers between devices: 607 us -> 311 us
  other arithmetic: 124 us -> 83.3 us
  starting transfers between devices: 214 us -> 198 us
    reduce_scatter x4, waiting for transfers between devices: 276 us -> 0.06 us  [over_outer(): return lax.psum_scatter(values, ('y', 'x'), scatter_dimension=0, tiled=True)]
    ppermute x24 -> x33, waiting for transfers between devices: 286 us -> 170 us  [hop(): return lax.ppermute(values, 'shard', pairs)]
    ppermute x1, starting transfers between devices: 70.7 us -> 4.71 us  [clip_body(): kv_other = lax.ppermute(kv, 'core', swap)]
    ppermute x24 -> x33, starting transfers between devices: 56.2 us -> 108 us  [hop(): return lax.ppermute(values, 'shard', pairs)]
    ppermute x2, waiting for transfers between devices: 7.93 us -> 59 us  [to_chip(): two = lax.ppermute(jnp.where(lower, pair[1], pair[0]), spot, there[1])]
    all_gather x1, waiting for transfers between devices: 0.01 us -> 30.9 us  [clip_body(): early = lax.all_gather(early, REPLICAS, axis=0)]
    ppermute x2, waiting for transfers between devices: 0.01 us -> 28.8 us  [from_chip(): two = lax.ppermute(jnp.where(even, late, early), spot, back[1])]
    ppermute x12 -> x5, starting transfers between devices: 32.9 us -> 6.23 us  [the longest x2 3.11 us: clip_body(): count += lax.ppermute(count, axis, swap)]
  transfers between devices with their start and end apart: 68 -> 71, of which waited for: 24 -> 28; matrix products, arithmetic and copies ran while one was open for 19% -> 33% of each run, Pallas kernels for 5% -> 14%
where the time goes in v4:
time: 1210 us; the launch traced here: 1200 us
  waiting for transfers between devices  311 us (26%)
  matrix products  310 us (26%)
  starting transfers between devices  198 us (16%)
  Pallas kernels  169 us (14%)
  local copies, waits for them, and re-layouts  105 us (9%)
  other arithmetic  83.3 us (7%)
  between operations  21.7 us (2%)
    ppermute x33, waiting for transfers between devices, hop(): return lax.ppermute(values, 'shard', pairs)  170 us
    dot_general x8, matrix products, project(): return jnp.dot(left, right, preferred_element_type=jnp.float32)  128 us
    ppermute x33, starting transfers between devices, hop(): return lax.ppermute(values, 'shard', pairs)  108 us
    dot_general x7, matrix products, back_project(): jnp.einsum('re,de->rd', grads, matrix, preferred_element_type=jnp.float32)  92.9 us
    dot_general x13, matrix products, outer_sum(): jnp.einsum('rd,re->de', left, right, preferred_element_type=jnp.float32)  89 us
    pallas_call x1, Pallas kernels, self_attend_back(): pl.pallas_call(self_backward_kernel, out_shape=(jax.ShapeDtypeStruct((row...  69.8 us
    ppermute x2, waiting for transfers between devices, to_chip(): two = lax.ppermute(jnp.where(lower, pair[1], pair[0]), spot, there[1])  59 us
    pallas_call x1, Pallas kernels, self_attend(): pl.pallas_call(self_forward_kernel, out_shape=(jax.ShapeDtypeStruct((rows...  58.5 us
  transfers between devices with their start and end apart: 71, of which 28 were waited for; matrix products, arithmetic and copies ran while one was open for 33% of the time, Pallas kernels for 14%

profile of v4, /device:TPU:0, one launch (start us, length us, event | category | flops | bytes accessed | tf_op | source)
XLA Modules:
  0.0 1197.6 jit_solution(7816803478693959138)
XLA Ops:
  20.9 12.3 %collective-permute-done = bf16[64,4608]{1,0:T(8,128)(2,1)} collective-permute-done((bf16[64,4608]{1,0:T(8,128)(2,1)S(1)}, bf16[64,4608]{1,0:T(8,128)(2,1)}, u32[]{:S(2)}, u32[]{:S(2)}) %collective-permute-start) | collective-permute-done | bytes 589856 | tf_op jit(solution)/shard_map/ppermute | solution.py:830
  34.2 23.4 %collective-permute-done.1 = bf16[64,4608]{1,0:T(8,128)(2,1)} collective-permute-done((bf16[64,4608]{1,0:T(8,128)(2,1)S(1)}, bf16[64,4608]{1,0:T(8,128)(2,1)}, u32[]{:S(2)}, u32[]{:S(2)}) %collective-permute-start.1) | collective-permute-done | bytes 589856 | tf_op jit(solution)/shard_map/ppermute | solution.py:830
  63.5 15.1 %collective-permute-start.4 = (bf16[384,1536]{1,0:T(8,128)(2,1)S(1)}, bf16[384,1536]{1,0:T(8,128)(2,1)S(1)}, u32[]{:S(2)}, u32[]{:S(2)}) collective-permute-start(bf16[384,1536]{1,0:T(8,128)(2,1)S(1)} %get-tuple-element.239), channel_id=1, source_target_pairs={{0,1},{1,5},{2,4},{3,0},{4,3},{5,7},{6,6},{7,2},{8,9},{9,13},{10,1... | collective-permute-start | bytes 3538952 | tf_op jit(solution)/shard_map/ppermute | solution.py:845
  80.8 37.8 %collective-permute-done.4 = bf16[384,1536]{1,0:T(8,128)(2,1)S(1)} collective-permute-done((bf16[384,1536]{1,0:T(8,128)(2,1)S(1)}, bf16[384,1536]{1,0:T(8,128)(2,1)S(1)}, u32[]{:S(2)}, u32[]{:S(2)}) %collective-permute-start.4) | collective-permute-done | bytes 1179680 | tf_op jit(solution)/shard_map/ppermute | solution.py:845
  119.8 15.7 %collective-permute-start.7 = (bf16[48,4608]{1,0:T(8,128)(2,1)S(1)}, bf16[48,4608]{1,0:T(8,128)(2,1)S(1)}, u32[]{:S(2)}, u32[]{:S(2)}) collective-permute-start(bf16[48,4608]{1,0:T(8,128)(2,1)S(1)} %pad_maximum_fusion.7), channel_id=1, source_target_pairs={{0,2},{1,3},{2,0},{3,1},{4,6},{5,7},{6,4},{7,5},{8,10},{9,11},{10,... | collective-permute-start | bytes 1327112 | tf_op jit(solution)/shard_map/ppermute | solution.py:830
  138.4 19.4 %collective-permute-done.7 = bf16[48,4608]{1,0:T(8,128)(2,1)S(1)} collective-permute-done((bf16[48,4608]{1,0:T(8,128)(2,1)S(1)}, bf16[48,4608]{1,0:T(8,128)(2,1)S(1)}, u32[]{:S(2)}, u32[]{:S(2)}) %collective-permute-start.7) | collective-permute-done | bytes 442400 | tf_op jit(solution)/shard_map/ppermute | solution.py:830
  169.4 10.8 fusion.14.own_k.own_v
  186.3 7.7 collective-permute-start.10
  198.0 8.3 fusion.61.q_ref
  206.3 14.6 %collective-permute-done.10 = bf16[48,6144]{1,0:T(8,128)(2,1)S(1)} collective-permute-done((bf16[48,6144]{1,0:T(8,128)(2,1)S(1)}, bf16[48,6144]{1,0:T(8,128)(2,1)S(1)}, u32[]{:S(2)}, u32[]{:S(2)}) %collective-permute-start.10) | collective-permute-done | bytes 589856 | tf_op jit(solution)/shard_map/ppermute | solution.py:830
  220.9 15.5 %collective-permute-done.9 = bf16[48,6144]{1,0:T(8,128)(2,1)S(1)} collective-permute-done((bf16[48,6144]{1,0:T(8,128)(2,1)S(1)}, bf16[48,6144]{1,0:T(8,128)(2,1)S(1)}, u32[]{:S(2)}, u32[]{:S(2)}) %collective-permute-start.9) | collective-permute-done | bytes 589856 | tf_op jit(solution)/shard_map/ppermute | solution.py:830
  251.8 10.3 collective-permute-start.19
  273.4 58.5 %self_attend.1 = (bf16[768,1536]{1,0:T(8,128)(2,1)S(1)}, f32[96,768]{1,0:T(8,128)S(1)}) custom-call(s32[5]{0:T(128)S(1)} %stack.66.place, bf16[768,1536]{1,0:T(8,128)(2,1)S(1)} %copy-done.21, bf16[768,3072]{1,0:T(8,128)(2,1)S(1)} %copy-done.13, bf16[768,3072]{1,0:T(8,128)(2,1)S(1)} %copy-done.13, bf16[768,3072]{1,0:T(8,128)(2,1)S(1)} %copy-done.15, ...), custom_call_target="tpu_custom_call" | custom-call | flops 7247757312 | bytes 18874368 | tf_op jit(solution)/shard_map/self_attend/pallas_call | solution.py:569
  349.5 7.2 fusion.127
  358.3 7.7 fusion.55.probe_ref
  373.8 6.8 cross_attend.1
  380.7 6.8 fusion.128
  390.2 21.2 %collective-permute-done.23 = bf16[384,1536]{1,0:T(8,128)(2,1)S(1)} collective-permute-done((bf16[384,1536]{1,0:T(8,128)(2,1)S(1)}, bf16[384,1536]{1,0:T(8,128)(2,1)S(1)}, u32[]{:S(2)}, u32[]{:S(2)}) %collective-permute-start.23) | collective-permute-done | bytes 1179680 | tf_op jit(solution)/shard_map/ppermute | solution.py:845
  413.1 61.5 %multiply_convert_fusion = (bf16[768,6144]{1,0:T(8,128)(2,1)}, f32[768,6144]{1,0:T(8,128)}, f32[768,6144]{1,0:T(8,128)}) fusion(bf16[1536,6144]{1,0:T(8,128)(2,1)} %bitcast.201, f32[768,1536]{1,0:T(8,128)} %copy-done.25, f32[1536]{0:T(1024)S(1)} %add.428, f32[1536]{0:T(1024)S(1)} %mul.314, f32[768]{0:T(1024)S(1)} %add_rsqrt_fusion, ...), kind=kOutput, calls=%fused_computation.5 | convolution fusion | flops 14808121344 | bytes 70797312 | tf_op jit(solution)/shard_map/dot_general | solution.py:28
  474.6 25.2 %multiply_convert_fusion.1 = (bf16[768,1536]{1,0:T(8,128)(2,1)S(1)}, f32[768,1536]{1,0:T(8,128)}) fusion(f32[]{:T(128)S(6)} %div.75, f32[768]{0:T(1024)S(1)} %copy-done.92, bf16[384,1536]{1,0:T(8,128)(2,1)S(1)} %copy-done.39, bf16[384,1536]{1,0:T(8,128)(2,1)S(1)} %copy-done.37, f32[768,1536]{1,0:T(8,128)} %copy-done.25, ...), kind=kOutput, calls=%fused_computation.66 | convolution fusion | flops 14506131456 | bytes 42470404 | tf_op jit(solution)/shard_map/dot_general | solution.py:28
  499.8 9.9 convolution_convert_fusion.2
  509.7 11.6 collective-permute-start.24
  521.3 29.6 %add_convert_fusion.2 = bf16[768,6144]{1,0:T(8,128)(2,1)} fusion(f32[768,6144]{1,0:T(8,128)} %get-tuple-element.211, f32[768,6144]{1,0:T(8,128)} %get-tuple-element.263, bf16[768,1536]{1,0:T(8,128)(2,1)} %copy-done.60, bf16[6144,1536]{1,0:T(8,128)(2,1)} %bitcast.204), kind=kOutput, calls=%fused_computation.4 | convolution fusion | flops 14561574912 | bytes 68419584 | tf_op jit(solution)/shard_map/re,de->rd/dot_general | solution.py:36
  550.9 14.9 %add_convert_fusion.1 = bf16[768,6144]{1,0:T(8,128)(2,1)} fusion(bf16[768,6144]{1,0:T(8,128)(2,1)} %collective-permute-done.24, bf16[768,6144]{1,0:T(8,128)(2,1)} %get-tuple-element.210, bf16[768,1536]{1,0:T(8,128)(2,1)S(1)} %copy-done.61, s32[]{:T(128)S(6)} %select_n.330), kind=kOutput, calls=%fused_computation.3 | convolution fusion | flops 7261913088 | bytes 29491204 | tf_op jit(solution)/shard_map/rd,re->de/dot_general | solution.py:32
  565.8 13.7 %convolution_convert_fusion.1 = bf16[3072,1536]{1,0:T(8,128)(2,1)} fusion(bf16[768,6144]{1,0:T(8,128)(2,1)} %add_convert_fusion.2, s32[]{:T(128)S(6)} %select_n.331, f32[768,1536]{1,0:T(8,128)} %copy-done.25, f32[1536]{0:T(1024)S(1)} %add.428, f32[1536]{0:T(1024)S(1)} %mul.314, f32[768]{0:T(1024)S(1)} %add_rsqrt_fusion, f32[768]{0:T(1024)S(1)} %broadcast_multiply_fusion.6), kind=kOutput, calls=%fused_computation.21 | convolution fusion | flops 7258374144 | bytes 18892804 | tf_op jit(solution)/shard_map/rd,re->de/dot_general | solution.py:32
  579.6 21.7 %fusion.129 = f32[768,1536]{1,0:T(8,128)} fusion(bf16[768,6144]{1,0:T(8,128)(2,1)} %add_convert_fusion.2, bf16[1536,6144]{1,0:T(8,128)(2,1)} %bitcast.202), kind=kOutput, calls=%fused_computation.298 | convolution fusion | flops 14495514624 | bytes 33030144 | tf_op jit(solution)/shard_map/re,de->rd/dot_general | solution.py:36
  601.2 14.2 %add_convert_fusion = bf16[3072,1536]{1,0:T(8,128)(2,1)} fusion(bf16[3072,1536]{1,0:T(8,128)(2,1)} %collective-permute-done.25, bf16[768,6144]{1,0:T(8,128)(2,1)} %add_convert_fusion.2, s32[]{:T(128)S(6)} %select_n.332, f32[768,1536]{1,0:T(8,128)S(1)} %bitcast.176, f32[1536]{0:T(1024)S(1)} %add.428, f32[1536]{0:T(1024)S(1)} %mul.314, ...), kind=kOutput, calls=%fused_computation.2 | convolution fusion | flops 7267811328 | bytes 28329988 | tf_op jit(solution)/shard_map/rd,re->de/dot_general | solution.py:32
  622.0 13.1 %fusion.124 = (bf16[768,1536]{1,0:T(8,128)(2,1)S(1)}, f32[768,1536]{1,0:T(8,128)}, f32[]{:T(128)}, bf16[768,1536]{1,0:T(8,128)(2,1)}) fusion(f32[768]{0:T(1024)S(1)} %broadcast_multiply_fusion.4, f32[768,1536]{1,0:T(8,128)} %copy-done.25, f32[768]{0:T(1024)S(1)} %broadcast_multiply_fusion.6, f32[768]{0:T(1024)S(1)} %broadcast_multiply_fusion.5, ...), kind=kLoop, calls=%fused_computation.294 | loop fusion | flops 22413312 | bytes 25973768 | tf_op jit(solution)/shard_map/convert_element_type | solution.py:1041
  645.5 9.5 cross_attend_back.1
  684.9 9.4 multiply_reduce_fusion.2
  705.5 7.5 fusion.52.grad_ref
  724.1 10.4 collective-permute-start.33
  747.7 69.8 %self_attend_back.1 = (bf16[768,1536]{1,0:T(8,128)(2,1)S(1)}, bf16[768,1536]{1,0:T(8,128)(2,1)S(1)}, bf16[768,1536]{1,0:T(8,128)(2,1)S(1)}, bf16[768,1536]{1,0:T(8,128)(2,1)}, bf16[768,1536]{1,0:T(8,128)(2,1)}) custom-call(s32[5]{0:T(128)S(1)} %copy-done.11, bf16[768,1536]{1,0:T(8,128)(2,1)S(1)} %copy-done.22, bf16[768,3072]{1,0:T(8,128)(2,1)} %copy-done.12, ...), custom_call_target="tpu_custom_call" | custom-call | flops 18119393280 | bytes 37748736 | tf_op jit(solution)/shard_map/self_attend_back/pallas_call | solution.py:598
  835.4 7.8 convolution_convert_fusion
  843.3 9.1 collective-permute-start.44
  866.6 17.5 %fusion.130 = f32[768,1536]{1,0:T(8,128)} fusion(bf16[768,4608]{1,0:T(8,128)(2,1)} %copy-done.34, bf16[1536,4608]{1,0:T(8,128)(2,1)} %bitcast.207), kind=kOutput, calls=%fused_computation.299 | convolution fusion | flops 10871635968 | bytes 25952256 | tf_op jit(solution)/shard_map/re,de->rd/dot_general | solution.py:36
  884.1 18.7 %collective-permute-done.42 = bf16[768,384]{1,0:T(8,128)(2,1)S(1)} collective-permute-done((bf16[768,384]{1,0:T(8,128)(2,1)S(1)}, bf16[768,384]{1,0:T(8,128)(2,1)S(1)}, u32[]{:S(2)}, u32[]{:S(2)}) %collective-permute-start.42) | collective-permute-done | bytes 589856 | tf_op jit(solution)/shard_map/ppermute | solution.py:830
  903.9 9.8 add_convert_fusion.3
  926.3 16.5 %collective-permute-start.54 = (bf16[384,1536]{1,0:T(8,128)(2,1)S(1)}, bf16[384,1536]{1,0:T(8,128)(2,1)}, u32[]{:S(2)}, u32[]{:S(2)}) collective-permute-start(bf16[384,1536]{1,0:T(8,128)(2,1)S(1)} %get-tuple-element.222), channel_id=1, source_target_pairs={{1,0},{5,1},{4,2},{0,3},{3,4},{7,5},{6,6},{2,7},{9,8},{13,9},{12,1... | collective-permute-start | bytes 3538952 | tf_op jit(solution)/shard_map/ppermute | solution.py:854
  946.4 28.7 %collective-permute-done.54 = bf16[384,1536]{1,0:T(8,128)(2,1)} collective-permute-done((bf16[384,1536]{1,0:T(8,128)(2,1)S(1)}, bf16[384,1536]{1,0:T(8,128)(2,1)}, u32[]{:S(2)}, u32[]{:S(2)}) %collective-permute-start.54) | collective-permute-done | bytes 1179680 | tf_op jit(solution)/shard_map/ppermute | solution.py:854
  978.0 17.3 %collective-permute-start.55 = (bf16[576,384]{1,0:T(8,128)(2,1)}, bf16[576,384]{1,0:T(8,128)(2,1)S(1)}, u32[]{:S(2)}, u32[]{:S(2)}) collective-permute-start(bf16[576,384]{1,0:T(8,128)(2,1)} %get-tuple-element.244), channel_id=1, source_target_pairs={{0,1},{1,2},{2,3},{3,0},{4,5},{5,6},{6,7},{7,4},{8,9},{9,10},{10,1... | collective-permute-start | bytes 1327112 | tf_op jit(solution)/shard_map/ppermute | solution.py:830
  1000.9 8.6 collective-permute-done.55
  1009.5 18.1 %collective-permute-done.56 = bf16[576,384]{1,0:T(8,128)(2,1)} collective-permute-done((bf16[576,384]{1,0:T(8,128)(2,1)}, bf16[576,384]{1,0:T(8,128)(2,1)}, u32[]{:S(2)}, u32[]{:S(2)}) %collective-permute-start.56) | collective-permute-done | bytes 442400 | tf_op jit(solution)/shard_map/ppermute | solution.py:830
  1040.3 10.1 collective-permute-start.51
  1063.4 10.5 collective-permute-done.58
  1073.9 14.2 %collective-permute-done.59 = bf16[576,384]{1,0:T(8,128)(2,1)S(1)} collective-permute-done((bf16[576,384]{1,0:T(8,128)(2,1)S(1)}, bf16[576,384]{1,0:T(8,128)(2,1)S(1)}, u32[]{:S(2)}, u32[]{:S(2)}) %collective-permute-start.59) | collective-permute-done | bytes 442400 | tf_op jit(solution)/shard_map/ppermute | solution.py:830
  1090.2 30.9 %all-gather.18.cloned.1.call-done = bf16[19968,384]{1,0:T(8,128)(2,1)} async-done(((bf16[2496,384]{1,0:T(8,128)(2,1)}), bf16[19968,384]{1,0:T(8,128)(2,1)}) %all-gather.18.cloned.1.call-update) | async-done | bytes 15335440 | tf_op jit(solution)/shard_map/all_gather | solution.py:1169
  1157.5 8.1 unpack.13
  (543 shorter events, 329.1 us)
Async XLA Ops:
  7.2 162.1 %all-gather.8.cloned.1.call-start = ((), (), s32[]{:S(2)}) async-start(), calls=%async_computation.4 | async-start | bytes 15925248 | tf_op jit(solution)/shard_map/all_gather | solution.py:865
  16.7 40.9 %collective-permute-start.1 = (bf16[64,4608]{1,0:T(8,128)(2,1)S(1)}, bf16[64,4608]{1,0:T(8,128)(2,1)}, u32[]{:S(2)}, u32[]{:S(2)}) collective-permute-start(bf16[64,4608]{1,0:T(8,128)(2,1)S(1)} %pad_maximum_fusion.5), channel_id=1, source_target_pairs={{0,2},{1,3},{2,0},{3,1},{4,6},{5,7},{6,4},{7,5},{8,10},{9,11},{10,... | collective-permute-start | bytes 1769480 | tf_op jit(solution)/shard_map/ppermute | solution.py:830
  19.3 39.3 %collective-permute-start.2 = (bf16[64,4608]{1,0:T(8,128)(2,1)S(1)}, bf16[64,4608]{1,0:T(8,128)(2,1)}, u32[]{:S(2)}, u32[]{:S(2)}) collective-permute-start(bf16[64,4608]{1,0:T(8,128)(2,1)S(1)} %pad_maximum_fusion.5), channel_id=1, source_target_pairs={{0,3},{1,0},{2,1},{3,2},{4,7},{5,4},{6,5},{7,6},{8,11},{9,8},{10,9... | collective-permute-start | bytes 1769480 | tf_op jit(solution)/shard_map/ppermute | solution.py:830
  61.0 288.6 %all-gather.10.cloned.1.call-start = ((), (), s32[]{:S(2)}) async-start(), calls=%async_computation.5 | async-start | bytes 15925248 | tf_op jit(solution)/shard_map/all_gather | solution.py:865
  63.5 55.1 %collective-permute-start.4 = (bf16[384,1536]{1,0:T(8,128)(2,1)S(1)}, bf16[384,1536]{1,0:T(8,128)(2,1)S(1)}, u32[]{:S(2)}, u32[]{:S(2)}) collective-permute-start(bf16[384,1536]{1,0:T(8,128)(2,1)S(1)} %get-tuple-element.239), channel_id=1, source_target_pairs={{0,1},{1,5},{2,4},{3,0},{4,3},{5,7},{6,6},{7,2},{8,9},{9,13},{10,1... | collective-permute-start | bytes 3538952 | tf_op jit(solution)/shard_map/ppermute | solution.py:845
  119.8 38.0 %collective-permute-start.7 = (bf16[48,4608]{1,0:T(8,128)(2,1)S(1)}, bf16[48,4608]{1,0:T(8,128)(2,1)S(1)}, u32[]{:S(2)}, u32[]{:S(2)}) collective-permute-start(bf16[48,4608]{1,0:T(8,128)(2,1)S(1)} %pad_maximum_fusion.7), channel_id=1, source_target_pairs={{0,2},{1,3},{2,0},{3,1},{4,6},{5,7},{6,4},{7,5},{8,10},{9,11},{10,... | collective-permute-start | bytes 1327112 | tf_op jit(solution)/shard_map/ppermute | solution.py:830
  135.5 22.8 %collective-permute-start.8 = (bf16[48,4608]{1,0:T(8,128)(2,1)S(1)}, bf16[48,4608]{1,0:T(8,128)(2,1)S(1)}, u32[]{:S(2)}, u32[]{:S(2)}) collective-permute-start(bf16[48,4608]{1,0:T(8,128)(2,1)S(1)} %pad_maximum_fusion.7), channel_id=1, source_target_pairs={{0,3},{1,0},{2,1},{3,2},{4,7},{5,4},{6,5},{7,6},{8,11},{9,8},{10,9... | collective-permute-start | bytes 1327112 | tf_op jit(solution)/shard_map/ppermute | solution.py:830
  159.5 253.6 %all-gather.12.cloned.1.call-start = ((), (), s32[]{:S(2)}) async-start(), calls=%async_computation.6 | async-start | bytes 21233664 | tf_op jit(solution)/shard_map/all_gather | solution.py:865
  180.2 56.2 %collective-permute-start.12 = (bf16[768,3072]{1,0:T(8,128)(2,1)S(1)}, bf16[768,3072]{1,0:T(8,128)(2,1)S(1)}, u32[]{:S(2)}, u32[]{:S(2)}) collective-permute-start(bf16[768,3072]{1,0:T(8,128)(2,1)S(1)} %fusion.14.own_k.own_v), channel_id=1, source_target_pairs={{0,4},{4,0},{1,5},{5,1},{2,6},{6,2},{3,7},{7,3},{8,12},{12,8},{9,1... | collective-permute-start | bytes 14155784 | tf_op jit(solution)/shard_map/ppermute | solution.py:958
  186.3 34.5 %collective-permute-start.10 = (bf16[48,6144]{1,0:T(8,128)(2,1)S(1)}, bf16[48,6144]{1,0:T(8,128)(2,1)S(1)}, u32[]{:S(2)}, u32[]{:S(2)}) collective-permute-start(bf16[48,6144]{1,0:T(8,128)(2,1)S(1)} %get-tuple-element.79), channel_id=1, source_target_pairs={{0,2},{1,3},{2,0},{3,1},{4,6},{5,7},{6,4},{7,5},{8,10},{9,11},{10,... | collective-permute-start | bytes 1769480 | tf_op jit(solution)/shard_map/ppermute | solution.py:830
  194.0 26.9 %collective-permute-start.11 = (bf16[48,6144]{1,0:T(8,128)(2,1)S(1)}, bf16[48,6144]{1,0:T(8,128)(2,1)S(1)}, u32[]{:S(2)}, u32[]{:S(2)}) collective-permute-start(bf16[48,6144]{1,0:T(8,128)(2,1)S(1)} %get-tuple-element.79), channel_id=1, source_target_pairs={{0,3},{1,0},{2,1},{3,2},{4,7},{5,4},{6,5},{7,6},{8,11},{9,8},{10,9... | collective-permute-start | bytes 1769480 | tf_op jit(solution)/shard_map/ppermute | solution.py:830
  197.5 38.9 %collective-permute-start.9 = (bf16[48,6144]{1,0:T(8,128)(2,1)S(1)}, bf16[48,6144]{1,0:T(8,128)(2,1)S(1)}, u32[]{:S(2)}, u32[]{:S(2)}) collective-permute-start(bf16[48,6144]{1,0:T(8,128)(2,1)S(1)} %get-tuple-element.79), channel_id=1, source_target_pairs={{0,1},{1,2},{2,3},{3,0},{4,5},{5,6},{6,7},{7,4},{8,9},{9,10},{10,1... | collective-permute-start | bytes 1769480 | tf_op jit(solution)/shard_map/ppermute | solution.py:830
  240.1 234.5 %all-gather.14.cloned.1.call-start = ((), (), s32[]{:S(2)}) async-start(), calls=%async_computation.7 | async-start | bytes 21233664 | tf_op jit(solution)/shard_map/all_gather | solution.py:865
  251.8 80.2 %collective-permute-start.19 = (bf16[192,1536]{1,0:T(8,128)(2,1)}, bf16[192,1536]{1,0:T(8,128)(2,1)S(1)}, u32[]{:S(2)}, u32[]{:S(2)}) collective-permute-start(bf16[192,1536]{1,0:T(8,128)(2,1)} %get-tuple-element.90), channel_id=1, source_target_pairs={{0,1},{1,2},{2,3},{3,0},{4,5},{5,6},{6,7},{7,4},{8,9},{9,10},{10,1... | collective-permute-start | bytes 1769480 | tf_op jit(solution)/shard_map/ppermute | solution.py:830
  262.1 69.9 %collective-permute-start.20 = (bf16[192,1536]{1,0:T(8,128)(2,1)}, bf16[192,1536]{1,0:T(8,128)(2,1)S(1)}, u32[]{:S(2)}, u32[]{:S(2)}) collective-permute-start(bf16[192,1536]{1,0:T(8,128)(2,1)} %get-tuple-element.90), channel_id=1, source_target_pairs={{0,2},{1,3},{2,0},{3,1},{4,6},{5,7},{6,4},{7,5},{8,10},{9,11},{10,... | collective-permute-start | bytes 1769480 | tf_op jit(solution)/shard_map/ppermute | solution.py:830
  264.2 67.8 %collective-permute-start.21 = (bf16[192,1536]{1,0:T(8,128)(2,1)}, bf16[192,1536]{1,0:T(8,128)(2,1)S(1)}, u32[]{:S(2)}, u32[]{:S(2)}) collective-permute-start(bf16[192,1536]{1,0:T(8,128)(2,1)} %get-tuple-element.90), channel_id=1, source_target_pairs={{0,3},{1,0},{2,1},{3,2},{4,7},{5,4},{6,5},{7,6},{8,11},{9,8},{10,9... | collective-permute-start | bytes 1769480 | tf_op jit(solution)/shard_map/ppermute | solution.py:830
  334.7 401.8 %reduce-scatter.5.cloned.1.call-start = ((), (), s32[]{:S(2)}) async-start(), calls=%async_computation.8 | async-start | bytes 11796480 | tf_op jit(solution)/shard_map/reduce_scatter | solution.py:1008
  338.6 27.5 %collective-permute-start.13 = (bf16[64,1536]{1,0:T(8,128)(2,1)}, bf16[64,1536]{1,0:T(8,128)(2,1)S(1)}, u32[]{:S(2)}, u32[]{:S(2)}) collective-permute-start(bf16[64,1536]{1,0:T(8,128)(2,1)} %get-tuple-element.251), channel_id=1, source_target_pairs={{0,1},{1,2},{2,3},{3,0},{4,5},{5,6},{6,7},{7,4},{8,9},{9,10},{10,1... | collective-permute-start | bytes 589832 | tf_op jit(solution)/shard_map/ppermute | solution.py:830
  338.6 27.5 %collective-permute-start.14 = (bf16[64,1536]{1,0:T(8,128)(2,1)}, bf16[64,1536]{1,0:T(8,128)(2,1)S(1)}, u32[]{:S(2)}, u32[]{:S(2)}) collective-permute-start(bf16[64,1536]{1,0:T(8,128)(2,1)} %get-tuple-element.250), channel_id=1, source_target_pairs={{0,2},{1,3},{2,0},{3,1},{4,6},{5,7},{6,4},{7,5},{8,10},{9,11},{10,... | collective-permute-start | bytes 589832 | tf_op jit(solution)/shard_map/ppermute | solution.py:830
  339.8 26.2 %collective-permute-start.15 = (bf16[64,1536]{1,0:T(8,128)(2,1)}, bf16[64,1536]{1,0:T(8,128)(2,1)S(1)}, u32[]{:S(2)}, u32[]{:S(2)}) collective-permute-start(bf16[64,1536]{1,0:T(8,128)(2,1)} %get-tuple-element.249), channel_id=1, source_target_pairs={{0,3},{1,0},{2,1},{3,2},{4,7},{5,4},{6,5},{7,6},{8,11},{9,8},{10,9... | collective-permute-start | bytes 589832 | tf_op jit(solution)/shard_map/ppermute | solution.py:830
  367.6 22.6 %collective-permute-start.22 = (bf16[384,1536]{1,0:T(8,128)(2,1)S(1)}, bf16[384,1536]{1,0:T(8,128)(2,1)S(1)}, u32[]{:S(2)}, u32[]{:S(2)}) collective-permute-start(bf16[384,1536]{1,0:T(8,128)(2,1)S(1)} %get-tuple-element.235), channel_id=1, source_target_pairs={{0,0},{1,4},{2,5},{3,1},{4,2},{5,6},{6,7},{7,3},{8,8},{9,12},{10,1... | collective-permute-start | bytes 3538952 | tf_op jit(solution)/shard_map/ppermute | solution.py:844
  368.4 43.1 %collective-permute-start.23 = (bf16[384,1536]{1,0:T(8,128)(2,1)S(1)}, bf16[384,1536]{1,0:T(8,128)(2,1)S(1)}, u32[]{:S(2)}, u32[]{:S(2)}) collective-permute-start(bf16[384,1536]{1,0:T(8,128)(2,1)S(1)} %get-tuple-element.236), channel_id=1, source_target_pairs={{0,1},{1,5},{2,4},{3,0},{4,3},{5,7},{6,6},{7,2},{8,9},{9,13},{10,1... | collective-permute-start | bytes 3538952 | tf_op jit(solution)/shard_map/ppermute | solution.py:845
  509.7 41.2 %collective-permute-start.24 = (bf16[768,6144]{1,0:T(8,128)(2,1)}, bf16[768,6144]{1,0:T(8,128)(2,1)}, u32[]{:S(2)}, u32[]{:S(2)}) collective-permute-start(bf16[768,6144]{1,0:T(8,128)(2,1)} %convolution_convert_fusion.2), channel_id=1, source_target_pairs={{0,4},{4,0},{1,5},{5,1},{2,6},{6,2},{3,7},{7,3},{8,12},{12,8},{9,1... | collective-permute-start | bytes 28311560 | tf_op jit(solution)/shard_map/ppermute | solution.py:1003
  565.8 291.5 %reduce-scatter.7.cloned.1.call-start = ((), (), s32[]{:S(2)}) async-start(), calls=%async_computation.9 | async-start | bytes 11796480 | tf_op jit(solution)/shard_map/reduce_scatter | solution.py:1008
  579.5 21.7 %collective-permute-start.25 = (bf16[3072,1536]{1,0:T(8,128)(2,1)}, bf16[3072,1536]{1,0:T(8,128)(2,1)}, u32[]{:S(2)}, u32[]{:S(2)}) collective-permute-start(bf16[3072,1536]{1,0:T(8,128)(2,1)} %convolution_convert_fusion.1), channel_id=1, source_target_pairs={{0,4},{4,0},{1,5},{5,1},{2,6},{6,2},{3,7},{7,3},{8,12},{12,8},{9,1... | collective-permute-start | bytes 28311560 | tf_op jit(solution)/shard_map/ppermute | solution.py:1003
  615.4 359.7 %reduce-scatter.11.cloned.1.call-start = ((), (), s32[]{:S(2)}) async-start(), calls=%async_computation.11 | async-start | bytes 10321920 | tf_op jit(solution)/shard_map/reduce_scatter | solution.py:1008
  638.6 38.5 %collective-permute-start.26 = (bf16[768,1536]{1,0:T(8,128)(2,1)}, bf16[768,1536]{1,0:T(8,128)(2,1)}, u32[]{:S(2)}, u32[]{:S(2)}) collective-permute-start(bf16[768,1536]{1,0:T(8,128)(2,1)} %convolution_convert_fusion.5), channel_id=1, source_target_pairs={{0,4},{4,0},{1,5},{5,1},{2,6},{6,2},{3,7},{7,3},{8,12},{12,8},{9,1... | collective-permute-start | bytes 7077896 | tf_op jit(solution)/shard_map/ppermute | solution.py:1003
  684.9 28.2 %collective-permute-start.27 = (bf16[768,1536]{1,0:T(8,128)(2,1)}, bf16[768,1536]{1,0:T(8,128)(2,1)S(1)}, u32[]{:S(2)}, u32[]{:S(2)}) collective-permute-start(bf16[768,1536]{1,0:T(8,128)(2,1)} %convolution_convert_fusion.4), channel_id=1, source_target_pairs={{0,4},{4,0},{1,5},{5,1},{2,6},{6,2},{3,7},{7,3},{8,12},{12,8},{9,1... | collective-permute-start | bytes 7077896 | tf_op jit(solution)/shard_map/ppermute | solution.py:1003
  720.9 336.6 %reduce-scatter.9.cloned.1.call-start = ((), (), s32[]{:S(2)}) async-start(), calls=%async_computation.10 | async-start | bytes 8847360 | tf_op jit(solution)/shard_map/reduce_scatter | solution.py:1008
  724.1 96.2 %collective-permute-start.33 = (bf16[384,1536]{1,0:T(8,128)(2,1)}, bf16[384,1536]{1,0:T(8,128)(2,1)}, u32[]{:S(2)}, u32[]{:S(2)}) collective-permute-start(bf16[384,1536]{1,0:T(8,128)(2,1)} %get-tuple-element.232), channel_id=1, source_target_pairs={{0,0},{4,1},{5,2},{1,3},{2,4},{6,5},{7,6},{3,7},{8,8},{12,9},{13,1... | collective-permute-start | bytes 3538952 | tf_op jit(solution)/shard_map/ppermute | solution.py:853
  734.5 85.9 %collective-permute-start.34 = (bf16[384,1536]{1,0:T(8,128)(2,1)}, bf16[384,1536]{1,0:T(8,128)(2,1)}, u32[]{:S(2)}, u32[]{:S(2)}) collective-permute-start(bf16[384,1536]{1,0:T(8,128)(2,1)} %get-tuple-element.231), channel_id=1, source_target_pairs={{1,0},{5,1},{4,2},{0,3},{3,4},{7,5},{6,6},{2,7},{9,8},{13,9},{12,1... | collective-permute-start | bytes 3538952 | tf_op jit(solution)/shard_map/ppermute | solution.py:854
  738.1 82.3 %collective-permute-start.36 = (bf16[192,1536]{1,0:T(8,128)(2,1)S(1)}, bf16[192,1536]{1,0:T(8,128)(2,1)S(1)}, u32[]{:S(2)}, u32[]{:S(2)}) collective-permute-start(bf16[192,1536]{1,0:T(8,128)(2,1)S(1)} %get-tuple-element.228), channel_id=1, source_target_pairs={{0,1},{1,2},{2,3},{3,0},{4,5},{5,6},{6,7},{7,4},{8,9},{9,10},{10,1... | collective-permute-start | bytes 1769480 | tf_op jit(solution)/shard_map/ppermute | solution.py:830
  740.1 80.3 %collective-permute-start.37 = (bf16[192,1536]{1,0:T(8,128)(2,1)S(1)}, bf16[192,1536]{1,0:T(8,128)(2,1)}, u32[]{:S(2)}, u32[]{:S(2)}) collective-permute-start(bf16[192,1536]{1,0:T(8,128)(2,1)S(1)} %get-tuple-element.227), channel_id=1, source_target_pairs={{0,2},{1,3},{2,0},{3,1},{4,6},{5,7},{6,4},{7,5},{8,10},{9,11},{10,... | collective-permute-start | bytes 1769480 | tf_op jit(solution)/shard_map/ppermute | solution.py:830
  740.1 80.3 %collective-permute-start.38 = (bf16[192,1536]{1,0:T(8,128)(2,1)S(1)}, bf16[192,1536]{1,0:T(8,128)(2,1)}, u32[]{:S(2)}, u32[]{:S(2)}) collective-permute-start(bf16[192,1536]{1,0:T(8,128)(2,1)S(1)} %get-tuple-element.226), channel_id=1, source_target_pairs={{0,3},{1,0},{2,1},{3,2},{4,7},{5,4},{6,5},{7,6},{8,11},{9,8},{10,9... | collective-permute-start | bytes 1769480 | tf_op jit(solution)/shard_map/ppermute | solution.py:830
  843.2 59.7 %collective-permute-start.47 = (bf16[2304,1536]{1,0:T(8,128)(2,1)}, bf16[2304,1536]{1,0:T(8,128)(2,1)}, u32[]{:S(2)}, u32[]{:S(2)}) collective-permute-start(bf16[2304,1536]{1,0:T(8,128)(2,1)} %convolution_convert_fusion), channel_id=1, source_target_pairs={{0,4},{4,0},{1,5},{5,1},{2,6},{6,2},{3,7},{7,3},{8,12},{12,8},{9,1... | collective-permute-start | bytes 21233672 | tf_op jit(solution)/shard_map/ppermute | solution.py:1003
  855.5 28.6 %collective-permute-start.46 = (bf16[2,64,384]{2,1,0:T(8,128)(2,1)}, bf16[2,64,384]{2,1,0:T(8,128)(2,1)S(1)}, u32[]{:S(2)}, u32[]{:S(2)}) collective-permute-start(bf16[2,64,384]{2,1,0:T(8,128)(2,1)} %fusion.89), channel_id=1, source_target_pairs={{0,3},{1,0},{2,1},{3,2},{4,7},{5,4},{6,5},{7,6},{8,11},{9,8},{10,9... | collective-permute-start | bytes 294920 | tf_op jit(solution)/shard_map/ppermute | solution.py:830
  858.9 25.2 %collective-permute-start.41 = (bf16[768,384]{1,0:T(8,128)(2,1)S(1)}, bf16[768,384]{1,0:T(8,128)(2,1)S(1)}, u32[]{:S(2)}, u32[]{:S(2)}) collective-permute-start(bf16[768,384]{1,0:T(8,128)(2,1)S(1)} %get-tuple-element.225), channel_id=1, source_target_pairs={{0,1},{1,2},{2,3},{3,0},{4,5},{5,6},{6,7},{7,4},{8,9},{9,10},{10,1... | collective-permute-start | bytes 1769480 | tf_op jit(solution)/shard_map/ppermute | solution.py:830
  861.0 41.9 %collective-permute-start.42 = (bf16[768,384]{1,0:T(8,128)(2,1)S(1)}, bf16[768,384]{1,0:T(8,128)(2,1)S(1)}, u32[]{:S(2)}, u32[]{:S(2)}) collective-permute-start(bf16[768,384]{1,0:T(8,128)(2,1)S(1)} %get-tuple-element.224), channel_id=1, source_target_pairs={{0,2},{1,3},{2,0},{3,1},{4,6},{5,7},{6,4},{7,5},{8,10},{9,11},{10,... | collective-permute-start | bytes 1769480 | tf_op jit(solution)/shard_map/ppermute | solution.py:830
  863.5 39.4 %collective-permute-start.43 = (bf16[768,384]{1,0:T(8,128)(2,1)S(1)}, bf16[768,384]{1,0:T(8,128)(2,1)S(1)}, u32[]{:S(2)}, u32[]{:S(2)}) collective-permute-start(bf16[768,384]{1,0:T(8,128)(2,1)S(1)} %get-tuple-element.223), channel_id=1, source_target_pairs={{0,3},{1,0},{2,1},{3,2},{4,7},{5,4},{6,5},{7,6},{8,11},{9,8},{10,9... | collective-permute-start | bytes 1769480 | tf_op jit(solution)/shard_map/ppermute | solution.py:830
  913.7 207.4 %all-gather.18.cloned.1.call-start = ((), (), s32[]{:S(2)}) async-start(), calls=%async_computation.13 | async-start | bytes 17252352 | tf_op jit(solution)/shard_map/all_gather | solution.py:1169
  925.4 21.0 %collective-permute-start.53 = (bf16[384,1536]{1,0:T(8,128)(2,1)S(1)}, bf16[384,1536]{1,0:T(8,128)(2,1)S(1)}, u32[]{:S(2)}, u32[]{:S(2)}) collective-permute-start(bf16[384,1536]{1,0:T(8,128)(2,1)S(1)} %get-tuple-element.221), channel_id=1, source_target_pairs={{0,0},{4,1},{5,2},{1,3},{2,4},{6,5},{7,6},{3,7},{8,8},{12,9},{13,1... | collective-permute-start | bytes 3538952 | tf_op jit(solution)/shard_map/ppermute | solution.py:853
  926.3 48.9 %collective-permute-start.54 = (bf16[384,1536]{1,0:T(8,128)(2,1)S(1)}, bf16[384,1536]{1,0:T(8,128)(2,1)}, u32[]{:S(2)}, u32[]{:S(2)}) collective-permute-start(bf16[384,1536]{1,0:T(8,128)(2,1)S(1)} %get-tuple-element.222), channel_id=1, source_target_pairs={{1,0},{5,1},{4,2},{0,3},{3,4},{7,5},{6,6},{2,7},{9,8},{13,9},{12,1... | collective-permute-start | bytes 3538952 | tf_op jit(solution)/shard_map/ppermute | solution.py:854
  978.0 31.5 %collective-permute-start.55 = (bf16[576,384]{1,0:T(8,128)(2,1)}, bf16[576,384]{1,0:T(8,128)(2,1)S(1)}, u32[]{:S(2)}, u32[]{:S(2)}) collective-permute-start(bf16[576,384]{1,0:T(8,128)(2,1)} %get-tuple-element.244), channel_id=1, source_target_pairs={{0,1},{1,2},{2,3},{3,0},{4,5},{5,6},{6,7},{7,4},{8,9},{9,10},{10,1... | collective-permute-start | bytes 1327112 | tf_op jit(solution)/shard_map/ppermute | solution.py:830
  995.3 32.3 %collective-permute-start.56 = (bf16[576,384]{1,0:T(8,128)(2,1)}, bf16[576,384]{1,0:T(8,128)(2,1)}, u32[]{:S(2)}, u32[]{:S(2)}) collective-permute-start(bf16[576,384]{1,0:T(8,128)(2,1)} %get-tuple-element.246), channel_id=1, source_target_pairs={{0,2},{1,3},{2,0},{3,1},{4,6},{5,7},{6,4},{7,5},{8,10},{9,11},{10,... | collective-permute-start | bytes 1327112 | tf_op jit(solution)/shard_map/ppermute | solution.py:830
  998.7 28.9 %collective-permute-start.57 = (bf16[576,384]{1,0:T(8,128)(2,1)}, bf16[576,384]{1,0:T(8,128)(2,1)}, u32[]{:S(2)}, u32[]{:S(2)}) collective-permute-start(bf16[576,384]{1,0:T(8,128)(2,1)} %get-tuple-element.245), channel_id=1, source_target_pairs={{0,3},{1,0},{2,1},{3,2},{4,7},{5,4},{6,5},{7,6},{8,11},{9,8},{10,9... | collective-permute-start | bytes 1327112 | tf_op jit(solution)/shard_map/ppermute | solution.py:830
  1029.7 146.7 %all-gather.16.cloned.1.call-start = ((), (), s32[]{:S(2)}) async-start(), calls=%async_computation.12 | async-start | bytes 3981312 | tf_op jit(solution)/shard_map/all_gather | solution.py:1184
  1061.0 27.2 %collective-permute-start.59 = (bf16[576,384]{1,0:T(8,128)(2,1)S(1)}, bf16[576,384]{1,0:T(8,128)(2,1)S(1)}, u32[]{:S(2)}, u32[]{:S(2)}) collective-permute-start(bf16[576,384]{1,0:T(8,128)(2,1)S(1)} %get-tuple-element.243), channel_id=1, source_target_pairs={{0,2},{1,3},{2,0},{3,1},{4,6},{5,7},{6,4},{7,5},{8,10},{9,11},{10,... | collective-permute-start | bytes 1327112 | tf_op jit(solution)/shard_map/ppermute | solution.py:830
  1062.0 26.2 %collective-permute-start.60 = (bf16[576,384]{1,0:T(8,128)(2,1)S(1)}, bf16[576,384]{1,0:T(8,128)(2,1)S(1)}, u32[]{:S(2)}, u32[]{:S(2)}) collective-permute-start(bf16[576,384]{1,0:T(8,128)(2,1)S(1)} %get-tuple-element.242), channel_id=1, source_target_pairs={{0,3},{1,0},{2,1},{3,2},{4,7},{5,4},{6,5},{7,6},{8,11},{9,8},{10,9... | collective-permute-start | bytes 1327112 | tf_op jit(solution)/shard_map/ppermute | solution.py:830
  (132 other events, 2195.1 us)
Sparse Core Ops, SparseCore 0:
  61.1 90.5 all-gather.7
  159.7 91.0 all-gather.9
  253.3 98.8 all-gather.11
  354.4 98.7 all-gather.13
  565.9 94.0 reduce-scatter.4
  663.5 95.0 reduce-scatter.6
  762.4 85.3 reduce-scatter.10
  913.8 86.6 reduce-scatter.8
  1029.8 91.1 all-gather.17
  1123.4 33.9 all-gather.15

commit v5 on v4

--- a/solution.py
+++ b/solution.py
@@ -880,23 +880,20 @@
         ]
     )
     vectors = jnp.pad(vectors[None, :], ((0, 15), (0, 3 * width - 6 * block)))
-    qkv_mine = jnp.concatenate([qkv_share, vectors], axis=0)
-    qkv_came = hops(qkv_mine)
-    share = qkv_share.shape[0]
-    qkv_line = line_up(qkv_share, [values[:share] for values in qkv_came])
-    qkv_matrix = from_replicas(qkv_line)
-    norms = line_up(qkv_mine[share], [values[share] for values in qkv_came])
-    norms = norms[:, : 6 * block].reshape(shards, 6, block).transpose(1, 0, 2)
-    norms = norms.reshape(6, width).astype(jnp.float32)
-
-    came = to_chip(after(frames, *qkv_came))
+    qkv_matrix = lax.all_gather(qkv_share, EVERY, axis=0, tiled=True)
+    came = to_chip(frames)
     x_low = by_time(*came)
     rest_share = jnp.concatenate(
         [share_of(self_output_weight), share_of(cross_query_weight), share_of(cross_output_weight)],
         axis=1,
     )
-    rest_came = hops(after(rest_share, *came))
-    rest = from_replicas(line_up(rest_share, rest_came))
+    share = rest_share.shape[0]
+    rest_mine = jnp.concatenate([rest_share, vectors], axis=0)
+    rest_came = hops(after(rest_mine, *came))
+    rest = from_replicas(line_up(rest_share, [values[:share] for values in rest_came]))
+    norms = line_up(vectors[0], [values[share] for values in rest_came])
+    norms = norms[:, : 6 * block].reshape(shards, 6, block).transpose(1, 0, 2)
+    norms = norms.reshape(6, width).astype(jnp.float32)
     output_matrix = rest[:, :width]
     probe_matrix = rest[:, width : 2 * width]
     merge_matrix = rest[:, 2 * width :]
@@ -937,33 +934,13 @@
     text_came = [
         hop(
             lax.dynamic_index_in_dim(
-                text_part, lax.rem(shard + distance, shards), 0, keepdims=False
+                after(text_part, *rest_came), lax.rem(shard + distance, shards), 0, keepdims=False
             ),
             distance,
         )
         for distance in (1, 2, 3)
     ]
 
-    places = jnp.stack([core, 3 - core, length, 1 - core, 2 + core]).astype(jnp.int32)
-    positions = jnp.concatenate(
-        [core * block + jnp.arange(block), (3 - core) * block + jnp.arange(block)]
-    )
-    valid_rows = ((positions < length) & (used > 0)).astype(jnp.float32)[:, None]
-    inputs = x_low.astype(jnp.float32)
-    parts_one = norm_parts(inputs)
-    hidden_one = ((inputs - parts_one[0]) * parts_one[1] * norms[0] + norms[1]).astype(
-        jnp.bfloat16
-    )
-    kv = project(hidden_one, qkv_matrix[:, width:]).astype(jnp.bfloat16)
-    kv_other = lax.ppermute(kv, "core", swap)
-    queries = project(after(hidden_one, kv), qkv_matrix[:, :width]).astype(jnp.bfloat16)
-    expand_line = line_up(expand_share, held(expand_came, queries, kv_other))
-    expand_matrix = from_replicas(expand_line)
-    reduce_share = share_of(feed_down_weight)
-    reduce_came = hops(after(reduce_share, *expand_came))
-    mixed_self, lse = self_attend(after(places, expand_line, text_part), queries, kv, kv_other)
-    reduce_matrix = from_replicas(line_up(reduce_share, held(reduce_came, mixed_self)))
-    text_came = held(text_came, mixed_self)
     text_half = lax.dynamic_index_in_dim(text_part, shard, 0, keepdims=False).astype(jnp.float32)
     for values in text_came:
         text_half += values.astype(jnp.float32)
@@ -971,14 +948,33 @@
     text_swap = lax.ppermute(text_half, "core", swap)
     lookups = jnp.where(first_core, text_half, text_swap)
     contents = jnp.where(first_core, text_swap, text_half)
+    places = jnp.stack([core, 3 - core, length, 1 - core, 2 + core]).astype(jnp.int32)
+    positions = jnp.concatenate(
+        [core * block + jnp.arange(block), (3 - core) * block + jnp.arange(block)]
+    )
+    valid_rows = ((positions < length) & (used > 0)).astype(jnp.float32)[:, None]
+    inputs = x_low.astype(jnp.float32)
+    parts_one = norm_parts(inputs)
+    hidden_one = ((inputs - parts_one[0]) * parts_one[1] * norms[0] + norms[1]).astype(
+        jnp.bfloat16
+    )
+    kv = project(after(hidden_one, lookups, contents, count), qkv_matrix[:, width:]).astype(jnp.bfloat16)
+    kv_other = lax.ppermute(kv, "core", swap)
+    queries = project(after(hidden_one, kv), qkv_matrix[:, :width]).astype(jnp.bfloat16)
+    mixed_self, lse = self_attend(places, queries, kv, kv_other)
+    expand_came = held(expand_came, mixed_self)
+    expand_matrix = from_replicas(line_up(expand_share, expand_came))
+    reduce_share = share_of(feed_down_weight)
+    reduce_came = hops(after(reduce_share, *expand_came))
     after_self = inputs + project(mixed_self, output_matrix)
     parts_two = norm_parts(after_self)
     hidden_two = ((after_self - parts_two[0]) * parts_two[1] * norms[2] + norms[3]).astype(
         jnp.bfloat16
     )
     probes = project(hidden_two, probe_matrix).astype(jnp.bfloat16)
+    reduce_matrix = from_replicas(line_up(reduce_share, held(reduce_came, probes)))
     teacher_low = by_time(*to_chip(after(teacher, *reduce_came, probes)))
-    cross_mixed = cross_attend(probes, lookups, contents, after(present, count))
+    cross_mixed = cross_attend(probes, lookups, contents, present)
     after_cross = after_self + project(cross_mixed, merge_matrix)
     parts_three = norm_parts(after_cross)
     hidden_three = (
@@ -1121,15 +1117,13 @@
     qkv_grads = jnp.concatenate([grad_queries, own_keys, own_values], axis=1)
     qkv_theirs = theirs_of(qkv_grads, hidden_one)
     grad_hidden_one = back_project(after(qkv_grads, qkv_theirs), qkv_matrix)
-    qkv_ours = ours_of(
-        after(qkv_grads, grad_hidden_one, *up_came, *text_came), hidden_one, qkv_theirs
-    )
+    qkv_ours = ours_of(after(qkv_grads, grad_hidden_one), hidden_one, qkv_theirs)
     up_piece = over_shard(up_sum, up_came)
     text_grad = line_up(text_own, text_came).astype(jnp.float32)
     text_grad = text_grad.transpose(1, 2, 0, 3).reshape(text_states.shape)
     qkv_sum = over_outer(qkv_ours)
     grad_norm, gain_self, bias_self = norm_back(
-        after(grad_hidden_one, qkv_ours), inputs, parts_one, norms[0]
+        after(grad_hidden_one, qkv_ours, *up_came, *text_came), inputs, parts_one, norms[0]
     )
     frames_came = from_chip((grad_after_self + grad_norm).astype(jnp.bfloat16))
     frames_grad = by_slot(*frames_came).astype(jnp.float32)
@@ -1166,7 +1160,7 @@
         + [text_piece, middle_piece],
         axis=0,
     )
-    early = lax.all_gather(early, REPLICAS, axis=0)
+    early = lax.all_gather(after(early, text_grad), REPLICAS, axis=0)
     piece = width // replicas
     square = (block, width)
     up_grad = unpack(early, hidden_units // replicas, 0, (block, hidden_units), 0, 1)
@@ -1182,8 +1176,8 @@
     qkv_sum = after(qkv_sum, middle_piece, small)
     late = over_shard(qkv_sum, shard_hops(qkv_sum))
     late = lax.all_gather(after(late, early), REPLICAS, axis=0, tiled=True)
-    late = late.reshape(3, width, block)
-    qkv_grad = [late[i].T.astype(jnp.float32) for i in range(3)]
+    late = late.reshape(-1, block, block)
+    qkv_grad = [unpack(late, block, 0, square, 2 * i, 2) for i in range(3)]
     return (
         output,
         loss,

time: 1210 us -> 1250 us (1.033)
  waiting for transfers between devices: 311 us -> 357 us
    ppermute x2, waiting for transfers between devices: 59 us -> 93.7 us  [to_chip(): two = lax.ppermute(jnp.where(lower, pair[1], pair[0]), spot, there[1])]
    ppermute x33 -> x30, starting transfers between devices: 108 us -> 132 us  [hop(): return lax.ppermute(values, 'shard', pairs)]
    unnamed x230 -> x235, local copies, waits for them, and re-layouts: 53.8 us -> 32.7 us
    all_gather x4 -> x3, waiting for transfers between devices: 0.04 us -> 19.4 us  [from_replicas(): full = lax.all_gather(line, ('y', 'x', 'core'), axis=1, tiled=True)]
    ppermute x2, waiting for transfers between devices: 28.8 us -> 13.3 us  [from_chip(): two = lax.ppermute(jnp.where(even, late, early), spot, back[1])]
    dynamic_update_slice x21 -> x18, local copies, waits for them, and re-layouts: 18 us -> 25.4 us  [line_up(): out = lax.dynamic_update_index_in_dim(out, values, owner, 0)]
    ppermute x33 -> x30, waiting for transfers between devices: 170 us -> 177 us  [hop(): return lax.ppermute(values, 'shard', pairs)]
    pallas_call x7 -> x10, Pallas kernels: 24.2 us -> 29 us  [unpack(): pl.pallas_call(unpack_kernel, out_shape=jax.ShapeDtypeStruct(out_shape, j...]
  transfers between devices with their start and end apart: 71 -> 68, of which waited for: 28 -> 28; matrix products, arithmetic and copies ran while one was open for 33% -> 33% of each run, Pallas kernels for 14% -> 14%
where the time goes in v5:
time: 1250 us; the launch traced here: 1240 us
  waiting for transfers between devices  357 us (29%)
  matrix products  313 us (25%)
  starting transfers between devices  197 us (16%)
  Pallas kernels  173 us (14%)
  local copies, waits for them, and re-layouts  96.4 us (8%)
  other arithmetic  85.4 us (7%)
  between operations  21.5 us (2%)
    ppermute x30, waiting for transfers between devices, hop(): return lax.ppermute(values, 'shard', pairs)  177 us
    ppermute x30, starting transfers between devices, hop(): return lax.ppermute(values, 'shard', pairs)  132 us
    dot_general x8, matrix products, project(): return jnp.dot(left, right, preferred_element_type=jnp.float32)  130 us
    dot_general x7, matrix products, back_project(): jnp.einsum('re,de->rd', grads, matrix, preferred_element_type=jnp.float32)  94.5 us
    ppermute x2, waiting for transfers between devices, to_chip(): two = lax.ppermute(jnp.where(lower, pair[1], pair[0]), spot, there[1])  93.7 us
    dot_general x13, matrix products, outer_sum(): jnp.einsum('rd,re->de', left, right, preferred_element_type=jnp.float32)  88.7 us
    pallas_call x1, Pallas kernels, self_attend_back(): pl.pallas_call(self_backward_kernel, out_shape=(jax.ShapeDtypeStruct((row...  70 us
    pallas_call x1, Pallas kernels, self_attend(): pl.pallas_call(self_forward_kernel, out_shape=(jax.ShapeDtypeStruct((rows...  57.7 us
  transfers between devices with their start and end apart: 68, of which 28 were waited for; matrix products, arithmetic and copies ran while one was open for 33% of the time, Pallas kernels for 14%

profile of v5, /device:TPU:0, one launch (start us, length us, event | category | flops | bytes accessed | tf_op | source)
XLA Modules:
  0.0 1244.5 jit_solution(929228142900090495)
XLA Ops:
  24.9 64.3 %collective-permute-done.1 = bf16[384,1536]{1,0:T(8,128)(2,1)S(1)} collective-permute-done((bf16[384,1536]{1,0:T(8,128)(2,1)}, bf16[384,1536]{1,0:T(8,128)(2,1)S(1)}, u32[]{:S(2)}, u32[]{:S(2)}) %collective-permute-start.1) | collective-permute-done | bytes 1179680 | tf_op jit(solution)/shard_map/ppermute | solution.py:845
  90.3 43.5 %collective-permute-start.4 = (bf16[64,4608]{1,0:T(8,128)(2,1)}, bf16[64,4608]{1,0:T(8,128)(2,1)S(1)}, u32[]{:S(2)}, u32[]{:S(2)}) collective-permute-start(bf16[64,4608]{1,0:T(8,128)(2,1)} %pad_maximum_fusion.5), channel_id=1, source_target_pairs={{0,2},{1,3},{2,0},{3,1},{4,6},{5,7},{6,4},{7,5},{8,10},{9,11},{10,... | collective-permute-start | bytes 1769480 | tf_op jit(solution)/shard_map/ppermute | solution.py:830
  136.8 39.3 %collective-permute-done.4 = bf16[64,4608]{1,0:T(8,128)(2,1)S(1)} collective-permute-done((bf16[64,4608]{1,0:T(8,128)(2,1)}, bf16[64,4608]{1,0:T(8,128)(2,1)S(1)}, u32[]{:S(2)}, u32[]{:S(2)}) %collective-permute-start.4) | collective-permute-done | bytes 589856 | tf_op jit(solution)/shard_map/ppermute | solution.py:830
  196.6 12.0 collective-permute-start.6
  211.4 9.8 collective-permute-start.8
  240.9 13.3 %fusion.14.own_k.own_v = bf16[768,3072]{1,0:T(8,128)(2,1)} fusion(bf16[768,1536]{1,0:T(8,128)(2,1)} %fusion.18, bf16[1536,4608]{1,0:T(8,128)(2,1)} %all-gather.8.cloned.1.call-done), kind=kOutput, calls=%fused_computation.36 | convolution fusion | flops 7250116608 | bytes 16515072 | tf_op jit(solution)/shard_map/dot_general | solution.py:28
  264.9 6.3 fusion.64.q_ref
  271.3 57.7 %self_attend.1 = (bf16[768,1536]{1,0:T(8,128)(2,1)S(1)}, f32[96,768]{1,0:T(8,128)S(1)}) custom-call(s32[5]{0:T(128)S(1)} %stack.66.place, bf16[768,1536]{1,0:T(8,128)(2,1)S(1)} %fusion.64.q_ref, bf16[768,3072]{1,0:T(8,128)(2,1)} %fusion.14.own_k.own_v, bf16[768,3072]{1,0:T(8,128)(2,1)} %fusion.14.own_k.own_v, ...), custom_call_target="tpu_custom_call" | custom-call | flops 7247757312 | bytes 18874368 | tf_op jit(solution)/shard_map/self_attend/pallas_call | solution.py:569
  340.0 8.0 fusion.130
  350.0 7.2 fusion.58.probe_ref
  357.3 20.6 %collective-permute-done.17 = bf16[192,1536]{1,0:T(8,128)(2,1)} collective-permute-done((bf16[192,1536]{1,0:T(8,128)(2,1)}, bf16[192,1536]{1,0:T(8,128)(2,1)}, u32[]{:S(2)}, u32[]{:S(2)}) %collective-permute-start.17) | collective-permute-done | bytes 589856 | tf_op jit(solution)/shard_map/ppermute | solution.py:830
  386.1 6.8 cross_attend.1
  393.8 15.7 %collective-permute-start.20 = (bf16[384,1536]{1,0:T(8,128)(2,1)S(1)}, bf16[384,1536]{1,0:T(8,128)(2,1)S(1)}, u32[]{:S(2)}, u32[]{:S(2)}) collective-permute-start(bf16[384,1536]{1,0:T(8,128)(2,1)S(1)} %get-tuple-element.187), channel_id=1, source_target_pairs={{0,1},{1,5},{2,4},{3,0},{4,3},{5,7},{6,6},{7,2},{8,9},{9,13},{10,1... | collective-permute-start | bytes 3538952 | tf_op jit(solution)/shard_map/ppermute | solution.py:845
  409.6 7.2 fusion.131
  419.6 29.5 %collective-permute-done.20 = bf16[384,1536]{1,0:T(8,128)(2,1)S(1)} collective-permute-done((bf16[384,1536]{1,0:T(8,128)(2,1)S(1)}, bf16[384,1536]{1,0:T(8,128)(2,1)S(1)}, u32[]{:S(2)}, u32[]{:S(2)}) %collective-permute-start.20) | collective-permute-done | bytes 1179680 | tf_op jit(solution)/shard_map/ppermute | solution.py:845
  450.8 61.2 %multiply_convert_fusion = (bf16[768,6144]{1,0:T(8,128)(2,1)}, f32[768,6144]{1,0:T(8,128)}, f32[768,6144]{1,0:T(8,128)}) fusion(bf16[1536,6144]{1,0:T(8,128)(2,1)} %bitcast.189, f32[768,1536]{1,0:T(8,128)} %copy-done.26, f32[1536]{0:T(1024)S(1)} %add.421, f32[1536]{0:T(1024)S(1)} %mul.314, f32[768]{0:T(1024)S(1)} %add_rsqrt_fusion, ...), kind=kOutput, calls=%fused_computation.5 | convolution fusion | flops 14808121344 | bytes 70797312 | tf_op jit(solution)/shard_map/dot_general | solution.py:28
  512.0 19.4 %all-gather.14.cloned.1.call-done = bf16[4,1536,1536]{2,1,0:T(8,128)(2,1)} async-done(((bf16[4,192,1536]{2,1,0:T(8,128)(2,1)}), bf16[4,1536,1536]{2,1,0:T(8,128)(2,1)}) %all-gather.14.cloned.1.call-update) | async-done | bytes 18874384 | tf_op jit(solution)/shard_map/all_gather | solution.py:865
  531.4 24.9 %multiply_convert_fusion.1 = (bf16[768,1536]{1,0:T(8,128)(2,1)S(1)}, f32[768,1536]{1,0:T(8,128)}) fusion(f32[]{:T(128)S(6)} %div.75, f32[768]{0:T(1024)S(1)} %copy-done.94, bf16[384,1536]{1,0:T(8,128)(2,1)S(1)} %copy-done.38, bf16[384,1536]{1,0:T(8,128)(2,1)S(1)} %copy-done.36, f32[768,1536]{1,0:T(8,128)} %copy-done.26, ...), kind=kOutput, calls=%fused_computation.66 | convolution fusion | flops 14506131456 | bytes 42470404 | tf_op jit(solution)/shard_map/dot_general | solution.py:28
  556.3 9.9 convolution_convert_fusion.2
  566.4 29.6 %add_convert_fusion.2 = bf16[768,6144]{1,0:T(8,128)(2,1)} fusion(f32[768,6144]{1,0:T(8,128)} %get-tuple-element.165, f32[768,6144]{1,0:T(8,128)} %get-tuple-element.214, bf16[768,1536]{1,0:T(8,128)(2,1)} %copy-done.57, bf16[6144,1536]{1,0:T(8,128)(2,1)} %bitcast.192), kind=kOutput, calls=%fused_computation.4 | convolution fusion | flops 14561574912 | bytes 68419584 | tf_op jit(solution)/shard_map/re,de->rd/dot_general | solution.py:36
  596.0 14.9 %add_convert_fusion.1 = bf16[768,6144]{1,0:T(8,128)(2,1)} fusion(bf16[768,6144]{1,0:T(8,128)(2,1)} %collective-permute-done.21, bf16[768,6144]{1,0:T(8,128)(2,1)} %get-tuple-element.164, bf16[768,1536]{1,0:T(8,128)(2,1)S(1)} %copy-done.58, s32[]{:T(128)S(6)} %select_n.326), kind=kOutput, calls=%fused_computation.3 | convolution fusion | flops 7261913088 | bytes 29491204 | tf_op jit(solution)/shard_map/rd,re->de/dot_general | solution.py:32
  610.9 13.7 %convolution_convert_fusion.1 = bf16[3072,1536]{1,0:T(8,128)(2,1)} fusion(bf16[768,6144]{1,0:T(8,128)(2,1)} %add_convert_fusion.2, s32[]{:T(128)S(6)} %select_n.327, f32[768,1536]{1,0:T(8,128)} %copy-done.26, f32[1536]{0:T(1024)S(1)} %add.421, f32[1536]{0:T(1024)S(1)} %mul.314, f32[768]{0:T(1024)S(1)} %add_rsqrt_fusion, f32[768]{0:T(1024)S(1)} %broadcast_multiply_fusion.6), kind=kOutput, calls=%fused_computation.21 | convolution fusion | flops 7258374144 | bytes 18892804 | tf_op jit(solution)/shard_map/rd,re->de/dot_general | solution.py:32
  624.9 21.6 %fusion.132 = f32[768,1536]{1,0:T(8,128)} fusion(bf16[768,6144]{1,0:T(8,128)(2,1)} %add_convert_fusion.2, bf16[1536,6144]{1,0:T(8,128)(2,1)} %bitcast.190), kind=kOutput, calls=%fused_computation.292 | convolution fusion | flops 14495514624 | bytes 33030144 | tf_op jit(solution)/shard_map/re,de->rd/dot_general | solution.py:36
  646.6 13.7 %add_convert_fusion = bf16[3072,1536]{1,0:T(8,128)(2,1)} fusion(bf16[3072,1536]{1,0:T(8,128)(2,1)} %collective-permute-done.22, bf16[768,6144]{1,0:T(8,128)(2,1)} %add_convert_fusion.2, s32[]{:T(128)S(6)} %select_n.328, f32[768,1536]{1,0:T(8,128)S(1)} %bitcast.165, f32[1536]{0:T(1024)S(1)} %add.421, f32[1536]{0:T(1024)S(1)} %mul.314, ...), kind=kOutput, calls=%fused_computation.2 | convolution fusion | flops 7267811328 | bytes 28329988 | tf_op jit(solution)/shard_map/rd,re->de/dot_general | solution.py:32
  660.4 6.1 multiply_reduce_fusion.1
  666.5 13.1 %fusion.127 = (bf16[768,1536]{1,0:T(8,128)(2,1)S(1)}, f32[768,1536]{1,0:T(8,128)}, f32[]{:T(128)}, bf16[768,1536]{1,0:T(8,128)(2,1)}) fusion(f32[768]{0:T(1024)S(1)} %broadcast_multiply_fusion.4, f32[768,1536]{1,0:T(8,128)} %copy-done.26, f32[768]{0:T(1024)S(1)} %broadcast_multiply_fusion.6, f32[768]{0:T(1024)S(1)} %broadcast_multiply_fusion.5, ...), kind=kLoop, calls=%fused_computation.288 | loop fusion | flops 22413312 | bytes 25973768 | tf_op jit(solution)/shard_map/convert_element_type | solution.py:1037
  683.7 6.9 fusion.61.grad_ref
  690.7 9.5 cross_attend_back.1
  713.2 6.9 collective-permute-done.28
  729.5 9.4 multiply_reduce_fusion.2
  749.9 7.8 fusion.55.grad_ref
  768.7 10.4 collective-permute-start.30
  792.4 70.0 %self_attend_back.1 = (bf16[768,1536]{1,0:T(8,128)(2,1)S(1)}, bf16[768,1536]{1,0:T(8,128)(2,1)S(1)}, bf16[768,1536]{1,0:T(8,128)(2,1)S(1)}, bf16[768,1536]{1,0:T(8,128)(2,1)}, bf16[768,1536]{1,0:T(8,128)(2,1)}) custom-call(s32[5]{0:T(128)S(1)} %copy-done.16, bf16[768,1536]{1,0:T(8,128)(2,1)S(1)} %copy-done.23, bf16[768,3072]{1,0:T(8,128)(2,1)} %fusion.14.own_k.own_v, ...), custom_call_target="tpu_custom_call" | custom-call | flops 18119393280 | bytes 37748736 | tf_op jit(solution)/shard_map/self_attend_back/pallas_call | solution.py:598
  880.6 7.8 convolution_convert_fusion
  888.7 18.6 %fusion.133 = f32[768,1536]{1,0:T(8,128)} fusion(bf16[768,4608]{1,0:T(8,128)(2,1)} %copy-done.33, bf16[1536,4608]{1,0:T(8,128)(2,1)} %all-gather.8.cloned.1.call-done), kind=kOutput, calls=%fused_computation.293 | convolution fusion | flops 10871635968 | bytes 25952256 | tf_op jit(solution)/shard_map/re,de->rd/dot_general | solution.py:36
  907.3 9.8 add_convert_fusion.3
  921.5 8.8 collective-permute-start.39
  935.4 39.2 %collective-permute-done.42 = bf16[2,64,384]{2,1,0:T(8,128)(2,1)S(1)} collective-permute-done((bf16[2,64,384]{2,1,0:T(8,128)(2,1)}, bf16[2,64,384]{2,1,0:T(8,128)(2,1)S(1)}, u32[]{:S(2)}, u32[]{:S(2)}) %collective-permute-start.42) | collective-permute-done | bytes 98336 | tf_op jit(solution)/shard_map/ppermute | solution.py:830
  974.5 16.5 %collective-permute-done.43 = bf16[2,64,384]{2,1,0:T(8,128)(2,1)S(1)} collective-permute-done((bf16[2,64,384]{2,1,0:T(8,128)(2,1)}, bf16[2,64,384]{2,1,0:T(8,128)(2,1)S(1)}, u32[]{:S(2)}, u32[]{:S(2)}) %collective-permute-start.43) | collective-permute-done | bytes 98336 | tf_op jit(solution)/shard_map/ppermute | solution.py:830
  1029.3 13.3 %collective-permute-done.51 = bf16[384,1536]{1,0:T(8,128)(2,1)} collective-permute-done((bf16[384,1536]{1,0:T(8,128)(2,1)}, bf16[384,1536]{1,0:T(8,128)(2,1)}, u32[]{:S(2)}, u32[]{:S(2)}) %collective-permute-start.51) | collective-permute-done | bytes 1179680 | tf_op jit(solution)/shard_map/ppermute | solution.py:854
  1045.5 19.3 %collective-permute-start.52 = (bf16[576,384]{1,0:T(8,128)(2,1)}, bf16[576,384]{1,0:T(8,128)(2,1)S(1)}, u32[]{:S(2)}, u32[]{:S(2)}) collective-permute-start(bf16[576,384]{1,0:T(8,128)(2,1)} %get-tuple-element.195), channel_id=1, source_target_pairs={{0,1},{1,2},{2,3},{3,0},{4,5},{5,6},{6,7},{7,4},{8,9},{9,10},{10,1... | collective-permute-start | bytes 1327112 | tf_op jit(solution)/shard_map/ppermute | solution.py:830
  1072.0 6.9 collective-permute-done.52
  1078.9 18.2 %collective-permute-done.53 = bf16[576,384]{1,0:T(8,128)(2,1)} collective-permute-done((bf16[576,384]{1,0:T(8,128)(2,1)}, bf16[576,384]{1,0:T(8,128)(2,1)}, u32[]{:S(2)}, u32[]{:S(2)}) %collective-permute-start.53) | collective-permute-done | bytes 442400 | tf_op jit(solution)/shard_map/ppermute | solution.py:830
  1109.8 10.5 collective-permute-start.48
  1133.6 10.3 collective-permute-done.55
  1143.9 13.8 %collective-permute-done.56 = bf16[576,384]{1,0:T(8,128)(2,1)S(1)} collective-permute-done((bf16[576,384]{1,0:T(8,128)(2,1)S(1)}, bf16[576,384]{1,0:T(8,128)(2,1)S(1)}, u32[]{:S(2)}, u32[]{:S(2)}) %collective-permute-start.56) | collective-permute-done | bytes 442400 | tf_op jit(solution)/shard_map/ppermute | solution.py:830
  1159.7 30.1 %all-gather.18.cloned.1.call-done = bf16[19968,384]{1,0:T(8,128)(2,1)} async-done(((bf16[2496,384]{1,0:T(8,128)(2,1)}), bf16[19968,384]{1,0:T(8,128)(2,1)}) %all-gather.18.cloned.1.call-update) | async-done | bytes 15335440 | tf_op jit(solution)/shard_map/all_gather | solution.py:1163
  1210.5 8.1 unpack.19
  (537 shorter events, 301.6 us)
Async XLA Ops:
  7.2 233.7 %all-gather.8.cloned.1.call-start = ((), (), s32[]{:S(2)}) async-start(), calls=%async_computation.4 | async-start | bytes 14598144 | tf_op jit(solution)/shard_map/all_gather | solution.py:883
  10.3 329.6 %all-gather.10.cloned.1.call-start = ((), (), s32[]{:S(2)}) async-start(), calls=%async_computation.5 | async-start | bytes 15925248 | tf_op jit(solution)/shard_map/all_gather | solution.py:865
  15.6 73.5 %collective-permute-start.1 = (bf16[384,1536]{1,0:T(8,128)(2,1)}, bf16[384,1536]{1,0:T(8,128)(2,1)S(1)}, u32[]{:S(2)}, u32[]{:S(2)}) collective-permute-start(bf16[384,1536]{1,0:T(8,128)(2,1)} %get-tuple-element.190), channel_id=1, source_target_pairs={{0,1},{1,5},{2,4},{3,0},{4,3},{5,7},{6,6},{7,2},{8,9},{9,13},{10,1... | collective-permute-start | bytes 3538952 | tf_op jit(solution)/shard_map/ppermute | solution.py:845
  89.1 46.6 %collective-permute-start.3 = (bf16[64,4608]{1,0:T(8,128)(2,1)}, bf16[64,4608]{1,0:T(8,128)(2,1)}, u32[]{:S(2)}, u32[]{:S(2)}) collective-permute-start(bf16[64,4608]{1,0:T(8,128)(2,1)} %pad_maximum_fusion.5), channel_id=1, source_target_pairs={{0,1},{1,2},{2,3},{3,0},{4,5},{5,6},{6,7},{7,4},{8,9},{9,10},{10,1... | collective-permute-start | bytes 1769480 | tf_op jit(solution)/shard_map/ppermute | solution.py:830
  90.3 85.8 %collective-permute-start.4 = (bf16[64,4608]{1,0:T(8,128)(2,1)}, bf16[64,4608]{1,0:T(8,128)(2,1)S(1)}, u32[]{:S(2)}, u32[]{:S(2)}) collective-permute-start(bf16[64,4608]{1,0:T(8,128)(2,1)} %pad_maximum_fusion.5), channel_id=1, source_target_pairs={{0,2},{1,3},{2,0},{3,1},{4,6},{5,7},{6,4},{7,5},{8,10},{9,11},{10,... | collective-permute-start | bytes 1769480 | tf_op jit(solution)/shard_map/ppermute | solution.py:830
  133.9 42.3 %collective-permute-start.5 = (bf16[64,4608]{1,0:T(8,128)(2,1)}, bf16[64,4608]{1,0:T(8,128)(2,1)S(1)}, u32[]{:S(2)}, u32[]{:S(2)}) collective-permute-start(bf16[64,4608]{1,0:T(8,128)(2,1)} %pad_maximum_fusion.5), channel_id=1, source_target_pairs={{0,3},{1,0},{2,1},{3,2},{4,7},{5,4},{6,5},{7,6},{8,11},{9,8},{10,9... | collective-permute-start | bytes 1769480 | tf_op jit(solution)/shard_map/ppermute | solution.py:830
  178.2 272.6 %all-gather.12.cloned.1.call-start = ((), (), s32[]{:S(2)}) async-start(), calls=%async_computation.6 | async-start | bytes 21233664 | tf_op jit(solution)/shard_map/all_gather | solution.py:865
  196.6 39.5 %collective-permute-start.6 = (bf16[64,1536]{1,0:T(8,128)(2,1)}, bf16[64,1536]{1,0:T(8,128)(2,1)S(1)}, u32[]{:S(2)}, u32[]{:S(2)}) collective-permute-start(bf16[64,1536]{1,0:T(8,128)(2,1)} %get-tuple-element.200), channel_id=1, source_target_pairs={{0,1},{1,2},{2,3},{3,0},{4,5},{5,6},{6,7},{7,4},{8,9},{9,10},{10,1... | collective-permute-start | bytes 589832 | tf_op jit(solution)/shard_map/ppermute | solution.py:830
  208.6 27.5 %collective-permute-start.7 = (bf16[64,1536]{1,0:T(8,128)(2,1)}, bf16[64,1536]{1,0:T(8,128)(2,1)}, u32[]{:S(2)}, u32[]{:S(2)}) collective-permute-start(bf16[64,1536]{1,0:T(8,128)(2,1)} %get-tuple-element.202), channel_id=1, source_target_pairs={{0,2},{1,3},{2,0},{3,1},{4,6},{5,7},{6,4},{7,5},{8,10},{9,11},{10,... | collective-permute-start | bytes 589832 | tf_op jit(solution)/shard_map/ppermute | solution.py:830
  211.4 24.7 %collective-permute-start.8 = (bf16[64,1536]{1,0:T(8,128)(2,1)S(1)}, bf16[64,1536]{1,0:T(8,128)(2,1)}, u32[]{:S(2)}, u32[]{:S(2)}) collective-permute-start(bf16[64,1536]{1,0:T(8,128)(2,1)S(1)} %get-tuple-element.201), channel_id=1, source_target_pairs={{0,3},{1,0},{2,1},{3,2},{4,7},{5,4},{6,5},{7,6},{8,11},{9,8},{10,9... | collective-permute-start | bytes 589832 | tf_op jit(solution)/shard_map/ppermute | solution.py:830
  260.5 68.5 %collective-permute-start.13 = (bf16[48,6144]{1,0:T(8,128)(2,1)}, bf16[48,6144]{1,0:T(8,128)(2,1)S(1)}, u32[]{:S(2)}, u32[]{:S(2)}) collective-permute-start(bf16[48,6144]{1,0:T(8,128)(2,1)} %get-tuple-element.79), channel_id=1, source_target_pairs={{0,1},{1,2},{2,3},{3,0},{4,5},{5,6},{6,7},{7,4},{8,9},{9,10},{10,1... | collective-permute-start | bytes 1769480 | tf_op jit(solution)/shard_map/ppermute | solution.py:830
  262.5 66.6 %collective-permute-start.14 = (bf16[48,6144]{1,0:T(8,128)(2,1)}, bf16[48,6144]{1,0:T(8,128)(2,1)S(1)}, u32[]{:S(2)}, u32[]{:S(2)}) collective-permute-start(bf16[48,6144]{1,0:T(8,128)(2,1)} %get-tuple-element.79), channel_id=1, source_target_pairs={{0,2},{1,3},{2,0},{3,1},{4,6},{5,7},{6,4},{7,5},{8,10},{9,11},{10,... | collective-permute-start | bytes 1769480 | tf_op jit(solution)/shard_map/ppermute | solution.py:830
  262.6 66.5 %collective-permute-start.15 = (bf16[48,6144]{1,0:T(8,128)(2,1)}, bf16[48,6144]{1,0:T(8,128)(2,1)S(1)}, u32[]{:S(2)}, u32[]{:S(2)}) collective-permute-start(bf16[48,6144]{1,0:T(8,128)(2,1)} %get-tuple-element.79), channel_id=1, source_target_pairs={{0,3},{1,0},{2,1},{3,2},{4,7},{5,4},{6,5},{7,6},{8,11},{9,8},{10,9... | collective-permute-start | bytes 1769480 | tf_op jit(solution)/shard_map/ppermute | solution.py:830
  331.8 199.6 %all-gather.14.cloned.1.call-start = ((), (), s32[]{:S(2)}) async-start(), calls=%async_computation.7 | async-start | bytes 21233664 | tf_op jit(solution)/shard_map/all_gather | solution.py:865
  335.6 21.7 %collective-permute-start.16 = (bf16[192,1536]{1,0:T(8,128)(2,1)}, bf16[192,1536]{1,0:T(8,128)(2,1)}, u32[]{:S(2)}, u32[]{:S(2)}) collective-permute-start(bf16[192,1536]{1,0:T(8,128)(2,1)} %get-tuple-element.83), channel_id=1, source_target_pairs={{0,1},{1,2},{2,3},{3,0},{4,5},{5,6},{6,7},{7,4},{8,9},{9,10},{10,1... | collective-permute-start | bytes 1769480 | tf_op jit(solution)/shard_map/ppermute | solution.py:830
  335.7 42.3 %collective-permute-start.17 = (bf16[192,1536]{1,0:T(8,128)(2,1)}, bf16[192,1536]{1,0:T(8,128)(2,1)}, u32[]{:S(2)}, u32[]{:S(2)}) collective-permute-start(bf16[192,1536]{1,0:T(8,128)(2,1)} %get-tuple-element.83), channel_id=1, source_target_pairs={{0,2},{1,3},{2,0},{3,1},{4,6},{5,7},{6,4},{7,5},{8,10},{9,11},{10,... | collective-permute-start | bytes 1769480 | tf_op jit(solution)/shard_map/ppermute | solution.py:830
  338.2 39.8 %collective-permute-start.18 = (bf16[192,1536]{1,0:T(8,128)(2,1)}, bf16[192,1536]{1,0:T(8,128)(2,1)}, u32[]{:S(2)}, u32[]{:S(2)}) collective-permute-start(bf16[192,1536]{1,0:T(8,128)(2,1)} %get-tuple-element.83), channel_id=1, source_target_pairs={{0,3},{1,0},{2,1},{3,2},{4,7},{5,4},{6,5},{7,6},{8,11},{9,8},{10,9... | collective-permute-start | bytes 1769480 | tf_op jit(solution)/shard_map/ppermute | solution.py:830
  383.8 397.3 %reduce-scatter.5.cloned.1.call-start = ((), (), s32[]{:S(2)}) async-start(), calls=%async_computation.8 | async-start | bytes 11796480 | tf_op jit(solution)/shard_map/reduce_scatter | solution.py:1004
  393.1 26.5 %collective-permute-start.19 = (bf16[384,1536]{1,0:T(8,128)(2,1)S(1)}, bf16[384,1536]{1,0:T(8,128)(2,1)S(1)}, u32[]{:S(2)}, u32[]{:S(2)}) collective-permute-start(bf16[384,1536]{1,0:T(8,128)(2,1)S(1)} %get-tuple-element.186), channel_id=1, source_target_pairs={{0,0},{1,4},{2,5},{3,1},{4,2},{5,6},{6,7},{7,3},{8,8},{9,12},{10,1... | collective-permute-start | bytes 3538952 | tf_op jit(solution)/shard_map/ppermute | solution.py:844
  393.8 55.2 %collective-permute-start.20 = (bf16[384,1536]{1,0:T(8,128)(2,1)S(1)}, bf16[384,1536]{1,0:T(8,128)(2,1)S(1)}, u32[]{:S(2)}, u32[]{:S(2)}) collective-permute-start(bf16[384,1536]{1,0:T(8,128)(2,1)S(1)} %get-tuple-element.187), channel_id=1, source_target_pairs={{0,1},{1,5},{2,4},{3,0},{4,3},{5,7},{6,6},{7,2},{8,9},{9,13},{10,1... | collective-permute-start | bytes 3538952 | tf_op jit(solution)/shard_map/ppermute | solution.py:845
  566.2 29.8 %collective-permute-start.21 = (bf16[768,6144]{1,0:T(8,128)(2,1)}, bf16[768,6144]{1,0:T(8,128)(2,1)}, u32[]{:S(2)}, u32[]{:S(2)}) collective-permute-start(bf16[768,6144]{1,0:T(8,128)(2,1)} %convolution_convert_fusion.2), channel_id=1, source_target_pairs={{0,4},{4,0},{1,5},{5,1},{2,6},{6,2},{3,7},{7,3},{8,12},{12,8},{9,1... | collective-permute-start | bytes 28311560 | tf_op jit(solution)/shard_map/ppermute | solution.py:999
  610.8 309.0 %reduce-scatter.7.cloned.1.call-start = ((), (), s32[]{:S(2)}) async-start(), calls=%async_computation.9 | async-start | bytes 11796480 | tf_op jit(solution)/shard_map/reduce_scatter | solution.py:1004
  624.6 22.0 %collective-permute-start.22 = (bf16[3072,1536]{1,0:T(8,128)(2,1)}, bf16[3072,1536]{1,0:T(8,128)(2,1)}, u32[]{:S(2)}, u32[]{:S(2)}) collective-permute-start(bf16[3072,1536]{1,0:T(8,128)(2,1)} %convolution_convert_fusion.1), channel_id=1, source_target_pairs={{0,4},{4,0},{1,5},{5,1},{2,6},{6,2},{3,7},{7,3},{8,12},{12,8},{9,1... | collective-permute-start | bytes 28311560 | tf_op jit(solution)/shard_map/ppermute | solution.py:999
  660.3 382.4 %reduce-scatter.11.cloned.1.call-start = ((), (), s32[]{:S(2)}) async-start(), calls=%async_computation.11 | async-start | bytes 10321920 | tf_op jit(solution)/shard_map/reduce_scatter | solution.py:1004
  683.1 38.4 %collective-permute-start.23 = (bf16[768,1536]{1,0:T(8,128)(2,1)}, bf16[768,1536]{1,0:T(8,128)(2,1)}, u32[]{:S(2)}, u32[]{:S(2)}) collective-permute-start(bf16[768,1536]{1,0:T(8,128)(2,1)} %convolution_convert_fusion.5), channel_id=1, source_target_pairs={{0,4},{4,0},{1,5},{5,1},{2,6},{6,2},{3,7},{7,3},{8,12},{12,8},{9,1... | collective-permute-start | bytes 7077896 | tf_op jit(solution)/shard_map/ppermute | solution.py:999
  729.5 28.2 %collective-permute-start.24 = (bf16[768,1536]{1,0:T(8,128)(2,1)}, bf16[768,1536]{1,0:T(8,128)(2,1)S(1)}, u32[]{:S(2)}, u32[]{:S(2)}) collective-permute-start(bf16[768,1536]{1,0:T(8,128)(2,1)} %convolution_convert_fusion.4), channel_id=1, source_target_pairs={{0,4},{4,0},{1,5},{5,1},{2,6},{6,2},{3,7},{7,3},{8,12},{12,8},{9,1... | collective-permute-start | bytes 7077896 | tf_op jit(solution)/shard_map/ppermute | solution.py:999
  765.6 361.9 %reduce-scatter.9.cloned.1.call-start = ((), (), s32[]{:S(2)}) async-start(), calls=%async_computation.10 | async-start | bytes 8847360 | tf_op jit(solution)/shard_map/reduce_scatter | solution.py:1004
  768.7 96.5 %collective-permute-start.30 = (bf16[384,1536]{1,0:T(8,128)(2,1)}, bf16[384,1536]{1,0:T(8,128)(2,1)}, u32[]{:S(2)}, u32[]{:S(2)}) collective-permute-start(bf16[384,1536]{1,0:T(8,128)(2,1)} %get-tuple-element.183), channel_id=1, source_target_pairs={{0,0},{4,1},{5,2},{1,3},{2,4},{6,5},{7,6},{3,7},{8,8},{12,9},{13,1... | collective-permute-start | bytes 3538952 | tf_op jit(solution)/shard_map/ppermute | solution.py:853
  779.1 86.1 %collective-permute-start.31 = (bf16[384,1536]{1,0:T(8,128)(2,1)}, bf16[384,1536]{1,0:T(8,128)(2,1)}, u32[]{:S(2)}, u32[]{:S(2)}) collective-permute-start(bf16[384,1536]{1,0:T(8,128)(2,1)} %get-tuple-element.182), channel_id=1, source_target_pairs={{1,0},{5,1},{4,2},{0,3},{3,4},{7,5},{6,6},{2,7},{9,8},{13,9},{12,1... | collective-permute-start | bytes 3538952 | tf_op jit(solution)/shard_map/ppermute | solution.py:854
  782.6 82.6 %collective-permute-start.33 = (bf16[192,1536]{1,0:T(8,128)(2,1)S(1)}, bf16[192,1536]{1,0:T(8,128)(2,1)S(1)}, u32[]{:S(2)}, u32[]{:S(2)}) collective-permute-start(bf16[192,1536]{1,0:T(8,128)(2,1)S(1)} %get-tuple-element.179), channel_id=1, source_target_pairs={{0,1},{1,2},{2,3},{3,0},{4,5},{5,6},{6,7},{7,4},{8,9},{9,10},{10,1... | collective-permute-start | bytes 1769480 | tf_op jit(solution)/shard_map/ppermute | solution.py:830
  784.9 80.4 %collective-permute-start.34 = (bf16[192,1536]{1,0:T(8,128)(2,1)S(1)}, bf16[192,1536]{1,0:T(8,128)(2,1)}, u32[]{:S(2)}, u32[]{:S(2)}) collective-permute-start(bf16[192,1536]{1,0:T(8,128)(2,1)S(1)} %get-tuple-element.178), channel_id=1, source_target_pairs={{0,2},{1,3},{2,0},{3,1},{4,6},{5,7},{6,4},{7,5},{8,10},{9,11},{10,... | collective-permute-start | bytes 1769480 | tf_op jit(solution)/shard_map/ppermute | solution.py:830
  784.9 80.4 %collective-permute-start.35 = (bf16[192,1536]{1,0:T(8,128)(2,1)S(1)}, bf16[192,1536]{1,0:T(8,128)(2,1)}, u32[]{:S(2)}, u32[]{:S(2)}) collective-permute-start(bf16[192,1536]{1,0:T(8,128)(2,1)S(1)} %get-tuple-element.177), channel_id=1, source_target_pairs={{0,3},{1,0},{2,1},{3,2},{4,7},{5,4},{6,5},{7,6},{8,11},{9,8},{10,9... | collective-permute-start | bytes 1769480 | tf_op jit(solution)/shard_map/ppermute | solution.py:830
  888.3 19.0 %collective-permute-start.38 = (bf16[2304,1536]{1,0:T(8,128)(2,1)}, bf16[2304,1536]{1,0:T(8,128)(2,1)}, u32[]{:S(2)}, u32[]{:S(2)}) collective-permute-start(bf16[2304,1536]{1,0:T(8,128)(2,1)} %convolution_convert_fusion), channel_id=1, source_target_pairs={{0,4},{4,0},{1,5},{5,1},{2,6},{6,2},{3,7},{7,3},{8,12},{12,8},{9,1... | collective-permute-start | bytes 21233672 | tf_op jit(solution)/shard_map/ppermute | solution.py:999
  917.2 272.6 %all-gather.18.cloned.1.call-start = ((), (), s32[]{:S(2)}) async-start(), calls=%async_computation.13 | async-start | bytes 17252352 | tf_op jit(solution)/shard_map/all_gather | solution.py:1163
  921.5 70.5 %collective-permute-start.39 = (bf16[768,384]{1,0:T(8,128)(2,1)S(1)}, bf16[768,384]{1,0:T(8,128)(2,1)S(1)}, u32[]{:S(2)}, u32[]{:S(2)}) collective-permute-start(bf16[768,384]{1,0:T(8,128)(2,1)S(1)} %get-tuple-element.176), channel_id=1, source_target_pairs={{0,1},{1,2},{2,3},{3,0},{4,5},{5,6},{6,7},{7,4},{8,9},{9,10},{10,1... | collective-permute-start | bytes 1769480 | tf_op jit(solution)/shard_map/ppermute | solution.py:830
  930.3 61.7 %collective-permute-start.40 = (bf16[768,384]{1,0:T(8,128)(2,1)S(1)}, bf16[768,384]{1,0:T(8,128)(2,1)}, u32[]{:S(2)}, u32[]{:S(2)}) collective-permute-start(bf16[768,384]{1,0:T(8,128)(2,1)S(1)} %get-tuple-element.175), channel_id=1, source_target_pairs={{0,2},{1,3},{2,0},{3,1},{4,6},{5,7},{6,4},{7,5},{8,10},{9,11},{10,... | collective-permute-start | bytes 1769480 | tf_op jit(solution)/shard_map/ppermute | solution.py:830
  933.3 59.3 %collective-permute-start.41 = (bf16[768,384]{1,0:T(8,128)(2,1)S(1)}, bf16[768,384]{1,0:T(8,128)(2,1)}, u32[]{:S(2)}, u32[]{:S(2)}) collective-permute-start(bf16[768,384]{1,0:T(8,128)(2,1)S(1)} %get-tuple-element.174), channel_id=1, source_target_pairs={{0,3},{1,0},{2,1},{3,2},{4,7},{5,4},{6,5},{7,6},{8,11},{9,8},{10,9... | collective-permute-start | bytes 1769480 | tf_op jit(solution)/shard_map/ppermute | solution.py:830
  933.3 41.2 %collective-permute-start.42 = (bf16[2,64,384]{2,1,0:T(8,128)(2,1)}, bf16[2,64,384]{2,1,0:T(8,128)(2,1)S(1)}, u32[]{:S(2)}, u32[]{:S(2)}) collective-permute-start(bf16[2,64,384]{2,1,0:T(8,128)(2,1)} %fusion.92), channel_id=1, source_target_pairs={{0,1},{1,2},{2,3},{3,0},{4,5},{5,6},{6,7},{7,4},{8,9},{9,10},{10,1... | collective-permute-start | bytes 294920 | tf_op jit(solution)/shard_map/ppermute | solution.py:830
  935.4 55.7 %collective-permute-start.43 = (bf16[2,64,384]{2,1,0:T(8,128)(2,1)}, bf16[2,64,384]{2,1,0:T(8,128)(2,1)S(1)}, u32[]{:S(2)}, u32[]{:S(2)}) collective-permute-start(bf16[2,64,384]{2,1,0:T(8,128)(2,1)} %fusion.92), channel_id=1, source_target_pairs={{0,2},{1,3},{2,0},{3,1},{4,6},{5,7},{6,4},{7,5},{8,10},{9,11},{10,... | collective-permute-start | bytes 294920 | tf_op jit(solution)/shard_map/ppermute | solution.py:830
  974.5 17.5 %collective-permute-start.44 = (bf16[2,64,384]{2,1,0:T(8,128)(2,1)}, bf16[2,64,384]{2,1,0:T(8,128)(2,1)S(1)}, u32[]{:S(2)}, u32[]{:S(2)}) collective-permute-start(bf16[2,64,384]{2,1,0:T(8,128)(2,1)} %fusion.92), channel_id=1, source_target_pairs={{0,3},{1,0},{2,1},{3,2},{4,7},{5,4},{6,5},{7,6},{8,11},{9,8},{10,9... | collective-permute-start | bytes 294920 | tf_op jit(solution)/shard_map/ppermute | solution.py:830
  1004.6 24.8 %collective-permute-start.50 = (bf16[384,1536]{1,0:T(8,128)(2,1)}, bf16[384,1536]{1,0:T(8,128)(2,1)S(1)}, u32[]{:S(2)}, u32[]{:S(2)}) collective-permute-start(bf16[384,1536]{1,0:T(8,128)(2,1)} %get-tuple-element.172), channel_id=1, source_target_pairs={{0,0},{4,1},{5,2},{1,3},{2,4},{6,5},{7,6},{3,7},{8,8},{12,9},{13,1... | collective-permute-start | bytes 3538952 | tf_op jit(solution)/shard_map/ppermute | solution.py:853
  1006.5 36.2 %collective-permute-start.51 = (bf16[384,1536]{1,0:T(8,128)(2,1)}, bf16[384,1536]{1,0:T(8,128)(2,1)}, u32[]{:S(2)}, u32[]{:S(2)}) collective-permute-start(bf16[384,1536]{1,0:T(8,128)(2,1)} %get-tuple-element.173), channel_id=1, source_target_pairs={{1,0},{5,1},{4,2},{0,3},{3,4},{7,5},{6,6},{2,7},{9,8},{13,9},{12,1... | collective-permute-start | bytes 3538952 | tf_op jit(solution)/shard_map/ppermute | solution.py:854
  1045.5 33.4 %collective-permute-start.52 = (bf16[576,384]{1,0:T(8,128)(2,1)}, bf16[576,384]{1,0:T(8,128)(2,1)S(1)}, u32[]{:S(2)}, u32[]{:S(2)}) collective-permute-start(bf16[576,384]{1,0:T(8,128)(2,1)} %get-tuple-element.195), channel_id=1, source_target_pairs={{0,1},{1,2},{2,3},{3,0},{4,5},{5,6},{6,7},{7,4},{8,9},{9,10},{10,1... | collective-permute-start | bytes 1327112 | tf_op jit(solution)/shard_map/ppermute | solution.py:830
  1064.8 32.3 %collective-permute-start.53 = (bf16[576,384]{1,0:T(8,128)(2,1)}, bf16[576,384]{1,0:T(8,128)(2,1)}, u32[]{:S(2)}, u32[]{:S(2)}) collective-permute-start(bf16[576,384]{1,0:T(8,128)(2,1)} %get-tuple-element.197), channel_id=1, source_target_pairs={{0,2},{1,3},{2,0},{3,1},{4,6},{5,7},{6,4},{7,5},{8,10},{9,11},{10,... | collective-permute-start | bytes 1327112 | tf_op jit(solution)/shard_map/ppermute | solution.py:830
  1068.1 29.0 %collective-permute-start.54 = (bf16[576,384]{1,0:T(8,128)(2,1)}, bf16[576,384]{1,0:T(8,128)(2,1)}, u32[]{:S(2)}, u32[]{:S(2)}) collective-permute-start(bf16[576,384]{1,0:T(8,128)(2,1)} %get-tuple-element.196), channel_id=1, source_target_pairs={{0,3},{1,0},{2,1},{3,2},{4,7},{5,4},{6,5},{7,6},{8,11},{9,8},{10,9... | collective-permute-start | bytes 1327112 | tf_op jit(solution)/shard_map/ppermute | solution.py:830
  1099.3 130.2 %all-gather.16.cloned.1.call-start = ((), (), s32[]{:S(2)}) async-start(), calls=%async_computation.12 | async-start | bytes 3981312 | tf_op jit(solution)/shard_map/all_gather | solution.py:1178
  1131.0 26.7 %collective-permute-start.56 = (bf16[576,384]{1,0:T(8,128)(2,1)S(1)}, bf16[576,384]{1,0:T(8,128)(2,1)S(1)}, u32[]{:S(2)}, u32[]{:S(2)}) collective-permute-start(bf16[576,384]{1,0:T(8,128)(2,1)S(1)} %get-tuple-element.194), channel_id=1, source_target_pairs={{0,2},{1,3},{2,0},{3,1},{4,6},{5,7},{6,4},{7,5},{8,10},{9,11},{10,... | collective-permute-start | bytes 1327112 | tf_op jit(solution)/shard_map/ppermute | solution.py:830
  1131.5 26.1 %collective-permute-start.57 = (bf16[576,384]{1,0:T(8,128)(2,1)S(1)}, bf16[576,384]{1,0:T(8,128)(2,1)S(1)}, u32[]{:S(2)}, u32[]{:S(2)}) collective-permute-start(bf16[576,384]{1,0:T(8,128)(2,1)S(1)} %get-tuple-element.193), channel_id=1, source_target_pairs={{0,3},{1,0},{2,1},{3,2},{4,7},{5,4},{6,5},{7,6},{8,11},{9,8},{10,9... | collective-permute-start | bytes 1327112 | tf_op jit(solution)/shard_map/ppermute | solution.py:830
  (133 other events, 3186.1 us)
Sparse Core Ops, SparseCore 0:
  11.6 161.2 all-gather.7
  178.3 91.0 all-gather.9
  331.9 98.2 all-gather.11
  432.6 98.7 all-gather.13
  611.0 95.0 reduce-scatter.4
  709.6 95.0 reduce-scatter.6
  808.4 85.2 reduce-scatter.10
  917.2 84.6 reduce-scatter.8
  1099.4 90.3 all-gather.17
  1192.1 33.9 all-gather.15

commit v6 on v4

--- a/solution.py
+++ b/solution.py
@@ -848,11 +848,13 @@
     def by_time(one, two):
         return jnp.concatenate([jnp.where(even, one, two), jnp.where(even, two, one)], axis=0)
 
+    def outgoing(values):
+        early, late = values[:block], values[block:]
+        return jnp.where(even, early, late), jnp.where(even, late, early)
+
     def from_chip(values):
-        early, late = values[:block], values[block:]
-        one = lax.ppermute(jnp.where(even, early, late), spot, back[0])
-        two = lax.ppermute(jnp.where(even, late, early), spot, back[1])
-        return one, two
+        one, two = outgoing(values)
+        return lax.ppermute(one, spot, back[0]), lax.ppermute(two, spot, back[1])
 
     def by_slot(one, two):
         return jnp.stack([jnp.where(lower, one, two), jnp.where(lower, two, one)])
@@ -880,15 +882,13 @@
         ]
     )
     vectors = jnp.pad(vectors[None, :], ((0, 15), (0, 3 * width - 6 * block)))
+    share = qkv_share.shape[0]
     qkv_mine = jnp.concatenate([qkv_share, vectors], axis=0)
     qkv_came = hops(qkv_mine)
-    share = qkv_share.shape[0]
-    qkv_line = line_up(qkv_share, [values[:share] for values in qkv_came])
-    qkv_matrix = from_replicas(qkv_line)
-    norms = line_up(qkv_mine[share], [values[share] for values in qkv_came])
+    qkv_matrix = from_replicas(line_up(qkv_share, [values[:share] for values in qkv_came]))
+    norms = line_up(vectors[0], [values[share] for values in qkv_came])
     norms = norms[:, : 6 * block].reshape(shards, 6, block).transpose(1, 0, 2)
     norms = norms.reshape(6, width).astype(jnp.float32)
-
     came = to_chip(after(frames, *qkv_came))
     x_low = by_time(*came)
     rest_share = jnp.concatenate(
@@ -896,12 +896,7 @@
         axis=1,
     )
     rest_came = hops(after(rest_share, *came))
-    rest = from_replicas(line_up(rest_share, rest_came))
-    output_matrix = rest[:, :width]
-    probe_matrix = rest[:, width : 2 * width]
-    merge_matrix = rest[:, 2 * width :]
     expand_share = share_of(feed_up_weight)
-    expand_came = hops(after(expand_share, *rest_came))
 
     facts = jnp.concatenate(
         [(clip_lengths // 64)[:, None], (clip_lengths % 64)[:, None], slot_used[:, None], text_mask],
@@ -954,16 +949,15 @@
     hidden_one = ((inputs - parts_one[0]) * parts_one[1] * norms[0] + norms[1]).astype(
         jnp.bfloat16
     )
-    kv = project(hidden_one, qkv_matrix[:, width:]).astype(jnp.bfloat16)
+    kv = project(after(hidden_one, count), qkv_matrix[:, width:]).astype(jnp.bfloat16)
     kv_other = lax.ppermute(kv, "core", swap)
     queries = project(after(hidden_one, kv), qkv_matrix[:, :width]).astype(jnp.bfloat16)
-    expand_line = line_up(expand_share, held(expand_came, queries, kv_other))
-    expand_matrix = from_replicas(expand_line)
-    reduce_share = share_of(feed_down_weight)
-    reduce_came = hops(after(reduce_share, *expand_came))
-    mixed_self, lse = self_attend(after(places, expand_line, text_part), queries, kv, kv_other)
-    reduce_matrix = from_replicas(line_up(reduce_share, held(reduce_came, mixed_self)))
-    text_came = held(text_came, mixed_self)
+    rest_came = held(rest_came, kv)
+    rest = from_replicas(line_up(rest_share, rest_came))
+    output_matrix = rest[:, :width]
+    probe_matrix = rest[:, width : 2 * width]
+    merge_matrix = rest[:, 2 * width :]
+    text_came = held(text_came, queries)
     text_half = lax.dynamic_index_in_dim(text_part, shard, 0, keepdims=False).astype(jnp.float32)
     for values in text_came:
         text_half += values.astype(jnp.float32)
@@ -971,14 +965,21 @@
     text_swap = lax.ppermute(text_half, "core", swap)
     lookups = jnp.where(first_core, text_half, text_swap)
     contents = jnp.where(first_core, text_swap, text_half)
+    expand_came = hops(after(expand_share, *rest_came, *text_came))
+    mixed_self, lse = self_attend(after(places, rest_came[0]), queries, kv, kv_other)
+    expand_came = held(expand_came, mixed_self)
+    expand_matrix = from_replicas(line_up(expand_share, expand_came))
+    reduce_share = share_of(feed_down_weight)
+    reduce_came = hops(after(reduce_share, *expand_came))
     after_self = inputs + project(mixed_self, output_matrix)
     parts_two = norm_parts(after_self)
     hidden_two = ((after_self - parts_two[0]) * parts_two[1] * norms[2] + norms[3]).astype(
         jnp.bfloat16
     )
     probes = project(hidden_two, probe_matrix).astype(jnp.bfloat16)
+    reduce_matrix = from_replicas(line_up(reduce_share, held(reduce_came, probes)))
     teacher_low = by_time(*to_chip(after(teacher, *reduce_came, probes)))
-    cross_mixed = cross_attend(probes, lookups, contents, after(present, count))
+    cross_mixed = cross_attend(probes, lookups, contents, present)
     after_cross = after_self + project(cross_mixed, merge_matrix)
     parts_three = norm_parts(after_cross)
     hidden_three = (
@@ -1027,13 +1028,21 @@
         return total.astype(jnp.bfloat16)
 
     down_theirs = theirs_of(grad_feed_low, activated_low)
+    to_send = outgoing(result.astype(jnp.bfloat16))
+    output_one = lax.ppermute(to_send[0], spot, back[0])
     grad_activated = back_project(after(grad_feed_low, down_theirs), reduce_matrix)
     grad_upward = gelu_pull(grad_activated)[0].astype(jnp.bfloat16)
-    down_ours = ours_of(after(grad_feed_low, grad_upward), activated_low, down_theirs)
+    output_one = after(output_one, grad_upward)
+    down_ours = ours_of(
+        after(grad_feed_low, grad_upward, output_one), activated_low, down_theirs
+    )
     down_sum = over_outer(down_ours)
     up_theirs = theirs_of(after(grad_upward, down_ours), hidden_three)
     grad_hidden_three = back_project(after(grad_upward, up_theirs), expand_matrix)
-    up_ours = ours_of(after(grad_upward, grad_hidden_three), hidden_three, up_theirs)
+    output_two = lax.ppermute(after(to_send[1], output_one), spot, back[1])
+    output_two = after(output_two, grad_hidden_three)
+    output = by_slot(output_one, output_two)
+    up_ours = ours_of(after(grad_upward, grad_hidden_three, output_two), hidden_three, up_theirs)
     grad_norm, gain_feed, bias_feed = norm_back(
         after(grad_hidden_three, up_ours), after_cross, parts_three, norms[4]
     )
@@ -1104,36 +1113,39 @@
     )
     text_own = text_own.astype(jnp.bfloat16)
     down_came = shard_hops(down_sum)
-    output_came = from_chip(after(result.astype(jnp.bfloat16), middle))
+    text_came = hops(text_own)
     grad_queries, own_keys, own_values, other_keys, other_values = self_attend_back(
         places, queries, kv, kv_other, mixed_self, after(grad_mixed, middle, text_own), lse
     )
+    text_came = held(text_came, grad_queries)
     down_came = held(down_came, grad_queries)
-    output_came = held(output_came, grad_queries)
-    other_keys, other_values = held([other_keys, other_values], *down_came, *output_came)
+    other_keys, other_values = held([other_keys, other_values], *text_came, *down_came)
     own_keys += lax.ppermute(other_keys, "core", swap)
     own_values += lax.ppermute(other_values, "core", swap)
     down_piece = over_shard(down_sum, down_came)
-    output = by_slot(*output_came)
     up_came = shard_hops(after(up_sum, down_piece))
-    text_came = hops(after(text_own, grad_queries))
 
     qkv_grads = jnp.concatenate([grad_queries, own_keys, own_values], axis=1)
     qkv_theirs = theirs_of(qkv_grads, hidden_one)
     grad_hidden_one = back_project(after(qkv_grads, qkv_theirs), qkv_matrix)
-    qkv_ours = ours_of(
-        after(qkv_grads, grad_hidden_one, *up_came, *text_came), hidden_one, qkv_theirs
-    )
+    qkv_ours = ours_of(after(qkv_grads, grad_hidden_one), hidden_one, qkv_theirs)
+    up_came = held(up_came, grad_hidden_one)
     up_piece = over_shard(up_sum, up_came)
     text_grad = line_up(text_own, text_came).astype(jnp.float32)
     text_grad = text_grad.transpose(1, 2, 0, 3).reshape(text_states.shape)
     qkv_sum = over_outer(qkv_ours)
     grad_norm, gain_self, bias_self = norm_back(
-        after(grad_hidden_one, qkv_ours), inputs, parts_one, norms[0]
-    )
-    frames_came = from_chip((grad_after_self + grad_norm).astype(jnp.bfloat16))
+        after(grad_hidden_one, qkv_ours, *up_came), inputs, parts_one, norms[0]
+    )
+    middle_kept = after(middle_sum[: middle_rows - text_split], qkv_ours, *up_came)
+    middle_came = shard_hops(middle_kept)
+    frames_came = from_chip(
+        after((grad_after_self + grad_norm).astype(jnp.bfloat16), *middle_came)
+    )
     frames_grad = by_slot(*frames_came).astype(jnp.float32)
 
+    qkv_sum = after(qkv_sum, *frames_came)
+    late_came = shard_hops(qkv_sum)
     small = jnp.stack(
         [
             gain_self,
@@ -1146,6 +1158,7 @@
             jnp.zeros((width,), jnp.float32),
         ]
     )
+    small = after(small, *late_came)
     for axis, pairs in (
         ("core", swap),
         ("x", swap),
@@ -1157,16 +1170,14 @@
     loss = small[6, 0] / (width * count)
     small_own = lax.dynamic_slice_in_dim(small, shard * block, block, 1)
 
-    middle_sum = after(middle_sum, up_piece, *frames_came)
-    middle_kept = middle_sum[: middle_rows - text_split]
-    middle_piece = over_shard(middle_kept, shard_hops(middle_kept))
+    middle_piece = over_shard(middle_kept, middle_came)
     early = jnp.concatenate(
         [up_piece]
         + [down_piece[:, i * block : (i + 1) * block] for i in range(4)]
         + [text_piece, middle_piece],
         axis=0,
     )
-    early = lax.all_gather(early, REPLICAS, axis=0)
+    early = lax.all_gather(after(early, text_grad), REPLICAS, axis=0)
     piece = width // replicas
     square = (block, width)
     up_grad = unpack(early, hidden_units // replicas, 0, (block, hidden_units), 0, 1)
@@ -1179,11 +1190,10 @@
     output_grad = unpack(early, piece, at, square, 0, 2)
     probe_grad = unpack(early, piece, at + 1, square, 0, 2)
     merge_grad = unpack(early, piece, at + 2, square, 0, 2)
-    qkv_sum = after(qkv_sum, middle_piece, small)
-    late = over_shard(qkv_sum, shard_hops(qkv_sum))
+    late = over_shard(qkv_sum, late_came)
     late = lax.all_gather(after(late, early), REPLICAS, axis=0, tiled=True)
-    late = late.reshape(3, width, block)
-    qkv_grad = [late[i].T.astype(jnp.float32) for i in range(3)]
+    late = late.reshape(-1, block, block)
+    qkv_grad = [unpack(late, block, 0, square, 2 * i, 2) for i in range(3)]
     return (
         output,
         loss,

time: 1210 us -> 1170 us (0.967)
  waiting for transfers between devices: 311 us -> 270 us
    all_gather x1, waiting for transfers between devices: 30.9 us -> 0.01 us  [clip_body(): early = lax.all_gather(after(early, text_grad), REPLICAS, axis=0)]
    ppermute x33, waiting for transfers between devices: 170 us -> 140 us  [hop(): return lax.ppermute(values, 'shard', pairs)]
    all_gather x4, waiting for transfers between devices: 0.04 us -> 21 us  [from_replicas(): full = lax.all_gather(line, ('y', 'x', 'core'), axis=1, tiled=True)]
    unnamed x230 -> x179, local copies, waits for them, and re-layouts: 53.8 us -> 35.5 us
    pallas_call x7 -> x10, Pallas kernels: 24.2 us -> 29 us  [unpack(): pl.pallas_call(unpack_kernel, out_shape=jax.ShapeDtypeStruct(out_shape, j...]
  transfers between devices with their start and end apart: 71 -> 71, of which waited for: 28 -> 27; matrix products, arithmetic and copies ran while one was open for 33% -> 35% of each run, Pallas kernels for 14% -> 15%
where the time goes in v6:
time: 1170 us; the launch traced here: 1160 us
  matrix products  313 us (27%)
  waiting for transfers between devices  270 us (23%)
  starting transfers between devices  202 us (17%)
  Pallas kernels  174 us (15%)
  local copies, waits for them, and re-layouts  98 us (8%)
  other arithmetic  80.7 us (7%)
  between operations  21.3 us (2%)
    ppermute x33, waiting for transfers between devices, hop(): return lax.ppermute(values, 'shard', pairs)  140 us
    dot_general x8, matrix products, project(): return jnp.dot(left, right, preferred_element_type=jnp.float32)  129 us
    ppermute x33, starting transfers between devices, hop(): return lax.ppermute(values, 'shard', pairs)  108 us
    dot_general x7, matrix products, back_project(): jnp.einsum('re,de->rd', grads, matrix, preferred_element_type=jnp.float32)  94 us
    dot_general x13, matrix products, outer_sum(): jnp.einsum('rd,re->de', left, right, preferred_element_type=jnp.float32)  90.5 us
    pallas_call x1, Pallas kernels, self_attend_back(): pl.pallas_call(self_backward_kernel, out_shape=(jax.ShapeDtypeStruct((row...  70 us
    pallas_call x1, Pallas kernels, self_attend(): pl.pallas_call(self_forward_kernel, out_shape=(jax.ShapeDtypeStruct((rows...  58.4 us
    ppermute x2, waiting for transfers between devices, to_chip(): two = lax.ppermute(jnp.where(lower, pair[1], pair[0]), spot, there[1])  57.9 us
  transfers between devices with their start and end apart: 71, of which 27 were waited for; matrix products, arithmetic and copies ran while one was open for 35% of the time, Pallas kernels for 15%

profile of v6, /device:TPU:0, one launch (start us, length us, event | category | flops | bytes accessed | tf_op | source)
XLA Modules:
  0.0 1158.6 jit_solution(16978738009909887797)
XLA Ops:
  20.9 12.3 %collective-permute-done = bf16[64,4608]{1,0:T(8,128)(2,1)} collective-permute-done((bf16[64,4608]{1,0:T(8,128)(2,1)S(1)}, bf16[64,4608]{1,0:T(8,128)(2,1)}, u32[]{:S(2)}, u32[]{:S(2)}) %collective-permute-start) | collective-permute-done | bytes 589856 | tf_op jit(solution)/shard_map/ppermute | solution.py:830
  34.3 23.4 %collective-permute-done.1 = bf16[64,4608]{1,0:T(8,128)(2,1)} collective-permute-done((bf16[64,4608]{1,0:T(8,128)(2,1)S(1)}, bf16[64,4608]{1,0:T(8,128)(2,1)}, u32[]{:S(2)}, u32[]{:S(2)}) %collective-permute-start.1) | collective-permute-done | bytes 589856 | tf_op jit(solution)/shard_map/ppermute | solution.py:830
  77.8 14.3 %collective-permute-start.4 = (bf16[384,1536]{1,0:T(8,128)(2,1)}, bf16[384,1536]{1,0:T(8,128)(2,1)}, u32[]{:S(2)}, u32[]{:S(2)}) collective-permute-start(bf16[384,1536]{1,0:T(8,128)(2,1)} %get-tuple-element.215), channel_id=1, source_target_pairs={{0,1},{1,5},{2,4},{3,0},{4,3},{5,7},{6,6},{7,2},{8,9},{9,13},{10,1... | collective-permute-start | bytes 3538952 | tf_op jit(solution)/shard_map/ppermute | solution.py:845
  97.6 34.8 %collective-permute-done.4 = bf16[384,1536]{1,0:T(8,128)(2,1)} collective-permute-done((bf16[384,1536]{1,0:T(8,128)(2,1)}, bf16[384,1536]{1,0:T(8,128)(2,1)}, u32[]{:S(2)}, u32[]{:S(2)}) %collective-permute-start.4) | collective-permute-done | bytes 1179680 | tf_op jit(solution)/shard_map/ppermute | solution.py:845
  132.4 14.5 %collective-permute-start.7 = (bf16[48,4608]{1,0:T(8,128)(2,1)}, bf16[48,4608]{1,0:T(8,128)(2,1)}, u32[]{:S(2)}, u32[]{:S(2)}) collective-permute-start(bf16[48,4608]{1,0:T(8,128)(2,1)} %pad_maximum_fusion.7), channel_id=1, source_target_pairs={{0,2},{1,3},{2,0},{3,1},{4,6},{5,7},{6,4},{7,5},{8,10},{9,11},{10,... | collective-permute-start | bytes 1327112 | tf_op jit(solution)/shard_map/ppermute | solution.py:830
  155.9 12.2 %fusion.14.own_k.own_v = bf16[768,3072]{1,0:T(8,128)(2,1)} fusion(bf16[768,1536]{1,0:T(8,128)(2,1)} %fusion.18, bf16[1536,4608]{1,0:T(8,128)(2,1)} %bitcast.204), kind=kOutput, calls=%fused_computation.36 | convolution fusion | flops 7250116608 | bytes 16515072 | tf_op jit(solution)/shard_map/dot_general | solution.py:28
  174.4 9.9 all-gather.12.cloned.1.call-start
  194.9 8.0 collective-permute-start.12
  207.9 7.0 fusion.64.q_ref
  227.3 58.4 %self_attend.1 = (bf16[768,1536]{1,0:T(8,128)(2,1)S(1)}, f32[96,768]{1,0:T(8,128)S(1)}) custom-call(s32[5]{0:T(128)S(1)} %stack.66.place, bf16[768,1536]{1,0:T(8,128)(2,1)S(1)} %fusion.64.q_ref, bf16[768,3072]{1,0:T(8,128)(2,1)S(1)} %bitcast.172, bf16[768,3072]{1,0:T(8,128)(2,1)S(1)} %bitcast.172, bf16[768,3072]{1,0:T(8,128)(2,1)} %collective-permute-done.11.other_k.other_v, ...), custom_call_target="tpu_custom_call" | custom-call | flops 7247757312 | bytes 18874368 | tf_op jit(solution)/shard_map/self_attend/pallas_call | solution.py:569
  297.4 8.0 fusion.132
  307.5 7.2 fusion.58.probe_ref
  314.8 21.2 %collective-permute-done.20 = bf16[192,1536]{1,0:T(8,128)(2,1)} collective-permute-done((bf16[192,1536]{1,0:T(8,128)(2,1)}, bf16[192,1536]{1,0:T(8,128)(2,1)}, u32[]{:S(2)}, u32[]{:S(2)}) %collective-permute-start.20) | collective-permute-done | bytes 589856 | tf_op jit(solution)/shard_map/ppermute | solution.py:830
  350.1 15.4 %collective-permute-start.24 = (bf16[384,1536]{1,0:T(8,128)(2,1)S(1)}, bf16[384,1536]{1,0:T(8,128)(2,1)S(1)}, u32[]{:S(2)}, u32[]{:S(2)}) collective-permute-start(bf16[384,1536]{1,0:T(8,128)(2,1)S(1)} %get-tuple-element.210), channel_id=1, source_target_pairs={{0,1},{1,5},{2,4},{3,0},{4,3},{5,7},{6,6},{7,2},{8,9},{9,13},{10,1... | collective-permute-start | bytes 3538952 | tf_op jit(solution)/shard_map/ppermute | solution.py:845
  365.5 6.8 cross_attend.1
  372.4 6.8 fusion.133
  382.0 23.1 %collective-permute-done.24 = bf16[384,1536]{1,0:T(8,128)(2,1)S(1)} collective-permute-done((bf16[384,1536]{1,0:T(8,128)(2,1)S(1)}, bf16[384,1536]{1,0:T(8,128)(2,1)S(1)}, u32[]{:S(2)}, u32[]{:S(2)}) %collective-permute-start.24) | collective-permute-done | bytes 1179680 | tf_op jit(solution)/shard_map/ppermute | solution.py:845
  406.6 61.1 %multiply_convert_fusion = (bf16[768,6144]{1,0:T(8,128)(2,1)}, f32[768,6144]{1,0:T(8,128)}, f32[768,6144]{1,0:T(8,128)}) fusion(bf16[1536,6144]{1,0:T(8,128)(2,1)} %bitcast.200, f32[768,1536]{1,0:T(8,128)} %copy-done.23, f32[1536]{0:T(1024)S(1)} %add.428, f32[1536]{0:T(1024)S(1)} %mul.314, f32[768]{0:T(1024)S(1)} %add_rsqrt_fusion, ...), kind=kOutput, calls=%fused_computation.5 | convolution fusion | flops 14808121344 | bytes 70797312 | tf_op jit(solution)/shard_map/dot_general | solution.py:28
  467.7 20.9 %all-gather.14.cloned.1.call-done = bf16[4,1536,1536]{2,1,0:T(8,128)(2,1)} async-done(((bf16[4,192,1536]{2,1,0:T(8,128)(2,1)}), bf16[4,1536,1536]{2,1,0:T(8,128)(2,1)}) %all-gather.14.cloned.1.call-update) | async-done | bytes 18874384 | tf_op jit(solution)/shard_map/all_gather | solution.py:867
  488.6 25.7 %multiply_convert_fusion.1 = (bf16[768,1536]{1,0:T(8,128)(2,1)S(1)}, bf16[768,1536]{1,0:T(8,128)(2,1)}, f32[768,1536]{1,0:T(8,128)}) fusion(f32[]{:T(128)S(6)} %div.75, f32[768]{0:T(1024)S(1)} %copy-done.70, bf16[384,1536]{1,0:T(8,128)(2,1)} %get-tuple-element.208, bf16[384,1536]{1,0:T(8,128)(2,1)} %get-tuple-element.207, f32[768,1536]{1,0:T(8,128)} %copy-done.23, ...), kind=kOutput, calls=%fused_computation.66 | convolution fusion | flops 14507311104 | bytes 44829700 | tf_op jit(solution)/shard_map/dot_general | solution.py:28
  514.3 10.0 convolution_convert_fusion.2
  529.1 29.5 %add_convert_fusion.2 = bf16[768,6144]{1,0:T(8,128)(2,1)} fusion(f32[768,6144]{1,0:T(8,128)} %get-tuple-element.189, f32[768,6144]{1,0:T(8,128)} %get-tuple-element.239, bf16[768,1536]{1,0:T(8,128)(2,1)} %copy-done.46, bf16[6144,1536]{1,0:T(8,128)(2,1)} %bitcast.203), kind=kOutput, calls=%fused_computation.4 | convolution fusion | flops 14561574912 | bytes 68419584 | tf_op jit(solution)/shard_map/re,de->rd/dot_general | solution.py:36
  558.6 14.1 %add_convert_fusion.1 = bf16[768,6144]{1,0:T(8,128)(2,1)} fusion(bf16[768,6144]{1,0:T(8,128)(2,1)} %collective-permute-done.26, bf16[768,6144]{1,0:T(8,128)(2,1)} %get-tuple-element.188, bf16[768,1536]{1,0:T(8,128)(2,1)} %copy-done.46, s32[]{:T(128)S(6)} %select_n.332), kind=kOutput, calls=%fused_computation.3 | convolution fusion | flops 7261913088 | bytes 29491204 | tf_op jit(solution)/shard_map/rd,re->de/dot_general | solution.py:32
  572.8 13.5 %convolution_convert_fusion.1 = bf16[3072,1536]{1,0:T(8,128)(2,1)} fusion(bf16[768,6144]{1,0:T(8,128)(2,1)} %add_convert_fusion.2, s32[]{:T(128)S(6)} %select_n.333, f32[768,1536]{1,0:T(8,128)} %copy-done.23, f32[1536]{0:T(1024)S(1)} %add.428, f32[1536]{0:T(1024)S(1)} %mul.314, f32[768]{0:T(1024)S(1)} %add_rsqrt_fusion, f32[768]{0:T(1024)S(1)} %broadcast_multiply_fusion.6), kind=kOutput, calls=%fused_computation.21 | convolution fusion | flops 7258374144 | bytes 18892804 | tf_op jit(solution)/shard_map/rd,re->de/dot_general | solution.py:32
  592.5 21.6 %fusion.134 = f32[768,1536]{1,0:T(8,128)} fusion(bf16[768,6144]{1,0:T(8,128)(2,1)} %add_convert_fusion.2, bf16[1536,6144]{1,0:T(8,128)(2,1)} %bitcast.201), kind=kOutput, calls=%fused_computation.296 | convolution fusion | flops 14495514624 | bytes 33030144 | tf_op jit(solution)/shard_map/re,de->rd/dot_general | solution.py:36
  619.7 14.0 %add_convert_fusion = bf16[3072,1536]{1,0:T(8,128)(2,1)} fusion(bf16[3072,1536]{1,0:T(8,128)(2,1)} %collective-permute-done.27, bf16[768,6144]{1,0:T(8,128)(2,1)} %add_convert_fusion.2, s32[]{:T(128)S(6)} %select_n.336, f32[768,1536]{1,0:T(8,128)S(1)} %bitcast.178, f32[1536]{0:T(1024)S(1)} %add.428, f32[1536]{0:T(1024)S(1)} %mul.314, ...), kind=kOutput, calls=%fused_computation.2 | convolution fusion | flops 7267811328 | bytes 28329988 | tf_op jit(solution)/shard_map/rd,re->de/dot_general | solution.py:32
  633.8 6.0 multiply_reduce_fusion.1
  639.9 9.6 fusion.129
  653.0 6.5 fusion.61.grad_ref
  659.6 9.5 cross_attend_back.1
  689.1 9.4 multiply_reduce_fusion.2
  706.3 7.8 fusion.55.grad_ref
  727.8 7.6 collective-permute-start.36
  750.8 70.0 %self_attend_back.1 = (bf16[768,1536]{1,0:T(8,128)(2,1)S(1)}, bf16[768,1536]{1,0:T(8,128)(2,1)S(1)}, bf16[768,1536]{1,0:T(8,128)(2,1)S(1)}, bf16[768,1536]{1,0:T(8,128)(2,1)}, bf16[768,1536]{1,0:T(8,128)(2,1)}) custom-call(s32[5]{0:T(128)S(1)} %copy-done.12, bf16[768,1536]{1,0:T(8,128)(2,1)S(1)} %copy-done.20, bf16[768,3072]{1,0:T(8,128)(2,1)} %fusion.14.own_k.own_v, ...), custom_call_target="tpu_custom_call" | custom-call | flops 18119393280 | bytes 37748736 | tf_op jit(solution)/shard_map/self_attend_back/pallas_call | solution.py:598
  835.9 7.8 convolution_convert_fusion
  843.8 18.5 %fusion.135 = f32[768,1536]{1,0:T(8,128)} fusion(bf16[768,4608]{1,0:T(8,128)(2,1)} %copy-done.29, bf16[1536,4608]{1,0:T(8,128)(2,1)} %bitcast.206), kind=kOutput, calls=%fused_computation.297 | convolution fusion | flops 10871635968 | bytes 25952256 | tf_op jit(solution)/shard_map/re,de->rd/dot_general | solution.py:36
  862.4 9.8 add_convert_fusion.3
  898.1 21.7 %collective-permute-done.46 = bf16[768,384]{1,0:T(8,128)(2,1)S(1)} collective-permute-done((bf16[768,384]{1,0:T(8,128)(2,1)}, bf16[768,384]{1,0:T(8,128)(2,1)S(1)}, u32[]{:S(2)}, u32[]{:S(2)}) %collective-permute-start.46) | collective-permute-done | bytes 589856 | tf_op jit(solution)/shard_map/ppermute | solution.py:830
  927.7 12.9 %collective-permute-start.48 = (bf16[576,384]{1,0:T(8,128)(2,1)}, bf16[576,384]{1,0:T(8,128)(2,1)}, u32[]{:S(2)}, u32[]{:S(2)}) collective-permute-start(bf16[576,384]{1,0:T(8,128)(2,1)} %get-tuple-element.222), channel_id=1, source_target_pairs={{0,1},{1,2},{2,3},{3,0},{4,5},{5,6},{6,7},{7,4},{8,9},{9,10},{10,1... | collective-permute-start | bytes 1327112 | tf_op jit(solution)/shard_map/ppermute | solution.py:830
  945.1 7.6 collective-permute-done.48
  952.8 17.9 %collective-permute-done.49 = bf16[576,384]{1,0:T(8,128)(2,1)} collective-permute-done((bf16[576,384]{1,0:T(8,128)(2,1)}, bf16[576,384]{1,0:T(8,128)(2,1)}, u32[]{:S(2)}, u32[]{:S(2)}) %collective-permute-start.49) | collective-permute-done | bytes 442400 | tf_op jit(solution)/shard_map/ppermute | solution.py:830
  984.4 15.2 %collective-permute-start.52 = (bf16[384,1536]{1,0:T(8,128)(2,1)S(1)}, bf16[384,1536]{1,0:T(8,128)(2,1)S(1)}, u32[]{:S(2)}, u32[]{:S(2)}) collective-permute-start(bf16[384,1536]{1,0:T(8,128)(2,1)S(1)} %get-tuple-element.197), channel_id=1, source_target_pairs={{1,0},{5,1},{4,2},{0,3},{3,4},{7,5},{6,6},{2,7},{9,8},{13,9},{12,1... | collective-permute-start | bytes 3538952 | tf_op jit(solution)/shard_map/ppermute | solution.py:857
  999.6 31.4 %collective-permute-done.52 = bf16[384,1536]{1,0:T(8,128)(2,1)S(1)} collective-permute-done((bf16[384,1536]{1,0:T(8,128)(2,1)S(1)}, bf16[384,1536]{1,0:T(8,128)(2,1)S(1)}, u32[]{:S(2)}, u32[]{:S(2)}) %collective-permute-start.52) | collective-permute-done | bytes 1179680 | tf_op jit(solution)/shard_map/ppermute | solution.py:857
  1032.5 16.7 %collective-permute-start.53 = (bf16[576,384]{1,0:T(8,128)(2,1)S(1)}, bf16[576,384]{1,0:T(8,128)(2,1)S(1)}, u32[]{:S(2)}, u32[]{:S(2)}) collective-permute-start(bf16[576,384]{1,0:T(8,128)(2,1)S(1)} %get-tuple-element.219), channel_id=1, source_target_pairs={{0,1},{1,2},{2,3},{3,0},{4,5},{5,6},{6,7},{7,4},{8,9},{9,10},{10,1... | collective-permute-start | bytes 1327112 | tf_op jit(solution)/shard_map/ppermute | solution.py:830
  1052.9 10.5 collective-permute-done.53
  1063.3 15.3 %collective-permute-done.54 = bf16[576,384]{1,0:T(8,128)(2,1)S(1)} collective-permute-done((bf16[576,384]{1,0:T(8,128)(2,1)S(1)}, bf16[576,384]{1,0:T(8,128)(2,1)S(1)}, u32[]{:S(2)}, u32[]{:S(2)}) %collective-permute-start.54) | collective-permute-done | bytes 442400 | tf_op jit(solution)/shard_map/ppermute | solution.py:830
  1093.9 11.0 collective-permute-start.59
  1124.6 8.1 unpack.19
  (494 shorter events, 312.7 us)
Async XLA Ops:
  7.2 148.7 %all-gather.8.cloned.1.call-start = ((), (), s32[]{:S(2)}) async-start(), calls=%async_computation.4 | async-start | bytes 15925248 | tf_op jit(solution)/shard_map/all_gather | solution.py:867
  16.8 40.9 %collective-permute-start.1 = (bf16[64,4608]{1,0:T(8,128)(2,1)S(1)}, bf16[64,4608]{1,0:T(8,128)(2,1)}, u32[]{:S(2)}, u32[]{:S(2)}) collective-permute-start(bf16[64,4608]{1,0:T(8,128)(2,1)S(1)} %pad_maximum_fusion.5), channel_id=1, source_target_pairs={{0,2},{1,3},{2,0},{3,1},{4,6},{5,7},{6,4},{7,5},{8,10},{9,11},{10,... | collective-permute-start | bytes 1769480 | tf_op jit(solution)/shard_map/ppermute | solution.py:830
  19.4 39.3 %collective-permute-start.2 = (bf16[64,4608]{1,0:T(8,128)(2,1)S(1)}, bf16[64,4608]{1,0:T(8,128)(2,1)}, u32[]{:S(2)}, u32[]{:S(2)}) collective-permute-start(bf16[64,4608]{1,0:T(8,128)(2,1)S(1)} %pad_maximum_fusion.5), channel_id=1, source_target_pairs={{0,3},{1,0},{2,1},{3,2},{4,7},{5,4},{6,5},{7,6},{8,11},{9,8},{10,9... | collective-permute-start | bytes 1769480 | tf_op jit(solution)/shard_map/ppermute | solution.py:830
  61.0 236.4 %all-gather.10.cloned.1.call-start = ((), (), s32[]{:S(2)}) async-start(), calls=%async_computation.5 | async-start | bytes 15925248 | tf_op jit(solution)/shard_map/all_gather | solution.py:867
  75.9 21.7 %collective-permute-start.3 = (bf16[384,1536]{1,0:T(8,128)(2,1)}, bf16[384,1536]{1,0:T(8,128)(2,1)S(1)}, u32[]{:S(2)}, u32[]{:S(2)}) collective-permute-start(bf16[384,1536]{1,0:T(8,128)(2,1)} %get-tuple-element.216), channel_id=1, source_target_pairs={{0,0},{1,4},{2,5},{3,1},{4,2},{5,6},{6,7},{7,3},{8,8},{9,12},{10,1... | collective-permute-start | bytes 3538952 | tf_op jit(solution)/shard_map/ppermute | solution.py:844
  77.8 54.5 %collective-permute-start.4 = (bf16[384,1536]{1,0:T(8,128)(2,1)}, bf16[384,1536]{1,0:T(8,128)(2,1)}, u32[]{:S(2)}, u32[]{:S(2)}) collective-permute-start(bf16[384,1536]{1,0:T(8,128)(2,1)} %get-tuple-element.215), channel_id=1, source_target_pairs={{0,1},{1,5},{2,4},{3,0},{4,3},{5,7},{6,6},{7,2},{8,9},{9,13},{10,1... | collective-permute-start | bytes 3538952 | tf_op jit(solution)/shard_map/ppermute | solution.py:845
  132.4 35.7 %collective-permute-start.6 = (bf16[48,4608]{1,0:T(8,128)(2,1)}, bf16[48,4608]{1,0:T(8,128)(2,1)}, u32[]{:S(2)}, u32[]{:S(2)}) collective-permute-start(bf16[48,4608]{1,0:T(8,128)(2,1)} %pad_maximum_fusion.7), channel_id=1, source_target_pairs={{0,1},{1,2},{2,3},{3,0},{4,5},{5,6},{6,7},{7,4},{8,9},{9,10},{10,1... | collective-permute-start | bytes 1327112 | tf_op jit(solution)/shard_map/ppermute | solution.py:830
  132.4 37.1 %collective-permute-start.7 = (bf16[48,4608]{1,0:T(8,128)(2,1)}, bf16[48,4608]{1,0:T(8,128)(2,1)}, u32[]{:S(2)}, u32[]{:S(2)}) collective-permute-start(bf16[48,4608]{1,0:T(8,128)(2,1)} %pad_maximum_fusion.7), channel_id=1, source_target_pairs={{0,2},{1,3},{2,0},{3,1},{4,6},{5,7},{6,4},{7,5},{8,10},{9,11},{10,... | collective-permute-start | bytes 1327112 | tf_op jit(solution)/shard_map/ppermute | solution.py:830
  146.8 23.1 %collective-permute-start.8 = (bf16[48,4608]{1,0:T(8,128)(2,1)}, bf16[48,4608]{1,0:T(8,128)(2,1)}, u32[]{:S(2)}, u32[]{:S(2)}) collective-permute-start(bf16[48,4608]{1,0:T(8,128)(2,1)} %pad_maximum_fusion.7), channel_id=1, source_target_pairs={{0,3},{1,0},{2,1},{3,2},{4,7},{5,4},{6,5},{7,6},{8,11},{9,8},{10,9... | collective-permute-start | bytes 1327112 | tf_op jit(solution)/shard_map/ppermute | solution.py:830
  174.4 232.2 %all-gather.12.cloned.1.call-start = ((), (), s32[]{:S(2)}) async-start(), calls=%async_computation.6 | async-start | bytes 21233664 | tf_op jit(solution)/shard_map/all_gather | solution.py:867
  184.3 43.0 %collective-permute-start.11 = (bf16[768,3072]{1,0:T(8,128)(2,1)}, bf16[768,3072]{1,0:T(8,128)(2,1)}, u32[]{:S(2)}, u32[]{:S(2)}) collective-permute-start(bf16[768,3072]{1,0:T(8,128)(2,1)} %fusion.14.own_k.own_v), channel_id=1, source_target_pairs={{0,4},{4,0},{1,5},{5,1},{2,6},{6,2},{3,7},{7,3},{8,12},{12,8},{9,1... | collective-permute-start | bytes 14155784 | tf_op jit(solution)/shard_map/ppermute | solution.py:953
  220.8 66.4 %collective-permute-start.16 = (bf16[48,6144]{1,0:T(8,128)(2,1)S(1)}, bf16[48,6144]{1,0:T(8,128)(2,1)S(1)}, u32[]{:S(2)}, u32[]{:S(2)}) collective-permute-start(bf16[48,6144]{1,0:T(8,128)(2,1)S(1)} %get-tuple-element.100), channel_id=1, source_target_pairs={{0,1},{1,2},{2,3},{3,0},{4,5},{5,6},{6,7},{7,4},{8,9},{9,10},{10,1... | collective-permute-start | bytes 1769480 | tf_op jit(solution)/shard_map/ppermute | solution.py:830
  224.9 62.3 %collective-permute-start.17 = (bf16[48,6144]{1,0:T(8,128)(2,1)S(1)}, bf16[48,6144]{1,0:T(8,128)(2,1)S(1)}, u32[]{:S(2)}, u32[]{:S(2)}) collective-permute-start(bf16[48,6144]{1,0:T(8,128)(2,1)S(1)} %get-tuple-element.100), channel_id=1, source_target_pairs={{0,2},{1,3},{2,0},{3,1},{4,6},{5,7},{6,4},{7,5},{8,10},{9,11},{10,... | collective-permute-start | bytes 1769480 | tf_op jit(solution)/shard_map/ppermute | solution.py:830
  224.9 62.3 %collective-permute-start.18 = (bf16[48,6144]{1,0:T(8,128)(2,1)S(1)}, bf16[48,6144]{1,0:T(8,128)(2,1)S(1)}, u32[]{:S(2)}, u32[]{:S(2)}) collective-permute-start(bf16[48,6144]{1,0:T(8,128)(2,1)S(1)} %get-tuple-element.100), channel_id=1, source_target_pairs={{0,3},{1,0},{2,1},{3,2},{4,7},{5,4},{6,5},{7,6},{8,11},{9,8},{10,9... | collective-permute-start | bytes 1769480 | tf_op jit(solution)/shard_map/ppermute | solution.py:830
  289.7 198.9 %all-gather.14.cloned.1.call-start = ((), (), s32[]{:S(2)}) async-start(), calls=%async_computation.7 | async-start | bytes 21233664 | tf_op jit(solution)/shard_map/all_gather | solution.py:867
  293.6 42.4 %collective-permute-start.20 = (bf16[192,1536]{1,0:T(8,128)(2,1)}, bf16[192,1536]{1,0:T(8,128)(2,1)}, u32[]{:S(2)}, u32[]{:S(2)}) collective-permute-start(bf16[192,1536]{1,0:T(8,128)(2,1)} %get-tuple-element.104), channel_id=1, source_target_pairs={{0,2},{1,3},{2,0},{3,1},{4,6},{5,7},{6,4},{7,5},{8,10},{9,11},{10,... | collective-permute-start | bytes 1769480 | tf_op jit(solution)/shard_map/ppermute | solution.py:830
  296.2 39.8 %collective-permute-start.21 = (bf16[192,1536]{1,0:T(8,128)(2,1)}, bf16[192,1536]{1,0:T(8,128)(2,1)}, u32[]{:S(2)}, u32[]{:S(2)}) collective-permute-start(bf16[192,1536]{1,0:T(8,128)(2,1)} %get-tuple-element.104), channel_id=1, source_target_pairs={{0,3},{1,0},{2,1},{3,2},{4,7},{5,4},{6,5},{7,6},{8,11},{9,8},{10,9... | collective-permute-start | bytes 1769480 | tf_op jit(solution)/shard_map/ppermute | solution.py:830
  341.8 398.4 %reduce-scatter.5.cloned.1.call-start = ((), (), s32[]{:S(2)}) async-start(), calls=%async_computation.8 | async-start | bytes 11796480 | tf_op jit(solution)/shard_map/reduce_scatter | solution.py:1009
  349.4 32.6 %collective-permute-start.23 = (bf16[384,1536]{1,0:T(8,128)(2,1)S(1)}, bf16[384,1536]{1,0:T(8,128)(2,1)S(1)}, u32[]{:S(2)}, u32[]{:S(2)}) collective-permute-start(bf16[384,1536]{1,0:T(8,128)(2,1)S(1)} %get-tuple-element.209), channel_id=1, source_target_pairs={{0,0},{1,4},{2,5},{3,1},{4,2},{5,6},{6,7},{7,3},{8,8},{9,12},{10,1... | collective-permute-start | bytes 3538952 | tf_op jit(solution)/shard_map/ppermute | solution.py:844
  350.1 55.0 %collective-permute-start.24 = (bf16[384,1536]{1,0:T(8,128)(2,1)S(1)}, bf16[384,1536]{1,0:T(8,128)(2,1)S(1)}, u32[]{:S(2)}, u32[]{:S(2)}) collective-permute-start(bf16[384,1536]{1,0:T(8,128)(2,1)S(1)} %get-tuple-element.210), channel_id=1, source_target_pairs={{0,1},{1,5},{2,4},{3,0},{4,3},{5,7},{6,6},{7,2},{8,9},{9,13},{10,1... | collective-permute-start | bytes 3538952 | tf_op jit(solution)/shard_map/ppermute | solution.py:845
  524.3 34.3 %collective-permute-start.26 = (bf16[768,6144]{1,0:T(8,128)(2,1)}, bf16[768,6144]{1,0:T(8,128)(2,1)}, u32[]{:S(2)}, u32[]{:S(2)}) collective-permute-start(bf16[768,6144]{1,0:T(8,128)(2,1)} %convolution_convert_fusion.2), channel_id=1, source_target_pairs={{0,4},{4,0},{1,5},{5,1},{2,6},{6,2},{3,7},{7,3},{8,12},{12,8},{9,1... | collective-permute-start | bytes 28311560 | tf_op jit(solution)/shard_map/ppermute | solution.py:1004
  527.4 31.2 %collective-permute-start.22 = (bf16[384,1536]{1,0:T(8,128)(2,1)S(1)}, bf16[384,1536]{1,0:T(8,128)(2,1)}, u32[]{:S(2)}, u32[]{:S(2)}) collective-permute-start(bf16[384,1536]{1,0:T(8,128)(2,1)S(1)} %get-tuple-element.211), channel_id=1, source_target_pairs={{0,0},{4,1},{5,2},{1,3},{2,4},{6,5},{7,6},{3,7},{8,8},{12,9},{13,1... | collective-permute-start | bytes 3538952 | tf_op jit(solution)/shard_map/ppermute | solution.py:1032
  572.7 301.5 %reduce-scatter.7.cloned.1.call-start = ((), (), s32[]{:S(2)}) async-start(), calls=%async_computation.9 | async-start | bytes 11796480 | tf_op jit(solution)/shard_map/reduce_scatter | solution.py:1009
  586.3 33.5 %collective-permute-start.27 = (bf16[3072,1536]{1,0:T(8,128)(2,1)}, bf16[3072,1536]{1,0:T(8,128)(2,1)}, u32[]{:S(2)}, u32[]{:S(2)}) collective-permute-start(bf16[3072,1536]{1,0:T(8,128)(2,1)} %convolution_convert_fusion.1), channel_id=1, source_target_pairs={{0,4},{4,0},{1,5},{5,1},{2,6},{6,2},{3,7},{7,3},{8,12},{12,8},{9,1... | collective-permute-start | bytes 28311560 | tf_op jit(solution)/shard_map/ppermute | solution.py:1004
  588.0 31.7 %collective-permute-start.25 = (bf16[384,1536]{1,0:T(8,128)(2,1)}, bf16[384,1536]{1,0:T(8,128)(2,1)}, u32[]{:S(2)}, u32[]{:S(2)}) collective-permute-start(bf16[384,1536]{1,0:T(8,128)(2,1)} %get-tuple-element.111), channel_id=1, source_target_pairs={{1,0},{5,1},{4,2},{0,3},{3,4},{7,5},{6,6},{2,7},{9,8},{13,9},{12,1... | collective-permute-start | bytes 3538952 | tf_op jit(solution)/shard_map/ppermute | solution.py:1042
  633.7 289.9 %reduce-scatter.11.cloned.1.call-start = ((), (), s32[]{:S(2)}) async-start(), calls=%async_computation.11 | async-start | bytes 10321920 | tf_op jit(solution)/shard_map/reduce_scatter | solution.py:1009
  652.9 27.7 %collective-permute-start.28 = (bf16[768,1536]{1,0:T(8,128)(2,1)}, bf16[768,1536]{1,0:T(8,128)(2,1)}, u32[]{:S(2)}, u32[]{:S(2)}) collective-permute-start(bf16[768,1536]{1,0:T(8,128)(2,1)} %convolution_convert_fusion.5), channel_id=1, source_target_pairs={{0,4},{4,0},{1,5},{5,1},{2,6},{6,2},{3,7},{7,3},{8,12},{12,8},{9,1... | collective-permute-start | bytes 7077896 | tf_op jit(solution)/shard_map/ppermute | solution.py:1004
  672.5 32.0 %collective-permute-start.33 = (bf16[64,1536]{1,0:T(8,128)(2,1)S(1)}, bf16[64,1536]{1,0:T(8,128)(2,1)S(1)}, u32[]{:S(2)}, u32[]{:S(2)}) collective-permute-start(bf16[64,1536]{1,0:T(8,128)(2,1)S(1)} %get-tuple-element.181), channel_id=1, source_target_pairs={{0,2},{1,3},{2,0},{3,1},{4,6},{5,7},{6,4},{7,5},{8,10},{9,11},{10,... | collective-permute-start | bytes 589832 | tf_op jit(solution)/shard_map/ppermute | solution.py:830
  674.3 30.3 %collective-permute-start.34 = (bf16[64,1536]{1,0:T(8,128)(2,1)S(1)}, bf16[64,1536]{1,0:T(8,128)(2,1)S(1)}, u32[]{:S(2)}, u32[]{:S(2)}) collective-permute-start(bf16[64,1536]{1,0:T(8,128)(2,1)S(1)} %get-tuple-element.181), channel_id=1, source_target_pairs={{0,3},{1,0},{2,1},{3,2},{4,7},{5,4},{6,5},{7,6},{8,11},{9,8},{10,9... | collective-permute-start | bytes 589832 | tf_op jit(solution)/shard_map/ppermute | solution.py:830
  689.1 25.0 %collective-permute-start.29 = (bf16[768,1536]{1,0:T(8,128)(2,1)}, bf16[768,1536]{1,0:T(8,128)(2,1)}, u32[]{:S(2)}, u32[]{:S(2)}) collective-permute-start(bf16[768,1536]{1,0:T(8,128)(2,1)} %convolution_convert_fusion.4), channel_id=1, source_target_pairs={{0,4},{4,0},{1,5},{5,1},{2,6},{6,2},{3,7},{7,3},{8,12},{12,8},{9,1... | collective-permute-start | bytes 7077896 | tf_op jit(solution)/shard_map/ppermute | solution.py:1004
  723.7 307.4 %reduce-scatter.9.cloned.1.call-start = ((), (), s32[]{:S(2)}) async-start(), calls=%async_computation.10 | async-start | bytes 8847360 | tf_op jit(solution)/shard_map/reduce_scatter | solution.py:1009
  735.4 88.2 %collective-permute-start.37 = (bf16[2,64,384]{2,1,0:T(8,128)(2,1)S(1)}, bf16[2,64,384]{2,1,0:T(8,128)(2,1)}, u32[]{:S(2)}, u32[]{:S(2)}) collective-permute-start(bf16[2,64,384]{2,1,0:T(8,128)(2,1)S(1)} %fusion.94), channel_id=1, source_target_pairs={{0,2},{1,3},{2,0},{3,1},{4,6},{5,7},{6,4},{7,5},{8,10},{9,11},{10,... | collective-permute-start | bytes 294920 | tf_op jit(solution)/shard_map/ppermute | solution.py:830
  737.3 86.3 %collective-permute-start.38 = (bf16[2,64,384]{2,1,0:T(8,128)(2,1)S(1)}, bf16[2,64,384]{2,1,0:T(8,128)(2,1)}, u32[]{:S(2)}, u32[]{:S(2)}) collective-permute-start(bf16[2,64,384]{2,1,0:T(8,128)(2,1)S(1)} %fusion.94), channel_id=1, source_target_pairs={{0,3},{1,0},{2,1},{3,2},{4,7},{5,4},{6,5},{7,6},{8,11},{9,8},{10,9... | collective-permute-start | bytes 294920 | tf_op jit(solution)/shard_map/ppermute | solution.py:830
  741.7 81.9 %collective-permute-start.39 = (bf16[192,1536]{1,0:T(8,128)(2,1)S(1)}, bf16[192,1536]{1,0:T(8,128)(2,1)S(1)}, u32[]{:S(2)}, u32[]{:S(2)}) collective-permute-start(bf16[192,1536]{1,0:T(8,128)(2,1)S(1)} %get-tuple-element.204), channel_id=1, source_target_pairs={{0,1},{1,2},{2,3},{3,0},{4,5},{5,6},{6,7},{7,4},{8,9},{9,10},{10,1... | collective-permute-start | bytes 1769480 | tf_op jit(solution)/shard_map/ppermute | solution.py:830
  741.7 81.9 %collective-permute-start.40 = (bf16[192,1536]{1,0:T(8,128)(2,1)S(1)}, bf16[192,1536]{1,0:T(8,128)(2,1)}, u32[]{:S(2)}, u32[]{:S(2)}) collective-permute-start(bf16[192,1536]{1,0:T(8,128)(2,1)S(1)} %get-tuple-element.203), channel_id=1, source_target_pairs={{0,2},{1,3},{2,0},{3,1},{4,6},{5,7},{6,4},{7,5},{8,10},{9,11},{10,... | collective-permute-start | bytes 1769480 | tf_op jit(solution)/shard_map/ppermute | solution.py:830
  742.3 81.3 %collective-permute-start.41 = (bf16[192,1536]{1,0:T(8,128)(2,1)S(1)}, bf16[192,1536]{1,0:T(8,128)(2,1)}, u32[]{:S(2)}, u32[]{:S(2)}) collective-permute-start(bf16[192,1536]{1,0:T(8,128)(2,1)S(1)} %get-tuple-element.202), channel_id=1, source_target_pairs={{0,3},{1,0},{2,1},{3,2},{4,7},{5,4},{6,5},{7,6},{8,11},{9,8},{10,9... | collective-permute-start | bytes 1769480 | tf_op jit(solution)/shard_map/ppermute | solution.py:830
  872.2 208.5 %all-gather.18.cloned.1.call-start = ((), (), s32[]{:S(2)}) async-start(), calls=%async_computation.13 | async-start | bytes 17252352 | tf_op jit(solution)/shard_map/all_gather | solution.py:1180
  876.8 21.3 %collective-permute-start.45 = (bf16[768,384]{1,0:T(8,128)(2,1)}, bf16[768,384]{1,0:T(8,128)(2,1)S(1)}, u32[]{:S(2)}, u32[]{:S(2)}) collective-permute-start(bf16[768,384]{1,0:T(8,128)(2,1)} %get-tuple-element.201), channel_id=1, source_target_pairs={{0,1},{1,2},{2,3},{3,0},{4,5},{5,6},{6,7},{7,4},{8,9},{9,10},{10,1... | collective-permute-start | bytes 1769480 | tf_op jit(solution)/shard_map/ppermute | solution.py:830
  877.7 42.2 %collective-permute-start.46 = (bf16[768,384]{1,0:T(8,128)(2,1)}, bf16[768,384]{1,0:T(8,128)(2,1)S(1)}, u32[]{:S(2)}, u32[]{:S(2)}) collective-permute-start(bf16[768,384]{1,0:T(8,128)(2,1)} %get-tuple-element.200), channel_id=1, source_target_pairs={{0,2},{1,3},{2,0},{3,1},{4,6},{5,7},{6,4},{7,5},{8,10},{9,11},{10,... | collective-permute-start | bytes 1769480 | tf_op jit(solution)/shard_map/ppermute | solution.py:830
  880.3 39.6 %collective-permute-start.47 = (bf16[768,384]{1,0:T(8,128)(2,1)S(1)}, bf16[768,384]{1,0:T(8,128)(2,1)}, u32[]{:S(2)}, u32[]{:S(2)}) collective-permute-start(bf16[768,384]{1,0:T(8,128)(2,1)S(1)} %get-tuple-element.199), channel_id=1, source_target_pairs={{0,3},{1,0},{2,1},{3,2},{4,7},{5,4},{6,5},{7,6},{8,11},{9,8},{10,9... | collective-permute-start | bytes 1769480 | tf_op jit(solution)/shard_map/ppermute | solution.py:830
  927.7 25.1 %collective-permute-start.48 = (bf16[576,384]{1,0:T(8,128)(2,1)}, bf16[576,384]{1,0:T(8,128)(2,1)}, u32[]{:S(2)}, u32[]{:S(2)}) collective-permute-start(bf16[576,384]{1,0:T(8,128)(2,1)} %get-tuple-element.222), channel_id=1, source_target_pairs={{0,1},{1,2},{2,3},{3,0},{4,5},{5,6},{6,7},{7,4},{8,9},{9,10},{10,1... | collective-permute-start | bytes 1327112 | tf_op jit(solution)/shard_map/ppermute | solution.py:830
  940.6 30.1 %collective-permute-start.49 = (bf16[576,384]{1,0:T(8,128)(2,1)}, bf16[576,384]{1,0:T(8,128)(2,1)}, u32[]{:S(2)}, u32[]{:S(2)}) collective-permute-start(bf16[576,384]{1,0:T(8,128)(2,1)} %get-tuple-element.221), channel_id=1, source_target_pairs={{0,2},{1,3},{2,0},{3,1},{4,6},{5,7},{6,4},{7,5},{8,10},{9,11},{10,... | collective-permute-start | bytes 1327112 | tf_op jit(solution)/shard_map/ppermute | solution.py:830
  941.9 28.8 %collective-permute-start.50 = (bf16[576,384]{1,0:T(8,128)(2,1)}, bf16[576,384]{1,0:T(8,128)(2,1)}, u32[]{:S(2)}, u32[]{:S(2)}) collective-permute-start(bf16[576,384]{1,0:T(8,128)(2,1)} %get-tuple-element.220), channel_id=1, source_target_pairs={{0,3},{1,0},{2,1},{3,2},{4,7},{5,4},{6,5},{7,6},{8,11},{9,8},{10,9... | collective-permute-start | bytes 1327112 | tf_op jit(solution)/shard_map/ppermute | solution.py:830
  973.1 170.4 %all-gather.16.cloned.1.call-start = ((), (), s32[]{:S(2)}) async-start(), calls=%async_computation.12 | async-start | bytes 3981312 | tf_op jit(solution)/shard_map/all_gather | solution.py:1194
  984.4 46.6 %collective-permute-start.52 = (bf16[384,1536]{1,0:T(8,128)(2,1)S(1)}, bf16[384,1536]{1,0:T(8,128)(2,1)S(1)}, u32[]{:S(2)}, u32[]{:S(2)}) collective-permute-start(bf16[384,1536]{1,0:T(8,128)(2,1)S(1)} %get-tuple-element.197), channel_id=1, source_target_pairs={{1,0},{5,1},{4,2},{0,3},{3,4},{7,5},{6,6},{2,7},{9,8},{13,9},{12,1... | collective-permute-start | bytes 3538952 | tf_op jit(solution)/shard_map/ppermute | solution.py:857
  1032.5 30.8 %collective-permute-start.53 = (bf16[576,384]{1,0:T(8,128)(2,1)S(1)}, bf16[576,384]{1,0:T(8,128)(2,1)S(1)}, u32[]{:S(2)}, u32[]{:S(2)}) collective-permute-start(bf16[576,384]{1,0:T(8,128)(2,1)S(1)} %get-tuple-element.219), channel_id=1, source_target_pairs={{0,1},{1,2},{2,3},{3,0},{4,5},{5,6},{6,7},{7,4},{8,9},{9,10},{10,1... | collective-permute-start | bytes 1327112 | tf_op jit(solution)/shard_map/ppermute | solution.py:830
  1049.2 29.4 %collective-permute-start.54 = (bf16[576,384]{1,0:T(8,128)(2,1)S(1)}, bf16[576,384]{1,0:T(8,128)(2,1)S(1)}, u32[]{:S(2)}, u32[]{:S(2)}) collective-permute-start(bf16[576,384]{1,0:T(8,128)(2,1)S(1)} %get-tuple-element.218), channel_id=1, source_target_pairs={{0,2},{1,3},{2,0},{3,1},{4,6},{5,7},{6,4},{7,5},{8,10},{9,11},{10,... | collective-permute-start | bytes 1327112 | tf_op jit(solution)/shard_map/ppermute | solution.py:830
  1052.6 26.0 %collective-permute-start.55 = (bf16[576,384]{1,0:T(8,128)(2,1)S(1)}, bf16[576,384]{1,0:T(8,128)(2,1)S(1)}, u32[]{:S(2)}, u32[]{:S(2)}) collective-permute-start(bf16[576,384]{1,0:T(8,128)(2,1)S(1)} %get-tuple-element.217), channel_id=1, source_target_pairs={{0,3},{1,0},{2,1},{3,2},{4,7},{5,4},{6,5},{7,6},{8,11},{9,8},{10,9... | collective-permute-start | bytes 1327112 | tf_op jit(solution)/shard_map/ppermute | solution.py:830
  (108 other events, 1865.7 us)
Sparse Core Ops, SparseCore 0:
  61.2 90.6 all-gather.7
  174.5 90.3 all-gather.9
  289.9 97.6 all-gather.11
  389.9 98.7 all-gather.13
  572.8 95.8 reduce-scatter.4
  672.2 95.0 reduce-scatter.6
  771.1 85.3 reduce-scatter.10
  872.3 76.9 reduce-scatter.8
  973.2 91.9 all-gather.17
  1080.8 43.5 all-gather.15

commit v7 on v6

--- a/solution.py
+++ b/solution.py
@@ -749,6 +749,40 @@
     )(full)
 
 
+def unpack_late_kernel(seat, one_ref, two_ref, out_ref):
+    pieces = jnp.concatenate([one_ref[0], two_ref[0]], axis=0)
+    out_ref[...] = pieces.T.astype(jnp.float32)
+
+
+def unpack_late(seat, full, rows, out_shape, which):
+    features = full.shape[2]
+    wide = out_shape[1] // (2 * rows)
+    parts = full.shape[1] // rows
+
+    def part_block(side):
+        def at(j, seat):
+            part = 2 * (which * wide + j) + side
+            return (part // parts) ^ seat[0], part % parts, 0
+
+        return pl.BlockSpec((1, rows, features), at)
+
+    return pl.pallas_call(
+        unpack_late_kernel,
+        out_shape=jax.ShapeDtypeStruct(out_shape, jnp.float32),
+        grid_spec=pltpu.PrefetchScalarGridSpec(
+            num_scalar_prefetch=1,
+            grid=(wide,),
+            in_specs=[part_block(0), part_block(1)],
+            out_specs=pl.BlockSpec((features, 2 * rows), lambda j, seat: (0, j)),
+        ),
+        compiler_params=pltpu.CompilerParams(vmem_limit_bytes=32 * 2**20),
+        cost_estimate=pl.CostEstimate(
+            flops=0, bytes_accessed=6 * out_shape[0] * out_shape[1], transcendentals=0
+        ),
+        name="unpack_late",
+    )(seat, full, full)
+
+
 def held(values, *others):
     return list(lax.optimization_barrier((*values, *others))[: len(values)])
 
@@ -889,14 +923,16 @@
     norms = line_up(vectors[0], [values[share] for values in qkv_came])
     norms = norms[:, : 6 * block].reshape(shards, 6, block).transpose(1, 0, 2)
     norms = norms.reshape(6, width).astype(jnp.float32)
-    came = to_chip(after(frames, *qkv_came))
-    x_low = by_time(*came)
     rest_share = jnp.concatenate(
         [share_of(self_output_weight), share_of(cross_query_weight), share_of(cross_output_weight)],
         axis=1,
     )
-    rest_came = hops(after(rest_share, *came))
+    rest_came = hops(after(rest_share, *qkv_came))
+    rest = from_replicas(line_up(rest_share, rest_came))
+    came = to_chip(after(frames, *rest_came))
+    x_low = by_time(*came)
     expand_share = share_of(feed_up_weight)
+    expand_came = hops(after(expand_share, *came))
 
     facts = jnp.concatenate(
         [(clip_lengths // 64)[:, None], (clip_lengths % 64)[:, None], slot_used[:, None], text_mask],
@@ -952,12 +988,17 @@
     kv = project(after(hidden_one, count), qkv_matrix[:, width:]).astype(jnp.bfloat16)
     kv_other = lax.ppermute(kv, "core", swap)
     queries = project(after(hidden_one, kv), qkv_matrix[:, :width]).astype(jnp.bfloat16)
-    rest_came = held(rest_came, kv)
-    rest = from_replicas(line_up(rest_share, rest_came))
+    expand_came = held(expand_came, kv_other, queries)
+    expand_matrix = from_replicas(line_up(expand_share, expand_came))
+    reduce_share = share_of(feed_down_weight)
+    reduce_came = hops(after(reduce_share, *expand_came))
     output_matrix = rest[:, :width]
     probe_matrix = rest[:, width : 2 * width]
     merge_matrix = rest[:, 2 * width :]
-    text_came = held(text_came, queries)
+    mixed_self, lse = self_attend(after(places, *expand_came), queries, kv, kv_other)
+    reduce_came = held(reduce_came, mixed_self)
+    reduce_matrix = from_replicas(line_up(reduce_share, reduce_came))
+    text_came = held(text_came, mixed_self)
     text_half = lax.dynamic_index_in_dim(text_part, shard, 0, keepdims=False).astype(jnp.float32)
     for values in text_came:
         text_half += values.astype(jnp.float32)
@@ -965,19 +1006,12 @@
     text_swap = lax.ppermute(text_half, "core", swap)
     lookups = jnp.where(first_core, text_half, text_swap)
     contents = jnp.where(first_core, text_swap, text_half)
-    expand_came = hops(after(expand_share, *rest_came, *text_came))
-    mixed_self, lse = self_attend(after(places, rest_came[0]), queries, kv, kv_other)
-    expand_came = held(expand_came, mixed_self)
-    expand_matrix = from_replicas(line_up(expand_share, expand_came))
-    reduce_share = share_of(feed_down_weight)
-    reduce_came = hops(after(reduce_share, *expand_came))
     after_self = inputs + project(mixed_self, output_matrix)
     parts_two = norm_parts(after_self)
     hidden_two = ((after_self - parts_two[0]) * parts_two[1] * norms[2] + norms[3]).astype(
         jnp.bfloat16
     )
     probes = project(hidden_two, probe_matrix).astype(jnp.bfloat16)
-    reduce_matrix = from_replicas(line_up(reduce_share, held(reduce_came, probes)))
     teacher_low = by_time(*to_chip(after(teacher, *reduce_came, probes)))
     cross_mixed = cross_attend(probes, lookups, contents, present)
     after_cross = after_self + project(cross_mixed, merge_matrix)
@@ -1027,17 +1061,14 @@
             total += part.astype(jnp.float32)
         return total.astype(jnp.bfloat16)
 
-    down_theirs = theirs_of(grad_feed_low, activated_low)
+    down_ours = outer_sum(grad_feed_low, activated_low).astype(jnp.bfloat16)
+    down_sum = lax.psum_scatter(down_ours, REPLICAS, scatter_dimension=0, tiled=True)
     to_send = outgoing(result.astype(jnp.bfloat16))
     output_one = lax.ppermute(to_send[0], spot, back[0])
-    grad_activated = back_project(after(grad_feed_low, down_theirs), reduce_matrix)
+    grad_activated = back_project(after(grad_feed_low, down_ours), reduce_matrix)
     grad_upward = gelu_pull(grad_activated)[0].astype(jnp.bfloat16)
     output_one = after(output_one, grad_upward)
-    down_ours = ours_of(
-        after(grad_feed_low, grad_upward, output_one), activated_low, down_theirs
-    )
-    down_sum = over_outer(down_ours)
-    up_theirs = theirs_of(after(grad_upward, down_ours), hidden_three)
+    up_theirs = theirs_of(after(grad_upward, output_one), hidden_three)
     grad_hidden_three = back_project(after(grad_upward, up_theirs), expand_matrix)
     output_two = lax.ppermute(after(to_send[1], output_one), spot, back[1])
     output_two = after(output_two, grad_hidden_three)
@@ -1139,13 +1170,12 @@
     )
     middle_kept = after(middle_sum[: middle_rows - text_split], qkv_ours, *up_came)
     middle_came = shard_hops(middle_kept)
+    late_came = shard_hops(after(qkv_sum, *middle_came))
     frames_came = from_chip(
-        after((grad_after_self + grad_norm).astype(jnp.bfloat16), *middle_came)
+        after((grad_after_self + grad_norm).astype(jnp.bfloat16), *late_came)
     )
     frames_grad = by_slot(*frames_came).astype(jnp.float32)
 
-    qkv_sum = after(qkv_sum, *frames_came)
-    late_came = shard_hops(qkv_sum)
     small = jnp.stack(
         [
             gain_self,
@@ -1158,7 +1188,6 @@
             jnp.zeros((width,), jnp.float32),
         ]
     )
-    small = after(small, *late_came)
     for axis, pairs in (
         ("core", swap),
         ("x", swap),
@@ -1191,9 +1220,16 @@
     probe_grad = unpack(early, piece, at + 1, square, 0, 2)
     merge_grad = unpack(early, piece, at + 2, square, 0, 2)
     late = over_shard(qkv_sum, late_came)
-    late = lax.all_gather(after(late, early), REPLICAS, axis=0, tiled=True)
-    late = late.reshape(-1, block, block)
-    qkv_grad = [unpack(late, block, 0, square, 2 * i, 2) for i in range(3)]
+    late_x = lax.ppermute(late, "x", swap)
+    late_y = lax.ppermute(late, "y", swap)
+    cut = late.shape[0] // 2
+    late_one = lax.ppermute(late_x[:cut], "y", swap)
+    late_two = lax.ppermute(late_y[cut:], "x", swap)
+    late = jnp.concatenate([late, late_x, late_y, late_one, late_two], axis=0)
+    late = jnp.concatenate([late, lax.ppermute(late, "core", swap)], axis=0)
+    late = late.reshape(replicas, -1, block)
+    seat = (4 * core + outer).astype(jnp.int32).reshape(1)
+    qkv_grad = [unpack_late(seat, late, piece, square, i) for i in range(3)]
     return (
         output,
         loss,

time: 1170 us -> 1180 us (level)
  waiting for transfers between devices: 270 us -> 296 us
  starting transfers between devices: 202 us -> 187 us
    ppermute x33, waiting for transfers between devices: 140 us -> 179 us  [hop(): return lax.ppermute(values, 'shard', pairs)]
    ppermute x2, waiting for transfers between devices: 31.4 us -> 0.01 us  [from_chip(): return (lax.ppermute(one, spot, back[0]), lax.ppermute(two, spot, back[1]))]
    all_gather x4, waiting for transfers between devices: 21 us -> 0.03 us  [from_replicas(): full = lax.all_gather(line, ('y', 'x', 'core'), axis=1, tiled=True)]
    ppermute x5, waiting for transfers between devices: 4.82 us -> 23.5 us  [clip_body(): small += lax.ppermute(small, axis, pairs)]
    ppermute x33, starting transfers between devices: 108 us -> 94.1 us  [hop(): return lax.ppermute(values, 'shard', pairs)]
    ppermute x6 -> x5, starting transfers between devices: 2.66 us -> 15.3 us  [ours_of(): sent = lax.ppermute(theirs, 'core', swap)]
    unnamed x179 -> x219, local copies, waits for them, and re-layouts: 35.5 us -> 47.3 us
    dot_general x13 -> x12, matrix products: 90.5 us -> 82.5 us  [outer_sum(): jnp.einsum('rd,re->de', left, right, preferred_element_type=jnp.float32)]
  transfers between devices with their start and end apart: 71 -> 74, of which waited for: 27 -> 29; matrix products, arithmetic and copies ran while one was open for 35% -> 34% of each run, Pallas kernels for 15% -> 13%
where the time goes in v7:
time: 1180 us; the launch traced here: 1170 us
  matrix products  305 us (26%)
  waiting for transfers between devices  296 us (25%)
  starting transfers between devices  187 us (16%)
  Pallas kernels  175 us (15%)
  local copies, waits for them, and re-layouts  100 us (8%)
  other arithmetic  81.9 us (7%)
  between operations  21.7 us (2%)
    ppermute x33, waiting for transfers between devices, hop(): return lax.ppermute(values, 'shard', pairs)  179 us
    dot_general x8, matrix products, project(): return jnp.dot(left, right, preferred_element_type=jnp.float32)  123 us
    dot_general x7, matrix products, back_project(): jnp.einsum('re,de->rd', grads, matrix, preferred_element_type=jnp.float32)  99.2 us
    ppermute x33, starting transfers between devices, hop(): return lax.ppermute(values, 'shard', pairs)  94.1 us
    dot_general x12, matrix products, outer_sum(): jnp.einsum('rd,re->de', left, right, preferred_element_type=jnp.float32)  82.5 us
    pallas_call x1, Pallas kernels, self_attend_back(): pl.pallas_call(self_backward_kernel, out_shape=(jax.ShapeDtypeStruct((row...  69.8 us
    ppermute x2, waiting for transfers between devices, to_chip(): two = lax.ppermute(jnp.where(lower, pair[1], pair[0]), spot, there[1])  66.2 us
    pallas_call x1, Pallas kernels, self_attend(): pl.pallas_call(self_forward_kernel, out_shape=(jax.ShapeDtypeStruct((rows...  58.5 us
  transfers between devices with their start and end apart: 74, of which 29 were waited for; matrix products, arithmetic and copies ran while one was open for 34% of the time, Pallas kernels for 13%

profile of v7, /device:TPU:0, one launch (start us, length us, event | category | flops | bytes accessed | tf_op | source)
XLA Modules:
  0.0 1166.0 jit_solution(15486383960367107680)
XLA Ops:
  20.9 12.3 %collective-permute-done = bf16[64,4608]{1,0:T(8,128)(2,1)} collective-permute-done((bf16[64,4608]{1,0:T(8,128)(2,1)S(1)}, bf16[64,4608]{1,0:T(8,128)(2,1)}, u32[]{:S(2)}, u32[]{:S(2)}) %collective-permute-start) | collective-permute-done | bytes 589856 | tf_op jit(solution)/shard_map/ppermute | solution.py:864
  34.2 23.4 %collective-permute-done.1 = bf16[64,4608]{1,0:T(8,128)(2,1)} collective-permute-done((bf16[64,4608]{1,0:T(8,128)(2,1)S(1)}, bf16[64,4608]{1,0:T(8,128)(2,1)}, u32[]{:S(2)}, u32[]{:S(2)}) %collective-permute-start.1) | collective-permute-done | bytes 589856 | tf_op jit(solution)/shard_map/ppermute | solution.py:864
  62.2 12.0 %collective-permute-start.3 = (bf16[48,4608]{1,0:T(8,128)(2,1)S(1)}, bf16[48,4608]{1,0:T(8,128)(2,1)S(1)}, u32[]{:S(2)}, u32[]{:S(2)}) collective-permute-start(bf16[48,4608]{1,0:T(8,128)(2,1)S(1)} %pad_maximum_fusion.7), channel_id=1, source_target_pairs={{0,1},{1,2},{2,3},{3,0},{4,5},{5,6},{6,7},{7,4},{8,9},{9,10},{10,1... | collective-permute-start | bytes 1327112 | tf_op jit(solution)/shard_map/ppermute | solution.py:864
  77.2 10.4 collective-permute-done.3
  87.7 17.1 %collective-permute-done.4 = bf16[48,4608]{1,0:T(8,128)(2,1)S(1)} collective-permute-done((bf16[48,4608]{1,0:T(8,128)(2,1)S(1)}, bf16[48,4608]{1,0:T(8,128)(2,1)S(1)}, u32[]{:S(2)}, u32[]{:S(2)}) %collective-permute-start.4) | collective-permute-done | bytes 442400 | tf_op jit(solution)/shard_map/ppermute | solution.py:864
  123.1 11.1 collective-permute-start.7
  139.1 35.3 %collective-permute-done.7 = bf16[384,1536]{1,0:T(8,128)(2,1)} collective-permute-done((bf16[384,1536]{1,0:T(8,128)(2,1)S(1)}, bf16[384,1536]{1,0:T(8,128)(2,1)}, u32[]{:S(2)}, u32[]{:S(2)}) %collective-permute-start.7) | collective-permute-done | bytes 1179680 | tf_op jit(solution)/shard_map/ppermute | solution.py:879
  179.0 10.8 fusion.14.own_k.own_v
  189.8 11.5 collective-permute-start.14
  205.1 8.3 fusion.64.q_ref
  213.5 15.7 %collective-permute-done.10 = bf16[48,6144]{1,0:T(8,128)(2,1)S(1)} collective-permute-done((bf16[48,6144]{1,0:T(8,128)(2,1)S(1)}, bf16[48,6144]{1,0:T(8,128)(2,1)S(1)}, u32[]{:S(2)}, u32[]{:S(2)}) %collective-permute-start.10) | collective-permute-done | bytes 589856 | tf_op jit(solution)/shard_map/ppermute | solution.py:864
  229.2 14.7 %collective-permute-done.11 = bf16[48,6144]{1,0:T(8,128)(2,1)S(1)} collective-permute-done((bf16[48,6144]{1,0:T(8,128)(2,1)S(1)}, bf16[48,6144]{1,0:T(8,128)(2,1)S(1)}, u32[]{:S(2)}, u32[]{:S(2)}) %collective-permute-start.11) | collective-permute-done | bytes 589856 | tf_op jit(solution)/shard_map/ppermute | solution.py:864
  253.4 10.8 collective-permute-start.19
  274.8 58.5 %self_attend.1 = (bf16[768,1536]{1,0:T(8,128)(2,1)S(1)}, f32[96,768]{1,0:T(8,128)S(1)}) custom-call(s32[5]{0:T(128)S(1)} %stack.66.place, bf16[768,1536]{1,0:T(8,128)(2,1)S(1)} %copy-done.27, bf16[768,3072]{1,0:T(8,128)(2,1)S(1)} %copy-done.19, bf16[768,3072]{1,0:T(8,128)(2,1)S(1)} %copy-done.19, bf16[768,3072]{1,0:T(8,128)(2,1)S(1)} %copy-done.21, ...), custom_call_target="tpu_custom_call" | custom-call | flops 7247757312 | bytes 18874368 | tf_op jit(solution)/shard_map/self_attend/pallas_call | solution.py:569
  350.5 7.0 collective-permute-done.16
  359.4 7.1 fusion.125
  374.9 6.8 cross_attend.1
  382.7 8.3 collective-permute-start.24
  399.6 30.9 %collective-permute-done.24 = bf16[384,1536]{1,0:T(8,128)(2,1)S(1)} collective-permute-done((bf16[384,1536]{1,0:T(8,128)(2,1)S(1)}, bf16[384,1536]{1,0:T(8,128)(2,1)S(1)}, u32[]{:S(2)}, u32[]{:S(2)}) %collective-permute-start.24) | collective-permute-done | bytes 1179680 | tf_op jit(solution)/shard_map/ppermute | solution.py:879
  432.1 61.2 %multiply_convert_fusion = (bf16[768,6144]{1,0:T(8,128)(2,1)}, f32[768,6144]{1,0:T(8,128)}, f32[768,6144]{1,0:T(8,128)}) fusion(bf16[1536,6144]{1,0:T(8,128)(2,1)} %bitcast.198, f32[768,1536]{1,0:T(8,128)} %get-tuple-element.236, f32[1536]{0:T(1024)S(1)} %add.426, f32[1536]{0:T(1024)S(1)} %mul.315, f32[768]{0:T(1024)S(1)} %add_rsqrt_fusion, ...), kind=kOutput, calls=%fused_computation.5 | convolution fusion | flops 14808121344 | bytes 70797312 | tf_op jit(solution)/shard_map/dot_general | solution.py:28
  493.4 25.3 %multiply_convert_fusion.1 = (bf16[768,1536]{1,0:T(8,128)(2,1)S(1)}, bf16[768,1536]{1,0:T(8,128)(2,1)}, f32[768,1536]{1,0:T(8,128)}) fusion(f32[]{:T(128)S(6)} %div.75, f32[768]{0:T(1024)S(1)} %copy-done.84, bf16[384,1536]{1,0:T(8,128)(2,1)S(1)} %copy-done.43, bf16[384,1536]{1,0:T(8,128)(2,1)S(1)} %copy-done.41, f32[768,1536]{1,0:T(8,128)} %get-tuple-element.236, ...), kind=kOutput, calls=%fused_computation.65 | convolution fusion | flops 14507311104 | bytes 44829700 | tf_op jit(solution)/shard_map/dot_general | solution.py:28
  520.0 17.8 %convolution_convert_fusion = bf16[1536,6144]{1,0:T(8,128)(2,1)} fusion(bf16[768,1536]{1,0:T(8,128)(2,1)S(1)} %get-tuple-element.100, bf16[768,6144]{1,0:T(8,128)(2,1)S(1)} %copy-done.89), kind=kOutput, calls=%fused_computation.1 | convolution fusion | flops 14504951808 | bytes 30670848 | tf_op jit(solution)/shard_map/rd,re->de/dot_general | solution.py:32
  541.4 35.8 %add_convert_fusion.1 = bf16[768,6144]{1,0:T(8,128)(2,1)} fusion(f32[768,6144]{1,0:T(8,128)} %get-tuple-element.179, f32[768,6144]{1,0:T(8,128)} %get-tuple-element.237, bf16[768,1536]{1,0:T(8,128)(2,1)} %copy-done.90, bf16[6144,1536]{1,0:T(8,128)(2,1)} %bitcast.201), kind=kOutput, calls=%fused_computation.4 | convolution fusion | flops 14561574912 | bytes 68419584 | tf_op jit(solution)/shard_map/re,de->rd/dot_general | solution.py:36
  577.2 13.9 %convolution_convert_fusion.2 = bf16[3072,1536]{1,0:T(8,128)(2,1)} fusion(bf16[768,6144]{1,0:T(8,128)(2,1)} %add_convert_fusion.1, s32[]{:T(128)S(6)} %select_n.329, f32[768,1536]{1,0:T(8,128)} %get-tuple-element.236, f32[1536]{0:T(1024)S(1)} %add.426, f32[1536]{0:T(1024)S(1)} %mul.315, f32[768]{0:T(1024)S(1)} %add_rsqrt_fusion, ...), kind=kOutput, calls=%fused_computation.21 | convolution fusion | flops 7258374144 | bytes 18892804 | tf_op jit(solution)/shard_map/rd,re->de/dot_general | solution.py:32
  591.2 13.2 %collective-permute-start.26 = (bf16[3072,1536]{1,0:T(8,128)(2,1)}, bf16[3072,1536]{1,0:T(8,128)(2,1)}, u32[]{:S(2)}, u32[]{:S(2)}) collective-permute-start(bf16[3072,1536]{1,0:T(8,128)(2,1)} %convolution_convert_fusion.2), channel_id=1, source_target_pairs={{0,4},{4,0},{1,5},{5,1},{2,6},{6,2},{3,7},{7,3},{8,12},{12,8},{9,1... | collective-permute-start | bytes 28311560 | tf_op jit(solution)/shard_map/ppermute | solution.py:1038
  606.8 22.1 %fusion.127 = f32[768,1536]{1,0:T(8,128)} fusion(bf16[768,6144]{1,0:T(8,128)(2,1)} %add_convert_fusion.1, bf16[1536,6144]{1,0:T(8,128)(2,1)} %bitcast.199), kind=kOutput, calls=%fused_computation.301 | convolution fusion | flops 14495514624 | bytes 33030144 | tf_op jit(solution)/shard_map/re,de->rd/dot_general | solution.py:36
  634.4 14.0 %add_convert_fusion = bf16[3072,1536]{1,0:T(8,128)(2,1)} fusion(bf16[3072,1536]{1,0:T(8,128)(2,1)} %collective-permute-done.26, bf16[768,6144]{1,0:T(8,128)(2,1)S(1)} %bitcast.214, s32[]{:T(128)S(6)} %select_n.332, f32[768,1536]{1,0:T(8,128)} %get-tuple-element.236, f32[1536]{0:T(1024)S(1)} %add.426, f32[1536]{0:T(1024)S(1)} %mul.315, ...), kind=kOutput, calls=%fused_computation.3 | convolution fusion | flops 7267811328 | bytes 28336132 | tf_op jit(solution)/shard_map/rd,re->de/dot_general | solution.py:32
  654.6 9.8 fusion.122
  669.8 6.4 fusion.61.grad_ref
  676.3 9.5 cross_attend_back.1
  705.7 9.4 multiply_reduce_fusion.2
  722.5 7.5 fusion.55.grad_ref
  745.1 6.9 collective-permute-start.36
  765.6 69.8 %self_attend_back.1 = (bf16[768,1536]{1,0:T(8,128)(2,1)S(1)}, bf16[768,1536]{1,0:T(8,128)(2,1)S(1)}, bf16[768,1536]{1,0:T(8,128)(2,1)S(1)}, bf16[768,1536]{1,0:T(8,128)(2,1)}, bf16[768,1536]{1,0:T(8,128)(2,1)}) custom-call(s32[5]{0:T(128)S(1)} %copy-done.17, bf16[768,1536]{1,0:T(8,128)(2,1)S(1)} %copy-done.28, bf16[768,3072]{1,0:T(8,128)(2,1)} %copy-done.18, ...), custom_call_target="tpu_custom_call" | custom-call | flops 18119393280 | bytes 37748736 | tf_op jit(solution)/shard_map/self_attend_back/pallas_call | solution.py:598
  850.9 7.8 convolution_convert_fusion.1
  858.7 17.4 %fusion.128 = f32[768,1536]{1,0:T(8,128)} fusion(bf16[768,4608]{1,0:T(8,128)(2,1)} %copy-done.36, bf16[1536,4608]{1,0:T(8,128)(2,1)} %bitcast.204), kind=kOutput, calls=%fused_computation.302 | convolution fusion | flops 10871635968 | bytes 25952256 | tf_op jit(solution)/shard_map/re,de->rd/dot_general | solution.py:36
  876.1 9.7 add_convert_fusion.2
  911.9 22.4 %collective-permute-done.45 = bf16[768,384]{1,0:T(8,128)(2,1)S(1)} collective-permute-done((bf16[768,384]{1,0:T(8,128)(2,1)}, bf16[768,384]{1,0:T(8,128)(2,1)S(1)}, u32[]{:S(2)}, u32[]{:S(2)}) %collective-permute-start.45) | collective-permute-done | bytes 589856 | tf_op jit(solution)/shard_map/ppermute | solution.py:864
  942.2 13.0 %collective-permute-start.52 = (bf16[576,384]{1,0:T(8,128)(2,1)}, bf16[576,384]{1,0:T(8,128)(2,1)}, u32[]{:S(2)}, u32[]{:S(2)}) collective-permute-start(bf16[576,384]{1,0:T(8,128)(2,1)} %get-tuple-element.212), channel_id=1, source_target_pairs={{0,1},{1,2},{2,3},{3,0},{4,5},{5,6},{6,7},{7,4},{8,9},{9,10},{10,1... | collective-permute-start | bytes 1327112 | tf_op jit(solution)/shard_map/ppermute | solution.py:864
  959.7 6.7 collective-permute-done.52
  966.4 18.8 %collective-permute-done.53 = bf16[576,384]{1,0:T(8,128)(2,1)} collective-permute-done((bf16[576,384]{1,0:T(8,128)(2,1)}, bf16[576,384]{1,0:T(8,128)(2,1)}, u32[]{:S(2)}, u32[]{:S(2)}) %collective-permute-start.53) | collective-permute-done | bytes 442400 | tf_op jit(solution)/shard_map/ppermute | solution.py:864
  1001.1 10.4 collective-permute-start.55
  1023.7 17.4 %collective-permute-done.56 = bf16[576,384]{1,0:T(8,128)(2,1)S(1)} collective-permute-done((bf16[576,384]{1,0:T(8,128)(2,1)S(1)}, bf16[576,384]{1,0:T(8,128)(2,1)S(1)}, u32[]{:S(2)}, u32[]{:S(2)}) %collective-permute-start.56) | collective-permute-done | bytes 442400 | tf_op jit(solution)/shard_map/ppermute | solution.py:864
  1048.2 10.4 collective-permute-start.58
  1070.7 7.2 collective-permute-done.62
  1081.7 9.1 collective-permute-start.51
  1092.4 20.0 %collective-permute-done.51 = f32[8,1536]{1,0:T(8,128)S(1)} collective-permute-done((f32[8,1536]{1,0:T(8,128)S(1)}, f32[8,1536]{1,0:T(8,128)S(1)}, u32[]{:S(2)}, u32[]{:S(2)}) %collective-permute-start.51) | collective-permute-done | bytes 49184 | tf_op jit(solution)/shard_map/ppermute | solution.py:1198
  1138.9 8.1 unpack.13
  (541 shorter events, 331.1 us)
Async XLA Ops:
  7.2 171.8 %all-gather.7.cloned.1.call-start = ((), (), s32[]{:S(2)}) async-start(), calls=%async_computation.4 | async-start | bytes 15925248 | tf_op jit(solution)/shard_map/all_gather | solution.py:901
  16.7 40.9 %collective-permute-start.1 = (bf16[64,4608]{1,0:T(8,128)(2,1)S(1)}, bf16[64,4608]{1,0:T(8,128)(2,1)}, u32[]{:S(2)}, u32[]{:S(2)}) collective-permute-start(bf16[64,4608]{1,0:T(8,128)(2,1)S(1)} %pad_maximum_fusion.5), channel_id=1, source_target_pairs={{0,2},{1,3},{2,0},{3,1},{4,6},{5,7},{6,4},{7,5},{8,10},{9,11},{10,... | collective-permute-start | bytes 1769480 | tf_op jit(solution)/shard_map/ppermute | solution.py:864
  19.3 39.3 %collective-permute-start.2 = (bf16[64,4608]{1,0:T(8,128)(2,1)S(1)}, bf16[64,4608]{1,0:T(8,128)(2,1)S(1)}, u32[]{:S(2)}, u32[]{:S(2)}) collective-permute-start(bf16[64,4608]{1,0:T(8,128)(2,1)S(1)} %pad_maximum_fusion.5), channel_id=1, source_target_pairs={{0,3},{1,0},{2,1},{3,2},{4,7},{5,4},{6,5},{7,6},{8,11},{9,8},{10,9... | collective-permute-start | bytes 1769480 | tf_op jit(solution)/shard_map/ppermute | solution.py:864
  60.1 299.3 %all-gather.9.cloned.1.call-start = ((), (), s32[]{:S(2)}) async-start(), calls=%async_computation.5 | async-start | bytes 15925248 | tf_op jit(solution)/shard_map/all_gather | solution.py:901
  62.2 25.4 %collective-permute-start.3 = (bf16[48,4608]{1,0:T(8,128)(2,1)S(1)}, bf16[48,4608]{1,0:T(8,128)(2,1)S(1)}, u32[]{:S(2)}, u32[]{:S(2)}) collective-permute-start(bf16[48,4608]{1,0:T(8,128)(2,1)S(1)} %pad_maximum_fusion.7), channel_id=1, source_target_pairs={{0,1},{1,2},{2,3},{3,0},{4,5},{5,6},{6,7},{7,4},{8,9},{9,10},{10,1... | collective-permute-start | bytes 1327112 | tf_op jit(solution)/shard_map/ppermute | solution.py:864
  74.4 30.4 %collective-permute-start.4 = (bf16[48,4608]{1,0:T(8,128)(2,1)S(1)}, bf16[48,4608]{1,0:T(8,128)(2,1)S(1)}, u32[]{:S(2)}, u32[]{:S(2)}) collective-permute-start(bf16[48,4608]{1,0:T(8,128)(2,1)S(1)} %pad_maximum_fusion.7), channel_id=1, source_target_pairs={{0,2},{1,3},{2,0},{3,1},{4,6},{5,7},{6,4},{7,5},{8,10},{9,11},{10,... | collective-permute-start | bytes 1327112 | tf_op jit(solution)/shard_map/ppermute | solution.py:864
  77.2 27.6 %collective-permute-start.5 = (bf16[48,4608]{1,0:T(8,128)(2,1)S(1)}, bf16[48,4608]{1,0:T(8,128)(2,1)S(1)}, u32[]{:S(2)}, u32[]{:S(2)}) collective-permute-start(bf16[48,4608]{1,0:T(8,128)(2,1)S(1)} %pad_maximum_fusion.7), channel_id=1, source_target_pairs={{0,3},{1,0},{2,1},{3,2},{4,7},{5,4},{6,5},{7,6},{8,11},{9,8},{10,9... | collective-permute-start | bytes 1327112 | tf_op jit(solution)/shard_map/ppermute | solution.py:864
  106.1 326.0 %all-gather.11.cloned.1.call-start = ((), (), s32[]{:S(2)}) async-start(), calls=%async_computation.6 | async-start | bytes 21233664 | tf_op jit(solution)/shard_map/all_gather | solution.py:901
  123.1 51.3 %collective-permute-start.7 = (bf16[384,1536]{1,0:T(8,128)(2,1)S(1)}, bf16[384,1536]{1,0:T(8,128)(2,1)}, u32[]{:S(2)}, u32[]{:S(2)}) collective-permute-start(bf16[384,1536]{1,0:T(8,128)(2,1)S(1)} %get-tuple-element.205), channel_id=1, source_target_pairs={{0,1},{1,5},{2,4},{3,0},{4,3},{5,7},{6,6},{7,2},{8,9},{9,13},{10,1... | collective-permute-start | bytes 3538952 | tf_op jit(solution)/shard_map/ppermute | solution.py:879
  189.8 54.1 %collective-permute-start.14 = (bf16[768,3072]{1,0:T(8,128)(2,1)S(1)}, bf16[768,3072]{1,0:T(8,128)(2,1)S(1)}, u32[]{:S(2)}, u32[]{:S(2)}) collective-permute-start(bf16[768,3072]{1,0:T(8,128)(2,1)S(1)} %fusion.14.own_k.own_v), channel_id=1, source_target_pairs={{0,4},{4,0},{1,5},{5,1},{2,6},{6,2},{3,7},{7,3},{8,12},{12,8},{9,1... | collective-permute-start | bytes 14155784 | tf_op jit(solution)/shard_map/ppermute | solution.py:989
  202.8 26.4 %collective-permute-start.10 = (bf16[48,6144]{1,0:T(8,128)(2,1)S(1)}, bf16[48,6144]{1,0:T(8,128)(2,1)S(1)}, u32[]{:S(2)}, u32[]{:S(2)}) collective-permute-start(bf16[48,6144]{1,0:T(8,128)(2,1)S(1)} %get-tuple-element.84), channel_id=1, source_target_pairs={{0,2},{1,3},{2,0},{3,1},{4,6},{5,7},{6,4},{7,5},{8,10},{9,11},{10,... | collective-permute-start | bytes 1769480 | tf_op jit(solution)/shard_map/ppermute | solution.py:864
  202.9 41.0 %collective-permute-start.11 = (bf16[48,6144]{1,0:T(8,128)(2,1)S(1)}, bf16[48,6144]{1,0:T(8,128)(2,1)S(1)}, u32[]{:S(2)}, u32[]{:S(2)}) collective-permute-start(bf16[48,6144]{1,0:T(8,128)(2,1)S(1)} %get-tuple-element.84), channel_id=1, source_target_pairs={{0,3},{1,0},{2,1},{3,2},{4,7},{5,4},{6,5},{7,6},{8,11},{9,8},{10,9... | collective-permute-start | bytes 1769480 | tf_op jit(solution)/shard_map/ppermute | solution.py:864
  202.9 41.0 %collective-permute-start.9 = (bf16[48,6144]{1,0:T(8,128)(2,1)S(1)}, bf16[48,6144]{1,0:T(8,128)(2,1)S(1)}, u32[]{:S(2)}, u32[]{:S(2)}) collective-permute-start(bf16[48,6144]{1,0:T(8,128)(2,1)S(1)} %get-tuple-element.84), channel_id=1, source_target_pairs={{0,1},{1,2},{2,3},{3,0},{4,5},{5,6},{6,7},{7,4},{8,9},{9,10},{10,1... | collective-permute-start | bytes 1769480 | tf_op jit(solution)/shard_map/ppermute | solution.py:864
  247.6 245.7 %all-gather.13.cloned.1.call-start = ((), (), s32[]{:S(2)}) async-start(), calls=%async_computation.7 | async-start | bytes 21233664 | tf_op jit(solution)/shard_map/all_gather | solution.py:901
  253.4 79.9 %collective-permute-start.19 = (bf16[192,1536]{1,0:T(8,128)(2,1)}, bf16[192,1536]{1,0:T(8,128)(2,1)S(1)}, u32[]{:S(2)}, u32[]{:S(2)}) collective-permute-start(bf16[192,1536]{1,0:T(8,128)(2,1)} %get-tuple-element.95), channel_id=1, source_target_pairs={{0,1},{1,2},{2,3},{3,0},{4,5},{5,6},{6,7},{7,4},{8,9},{9,10},{10,1... | collective-permute-start | bytes 1769480 | tf_op jit(solution)/shard_map/ppermute | solution.py:864
  264.3 69.1 %collective-permute-start.20 = (bf16[192,1536]{1,0:T(8,128)(2,1)}, bf16[192,1536]{1,0:T(8,128)(2,1)S(1)}, u32[]{:S(2)}, u32[]{:S(2)}) collective-permute-start(bf16[192,1536]{1,0:T(8,128)(2,1)} %get-tuple-element.95), channel_id=1, source_target_pairs={{0,2},{1,3},{2,0},{3,1},{4,6},{5,7},{6,4},{7,5},{8,10},{9,11},{10,... | collective-permute-start | bytes 1769480 | tf_op jit(solution)/shard_map/ppermute | solution.py:864
  265.5 67.8 %collective-permute-start.21 = (bf16[192,1536]{1,0:T(8,128)(2,1)}, bf16[192,1536]{1,0:T(8,128)(2,1)S(1)}, u32[]{:S(2)}, u32[]{:S(2)}) collective-permute-start(bf16[192,1536]{1,0:T(8,128)(2,1)} %get-tuple-element.95), channel_id=1, source_target_pairs={{0,3},{1,0},{2,1},{3,2},{4,7},{5,4},{6,5},{7,6},{8,11},{9,8},{10,9... | collective-permute-start | bytes 1769480 | tf_op jit(solution)/shard_map/ppermute | solution.py:864
  336.0 418.8 %reduce-scatter.5.cloned.1.call-start = ((), (), s32[]{:S(2)}) async-start(), calls=%async_computation.8 | async-start | bytes 21233664 | tf_op jit(solution)/shard_map/reduce_scatter | solution.py:1065
  382.7 47.8 %collective-permute-start.24 = (bf16[384,1536]{1,0:T(8,128)(2,1)S(1)}, bf16[384,1536]{1,0:T(8,128)(2,1)S(1)}, u32[]{:S(2)}, u32[]{:S(2)}) collective-permute-start(bf16[384,1536]{1,0:T(8,128)(2,1)S(1)} %get-tuple-element.200), channel_id=1, source_target_pairs={{0,1},{1,5},{2,4},{3,0},{4,3},{5,7},{6,6},{7,2},{8,9},{9,13},{10,1... | collective-permute-start | bytes 3538952 | tf_op jit(solution)/shard_map/ppermute | solution.py:879
  537.9 350.0 %reduce-scatter.7.cloned.1.call-start = ((), (), s32[]{:S(2)}) async-start(), calls=%async_computation.9 | async-start | bytes 11796480 | tf_op jit(solution)/shard_map/reduce_scatter | solution.py:1043
  540.7 36.5 %collective-permute-start.22 = (bf16[384,1536]{1,0:T(8,128)(2,1)S(1)}, bf16[384,1536]{1,0:T(8,128)(2,1)S(1)}, u32[]{:S(2)}, u32[]{:S(2)}) collective-permute-start(bf16[384,1536]{1,0:T(8,128)(2,1)S(1)} %get-tuple-element.201), channel_id=1, source_target_pairs={{0,0},{4,1},{5,2},{1,3},{2,4},{6,5},{7,6},{3,7},{8,8},{12,9},{13,1... | collective-permute-start | bytes 3538952 | tf_op jit(solution)/shard_map/ppermute | solution.py:1067
  591.2 43.2 %collective-permute-start.26 = (bf16[3072,1536]{1,0:T(8,128)(2,1)}, bf16[3072,1536]{1,0:T(8,128)(2,1)}, u32[]{:S(2)}, u32[]{:S(2)}) collective-permute-start(bf16[3072,1536]{1,0:T(8,128)(2,1)} %convolution_convert_fusion.2), channel_id=1, source_target_pairs={{0,4},{4,0},{1,5},{5,1},{2,6},{6,2},{3,7},{7,3},{8,12},{12,8},{9,1... | collective-permute-start | bytes 28311560 | tf_op jit(solution)/shard_map/ppermute | solution.py:1038
  604.4 29.9 %collective-permute-start.25 = (bf16[384,1536]{1,0:T(8,128)(2,1)S(1)}, bf16[384,1536]{1,0:T(8,128)(2,1)}, u32[]{:S(2)}, u32[]{:S(2)}) collective-permute-start(bf16[384,1536]{1,0:T(8,128)(2,1)S(1)} %copy-done.57), channel_id=1, source_target_pairs={{1,0},{5,1},{4,2},{0,3},{3,4},{7,5},{6,6},{2,7},{9,8},{13,9},{12,1... | collective-permute-start | bytes 3538952 | tf_op jit(solution)/shard_map/ppermute | solution.py:1073
  648.4 289.8 %reduce-scatter.11.cloned.1.call-start = ((), (), s32[]{:S(2)}) async-start(), calls=%async_computation.11 | async-start | bytes 10321920 | tf_op jit(solution)/shard_map/reduce_scatter | solution.py:1043
  667.9 31.3 %collective-permute-start.27 = (bf16[768,1536]{1,0:T(8,128)(2,1)}, bf16[768,1536]{1,0:T(8,128)(2,1)}, u32[]{:S(2)}, u32[]{:S(2)}) collective-permute-start(bf16[768,1536]{1,0:T(8,128)(2,1)} %convolution_convert_fusion.5), channel_id=1, source_target_pairs={{0,4},{4,0},{1,5},{5,1},{2,6},{6,2},{3,7},{7,3},{8,12},{12,8},{9,1... | collective-permute-start | bytes 7077896 | tf_op jit(solution)/shard_map/ppermute | solution.py:1038
  688.2 32.5 %collective-permute-start.32 = (bf16[64,1536]{1,0:T(8,128)(2,1)}, bf16[64,1536]{1,0:T(8,128)(2,1)S(1)}, u32[]{:S(2)}, u32[]{:S(2)}) collective-permute-start(bf16[64,1536]{1,0:T(8,128)(2,1)} %get-tuple-element.171), channel_id=1, source_target_pairs={{0,2},{1,3},{2,0},{3,1},{4,6},{5,7},{6,4},{7,5},{8,10},{9,11},{10,... | collective-permute-start | bytes 589832 | tf_op jit(solution)/shard_map/ppermute | solution.py:864
  690.3 30.5 %collective-permute-start.33 = (bf16[64,1536]{1,0:T(8,128)(2,1)}, bf16[64,1536]{1,0:T(8,128)(2,1)S(1)}, u32[]{:S(2)}, u32[]{:S(2)}) collective-permute-start(bf16[64,1536]{1,0:T(8,128)(2,1)} %get-tuple-element.171), channel_id=1, source_target_pairs={{0,3},{1,0},{2,1},{3,2},{4,7},{5,4},{6,5},{7,6},{8,11},{9,8},{10,9... | collective-permute-start | bytes 589832 | tf_op jit(solution)/shard_map/ppermute | solution.py:864
  705.6 24.4 %collective-permute-start.28 = (bf16[768,1536]{1,0:T(8,128)(2,1)S(1)}, bf16[768,1536]{1,0:T(8,128)(2,1)}, u32[]{:S(2)}, u32[]{:S(2)}) collective-permute-start(bf16[768,1536]{1,0:T(8,128)(2,1)S(1)} %convolution_convert_fusion.4), channel_id=1, source_target_pairs={{0,4},{4,0},{1,5},{5,1},{2,6},{6,2},{3,7},{7,3},{8,12},{12,8},{9,1... | collective-permute-start | bytes 7077896 | tf_op jit(solution)/shard_map/ppermute | solution.py:1038
  739.6 260.0 %reduce-scatter.9.cloned.1.call-start = ((), (), s32[]{:S(2)}) async-start(), calls=%async_computation.10 | async-start | bytes 8847360 | tf_op jit(solution)/shard_map/reduce_scatter | solution.py:1043
  745.1 93.1 %collective-permute-start.36 = (bf16[2,64,384]{2,1,0:T(8,128)(2,1)S(1)}, bf16[2,64,384]{2,1,0:T(8,128)(2,1)}, u32[]{:S(2)}, u32[]{:S(2)}) collective-permute-start(bf16[2,64,384]{2,1,0:T(8,128)(2,1)S(1)} %fusion.89), channel_id=1, source_target_pairs={{0,2},{1,3},{2,0},{3,1},{4,6},{5,7},{6,4},{7,5},{8,10},{9,11},{10,... | collective-permute-start | bytes 294920 | tf_op jit(solution)/shard_map/ppermute | solution.py:864
  752.0 86.2 %collective-permute-start.37 = (bf16[2,64,384]{2,1,0:T(8,128)(2,1)S(1)}, bf16[2,64,384]{2,1,0:T(8,128)(2,1)}, u32[]{:S(2)}, u32[]{:S(2)}) collective-permute-start(bf16[2,64,384]{2,1,0:T(8,128)(2,1)S(1)} %fusion.89), channel_id=1, source_target_pairs={{0,3},{1,0},{2,1},{3,2},{4,7},{5,4},{6,5},{7,6},{8,11},{9,8},{10,9... | collective-permute-start | bytes 294920 | tf_op jit(solution)/shard_map/ppermute | solution.py:864
  756.6 81.6 %collective-permute-start.38 = (bf16[192,1536]{1,0:T(8,128)(2,1)S(1)}, bf16[192,1536]{1,0:T(8,128)(2,1)S(1)}, u32[]{:S(2)}, u32[]{:S(2)}) collective-permute-start(bf16[192,1536]{1,0:T(8,128)(2,1)S(1)} %get-tuple-element.194), channel_id=1, source_target_pairs={{0,1},{1,2},{2,3},{3,0},{4,5},{5,6},{6,7},{7,4},{8,9},{9,10},{10,1... | collective-permute-start | bytes 1769480 | tf_op jit(solution)/shard_map/ppermute | solution.py:864
  756.7 81.5 %collective-permute-start.39 = (bf16[192,1536]{1,0:T(8,128)(2,1)S(1)}, bf16[192,1536]{1,0:T(8,128)(2,1)}, u32[]{:S(2)}, u32[]{:S(2)}) collective-permute-start(bf16[192,1536]{1,0:T(8,128)(2,1)S(1)} %get-tuple-element.193), channel_id=1, source_target_pairs={{0,2},{1,3},{2,0},{3,1},{4,6},{5,7},{6,4},{7,5},{8,10},{9,11},{10,... | collective-permute-start | bytes 1769480 | tf_op jit(solution)/shard_map/ppermute | solution.py:864
  757.1 81.1 %collective-permute-start.40 = (bf16[192,1536]{1,0:T(8,128)(2,1)S(1)}, bf16[192,1536]{1,0:T(8,128)(2,1)}, u32[]{:S(2)}, u32[]{:S(2)}) collective-permute-start(bf16[192,1536]{1,0:T(8,128)(2,1)S(1)} %get-tuple-element.192), channel_id=1, source_target_pairs={{0,3},{1,0},{2,1},{3,2},{4,7},{5,4},{6,5},{7,6},{8,11},{9,8},{10,9... | collective-permute-start | bytes 1769480 | tf_op jit(solution)/shard_map/ppermute | solution.py:864
  885.9 242.4 %all-gather.15.cloned.1.call-start = ((), (), s32[]{:S(2)}) async-start(), calls=%async_computation.12 | async-start | bytes 17252352 | tf_op jit(solution)/shard_map/all_gather | solution.py:1209
  892.5 41.9 %collective-permute-start.45 = (bf16[768,384]{1,0:T(8,128)(2,1)}, bf16[768,384]{1,0:T(8,128)(2,1)S(1)}, u32[]{:S(2)}, u32[]{:S(2)}) collective-permute-start(bf16[768,384]{1,0:T(8,128)(2,1)} %get-tuple-element.190), channel_id=1, source_target_pairs={{0,2},{1,3},{2,0},{3,1},{4,6},{5,7},{6,4},{7,5},{8,10},{9,11},{10,... | collective-permute-start | bytes 1769480 | tf_op jit(solution)/shard_map/ppermute | solution.py:864
  895.1 39.2 %collective-permute-start.46 = (bf16[768,384]{1,0:T(8,128)(2,1)S(1)}, bf16[768,384]{1,0:T(8,128)(2,1)}, u32[]{:S(2)}, u32[]{:S(2)}) collective-permute-start(bf16[768,384]{1,0:T(8,128)(2,1)S(1)} %get-tuple-element.189), channel_id=1, source_target_pairs={{0,3},{1,0},{2,1},{3,2},{4,7},{5,4},{6,5},{7,6},{8,11},{9,8},{10,9... | collective-permute-start | bytes 1769480 | tf_op jit(solution)/shard_map/ppermute | solution.py:864
  942.2 24.3 %collective-permute-start.52 = (bf16[576,384]{1,0:T(8,128)(2,1)}, bf16[576,384]{1,0:T(8,128)(2,1)}, u32[]{:S(2)}, u32[]{:S(2)}) collective-permute-start(bf16[576,384]{1,0:T(8,128)(2,1)} %get-tuple-element.212), channel_id=1, source_target_pairs={{0,1},{1,2},{2,3},{3,0},{4,5},{5,6},{6,7},{7,4},{8,9},{9,10},{10,1... | collective-permute-start | bytes 1327112 | tf_op jit(solution)/shard_map/ppermute | solution.py:864
  955.1 30.1 %collective-permute-start.53 = (bf16[576,384]{1,0:T(8,128)(2,1)}, bf16[576,384]{1,0:T(8,128)(2,1)}, u32[]{:S(2)}, u32[]{:S(2)}) collective-permute-start(bf16[576,384]{1,0:T(8,128)(2,1)} %get-tuple-element.211), channel_id=1, source_target_pairs={{0,2},{1,3},{2,0},{3,1},{4,6},{5,7},{6,4},{7,5},{8,10},{9,11},{10,... | collective-permute-start | bytes 1327112 | tf_op jit(solution)/shard_map/ppermute | solution.py:864
  955.5 29.7 %collective-permute-start.54 = (bf16[576,384]{1,0:T(8,128)(2,1)}, bf16[576,384]{1,0:T(8,128)(2,1)}, u32[]{:S(2)}, u32[]{:S(2)}) collective-permute-start(bf16[576,384]{1,0:T(8,128)(2,1)} %get-tuple-element.210), channel_id=1, source_target_pairs={{0,3},{1,0},{2,1},{3,2},{4,7},{5,4},{6,5},{7,6},{8,11},{9,8},{10,9... | collective-permute-start | bytes 1327112 | tf_op jit(solution)/shard_map/ppermute | solution.py:864
  1001.1 22.6 %collective-permute-start.55 = (bf16[576,384]{1,0:T(8,128)(2,1)S(1)}, bf16[576,384]{1,0:T(8,128)(2,1)S(1)}, u32[]{:S(2)}, u32[]{:S(2)}) collective-permute-start(bf16[576,384]{1,0:T(8,128)(2,1)S(1)} %get-tuple-element.209), channel_id=1, source_target_pairs={{0,1},{1,2},{2,3},{3,0},{4,5},{5,6},{6,7},{7,4},{8,9},{9,10},{10,1... | collective-permute-start | bytes 1327112 | tf_op jit(solution)/shard_map/ppermute | solution.py:864
  1011.4 29.6 %collective-permute-start.56 = (bf16[576,384]{1,0:T(8,128)(2,1)S(1)}, bf16[576,384]{1,0:T(8,128)(2,1)S(1)}, u32[]{:S(2)}, u32[]{:S(2)}) collective-permute-start(bf16[576,384]{1,0:T(8,128)(2,1)S(1)} %get-tuple-element.208), channel_id=1, source_target_pairs={{0,2},{1,3},{2,0},{3,1},{4,6},{5,7},{6,4},{7,5},{8,10},{9,11},{10,... | collective-permute-start | bytes 1327112 | tf_op jit(solution)/shard_map/ppermute | solution.py:864
  1013.0 28.1 %collective-permute-start.57 = (bf16[576,384]{1,0:T(8,128)(2,1)S(1)}, bf16[576,384]{1,0:T(8,128)(2,1)S(1)}, u32[]{:S(2)}, u32[]{:S(2)}) collective-permute-start(bf16[576,384]{1,0:T(8,128)(2,1)S(1)} %get-tuple-element.207), channel_id=1, source_target_pairs={{0,3},{1,0},{2,1},{3,2},{4,7},{5,4},{6,5},{7,6},{8,11},{9,8},{10,9... | collective-permute-start | bytes 1327112 | tf_op jit(solution)/shard_map/ppermute | solution.py:864
  1018.9 62.8 %collective-permute-start.50 = (f32[8,1536]{1,0:T(8,128)S(1)}, f32[8,1536]{1,0:T(8,128)S(1)}, u32[]{:S(2)}, u32[]{:S(2)}) collective-permute-start(f32[8,1536]{1,0:T(8,128)S(1)} %add.465), channel_id=1, source_target_pairs={{0,1},{1,0},{2,3},{3,2},{4,5},{5,4},{6,7},{7,6},{8,9},{9,8},{10,11... | collective-permute-start | bytes 147464 | tf_op jit(solution)/shard_map/ppermute | solution.py:1198
  1048.2 67.6 %collective-permute-start.58 = (bf16[384,1536]{1,0:T(8,128)(2,1)}, bf16[384,1536]{1,0:T(8,128)(2,1)}, u32[]{:S(2)}, u32[]{:S(2)}) collective-permute-start(bf16[384,1536]{1,0:T(8,128)(2,1)} %get-tuple-element.187), channel_id=1, source_target_pairs={{0,0},{4,1},{5,2},{1,3},{2,4},{6,5},{7,6},{3,7},{8,8},{12,9},{13,1... | collective-permute-start | bytes 3538952 | tf_op jit(solution)/shard_map/ppermute | solution.py:891
  1058.6 57.2 %collective-permute-start.59 = (bf16[384,1536]{1,0:T(8,128)(2,1)}, bf16[384,1536]{1,0:T(8,128)(2,1)}, u32[]{:S(2)}, u32[]{:S(2)}) collective-permute-start(bf16[384,1536]{1,0:T(8,128)(2,1)} %get-tuple-element.188), channel_id=1, source_target_pairs={{1,0},{5,1},{4,2},{0,3},{3,4},{7,5},{6,6},{2,7},{9,8},{13,9},{12,1... | collective-permute-start | bytes 3538952 | tf_op jit(solution)/shard_map/ppermute | solution.py:891
  1080.2 39.9 %collective-permute-start.64 = (bf16[2304,384]{1,0:T(8,128)(2,1)}, bf16[2304,384]{1,0:T(8,128)(2,1)}, u32[]{:S(2)}, u32[]{:S(2)}) collective-permute-start(bf16[2304,384]{1,0:T(8,128)(2,1)} %get-tuple-element.224), channel_id=1, source_target_pairs={{0,4},{4,0},{1,5},{5,1},{2,6},{6,2},{3,7},{7,3},{8,12},{12,8},{9,1... | collective-permute-start | bytes 5308424 | tf_op jit(solution)/shard_map/ppermute | solution.py:1229
  1081.7 30.7 %collective-permute-start.51 = (f32[8,1536]{1,0:T(8,128)S(1)}, f32[8,1536]{1,0:T(8,128)S(1)}, u32[]{:S(2)}, u32[]{:S(2)}) collective-permute-start(f32[8,1536]{1,0:T(8,128)S(1)} %add.466), channel_id=1, source_target_pairs={{0,2},{2,0},{1,3},{3,1},{4,6},{6,4},{5,7},{7,5},{8,10},{10,8},{9,1... | collective-permute-start | bytes 147464 | tf_op jit(solution)/shard_map/ppermute | solution.py:1198
  (129 other events, 2060.1 us)
Sparse Core Ops, SparseCore 0:
  60.2 90.6 all-gather.6
  153.4 78.7 all-gather.8
  247.7 107.4 all-gather.10
  357.6 98.7 all-gather.12
  538.0 134.9 reduce-scatter.4
  676.5 94.9 reduce-scatter.6
  775.3 85.3 reduce-scatter.10
  886.0 77.7 reduce-scatter.8
  987.8 107.2 all-gather.14

commit v8 on v6

--- a/solution.py
+++ b/solution.py
@@ -889,14 +889,16 @@
     norms = line_up(vectors[0], [values[share] for values in qkv_came])
     norms = norms[:, : 6 * block].reshape(shards, 6, block).transpose(1, 0, 2)
     norms = norms.reshape(6, width).astype(jnp.float32)
-    came = to_chip(after(frames, *qkv_came))
-    x_low = by_time(*came)
     rest_share = jnp.concatenate(
         [share_of(self_output_weight), share_of(cross_query_weight), share_of(cross_output_weight)],
         axis=1,
     )
-    rest_came = hops(after(rest_share, *came))
+    rest_came = hops(after(rest_share, *qkv_came))
+    rest = from_replicas(line_up(rest_share, rest_came))
+    came = to_chip(after(frames, *rest_came))
+    x_low = by_time(*came)
     expand_share = share_of(feed_up_weight)
+    expand_came = hops(after(expand_share, *came))
 
     facts = jnp.concatenate(
         [(clip_lengths // 64)[:, None], (clip_lengths % 64)[:, None], slot_used[:, None], text_mask],
@@ -952,12 +954,15 @@
     kv = project(after(hidden_one, count), qkv_matrix[:, width:]).astype(jnp.bfloat16)
     kv_other = lax.ppermute(kv, "core", swap)
     queries = project(after(hidden_one, kv), qkv_matrix[:, :width]).astype(jnp.bfloat16)
-    rest_came = held(rest_came, kv)
-    rest = from_replicas(line_up(rest_share, rest_came))
+    expand_came = held(expand_came, kv_other, queries)
+    expand_matrix = from_replicas(line_up(expand_share, expand_came))
     output_matrix = rest[:, :width]
     probe_matrix = rest[:, width : 2 * width]
     merge_matrix = rest[:, 2 * width :]
-    text_came = held(text_came, queries)
+    mixed_self, lse = self_attend(after(places, *expand_came), queries, kv, kv_other)
+    reduce_share = share_of(feed_down_weight)
+    text_came = held(text_came, mixed_self)
+    reduce_came = hops(after(reduce_share, *text_came))
     text_half = lax.dynamic_index_in_dim(text_part, shard, 0, keepdims=False).astype(jnp.float32)
     for values in text_came:
         text_half += values.astype(jnp.float32)
@@ -965,20 +970,15 @@
     text_swap = lax.ppermute(text_half, "core", swap)
     lookups = jnp.where(first_core, text_half, text_swap)
     contents = jnp.where(first_core, text_swap, text_half)
-    expand_came = hops(after(expand_share, *rest_came, *text_came))
-    mixed_self, lse = self_attend(after(places, rest_came[0]), queries, kv, kv_other)
-    expand_came = held(expand_came, mixed_self)
-    expand_matrix = from_replicas(line_up(expand_share, expand_came))
-    reduce_share = share_of(feed_down_weight)
-    reduce_came = hops(after(reduce_share, *expand_came))
     after_self = inputs + project(mixed_self, output_matrix)
     parts_two = norm_parts(after_self)
     hidden_two = ((after_self - parts_two[0]) * parts_two[1] * norms[2] + norms[3]).astype(
         jnp.bfloat16
     )
     probes = project(hidden_two, probe_matrix).astype(jnp.bfloat16)
-    reduce_matrix = from_replicas(line_up(reduce_share, held(reduce_came, probes)))
-    teacher_low = by_time(*to_chip(after(teacher, *reduce_came, probes)))
+    reduce_came = held(reduce_came, probes)
+    reduce_matrix = from_replicas(line_up(reduce_share, reduce_came))
+    teacher_came = to_chip(after(teacher, *reduce_came, probes))
     cross_mixed = cross_attend(probes, lookups, contents, present)
     after_cross = after_self + project(cross_mixed, merge_matrix)
     parts_three = norm_parts(after_cross)
@@ -988,6 +988,7 @@
     upward = project(hidden_three, expand_matrix)
     activated, gelu_pull = jax.vjp(exact_gelu, upward)
     activated_low = activated.astype(jnp.bfloat16)
+    teacher_low = by_time(*held(teacher_came, activated_low))
     result = after_cross + project(activated_low, reduce_matrix)
     errors = (result - teacher_low.astype(jnp.float32)) * valid_rows
     squares = jnp.sum(errors * errors)
@@ -1113,13 +1114,11 @@
     )
     text_own = text_own.astype(jnp.bfloat16)
     down_came = shard_hops(down_sum)
-    text_came = hops(text_own)
     grad_queries, own_keys, own_values, other_keys, other_values = self_attend_back(
         places, queries, kv, kv_other, mixed_self, after(grad_mixed, middle, text_own), lse
     )
-    text_came = held(text_came, grad_queries)
     down_came = held(down_came, grad_queries)
-    other_keys, other_values = held([other_keys, other_values], *text_came, *down_came)
+    other_keys, other_values = held([other_keys, other_values], *down_came)
     own_keys += lax.ppermute(other_keys, "core", swap)
     own_values += lax.ppermute(other_values, "core", swap)
     down_piece = over_shard(down_sum, down_came)
@@ -1131,21 +1130,13 @@
     qkv_ours = ours_of(after(qkv_grads, grad_hidden_one), hidden_one, qkv_theirs)
     up_came = held(up_came, grad_hidden_one)
     up_piece = over_shard(up_sum, up_came)
-    text_grad = line_up(text_own, text_came).astype(jnp.float32)
-    text_grad = text_grad.transpose(1, 2, 0, 3).reshape(text_states.shape)
     qkv_sum = over_outer(qkv_ours)
     grad_norm, gain_self, bias_self = norm_back(
         after(grad_hidden_one, qkv_ours, *up_came), inputs, parts_one, norms[0]
     )
     middle_kept = after(middle_sum[: middle_rows - text_split], qkv_ours, *up_came)
     middle_came = shard_hops(middle_kept)
-    frames_came = from_chip(
-        after((grad_after_self + grad_norm).astype(jnp.bfloat16), *middle_came)
-    )
-    frames_grad = by_slot(*frames_came).astype(jnp.float32)
-
-    qkv_sum = after(qkv_sum, *frames_came)
-    late_came = shard_hops(qkv_sum)
+
     small = jnp.stack(
         [
             gain_self,
@@ -1158,7 +1149,6 @@
             jnp.zeros((width,), jnp.float32),
         ]
     )
-    small = after(small, *late_came)
     for axis, pairs in (
         ("core", swap),
         ("x", swap),
@@ -1167,6 +1157,14 @@
         ("shard", [(0, 2), (2, 0), (1, 3), (3, 1)]),
     ):
         small += lax.ppermute(small, axis, pairs)
+    late_came = shard_hops(after(qkv_sum, *middle_came, small))
+    frames_came = from_chip(
+        after((grad_after_self + grad_norm).astype(jnp.bfloat16), *late_came)
+    )
+    frames_grad = by_slot(*frames_came).astype(jnp.float32)
+    text_came = hops(after(text_own, *late_came))
+    text_grad = line_up(text_own, text_came).astype(jnp.float32)
+    text_grad = text_grad.transpose(1, 2, 0, 3).reshape(text_states.shape)
     loss = small[6, 0] / (width * count)
     small_own = lax.dynamic_slice_in_dim(small, shard * block, block, 1)
 
@@ -1177,7 +1175,7 @@
         + [text_piece, middle_piece],
         axis=0,
     )
-    early = lax.all_gather(after(early, text_grad), REPLICAS, axis=0)
+    early = lax.all_gather(early, REPLICAS, axis=0)
     piece = width // replicas
     square = (block, width)
     up_grad = unpack(early, hidden_units // replicas, 0, (block, hidden_units), 0, 1)
@@ -1191,7 +1189,9 @@
     probe_grad = unpack(early, piece, at + 1, square, 0, 2)
     merge_grad = unpack(early, piece, at + 2, square, 0, 2)
     late = over_shard(qkv_sum, late_came)
-    late = lax.all_gather(after(late, early), REPLICAS, axis=0, tiled=True)
+    late = lax.all_gather(
+        after(late, early, text_grad, *frames_came), REPLICAS, axis=0, tiled=True
+    )
     late = late.reshape(-1, block, block)
     qkv_grad = [unpack(late, block, 0, square, 2 * i, 2) for i in range(3)]
     return (

time: 1170 us -> 1190 us (1.017)
  waiting for transfers between devices: 270 us -> 295 us
  starting transfers between devices: 202 us -> 181 us
    ppermute x33, waiting for transfers between devices: 140 us -> 244 us  [hop(): return lax.ppermute(values, 'shard', pairs)]
    ppermute x2, waiting for transfers between devices: 57.9 us -> 20.8 us  [to_chip(): two = lax.ppermute(jnp.where(lower, pair[1], pair[0]), spot, there[1])]
    ppermute x2, waiting for transfers between devices: 31.4 us -> 0.01 us  [from_chip(): return (lax.ppermute(one, spot, back[0]), lax.ppermute(two, spot, back[1]))]
    all_gather x4, waiting for transfers between devices: 21 us -> 3.22 us  [from_replicas(): full = lax.all_gather(line, ('y', 'x', 'core'), axis=1, tiled=True)]
    ppermute x33, starting transfers between devices: 108 us -> 91 us  [hop(): return lax.ppermute(values, 'shard', pairs)]
    ppermute x2, starting transfers between devices: 29.7 us -> 17.2 us  [to_chip(): two = lax.ppermute(jnp.where(lower, pair[1], pair[0]), spot, there[1])]
    unnamed x179 -> x189, local copies, waits for them, and re-layouts: 35.5 us -> 43.8 us
  transfers between devices with their start and end apart: 71 -> 71, of which waited for: 27 -> 31; matrix products, arithmetic and copies ran while one was open for 35% -> 35% of each run, Pallas kernels for 15% -> 14%
where the time goes in v8:
time: 1190 us; the launch traced here: 1170 us
  matrix products  309 us (26%)
  waiting for transfers between devices  295 us (25%)
  starting transfers between devices  181 us (15%)
  Pallas kernels  174 us (15%)
  local copies, waits for them, and re-layouts  108 us (9%)
  other arithmetic  83.5 us (7%)
  between operations  21.7 us (2%)
    ppermute x33, waiting for transfers between devices, hop(): return lax.ppermute(values, 'shard', pairs)  244 us
    dot_general x8, matrix products, project(): return jnp.dot(left, right, preferred_element_type=jnp.float32)  125 us
    dot_general x7, matrix products, back_project(): jnp.einsum('re,de->rd', grads, matrix, preferred_element_type=jnp.float32)  93 us
    ppermute x33, starting transfers between devices, hop(): return lax.ppermute(values, 'shard', pairs)  91 us
    dot_general x13, matrix products, outer_sum(): jnp.einsum('rd,re->de', left, right, preferred_element_type=jnp.float32)  90.9 us
    pallas_call x1, Pallas kernels, self_attend_back(): pl.pallas_call(self_backward_kernel, out_shape=(jax.ShapeDtypeStruct((row...  70 us
    pallas_call x1, Pallas kernels, self_attend(): pl.pallas_call(self_forward_kernel, out_shape=(jax.ShapeDtypeStruct((rows...  58.5 us
    unnamed x189, local copies, waits for them, and re-layouts  43.8 us
  transfers between devices with their start and end apart: 71, of which 31 were waited for; matrix products, arithmetic and copies ran while one was open for 35% of the time, Pallas kernels for 14%

profile of v8, /device:TPU:0, one launch (start us, length us, event | category | flops | bytes accessed | tf_op | source)
XLA Modules:
  0.0 1172.1 jit_solution(5548194588425232586)
XLA Ops:
  20.9 12.3 %collective-permute-done = bf16[64,4608]{1,0:T(8,128)(2,1)} collective-permute-done((bf16[64,4608]{1,0:T(8,128)(2,1)S(1)}, bf16[64,4608]{1,0:T(8,128)(2,1)}, u32[]{:S(2)}, u32[]{:S(2)}) %collective-permute-start) | collective-permute-done | bytes 589856 | tf_op jit(solution)/shard_map/ppermute | solution.py:830
  34.2 23.4 %collective-permute-done.1 = bf16[64,4608]{1,0:T(8,128)(2,1)} collective-permute-done((bf16[64,4608]{1,0:T(8,128)(2,1)S(1)}, bf16[64,4608]{1,0:T(8,128)(2,1)}, u32[]{:S(2)}, u32[]{:S(2)}) %collective-permute-start.1) | collective-permute-done | bytes 589856 | tf_op jit(solution)/shard_map/ppermute | solution.py:830
  63.1 12.1 %collective-permute-start.3 = (bf16[48,4608]{1,0:T(8,128)(2,1)S(1)}, bf16[48,4608]{1,0:T(8,128)(2,1)S(1)}, u32[]{:S(2)}, u32[]{:S(2)}) collective-permute-start(bf16[48,4608]{1,0:T(8,128)(2,1)S(1)} %pad_maximum_fusion.7), channel_id=1, source_target_pairs={{0,1},{1,2},{2,3},{3,0},{4,5},{5,6},{6,7},{7,4},{8,9},{9,10},{10,1... | collective-permute-start | bytes 1327112 | tf_op jit(solution)/shard_map/ppermute | solution.py:830
  78.1 10.4 collective-permute-done.3
  88.5 17.1 %collective-permute-done.4 = bf16[48,4608]{1,0:T(8,128)(2,1)S(1)} collective-permute-done((bf16[48,4608]{1,0:T(8,128)(2,1)S(1)}, bf16[48,4608]{1,0:T(8,128)(2,1)S(1)}, u32[]{:S(2)}, u32[]{:S(2)}) %collective-permute-start.4) | collective-permute-done | bytes 442400 | tf_op jit(solution)/shard_map/ppermute | solution.py:830
  123.7 11.1 collective-permute-start.7
  154.2 20.8 %collective-permute-done.7 = bf16[384,1536]{1,0:T(8,128)(2,1)S(1)} collective-permute-done((bf16[384,1536]{1,0:T(8,128)(2,1)S(1)}, bf16[384,1536]{1,0:T(8,128)(2,1)S(1)}, u32[]{:S(2)}, u32[]{:S(2)}) %collective-permute-start.7) | collective-permute-done | bytes 1179680 | tf_op jit(solution)/shard_map/ppermute | solution.py:845
  178.3 10.8 fusion.14.own_k.own_v
  189.1 11.2 collective-permute-start.14
  204.0 8.3 fusion.64.q_ref
  212.3 16.3 %collective-permute-done.10 = bf16[48,6144]{1,0:T(8,128)(2,1)S(1)} collective-permute-done((bf16[48,6144]{1,0:T(8,128)(2,1)S(1)}, bf16[48,6144]{1,0:T(8,128)(2,1)S(1)}, u32[]{:S(2)}, u32[]{:S(2)}) %collective-permute-start.10) | collective-permute-done | bytes 589856 | tf_op jit(solution)/shard_map/ppermute | solution.py:830
  228.6 14.2 %collective-permute-done.11 = bf16[48,6144]{1,0:T(8,128)(2,1)S(1)} collective-permute-done((bf16[48,6144]{1,0:T(8,128)(2,1)S(1)}, bf16[48,6144]{1,0:T(8,128)(2,1)S(1)}, u32[]{:S(2)}, u32[]{:S(2)}) %collective-permute-start.11) | collective-permute-done | bytes 589856 | tf_op jit(solution)/shard_map/ppermute | solution.py:830
  254.6 11.3 collective-permute-start.15
  279.1 58.5 %self_attend.1 = (bf16[768,1536]{1,0:T(8,128)(2,1)S(1)}, f32[96,768]{1,0:T(8,128)S(1)}) custom-call(s32[5]{0:T(128)S(1)} %stack.66.place, bf16[768,1536]{1,0:T(8,128)(2,1)S(1)} %copy-done.22, bf16[768,3072]{1,0:T(8,128)(2,1)S(1)} %copy-done.14, bf16[768,3072]{1,0:T(8,128)(2,1)S(1)} %copy-done.14, bf16[768,3072]{1,0:T(8,128)(2,1)S(1)} %copy-done.16, ...), custom_call_target="tpu_custom_call" | custom-call | flops 7247757312 | bytes 18874368 | tf_op jit(solution)/shard_map/self_attend/pallas_call | solution.py:569
  341.7 6.9 fusion.132
  350.8 7.5 fusion.58.probe_ref
  358.4 21.0 %collective-permute-done.20 = bf16[192,1536]{1,0:T(8,128)(2,1)} collective-permute-done((bf16[192,1536]{1,0:T(8,128)(2,1)}, bf16[192,1536]{1,0:T(8,128)(2,1)}, u32[]{:S(2)}, u32[]{:S(2)}) %collective-permute-start.20) | collective-permute-done | bytes 589856 | tf_op jit(solution)/shard_map/ppermute | solution.py:830
  390.5 6.8 cross_attend.1
  397.3 6.8 fusion.133
  409.2 10.4 collective-permute-start.23
  425.6 61.1 %multiply_convert_fusion = (bf16[768,6144]{1,0:T(8,128)(2,1)}, f32[768,6144]{1,0:T(8,128)}, f32[768,6144]{1,0:T(8,128)}) fusion(bf16[1536,6144]{1,0:T(8,128)(2,1)} %bitcast.198, f32[768,1536]{1,0:T(8,128)} %copy-done.27, f32[1536]{0:T(1024)S(1)} %add.428, f32[1536]{0:T(1024)S(1)} %mul.314, f32[768]{0:T(1024)S(1)} %add_rsqrt_fusion, ...), kind=kOutput, calls=%fused_computation.5 | convolution fusion | flops 14808121344 | bytes 70797312 | tf_op jit(solution)/shard_map/dot_general | solution.py:28
  493.1 23.3 %multiply_convert_fusion.1 = (bf16[768,1536]{1,0:T(8,128)(2,1)S(1)}, bf16[768,1536]{1,0:T(8,128)(2,1)}, f32[768,1536]{1,0:T(8,128)}) fusion(f32[]{:T(128)S(6)} %div.75, f32[768]{0:T(1024)S(1)} %copy-done.79, bf16[384,1536]{1,0:T(8,128)(2,1)} %get-tuple-element.198, bf16[384,1536]{1,0:T(8,128)(2,1)} %get-tuple-element.197, f32[768,1536]{1,0:T(8,128)} %copy-done.27, ...), kind=kOutput, calls=%fused_computation.66 | convolution fusion | flops 14507311104 | bytes 44829700 | tf_op jit(solution)/shard_map/dot_general | solution.py:28
  516.4 10.1 convolution_convert_fusion.2
  531.2 29.5 %add_convert_fusion.2 = bf16[768,6144]{1,0:T(8,128)(2,1)} fusion(f32[768,6144]{1,0:T(8,128)} %get-tuple-element.179, f32[768,6144]{1,0:T(8,128)} %get-tuple-element.229, bf16[768,1536]{1,0:T(8,128)(2,1)} %copy-done.54, bf16[6144,1536]{1,0:T(8,128)(2,1)} %bitcast.201), kind=kOutput, calls=%fused_computation.4 | convolution fusion | flops 14561574912 | bytes 68419584 | tf_op jit(solution)/shard_map/re,de->rd/dot_general | solution.py:36
  560.7 14.1 %add_convert_fusion.1 = bf16[768,6144]{1,0:T(8,128)(2,1)} fusion(bf16[768,6144]{1,0:T(8,128)(2,1)} %collective-permute-done.26, bf16[768,6144]{1,0:T(8,128)(2,1)} %get-tuple-element.178, bf16[768,1536]{1,0:T(8,128)(2,1)} %copy-done.54, s32[]{:T(128)S(6)} %select_n.332), kind=kOutput, calls=%fused_computation.3 | convolution fusion | flops 7261913088 | bytes 29491204 | tf_op jit(solution)/shard_map/rd,re->de/dot_general | solution.py:32
  574.9 13.7 %convolution_convert_fusion.1 = bf16[3072,1536]{1,0:T(8,128)(2,1)} fusion(bf16[768,6144]{1,0:T(8,128)(2,1)} %add_convert_fusion.2, s32[]{:T(128)S(6)} %select_n.333, f32[768,1536]{1,0:T(8,128)} %copy-done.27, f32[1536]{0:T(1024)S(1)} %add.428, f32[1536]{0:T(1024)S(1)} %mul.314, f32[768]{0:T(1024)S(1)} %add_rsqrt_fusion, f32[768]{0:T(1024)S(1)} %broadcast_multiply_fusion.6), kind=kOutput, calls=%fused_computation.21 | convolution fusion | flops 7258374144 | bytes 18892804 | tf_op jit(solution)/shard_map/rd,re->de/dot_general | solution.py:32
  596.8 21.5 %fusion.134 = f32[768,1536]{1,0:T(8,128)} fusion(bf16[768,6144]{1,0:T(8,128)(2,1)} %add_convert_fusion.2, bf16[1536,6144]{1,0:T(8,128)(2,1)} %bitcast.199), kind=kOutput, calls=%fused_computation.296 | convolution fusion | flops 14495514624 | bytes 33030144 | tf_op jit(solution)/shard_map/re,de->rd/dot_general | solution.py:36
  623.6 14.0 %add_convert_fusion = bf16[3072,1536]{1,0:T(8,128)(2,1)} fusion(bf16[3072,1536]{1,0:T(8,128)(2,1)} %collective-permute-done.27, bf16[768,6144]{1,0:T(8,128)(2,1)} %add_convert_fusion.2, s32[]{:T(128)S(6)} %select_n.336, f32[768,1536]{1,0:T(8,128)S(1)} %bitcast.174, f32[1536]{0:T(1024)S(1)} %add.428, f32[1536]{0:T(1024)S(1)} %mul.314, ...), kind=kOutput, calls=%fused_computation.2 | convolution fusion | flops 7267811328 | bytes 28329988 | tf_op jit(solution)/shard_map/rd,re->de/dot_general | solution.py:32
  643.6 9.8 fusion.129
  656.9 6.7 fusion.61.grad_ref
  663.6 9.5 cross_attend_back.1
  693.1 8.8 multiply_reduce_fusion.2
  709.6 7.5 fusion.55.grad_ref
  733.5 7.6 collective-permute-start.36
  751.0 70.0 %self_attend_back.1 = (bf16[768,1536]{1,0:T(8,128)(2,1)S(1)}, bf16[768,1536]{1,0:T(8,128)(2,1)S(1)}, bf16[768,1536]{1,0:T(8,128)(2,1)S(1)}, bf16[768,1536]{1,0:T(8,128)(2,1)}, bf16[768,1536]{1,0:T(8,128)(2,1)}) custom-call(s32[5]{0:T(128)S(1)} %copy-done.12, bf16[768,1536]{1,0:T(8,128)(2,1)S(1)} %copy-done.23, bf16[768,3072]{1,0:T(8,128)(2,1)} %copy-done.13, ...), custom_call_target="tpu_custom_call" | custom-call | flops 18119393280 | bytes 37748736 | tf_op jit(solution)/shard_map/self_attend_back/pallas_call | solution.py:598
  836.5 7.8 convolution_convert_fusion
  844.5 18.5 %fusion.135 = f32[768,1536]{1,0:T(8,128)} fusion(bf16[768,4608]{1,0:T(8,128)(2,1)} %copy-done.34, bf16[1536,4608]{1,0:T(8,128)(2,1)} %bitcast.204), kind=kOutput, calls=%fused_computation.297 | convolution fusion | flops 10871635968 | bytes 25952256 | tf_op jit(solution)/shard_map/re,de->rd/dot_general | solution.py:36
  863.1 9.8 add_convert_fusion.3
  880.4 14.3 %collective-permute-done.42 = bf16[768,384]{1,0:T(8,128)(2,1)S(1)} collective-permute-done((bf16[768,384]{1,0:T(8,128)(2,1)S(1)}, bf16[768,384]{1,0:T(8,128)(2,1)S(1)}, u32[]{:S(2)}, u32[]{:S(2)}) %collective-permute-start.42) | collective-permute-done | bytes 589856 | tf_op jit(solution)/shard_map/ppermute | solution.py:830
  894.7 24.4 %collective-permute-done.43 = bf16[768,384]{1,0:T(8,128)(2,1)S(1)} collective-permute-done((bf16[768,384]{1,0:T(8,128)(2,1)S(1)}, bf16[768,384]{1,0:T(8,128)(2,1)S(1)}, u32[]{:S(2)}, u32[]{:S(2)}) %collective-permute-start.43) | collective-permute-done | bytes 589856 | tf_op jit(solution)/shard_map/ppermute | solution.py:830
  926.7 12.6 %collective-permute-start.50 = (bf16[576,384]{1,0:T(8,128)(2,1)}, bf16[576,384]{1,0:T(8,128)(2,1)}, u32[]{:S(2)}, u32[]{:S(2)}) collective-permute-start(bf16[576,384]{1,0:T(8,128)(2,1)} %get-tuple-element.212), channel_id=1, source_target_pairs={{0,1},{1,2},{2,3},{3,0},{4,5},{5,6},{6,7},{7,4},{8,9},{9,10},{10,1... | collective-permute-start | bytes 1327112 | tf_op jit(solution)/shard_map/ppermute | solution.py:830
  950.2 16.6 %collective-permute-done.51 = bf16[576,384]{1,0:T(8,128)(2,1)} collective-permute-done((bf16[576,384]{1,0:T(8,128)(2,1)}, bf16[576,384]{1,0:T(8,128)(2,1)}, u32[]{:S(2)}, u32[]{:S(2)}) %collective-permute-start.51) | collective-permute-done | bytes 442400 | tf_op jit(solution)/shard_map/ppermute | solution.py:830
  985.5 10.5 collective-permute-start.48
  1021.5 14.8 %collective-permute-done.54 = bf16[576,384]{1,0:T(8,128)(2,1)S(1)} collective-permute-done((bf16[576,384]{1,0:T(8,128)(2,1)S(1)}, bf16[576,384]{1,0:T(8,128)(2,1)S(1)}, u32[]{:S(2)}, u32[]{:S(2)}) %collective-permute-start.54) | collective-permute-done | bytes 442400 | tf_op jit(solution)/shard_map/ppermute | solution.py:830
  1040.0 12.5 %collective-permute-start.57 = (bf16[384,1536]{1,0:T(8,128)(2,1)}, bf16[384,1536]{1,0:T(8,128)(2,1)S(1)}, u32[]{:S(2)}, u32[]{:S(2)}) collective-permute-start(bf16[384,1536]{1,0:T(8,128)(2,1)} %get-tuple-element.188), channel_id=1, source_target_pairs={{1,0},{5,1},{4,2},{0,3},{3,4},{7,5},{6,6},{2,7},{9,8},{13,9},{12,1... | collective-permute-start | bytes 3538952 | tf_op jit(solution)/shard_map/ppermute | solution.py:857
  1062.4 22.1 %collective-permute-done.58 = bf16[2,64,384]{2,1,0:T(8,128)(2,1)S(1)} collective-permute-done((bf16[2,64,384]{2,1,0:T(8,128)(2,1)S(1)}, bf16[2,64,384]{2,1,0:T(8,128)(2,1)S(1)}, u32[]{:S(2)}, u32[]{:S(2)}) %collective-permute-start.58) | collective-permute-done | bytes 98336 | tf_op jit(solution)/shard_map/ppermute | solution.py:830
  1084.7 21.0 %collective-permute-done.59 = bf16[2,64,384]{2,1,0:T(8,128)(2,1)S(1)} collective-permute-done((bf16[2,64,384]{2,1,0:T(8,128)(2,1)S(1)}, bf16[2,64,384]{2,1,0:T(8,128)(2,1)S(1)}, u32[]{:S(2)}, u32[]{:S(2)}) %collective-permute-start.59) | collective-permute-done | bytes 98336 | tf_op jit(solution)/shard_map/ppermute | solution.py:830
  1137.9 8.1 unpack.19
  (502 shorter events, 353.1 us)
Async XLA Ops:
  7.2 171.0 %all-gather.8.cloned.1.call-start = ((), (), s32[]{:S(2)}) async-start(), calls=%async_computation.4 | async-start | bytes 15925248 | tf_op jit(solution)/shard_map/all_gather | solution.py:867
  16.7 40.9 %collective-permute-start.1 = (bf16[64,4608]{1,0:T(8,128)(2,1)S(1)}, bf16[64,4608]{1,0:T(8,128)(2,1)}, u32[]{:S(2)}, u32[]{:S(2)}) collective-permute-start(bf16[64,4608]{1,0:T(8,128)(2,1)S(1)} %pad_maximum_fusion.5), channel_id=1, source_target_pairs={{0,2},{1,3},{2,0},{3,1},{4,6},{5,7},{6,4},{7,5},{8,10},{9,11},{10,... | collective-permute-start | bytes 1769480 | tf_op jit(solution)/shard_map/ppermute | solution.py:830
  19.3 39.3 %collective-permute-start.2 = (bf16[64,4608]{1,0:T(8,128)(2,1)S(1)}, bf16[64,4608]{1,0:T(8,128)(2,1)}, u32[]{:S(2)}, u32[]{:S(2)}) collective-permute-start(bf16[64,4608]{1,0:T(8,128)(2,1)S(1)} %pad_maximum_fusion.5), channel_id=1, source_target_pairs={{0,3},{1,0},{2,1},{3,2},{4,7},{5,4},{6,5},{7,6},{8,11},{9,8},{10,9... | collective-permute-start | bytes 1769480 | tf_op jit(solution)/shard_map/ppermute | solution.py:830
  61.0 280.8 %all-gather.10.cloned.1.call-start = ((), (), s32[]{:S(2)}) async-start(), calls=%async_computation.5 | async-start | bytes 15925248 | tf_op jit(solution)/shard_map/all_gather | solution.py:867
  75.4 30.3 %collective-permute-start.4 = (bf16[48,4608]{1,0:T(8,128)(2,1)S(1)}, bf16[48,4608]{1,0:T(8,128)(2,1)S(1)}, u32[]{:S(2)}, u32[]{:S(2)}) collective-permute-start(bf16[48,4608]{1,0:T(8,128)(2,1)S(1)} %pad_maximum_fusion.7), channel_id=1, source_target_pairs={{0,2},{1,3},{2,0},{3,1},{4,6},{5,7},{6,4},{7,5},{8,10},{9,11},{10,... | collective-permute-start | bytes 1327112 | tf_op jit(solution)/shard_map/ppermute | solution.py:830
  78.1 27.6 %collective-permute-start.5 = (bf16[48,4608]{1,0:T(8,128)(2,1)S(1)}, bf16[48,4608]{1,0:T(8,128)(2,1)S(1)}, u32[]{:S(2)}, u32[]{:S(2)}) collective-permute-start(bf16[48,4608]{1,0:T(8,128)(2,1)S(1)} %pad_maximum_fusion.7), channel_id=1, source_target_pairs={{0,3},{1,0},{2,1},{3,2},{4,7},{5,4},{6,5},{7,6},{8,11},{9,8},{10,9... | collective-permute-start | bytes 1327112 | tf_op jit(solution)/shard_map/ppermute | solution.py:830
  107.0 318.6 %all-gather.12.cloned.1.call-start = ((), (), s32[]{:S(2)}) async-start(), calls=%async_computation.6 | async-start | bytes 21233664 | tf_op jit(solution)/shard_map/all_gather | solution.py:867
  121.8 32.4 %collective-permute-start.6 = (bf16[384,1536]{1,0:T(8,128)(2,1)}, bf16[384,1536]{1,0:T(8,128)(2,1)S(1)}, u32[]{:S(2)}, u32[]{:S(2)}) collective-permute-start(bf16[384,1536]{1,0:T(8,128)(2,1)} %get-tuple-element.206), channel_id=1, source_target_pairs={{0,0},{1,4},{2,5},{3,1},{4,2},{5,6},{6,7},{7,3},{8,8},{9,12},{10,1... | collective-permute-start | bytes 3538952 | tf_op jit(solution)/shard_map/ppermute | solution.py:844
  123.7 51.2 %collective-permute-start.7 = (bf16[384,1536]{1,0:T(8,128)(2,1)S(1)}, bf16[384,1536]{1,0:T(8,128)(2,1)S(1)}, u32[]{:S(2)}, u32[]{:S(2)}) collective-permute-start(bf16[384,1536]{1,0:T(8,128)(2,1)S(1)} %get-tuple-element.205), channel_id=1, source_target_pairs={{0,1},{1,5},{2,4},{3,0},{4,3},{5,7},{6,6},{7,2},{8,9},{9,13},{10,1... | collective-permute-start | bytes 3538952 | tf_op jit(solution)/shard_map/ppermute | solution.py:845
  189.1 53.7 %collective-permute-start.14 = (bf16[768,3072]{1,0:T(8,128)(2,1)S(1)}, bf16[768,3072]{1,0:T(8,128)(2,1)S(1)}, u32[]{:S(2)}, u32[]{:S(2)}) collective-permute-start(bf16[768,3072]{1,0:T(8,128)(2,1)S(1)} %fusion.14.own_k.own_v), channel_id=1, source_target_pairs={{0,4},{4,0},{1,5},{5,1},{2,6},{6,2},{3,7},{7,3},{8,12},{12,8},{9,1... | collective-permute-start | bytes 14155784 | tf_op jit(solution)/shard_map/ppermute | solution.py:955
  201.7 26.9 %collective-permute-start.10 = (bf16[48,6144]{1,0:T(8,128)(2,1)S(1)}, bf16[48,6144]{1,0:T(8,128)(2,1)S(1)}, u32[]{:S(2)}, u32[]{:S(2)}) collective-permute-start(bf16[48,6144]{1,0:T(8,128)(2,1)S(1)} %get-tuple-element.85), channel_id=1, source_target_pairs={{0,2},{1,3},{2,0},{3,1},{4,6},{5,7},{6,4},{7,5},{8,10},{9,11},{10,... | collective-permute-start | bytes 1769480 | tf_op jit(solution)/shard_map/ppermute | solution.py:830
  201.8 41.0 %collective-permute-start.11 = (bf16[48,6144]{1,0:T(8,128)(2,1)S(1)}, bf16[48,6144]{1,0:T(8,128)(2,1)S(1)}, u32[]{:S(2)}, u32[]{:S(2)}) collective-permute-start(bf16[48,6144]{1,0:T(8,128)(2,1)S(1)} %get-tuple-element.85), channel_id=1, source_target_pairs={{0,3},{1,0},{2,1},{3,2},{4,7},{5,4},{6,5},{7,6},{8,11},{9,8},{10,9... | collective-permute-start | bytes 1769480 | tf_op jit(solution)/shard_map/ppermute | solution.py:830
  201.8 41.0 %collective-permute-start.9 = (bf16[48,6144]{1,0:T(8,128)(2,1)S(1)}, bf16[48,6144]{1,0:T(8,128)(2,1)S(1)}, u32[]{:S(2)}, u32[]{:S(2)}) collective-permute-start(bf16[48,6144]{1,0:T(8,128)(2,1)S(1)} %get-tuple-element.85), channel_id=1, source_target_pairs={{0,1},{1,2},{2,3},{3,0},{4,5},{5,6},{6,7},{7,4},{8,9},{9,10},{10,1... | collective-permute-start | bytes 1769480 | tf_op jit(solution)/shard_map/ppermute | solution.py:830
  246.5 246.5 %all-gather.14.cloned.1.call-start = ((), (), s32[]{:S(2)}) async-start(), calls=%async_computation.7 | async-start | bytes 21233664 | tf_op jit(solution)/shard_map/all_gather | solution.py:867
  254.6 83.1 %collective-permute-start.15 = (bf16[64,1536]{1,0:T(8,128)(2,1)}, bf16[64,1536]{1,0:T(8,128)(2,1)}, u32[]{:S(2)}, u32[]{:S(2)}) collective-permute-start(bf16[64,1536]{1,0:T(8,128)(2,1)} %get-tuple-element.217), channel_id=1, source_target_pairs={{0,1},{1,2},{2,3},{3,0},{4,5},{5,6},{6,7},{7,4},{8,9},{9,10},{10,1... | collective-permute-start | bytes 589832 | tf_op jit(solution)/shard_map/ppermute | solution.py:830
  265.9 71.7 %collective-permute-start.16 = (bf16[64,1536]{1,0:T(8,128)(2,1)}, bf16[64,1536]{1,0:T(8,128)(2,1)}, u32[]{:S(2)}, u32[]{:S(2)}) collective-permute-start(bf16[64,1536]{1,0:T(8,128)(2,1)} %get-tuple-element.216), channel_id=1, source_target_pairs={{0,2},{1,3},{2,0},{3,1},{4,6},{5,7},{6,4},{7,5},{8,10},{9,11},{10,... | collective-permute-start | bytes 589832 | tf_op jit(solution)/shard_map/ppermute | solution.py:830
  267.1 70.6 %collective-permute-start.17 = (bf16[64,1536]{1,0:T(8,128)(2,1)}, bf16[64,1536]{1,0:T(8,128)(2,1)}, u32[]{:S(2)}, u32[]{:S(2)}) collective-permute-start(bf16[64,1536]{1,0:T(8,128)(2,1)} %get-tuple-element.215), channel_id=1, source_target_pairs={{0,3},{1,0},{2,1},{3,2},{4,7},{5,4},{6,5},{7,6},{8,11},{9,8},{10,9... | collective-permute-start | bytes 589832 | tf_op jit(solution)/shard_map/ppermute | solution.py:830
  337.7 41.7 %collective-permute-start.20 = (bf16[192,1536]{1,0:T(8,128)(2,1)}, bf16[192,1536]{1,0:T(8,128)(2,1)}, u32[]{:S(2)}, u32[]{:S(2)}) collective-permute-start(bf16[192,1536]{1,0:T(8,128)(2,1)} %get-tuple-element.96), channel_id=1, source_target_pairs={{0,2},{1,3},{2,0},{3,1},{4,6},{5,7},{6,4},{7,5},{8,10},{9,11},{10,... | collective-permute-start | bytes 1769480 | tf_op jit(solution)/shard_map/ppermute | solution.py:830
  338.6 40.8 %collective-permute-start.21 = (bf16[192,1536]{1,0:T(8,128)(2,1)}, bf16[192,1536]{1,0:T(8,128)(2,1)}, u32[]{:S(2)}, u32[]{:S(2)}) collective-permute-start(bf16[192,1536]{1,0:T(8,128)(2,1)} %get-tuple-element.96), channel_id=1, source_target_pairs={{0,3},{1,0},{2,1},{3,2},{4,7},{5,4},{6,5},{7,6},{8,11},{9,8},{10,9... | collective-permute-start | bytes 1769480 | tf_op jit(solution)/shard_map/ppermute | solution.py:830
  385.2 346.8 %reduce-scatter.5.cloned.1.call-start = ((), (), s32[]{:S(2)}) async-start(), calls=%async_computation.8 | async-start | bytes 11796480 | tf_op jit(solution)/shard_map/reduce_scatter | solution.py:1010
  409.2 77.5 %collective-permute-start.23 = (bf16[384,1536]{1,0:T(8,128)(2,1)}, bf16[384,1536]{1,0:T(8,128)(2,1)}, u32[]{:S(2)}, u32[]{:S(2)}) collective-permute-start(bf16[384,1536]{1,0:T(8,128)(2,1)} %get-tuple-element.200), channel_id=1, source_target_pairs={{0,0},{1,4},{2,5},{3,1},{4,2},{5,6},{6,7},{7,3},{8,8},{9,12},{10,1... | collective-permute-start | bytes 3538952 | tf_op jit(solution)/shard_map/ppermute | solution.py:844
  419.5 67.2 %collective-permute-start.24 = (bf16[384,1536]{1,0:T(8,128)(2,1)}, bf16[384,1536]{1,0:T(8,128)(2,1)}, u32[]{:S(2)}, u32[]{:S(2)}) collective-permute-start(bf16[384,1536]{1,0:T(8,128)(2,1)} %get-tuple-element.199), channel_id=1, source_target_pairs={{0,1},{1,5},{2,4},{3,0},{4,3},{5,7},{6,6},{7,2},{8,9},{9,13},{10,1... | collective-permute-start | bytes 3538952 | tf_op jit(solution)/shard_map/ppermute | solution.py:845
  526.4 34.3 %collective-permute-start.26 = (bf16[768,6144]{1,0:T(8,128)(2,1)}, bf16[768,6144]{1,0:T(8,128)(2,1)}, u32[]{:S(2)}, u32[]{:S(2)}) collective-permute-start(bf16[768,6144]{1,0:T(8,128)(2,1)} %convolution_convert_fusion.2), channel_id=1, source_target_pairs={{0,4},{4,0},{1,5},{5,1},{2,6},{6,2},{3,7},{7,3},{8,12},{12,8},{9,1... | collective-permute-start | bytes 28311560 | tf_op jit(solution)/shard_map/ppermute | solution.py:1005
  529.5 31.2 %collective-permute-start.22 = (bf16[384,1536]{1,0:T(8,128)(2,1)S(1)}, bf16[384,1536]{1,0:T(8,128)(2,1)}, u32[]{:S(2)}, u32[]{:S(2)}) collective-permute-start(bf16[384,1536]{1,0:T(8,128)(2,1)S(1)} %get-tuple-element.201), channel_id=1, source_target_pairs={{0,0},{4,1},{5,2},{1,3},{2,4},{6,5},{7,6},{3,7},{8,8},{12,9},{13,1... | collective-permute-start | bytes 3538952 | tf_op jit(solution)/shard_map/ppermute | solution.py:1033
  574.8 300.1 %reduce-scatter.7.cloned.1.call-start = ((), (), s32[]{:S(2)}) async-start(), calls=%async_computation.9 | async-start | bytes 11796480 | tf_op jit(solution)/shard_map/reduce_scatter | solution.py:1010
  588.6 35.0 %collective-permute-start.27 = (bf16[3072,1536]{1,0:T(8,128)(2,1)}, bf16[3072,1536]{1,0:T(8,128)(2,1)}, u32[]{:S(2)}, u32[]{:S(2)}) collective-permute-start(bf16[3072,1536]{1,0:T(8,128)(2,1)} %convolution_convert_fusion.1), channel_id=1, source_target_pairs={{0,4},{4,0},{1,5},{5,1},{2,6},{6,2},{3,7},{7,3},{8,12},{12,8},{9,1... | collective-permute-start | bytes 28311560 | tf_op jit(solution)/shard_map/ppermute | solution.py:1005
  590.4 33.2 %collective-permute-start.25 = (bf16[384,1536]{1,0:T(8,128)(2,1)}, bf16[384,1536]{1,0:T(8,128)(2,1)}, u32[]{:S(2)}, u32[]{:S(2)}) collective-permute-start(bf16[384,1536]{1,0:T(8,128)(2,1)} %get-tuple-element.105), channel_id=1, source_target_pairs={{1,0},{5,1},{4,2},{0,3},{3,4},{7,5},{6,6},{2,7},{9,8},{13,9},{12,1... | collective-permute-start | bytes 3538952 | tf_op jit(solution)/shard_map/ppermute | solution.py:1043
  637.6 285.1 %reduce-scatter.11.cloned.1.call-start = ((), (), s32[]{:S(2)}) async-start(), calls=%async_computation.11 | async-start | bytes 10321920 | tf_op jit(solution)/shard_map/reduce_scatter | solution.py:1010
  656.9 27.7 %collective-permute-start.28 = (bf16[768,1536]{1,0:T(8,128)(2,1)}, bf16[768,1536]{1,0:T(8,128)(2,1)}, u32[]{:S(2)}, u32[]{:S(2)}) collective-permute-start(bf16[768,1536]{1,0:T(8,128)(2,1)} %convolution_convert_fusion.5), channel_id=1, source_target_pairs={{0,4},{4,0},{1,5},{5,1},{2,6},{6,2},{3,7},{7,3},{8,12},{12,8},{9,1... | collective-permute-start | bytes 7077896 | tf_op jit(solution)/shard_map/ppermute | solution.py:1005
  676.0 31.8 %collective-permute-start.33 = (bf16[64,1536]{1,0:T(8,128)(2,1)S(1)}, bf16[64,1536]{1,0:T(8,128)(2,1)S(1)}, u32[]{:S(2)}, u32[]{:S(2)}) collective-permute-start(bf16[64,1536]{1,0:T(8,128)(2,1)S(1)} %get-tuple-element.171), channel_id=1, source_target_pairs={{0,2},{1,3},{2,0},{3,1},{4,6},{5,7},{6,4},{7,5},{8,10},{9,11},{10,... | collective-permute-start | bytes 589832 | tf_op jit(solution)/shard_map/ppermute | solution.py:830
  678.3 29.6 %collective-permute-start.34 = (bf16[64,1536]{1,0:T(8,128)(2,1)S(1)}, bf16[64,1536]{1,0:T(8,128)(2,1)S(1)}, u32[]{:S(2)}, u32[]{:S(2)}) collective-permute-start(bf16[64,1536]{1,0:T(8,128)(2,1)S(1)} %get-tuple-element.171), channel_id=1, source_target_pairs={{0,3},{1,0},{2,1},{3,2},{4,7},{5,4},{6,5},{7,6},{8,11},{9,8},{10,9... | collective-permute-start | bytes 589832 | tf_op jit(solution)/shard_map/ppermute | solution.py:830
  726.8 277.7 %reduce-scatter.9.cloned.1.call-start = ((), (), s32[]{:S(2)}) async-start(), calls=%async_computation.10 | async-start | bytes 8847360 | tf_op jit(solution)/shard_map/reduce_scatter | solution.py:1010
  733.5 90.3 %collective-permute-start.36 = (bf16[192,1536]{1,0:T(8,128)(2,1)S(1)}, bf16[192,1536]{1,0:T(8,128)(2,1)S(1)}, u32[]{:S(2)}, u32[]{:S(2)}) collective-permute-start(bf16[192,1536]{1,0:T(8,128)(2,1)S(1)} %get-tuple-element.194), channel_id=1, source_target_pairs={{0,1},{1,2},{2,3},{3,0},{4,5},{5,6},{6,7},{7,4},{8,9},{9,10},{10,1... | collective-permute-start | bytes 1769480 | tf_op jit(solution)/shard_map/ppermute | solution.py:830
  741.2 82.6 %collective-permute-start.37 = (bf16[192,1536]{1,0:T(8,128)(2,1)S(1)}, bf16[192,1536]{1,0:T(8,128)(2,1)}, u32[]{:S(2)}, u32[]{:S(2)}) collective-permute-start(bf16[192,1536]{1,0:T(8,128)(2,1)S(1)} %get-tuple-element.193), channel_id=1, source_target_pairs={{0,2},{1,3},{2,0},{3,1},{4,6},{5,7},{6,4},{7,5},{8,10},{9,11},{10,... | collective-permute-start | bytes 1769480 | tf_op jit(solution)/shard_map/ppermute | solution.py:830
  743.0 80.7 %collective-permute-start.38 = (bf16[192,1536]{1,0:T(8,128)(2,1)S(1)}, bf16[192,1536]{1,0:T(8,128)(2,1)}, u32[]{:S(2)}, u32[]{:S(2)}) collective-permute-start(bf16[192,1536]{1,0:T(8,128)(2,1)S(1)} %get-tuple-element.192), channel_id=1, source_target_pairs={{0,3},{1,0},{2,1},{3,2},{4,7},{5,4},{6,5},{7,6},{8,11},{9,8},{10,9... | collective-permute-start | bytes 1769480 | tf_op jit(solution)/shard_map/ppermute | solution.py:830
  872.9 243.9 %all-gather.18.cloned.1.call-start = ((), (), s32[]{:S(2)}) async-start(), calls=%async_computation.13 | async-start | bytes 17252352 | tf_op jit(solution)/shard_map/all_gather | solution.py:1178
  876.6 42.4 %collective-permute-start.43 = (bf16[768,384]{1,0:T(8,128)(2,1)S(1)}, bf16[768,384]{1,0:T(8,128)(2,1)S(1)}, u32[]{:S(2)}, u32[]{:S(2)}) collective-permute-start(bf16[768,384]{1,0:T(8,128)(2,1)S(1)} %get-tuple-element.190), channel_id=1, source_target_pairs={{0,2},{1,3},{2,0},{3,1},{4,6},{5,7},{6,4},{7,5},{8,10},{9,11},{10,... | collective-permute-start | bytes 1769480 | tf_op jit(solution)/shard_map/ppermute | solution.py:830
  877.0 42.1 %collective-permute-start.44 = (bf16[768,384]{1,0:T(8,128)(2,1)S(1)}, bf16[768,384]{1,0:T(8,128)(2,1)S(1)}, u32[]{:S(2)}, u32[]{:S(2)}) collective-permute-start(bf16[768,384]{1,0:T(8,128)(2,1)S(1)} %get-tuple-element.189), channel_id=1, source_target_pairs={{0,3},{1,0},{2,1},{3,2},{4,7},{5,4},{6,5},{7,6},{8,11},{9,8},{10,9... | collective-permute-start | bytes 1769480 | tf_op jit(solution)/shard_map/ppermute | solution.py:830
  939.2 27.5 %collective-permute-start.51 = (bf16[576,384]{1,0:T(8,128)(2,1)}, bf16[576,384]{1,0:T(8,128)(2,1)}, u32[]{:S(2)}, u32[]{:S(2)}) collective-permute-start(bf16[576,384]{1,0:T(8,128)(2,1)} %get-tuple-element.211), channel_id=1, source_target_pairs={{0,2},{1,3},{2,0},{3,1},{4,6},{5,7},{6,4},{7,5},{8,10},{9,11},{10,... | collective-permute-start | bytes 1327112 | tf_op jit(solution)/shard_map/ppermute | solution.py:830
  939.2 28.5 %collective-permute-start.52 = (bf16[576,384]{1,0:T(8,128)(2,1)}, bf16[576,384]{1,0:T(8,128)(2,1)}, u32[]{:S(2)}, u32[]{:S(2)}) collective-permute-start(bf16[576,384]{1,0:T(8,128)(2,1)} %get-tuple-element.210), channel_id=1, source_target_pairs={{0,3},{1,0},{2,1},{3,2},{4,7},{5,4},{6,5},{7,6},{8,11},{9,8},{10,9... | collective-permute-start | bytes 1327112 | tf_op jit(solution)/shard_map/ppermute | solution.py:830
  970.2 186.6 %all-gather.16.cloned.1.call-start = ((), (), s32[]{:S(2)}) async-start(), calls=%async_computation.12 | async-start | bytes 3981312 | tf_op jit(solution)/shard_map/all_gather | solution.py:1192
  1008.0 28.4 %collective-permute-start.54 = (bf16[576,384]{1,0:T(8,128)(2,1)S(1)}, bf16[576,384]{1,0:T(8,128)(2,1)S(1)}, u32[]{:S(2)}, u32[]{:S(2)}) collective-permute-start(bf16[576,384]{1,0:T(8,128)(2,1)S(1)} %get-tuple-element.208), channel_id=1, source_target_pairs={{0,2},{1,3},{2,0},{3,1},{4,6},{5,7},{6,4},{7,5},{8,10},{9,11},{10,... | collective-permute-start | bytes 1327112 | tf_op jit(solution)/shard_map/ppermute | solution.py:830
  1010.9 25.4 %collective-permute-start.55 = (bf16[576,384]{1,0:T(8,128)(2,1)S(1)}, bf16[576,384]{1,0:T(8,128)(2,1)S(1)}, u32[]{:S(2)}, u32[]{:S(2)}) collective-permute-start(bf16[576,384]{1,0:T(8,128)(2,1)S(1)} %get-tuple-element.207), channel_id=1, source_target_pairs={{0,3},{1,0},{2,1},{3,2},{4,7},{5,4},{6,5},{7,6},{8,11},{9,8},{10,9... | collective-permute-start | bytes 1327112 | tf_op jit(solution)/shard_map/ppermute | solution.py:830
  1038.0 78.7 %collective-permute-start.56 = (bf16[384,1536]{1,0:T(8,128)(2,1)}, bf16[384,1536]{1,0:T(8,128)(2,1)S(1)}, u32[]{:S(2)}, u32[]{:S(2)}) collective-permute-start(bf16[384,1536]{1,0:T(8,128)(2,1)} %get-tuple-element.187), channel_id=1, source_target_pairs={{0,0},{4,1},{5,2},{1,3},{2,4},{6,5},{7,6},{3,7},{8,8},{12,9},{13,1... | collective-permute-start | bytes 3538952 | tf_op jit(solution)/shard_map/ppermute | solution.py:857
  1040.0 76.8 %collective-permute-start.57 = (bf16[384,1536]{1,0:T(8,128)(2,1)}, bf16[384,1536]{1,0:T(8,128)(2,1)S(1)}, u32[]{:S(2)}, u32[]{:S(2)}) collective-permute-start(bf16[384,1536]{1,0:T(8,128)(2,1)} %get-tuple-element.188), channel_id=1, source_target_pairs={{1,0},{5,1},{4,2},{0,3},{3,4},{7,5},{6,6},{2,7},{9,8},{13,9},{12,1... | collective-permute-start | bytes 3538952 | tf_op jit(solution)/shard_map/ppermute | solution.py:857
  1055.9 28.7 %collective-permute-start.58 = (bf16[2,64,384]{2,1,0:T(8,128)(2,1)S(1)}, bf16[2,64,384]{2,1,0:T(8,128)(2,1)S(1)}, u32[]{:S(2)}, u32[]{:S(2)}) collective-permute-start(bf16[2,64,384]{2,1,0:T(8,128)(2,1)S(1)} %copy-done.58), channel_id=1, source_target_pairs={{0,1},{1,2},{2,3},{3,0},{4,5},{5,6},{6,7},{7,4},{8,9},{9,10},{10,1... | collective-permute-start | bytes 294920 | tf_op jit(solution)/shard_map/ppermute | solution.py:830
  1056.5 49.2 %collective-permute-start.59 = (bf16[2,64,384]{2,1,0:T(8,128)(2,1)S(1)}, bf16[2,64,384]{2,1,0:T(8,128)(2,1)S(1)}, u32[]{:S(2)}, u32[]{:S(2)}) collective-permute-start(bf16[2,64,384]{2,1,0:T(8,128)(2,1)S(1)} %copy-done.58), channel_id=1, source_target_pairs={{0,2},{1,3},{2,0},{3,1},{4,6},{5,7},{6,4},{7,5},{8,10},{9,11},{10,... | collective-permute-start | bytes 294920 | tf_op jit(solution)/shard_map/ppermute | solution.py:830
  1059.3 46.5 %collective-permute-start.60 = (bf16[2,64,384]{2,1,0:T(8,128)(2,1)S(1)}, bf16[2,64,384]{2,1,0:T(8,128)(2,1)S(1)}, u32[]{:S(2)}, u32[]{:S(2)}) collective-permute-start(bf16[2,64,384]{2,1,0:T(8,128)(2,1)S(1)} %copy-done.58), channel_id=1, source_target_pairs={{0,3},{1,0},{2,1},{3,2},{4,7},{5,4},{6,5},{7,6},{8,11},{9,8},{10,9... | collective-permute-start | bytes 294920 | tf_op jit(solution)/shard_map/ppermute | solution.py:830
  (113 other events, 1627.0 us)
Sparse Core Ops, SparseCore 0:
  61.1 90.6 all-gather.7
  154.2 78.7 all-gather.9
  246.6 107.9 all-gather.11
  385.3 107.7 all-gather.13
  575.0 97.8 reduce-scatter.4
  676.4 95.0 reduce-scatter.6
  775.3 85.3 reduce-scatter.10
  873.0 74.3 reduce-scatter.8
  970.3 94.5 all-gather.17
  1116.9 37.4 all-gather.15

commit v9 on v8

--- a/solution.py
+++ b/solution.py
@@ -956,13 +956,15 @@
     queries = project(after(hidden_one, kv), qkv_matrix[:, :width]).astype(jnp.bfloat16)
     expand_came = held(expand_came, kv_other, queries)
     expand_matrix = from_replicas(line_up(expand_share, expand_came))
+    reduce_share = share_of(feed_down_weight)
+    reduce_came = hops(after(reduce_share, *expand_came))
     output_matrix = rest[:, :width]
     probe_matrix = rest[:, width : 2 * width]
     merge_matrix = rest[:, 2 * width :]
     mixed_self, lse = self_attend(after(places, *expand_came), queries, kv, kv_other)
-    reduce_share = share_of(feed_down_weight)
+    reduce_came = held(reduce_came, mixed_self)
+    reduce_matrix = from_replicas(line_up(reduce_share, reduce_came))
     text_came = held(text_came, mixed_self)
-    reduce_came = hops(after(reduce_share, *text_came))
     text_half = lax.dynamic_index_in_dim(text_part, shard, 0, keepdims=False).astype(jnp.float32)
     for values in text_came:
         text_half += values.astype(jnp.float32)
@@ -976,8 +978,6 @@
         jnp.bfloat16
     )
     probes = project(hidden_two, probe_matrix).astype(jnp.bfloat16)
-    reduce_came = held(reduce_came, probes)
-    reduce_matrix = from_replicas(line_up(reduce_share, reduce_came))
     teacher_came = to_chip(after(teacher, *reduce_came, probes))
     cross_mixed = cross_attend(probes, lookups, contents, present)
     after_cross = after_self + project(cross_mixed, merge_matrix)
@@ -1114,11 +1114,13 @@
     )
     text_own = text_own.astype(jnp.bfloat16)
     down_came = shard_hops(down_sum)
+    text_came = hops(text_own)
     grad_queries, own_keys, own_values, other_keys, other_values = self_attend_back(
         places, queries, kv, kv_other, mixed_self, after(grad_mixed, middle, text_own), lse
     )
+    text_came = held(text_came, grad_queries)
     down_came = held(down_came, grad_queries)
-    other_keys, other_values = held([other_keys, other_values], *down_came)
+    other_keys, other_values = held([other_keys, other_values], *text_came, *down_came)
     own_keys += lax.ppermute(other_keys, "core", swap)
     own_values += lax.ppermute(other_values, "core", swap)
     down_piece = over_shard(down_sum, down_came)
@@ -1130,13 +1132,14 @@
     qkv_ours = ours_of(after(qkv_grads, grad_hidden_one), hidden_one, qkv_theirs)
     up_came = held(up_came, grad_hidden_one)
     up_piece = over_shard(up_sum, up_came)
+    text_grad = line_up(text_own, text_came).astype(jnp.float32)
+    text_grad = text_grad.transpose(1, 2, 0, 3).reshape(text_states.shape)
     qkv_sum = over_outer(qkv_ours)
     grad_norm, gain_self, bias_self = norm_back(
         after(grad_hidden_one, qkv_ours, *up_came), inputs, parts_one, norms[0]
     )
     middle_kept = after(middle_sum[: middle_rows - text_split], qkv_ours, *up_came)
     middle_came = shard_hops(middle_kept)
-
     small = jnp.stack(
         [
             gain_self,
@@ -1149,24 +1152,18 @@
             jnp.zeros((width,), jnp.float32),
         ]
     )
-    for axis, pairs in (
-        ("core", swap),
-        ("x", swap),
-        ("y", swap),
-        ("shard", [(0, 1), (1, 0), (2, 3), (3, 2)]),
-        ("shard", [(0, 2), (2, 0), (1, 3), (3, 1)]),
-    ):
-        small += lax.ppermute(small, axis, pairs)
+    for axis in ("core", "x", "y"):
+        small += lax.ppermute(small, axis, swap)
     late_came = shard_hops(after(qkv_sum, *middle_came, small))
+    small_came = shard_hops(small)
+    small_own = lax.dynamic_slice_in_dim(small, shard * block, block, 1)
+    for part in small_came:
+        small_own += part
+    loss = small_own[6, 0] / (width * count)
     frames_came = from_chip(
-        after((grad_after_self + grad_norm).astype(jnp.bfloat16), *late_came)
+        after((grad_after_self + grad_norm).astype(jnp.bfloat16), *late_came, *small_came)
     )
     frames_grad = by_slot(*frames_came).astype(jnp.float32)
-    text_came = hops(after(text_own, *late_came))
-    text_grad = line_up(text_own, text_came).astype(jnp.float32)
-    text_grad = text_grad.transpose(1, 2, 0, 3).reshape(text_states.shape)
-    loss = small[6, 0] / (width * count)
-    small_own = lax.dynamic_slice_in_dim(small, shard * block, block, 1)
 
     middle_piece = over_shard(middle_kept, middle_came)
     early = jnp.concatenate(
@@ -1175,7 +1172,7 @@
         + [text_piece, middle_piece],
         axis=0,
     )
-    early = lax.all_gather(early, REPLICAS, axis=0)
+    early = lax.all_gather(after(early, text_grad), REPLICAS, axis=0)
     piece = width // replicas
     square = (block, width)
     up_grad = unpack(early, hidden_units // replicas, 0, (block, hidden_units), 0, 1)
@@ -1189,9 +1186,7 @@
     probe_grad = unpack(early, piece, at + 1, square, 0, 2)
     merge_grad = unpack(early, piece, at + 2, square, 0, 2)
     late = over_shard(qkv_sum, late_came)
-    late = lax.all_gather(
-        after(late, early, text_grad, *frames_came), REPLICAS, axis=0, tiled=True
-    )
+    late = lax.all_gather(after(late, early, *frames_came), REPLICAS, axis=0, tiled=True)
     late = late.reshape(-1, block, block)
     qkv_grad = [unpack(late, block, 0, square, 2 * i, 2) for i in range(3)]
     return (

time: 1190 us -> 1130 us (0.950)
  waiting for transfers between devices: 295 us -> 266 us
  starting transfers between devices: 181 us -> 162 us
    ppermute x33 -> x36, waiting for transfers between devices: 244 us -> 179 us  [hop(): return lax.ppermute(values, 'shard', pairs)]
    ppermute x2, waiting for transfers between devices: 0.01 us -> 29.9 us  [from_chip(): return (lax.ppermute(one, spot, back[0]), lax.ppermute(two, spot, back[1]))]
    ppermute x5 -> x3, starting transfers between devices: 17.9 us -> 3.21 us  [clip_body(): small += lax.ppermute(small, axis, swap)]
    all_gather x2, waiting for transfers between devices: 0.01 us -> 13 us  [the longest x1 13 us: clip_body(): lax.all_gather(after(late, early, *frames_came), REPLICAS, axis=0, tiled=...]
    ppermute x33 -> x36, starting transfers between devices: 91 us -> 94.1 us  [hop(): return lax.ppermute(values, 'shard', pairs)]
    unnamed x189 -> x223, local copies, waits for them, and re-layouts: 43.8 us -> 46.5 us
  transfers between devices with their start and end apart: 71 -> 72, of which waited for: 31 -> 27; matrix products, arithmetic and copies ran while one was open for 35% -> 36% of each run, Pallas kernels for 14% -> 15%
where the time goes in v9:
time: 1130 us; the launch traced here: 1120 us
  matrix products  301 us (27%)
  waiting for transfers between devices  266 us (24%)
  Pallas kernels  174 us (15%)
  starting transfers between devices  162 us (14%)
  local copies, waits for them, and re-layouts  109 us (10%)
  other arithmetic  81.6 us (7%)
  between operations  21.9 us (2%)
    ppermute x36, waiting for transfers between devices, hop(): return lax.ppermute(values, 'shard', pairs)  179 us
    dot_general x8, matrix products, project(): return jnp.dot(left, right, preferred_element_type=jnp.float32)  121 us
    ppermute x36, starting transfers between devices, hop(): return lax.ppermute(values, 'shard', pairs)  94.1 us
    dot_general x7, matrix products, back_project(): jnp.einsum('re,de->rd', grads, matrix, preferred_element_type=jnp.float32)  92.7 us
    dot_general x13, matrix products, outer_sum(): jnp.einsum('rd,re->de', left, right, preferred_element_type=jnp.float32)  87.8 us
    pallas_call x1, Pallas kernels, self_attend_back(): pl.pallas_call(self_backward_kernel, out_shape=(jax.ShapeDtypeStruct((row...  69.9 us
    pallas_call x1, Pallas kernels, self_attend(): pl.pallas_call(self_forward_kernel, out_shape=(jax.ShapeDtypeStruct((rows...  58.6 us
    unnamed x223, local copies, waits for them, and re-layouts  46.5 us
  transfers between devices with their start and end apart: 72, of which 27 were waited for; matrix products, arithmetic and copies ran while one was open for 36% of the time, Pallas kernels for 15%

profile of v9, /device:TPU:0, one launch (start us, length us, event | category | flops | bytes accessed | tf_op | source)
XLA Modules:
  0.0 1116.0 jit_solution(3327288743214676169)
XLA Ops:
  20.9 12.3 %collective-permute-done = bf16[64,4608]{1,0:T(8,128)(2,1)} collective-permute-done((bf16[64,4608]{1,0:T(8,128)(2,1)S(1)}, bf16[64,4608]{1,0:T(8,128)(2,1)}, u32[]{:S(2)}, u32[]{:S(2)}) %collective-permute-start) | collective-permute-done | bytes 589856 | tf_op jit(solution)/shard_map/ppermute | solution.py:830
  34.2 23.4 %collective-permute-done.1 = bf16[64,4608]{1,0:T(8,128)(2,1)} collective-permute-done((bf16[64,4608]{1,0:T(8,128)(2,1)S(1)}, bf16[64,4608]{1,0:T(8,128)(2,1)}, u32[]{:S(2)}, u32[]{:S(2)}) %collective-permute-start.1) | collective-permute-done | bytes 589856 | tf_op jit(solution)/shard_map/ppermute | solution.py:830
  63.1 12.1 %collective-permute-start.3 = (bf16[48,4608]{1,0:T(8,128)(2,1)S(1)}, bf16[48,4608]{1,0:T(8,128)(2,1)S(1)}, u32[]{:S(2)}, u32[]{:S(2)}) collective-permute-start(bf16[48,4608]{1,0:T(8,128)(2,1)S(1)} %pad_maximum_fusion.7), channel_id=1, source_target_pairs={{0,1},{1,2},{2,3},{3,0},{4,5},{5,6},{6,7},{7,4},{8,9},{9,10},{10,1... | collective-permute-start | bytes 1327112 | tf_op jit(solution)/shard_map/ppermute | solution.py:830
  78.1 10.4 collective-permute-done.3
  88.5 17.1 %collective-permute-done.4 = bf16[48,4608]{1,0:T(8,128)(2,1)S(1)} collective-permute-done((bf16[48,4608]{1,0:T(8,128)(2,1)S(1)}, bf16[48,4608]{1,0:T(8,128)(2,1)S(1)}, u32[]{:S(2)}, u32[]{:S(2)}) %collective-permute-start.4) | collective-permute-done | bytes 442400 | tf_op jit(solution)/shard_map/ppermute | solution.py:830
  123.7 11.1 collective-permute-start.7
  154.2 20.8 %collective-permute-done.7 = bf16[384,1536]{1,0:T(8,128)(2,1)S(1)} collective-permute-done((bf16[384,1536]{1,0:T(8,128)(2,1)S(1)}, bf16[384,1536]{1,0:T(8,128)(2,1)S(1)}, u32[]{:S(2)}, u32[]{:S(2)}) %collective-permute-start.7) | collective-permute-done | bytes 1179680 | tf_op jit(solution)/shard_map/ppermute | solution.py:845
  178.3 10.8 fusion.14.own_k.own_v
  189.1 11.2 %collective-permute-start.14 = (bf16[768,3072]{1,0:T(8,128)(2,1)S(1)}, bf16[768,3072]{1,0:T(8,128)(2,1)S(1)}, u32[]{:S(2)}, u32[]{:S(2)}) collective-permute-start(bf16[768,3072]{1,0:T(8,128)(2,1)S(1)} %fusion.14.own_k.own_v), channel_id=1, source_target_pairs={{0,4},{4,0},{1,5},{5,1},{2,6},{6,2},{3,7},{7,3},{8,12},{12,8},{9,1... | collective-permute-start | bytes 14155784 | tf_op jit(solution)/shard_map/ppermute | solution.py:955
  204.0 8.3 fusion.64.q_ref
  212.3 16.3 %collective-permute-done.10 = bf16[48,6144]{1,0:T(8,128)(2,1)S(1)} collective-permute-done((bf16[48,6144]{1,0:T(8,128)(2,1)S(1)}, bf16[48,6144]{1,0:T(8,128)(2,1)S(1)}, u32[]{:S(2)}, u32[]{:S(2)}) %collective-permute-start.10) | collective-permute-done | bytes 589856 | tf_op jit(solution)/shard_map/ppermute | solution.py:830
  228.6 14.2 %collective-permute-done.11 = bf16[48,6144]{1,0:T(8,128)(2,1)S(1)} collective-permute-done((bf16[48,6144]{1,0:T(8,128)(2,1)S(1)}, bf16[48,6144]{1,0:T(8,128)(2,1)S(1)}, u32[]{:S(2)}, u32[]{:S(2)}) %collective-permute-start.11) | collective-permute-done | bytes 589856 | tf_op jit(solution)/shard_map/ppermute | solution.py:830
  252.3 11.3 %collective-permute-start.19 = (bf16[192,1536]{1,0:T(8,128)(2,1)}, bf16[192,1536]{1,0:T(8,128)(2,1)S(1)}, u32[]{:S(2)}, u32[]{:S(2)}) collective-permute-start(bf16[192,1536]{1,0:T(8,128)(2,1)} %get-tuple-element.99), channel_id=1, source_target_pairs={{0,1},{1,2},{2,3},{3,0},{4,5},{5,6},{6,7},{7,4},{8,9},{9,10},{10,1... | collective-permute-start | bytes 1769480 | tf_op jit(solution)/shard_map/ppermute | solution.py:830
  274.1 58.6 %self_attend.1 = (bf16[768,1536]{1,0:T(8,128)(2,1)S(1)}, f32[96,768]{1,0:T(8,128)S(1)}) custom-call(s32[5]{0:T(128)S(1)} %stack.66.place, bf16[768,1536]{1,0:T(8,128)(2,1)S(1)} %copy-done.24, bf16[768,3072]{1,0:T(8,128)(2,1)S(1)} %copy-done.16, bf16[768,3072]{1,0:T(8,128)(2,1)S(1)} %copy-done.16, bf16[768,3072]{1,0:T(8,128)(2,1)S(1)} %copy-done.18, ...), custom_call_target="tpu_custom_call" | custom-call | flops 7247757312 | bytes 18874368 | tf_op jit(solution)/shard_map/self_attend/pallas_call | solution.py:569
  350.1 7.0 collective-permute-done.16
  358.5 7.1 fusion.134
  372.7 6.8 cross_attend.1
  388.4 10.3 collective-permute-start.23
  401.1 62.7 %multiply_convert_fusion = (bf16[768,6144]{1,0:T(8,128)(2,1)}, f32[768,6144]{1,0:T(8,128)}, f32[768,6144]{1,0:T(8,128)}) fusion(bf16[1536,6144]{1,0:T(8,128)(2,1)} %bitcast.198, f32[768,1536]{1,0:T(8,128)} %copy-done.28, f32[1536]{0:T(1024)S(1)} %add.437, f32[1536]{0:T(1024)S(1)} %mul.317, f32[768]{0:T(1024)S(1)} %add_rsqrt_fusion, ...), kind=kOutput, calls=%fused_computation.5 | convolution fusion | flops 14808121344 | bytes 70797312 | tf_op jit(solution)/shard_map/dot_general | solution.py:28
  466.7 23.5 %multiply_convert_fusion.1 = (bf16[768,1536]{1,0:T(8,128)(2,1)S(1)}, bf16[768,1536]{1,0:T(8,128)(2,1)}, f32[768,1536]{1,0:T(8,128)}) fusion(f32[]{:T(128)S(6)} %div.75, f32[768]{0:T(1024)S(1)} %copy-done.85, bf16[384,1536]{1,0:T(8,128)(2,1)} %get-tuple-element.204, bf16[384,1536]{1,0:T(8,128)(2,1)S(1)} %get-tuple-element.203, f32[768,1536]{1,0:T(8,128)} %copy-done.28, ...), kind=kOutput, calls=%fused_computation.66 | convolution fusion | flops 14507311104 | bytes 44829700 | tf_op jit(solution)/shard_map/dot_general | solution.py:28
  490.2 9.8 convolution_convert_fusion.2
  503.5 29.5 %add_convert_fusion.2 = bf16[768,6144]{1,0:T(8,128)(2,1)} fusion(f32[768,6144]{1,0:T(8,128)} %get-tuple-element.185, f32[768,6144]{1,0:T(8,128)} %get-tuple-element.238, bf16[768,1536]{1,0:T(8,128)(2,1)} %copy-done.59, bf16[6144,1536]{1,0:T(8,128)(2,1)} %bitcast.201), kind=kOutput, calls=%fused_computation.4 | convolution fusion | flops 14561574912 | bytes 68419584 | tf_op jit(solution)/shard_map/re,de->rd/dot_general | solution.py:36
  533.0 14.2 %add_convert_fusion.1 = bf16[768,6144]{1,0:T(8,128)(2,1)} fusion(bf16[768,6144]{1,0:T(8,128)(2,1)} %collective-permute-done.26, bf16[768,6144]{1,0:T(8,128)(2,1)} %get-tuple-element.184, bf16[768,1536]{1,0:T(8,128)(2,1)} %copy-done.59, s32[]{:T(128)S(6)} %select_n.335), kind=kOutput, calls=%fused_computation.3 | convolution fusion | flops 7261913088 | bytes 29491204 | tf_op jit(solution)/shard_map/rd,re->de/dot_general | solution.py:32
  547.3 13.7 %convolution_convert_fusion.1 = bf16[3072,1536]{1,0:T(8,128)(2,1)} fusion(bf16[768,6144]{1,0:T(8,128)(2,1)} %add_convert_fusion.2, s32[]{:T(128)S(6)} %select_n.336, f32[768,1536]{1,0:T(8,128)} %copy-done.28, f32[1536]{0:T(1024)S(1)} %add.437, f32[1536]{0:T(1024)S(1)} %mul.317, f32[768]{0:T(1024)S(1)} %add_rsqrt_fusion, f32[768]{0:T(1024)S(1)} %broadcast_multiply_fusion.6), kind=kOutput, calls=%fused_computation.21 | convolution fusion | flops 7258374144 | bytes 18892804 | tf_op jit(solution)/shard_map/rd,re->de/dot_general | solution.py:32
  561.8 6.0 collective-permute-start.25
  567.8 21.5 %fusion.136 = f32[768,1536]{1,0:T(8,128)} fusion(bf16[768,6144]{1,0:T(8,128)(2,1)} %add_convert_fusion.2, bf16[1536,6144]{1,0:T(8,128)(2,1)} %bitcast.199), kind=kOutput, calls=%fused_computation.302 | convolution fusion | flops 14495514624 | bytes 33030144 | tf_op jit(solution)/shard_map/re,de->rd/dot_general | solution.py:36
  594.6 13.7 %add_convert_fusion = bf16[3072,1536]{1,0:T(8,128)(2,1)} fusion(bf16[3072,1536]{1,0:T(8,128)(2,1)} %collective-permute-done.27, bf16[768,6144]{1,0:T(8,128)(2,1)} %add_convert_fusion.2, s32[]{:T(128)S(6)} %select_n.339, f32[768,1536]{1,0:T(8,128)S(1)} %bitcast.174, f32[1536]{0:T(1024)S(1)} %add.437, f32[1536]{0:T(1024)S(1)} %mul.317, ...), kind=kOutput, calls=%fused_computation.2 | convolution fusion | flops 7267811328 | bytes 28329988 | tf_op jit(solution)/shard_map/rd,re->de/dot_general | solution.py:32
  608.4 6.1 multiply_reduce_fusion.1
  614.5 10.2 fusion.131
  628.2 6.7 fusion.61.grad_ref
  635.0 9.5 cross_attend_back.1
  651.6 6.1 collective-permute-done.32
  666.1 8.8 multiply_reduce_fusion.2
  682.7 7.8 fusion.55.grad_ref
  719.2 69.9 %self_attend_back.1 = (bf16[768,1536]{1,0:T(8,128)(2,1)S(1)}, bf16[768,1536]{1,0:T(8,128)(2,1)S(1)}, bf16[768,1536]{1,0:T(8,128)(2,1)S(1)}, bf16[768,1536]{1,0:T(8,128)(2,1)}, bf16[768,1536]{1,0:T(8,128)(2,1)}) custom-call(s32[5]{0:T(128)S(1)} %copy-done.14, bf16[768,1536]{1,0:T(8,128)(2,1)S(1)} %copy-done.25, bf16[768,3072]{1,0:T(8,128)(2,1)} %copy-done.15, ...), custom_call_target="tpu_custom_call" | custom-call | flops 18119393280 | bytes 37748736 | tf_op jit(solution)/shard_map/self_attend_back/pallas_call | solution.py:598
  804.3 7.8 convolution_convert_fusion
  812.1 17.7 %fusion.137 = f32[768,1536]{1,0:T(8,128)} fusion(bf16[768,4608]{1,0:T(8,128)(2,1)} %copy-done.34, bf16[1536,4608]{1,0:T(8,128)(2,1)} %bitcast.204), kind=kOutput, calls=%fused_computation.303 | convolution fusion | flops 10871635968 | bytes 25952256 | tf_op jit(solution)/shard_map/re,de->rd/dot_general | solution.py:36
  829.9 9.7 add_convert_fusion.3
  865.5 22.2 %collective-permute-done.46 = bf16[768,384]{1,0:T(8,128)(2,1)S(1)} collective-permute-done((bf16[768,384]{1,0:T(8,128)(2,1)}, bf16[768,384]{1,0:T(8,128)(2,1)S(1)}, u32[]{:S(2)}, u32[]{:S(2)}) %collective-permute-start.46) | collective-permute-done | bytes 589856 | tf_op jit(solution)/shard_map/ppermute | solution.py:830
  895.4 13.0 %collective-permute-start.54 = (bf16[576,384]{1,0:T(8,128)(2,1)}, bf16[576,384]{1,0:T(8,128)(2,1)}, u32[]{:S(2)}, u32[]{:S(2)}) collective-permute-start(bf16[576,384]{1,0:T(8,128)(2,1)} %get-tuple-element.218), channel_id=1, source_target_pairs={{0,1},{1,2},{2,3},{3,0},{4,5},{5,6},{6,7},{7,4},{8,9},{9,10},{10,1... | collective-permute-start | bytes 1327112 | tf_op jit(solution)/shard_map/ppermute | solution.py:830
  913.1 7.1 collective-permute-done.54
  920.2 17.9 %collective-permute-done.55 = bf16[576,384]{1,0:T(8,128)(2,1)} collective-permute-done((bf16[576,384]{1,0:T(8,128)(2,1)}, bf16[576,384]{1,0:T(8,128)(2,1)}, u32[]{:S(2)}, u32[]{:S(2)}) %collective-permute-start.55) | collective-permute-done | bytes 442400 | tf_op jit(solution)/shard_map/ppermute | solution.py:830
  956.4 10.9 collective-permute-start.51
  986.2 15.4 %collective-permute-done.58 = bf16[576,384]{1,0:T(8,128)(2,1)S(1)} collective-permute-done((bf16[576,384]{1,0:T(8,128)(2,1)S(1)}, bf16[576,384]{1,0:T(8,128)(2,1)S(1)}, u32[]{:S(2)}, u32[]{:S(2)}) %collective-permute-start.58) | collective-permute-done | bytes 442400 | tf_op jit(solution)/shard_map/ppermute | solution.py:830
  1004.7 12.2 %collective-permute-start.61 = (bf16[384,1536]{1,0:T(8,128)(2,1)S(1)}, bf16[384,1536]{1,0:T(8,128)(2,1)S(1)}, u32[]{:S(2)}, u32[]{:S(2)}) collective-permute-start(bf16[384,1536]{1,0:T(8,128)(2,1)S(1)} %get-tuple-element.194), channel_id=1, source_target_pairs={{1,0},{5,1},{4,2},{0,3},{3,4},{7,5},{6,6},{2,7},{9,8},{13,9},{12,1... | collective-permute-start | bytes 3538952 | tf_op jit(solution)/shard_map/ppermute | solution.py:857
  1019.0 29.9 %collective-permute-done.61 = bf16[384,1536]{1,0:T(8,128)(2,1)S(1)} collective-permute-done((bf16[384,1536]{1,0:T(8,128)(2,1)S(1)}, bf16[384,1536]{1,0:T(8,128)(2,1)S(1)}, u32[]{:S(2)}, u32[]{:S(2)}) %collective-permute-start.61) | collective-permute-done | bytes 1179680 | tf_op jit(solution)/shard_map/ppermute | solution.py:857
  1068.8 8.1 unpack.19
  1087.7 13.0 %all-gather.16.cloned.1.call-done = bf16[4608,384]{1,0:T(8,128)(2,1)} async-done(((bf16[576,384]{1,0:T(8,128)(2,1)}), bf16[4608,384]{1,0:T(8,128)(2,1)}) %all-gather.16.cloned.1.call-update) | async-done | bytes 3538960 | tf_op jit(solution)/shard_map/all_gather | solution.py:1189
  (540 shorter events, 320.2 us)
Async XLA Ops:
  7.2 171.0 %all-gather.8.cloned.1.call-start = ((), (), s32[]{:S(2)}) async-start(), calls=%async_computation.4 | async-start | bytes 15925248 | tf_op jit(solution)/shard_map/all_gather | solution.py:867
  16.7 40.9 %collective-permute-start.1 = (bf16[64,4608]{1,0:T(8,128)(2,1)S(1)}, bf16[64,4608]{1,0:T(8,128)(2,1)}, u32[]{:S(2)}, u32[]{:S(2)}) collective-permute-start(bf16[64,4608]{1,0:T(8,128)(2,1)S(1)} %pad_maximum_fusion.5), channel_id=1, source_target_pairs={{0,2},{1,3},{2,0},{3,1},{4,6},{5,7},{6,4},{7,5},{8,10},{9,11},{10,... | collective-permute-start | bytes 1769480 | tf_op jit(solution)/shard_map/ppermute | solution.py:830
  19.3 39.3 %collective-permute-start.2 = (bf16[64,4608]{1,0:T(8,128)(2,1)S(1)}, bf16[64,4608]{1,0:T(8,128)(2,1)}, u32[]{:S(2)}, u32[]{:S(2)}) collective-permute-start(bf16[64,4608]{1,0:T(8,128)(2,1)S(1)} %pad_maximum_fusion.5), channel_id=1, source_target_pairs={{0,3},{1,0},{2,1},{3,2},{4,7},{5,4},{6,5},{7,6},{8,11},{9,8},{10,9... | collective-permute-start | bytes 1769480 | tf_op jit(solution)/shard_map/ppermute | solution.py:830
  61.0 297.5 %all-gather.10.cloned.1.call-start = ((), (), s32[]{:S(2)}) async-start(), calls=%async_computation.5 | async-start | bytes 15925248 | tf_op jit(solution)/shard_map/all_gather | solution.py:867
  63.1 25.4 %collective-permute-start.3 = (bf16[48,4608]{1,0:T(8,128)(2,1)S(1)}, bf16[48,4608]{1,0:T(8,128)(2,1)S(1)}, u32[]{:S(2)}, u32[]{:S(2)}) collective-permute-start(bf16[48,4608]{1,0:T(8,128)(2,1)S(1)} %pad_maximum_fusion.7), channel_id=1, source_target_pairs={{0,1},{1,2},{2,3},{3,0},{4,5},{5,6},{6,7},{7,4},{8,9},{9,10},{10,1... | collective-permute-start | bytes 1327112 | tf_op jit(solution)/shard_map/ppermute | solution.py:830
  75.4 30.3 %collective-permute-start.4 = (bf16[48,4608]{1,0:T(8,128)(2,1)S(1)}, bf16[48,4608]{1,0:T(8,128)(2,1)S(1)}, u32[]{:S(2)}, u32[]{:S(2)}) collective-permute-start(bf16[48,4608]{1,0:T(8,128)(2,1)S(1)} %pad_maximum_fusion.7), channel_id=1, source_target_pairs={{0,2},{1,3},{2,0},{3,1},{4,6},{5,7},{6,4},{7,5},{8,10},{9,11},{10,... | collective-permute-start | bytes 1327112 | tf_op jit(solution)/shard_map/ppermute | solution.py:830
  78.1 27.6 %collective-permute-start.5 = (bf16[48,4608]{1,0:T(8,128)(2,1)S(1)}, bf16[48,4608]{1,0:T(8,128)(2,1)S(1)}, u32[]{:S(2)}, u32[]{:S(2)}) collective-permute-start(bf16[48,4608]{1,0:T(8,128)(2,1)S(1)} %pad_maximum_fusion.7), channel_id=1, source_target_pairs={{0,3},{1,0},{2,1},{3,2},{4,7},{5,4},{6,5},{7,6},{8,11},{9,8},{10,9... | collective-permute-start | bytes 1327112 | tf_op jit(solution)/shard_map/ppermute | solution.py:830
  107.0 294.1 %all-gather.12.cloned.1.call-start = ((), (), s32[]{:S(2)}) async-start(), calls=%async_computation.6 | async-start | bytes 21233664 | tf_op jit(solution)/shard_map/all_gather | solution.py:867
  121.8 32.4 %collective-permute-start.6 = (bf16[384,1536]{1,0:T(8,128)(2,1)}, bf16[384,1536]{1,0:T(8,128)(2,1)S(1)}, u32[]{:S(2)}, u32[]{:S(2)}) collective-permute-start(bf16[384,1536]{1,0:T(8,128)(2,1)} %get-tuple-element.212), channel_id=1, source_target_pairs={{0,0},{1,4},{2,5},{3,1},{4,2},{5,6},{6,7},{7,3},{8,8},{9,12},{10,1... | collective-permute-start | bytes 3538952 | tf_op jit(solution)/shard_map/ppermute | solution.py:844
  123.7 51.2 %collective-permute-start.7 = (bf16[384,1536]{1,0:T(8,128)(2,1)S(1)}, bf16[384,1536]{1,0:T(8,128)(2,1)S(1)}, u32[]{:S(2)}, u32[]{:S(2)}) collective-permute-start(bf16[384,1536]{1,0:T(8,128)(2,1)S(1)} %get-tuple-element.211), channel_id=1, source_target_pairs={{0,1},{1,5},{2,4},{3,0},{4,3},{5,7},{6,6},{7,2},{8,9},{9,13},{10,1... | collective-permute-start | bytes 3538952 | tf_op jit(solution)/shard_map/ppermute | solution.py:845
  189.1 53.7 %collective-permute-start.14 = (bf16[768,3072]{1,0:T(8,128)(2,1)S(1)}, bf16[768,3072]{1,0:T(8,128)(2,1)S(1)}, u32[]{:S(2)}, u32[]{:S(2)}) collective-permute-start(bf16[768,3072]{1,0:T(8,128)(2,1)S(1)} %fusion.14.own_k.own_v), channel_id=1, source_target_pairs={{0,4},{4,0},{1,5},{5,1},{2,6},{6,2},{3,7},{7,3},{8,12},{12,8},{9,1... | collective-permute-start | bytes 14155784 | tf_op jit(solution)/shard_map/ppermute | solution.py:955
  201.7 26.9 %collective-permute-start.10 = (bf16[48,6144]{1,0:T(8,128)(2,1)S(1)}, bf16[48,6144]{1,0:T(8,128)(2,1)S(1)}, u32[]{:S(2)}, u32[]{:S(2)}) collective-permute-start(bf16[48,6144]{1,0:T(8,128)(2,1)S(1)} %get-tuple-element.88), channel_id=1, source_target_pairs={{0,2},{1,3},{2,0},{3,1},{4,6},{5,7},{6,4},{7,5},{8,10},{9,11},{10,... | collective-permute-start | bytes 1769480 | tf_op jit(solution)/shard_map/ppermute | solution.py:830
  201.8 41.0 %collective-permute-start.11 = (bf16[48,6144]{1,0:T(8,128)(2,1)S(1)}, bf16[48,6144]{1,0:T(8,128)(2,1)S(1)}, u32[]{:S(2)}, u32[]{:S(2)}) collective-permute-start(bf16[48,6144]{1,0:T(8,128)(2,1)S(1)} %get-tuple-element.88), channel_id=1, source_target_pairs={{0,3},{1,0},{2,1},{3,2},{4,7},{5,4},{6,5},{7,6},{8,11},{9,8},{10,9... | collective-permute-start | bytes 1769480 | tf_op jit(solution)/shard_map/ppermute | solution.py:830
  201.8 41.0 %collective-permute-start.9 = (bf16[48,6144]{1,0:T(8,128)(2,1)S(1)}, bf16[48,6144]{1,0:T(8,128)(2,1)S(1)}, u32[]{:S(2)}, u32[]{:S(2)}) collective-permute-start(bf16[48,6144]{1,0:T(8,128)(2,1)S(1)} %get-tuple-element.88), channel_id=1, source_target_pairs={{0,1},{1,2},{2,3},{3,0},{4,5},{5,6},{6,7},{7,4},{8,9},{9,10},{10,1... | collective-permute-start | bytes 1769480 | tf_op jit(solution)/shard_map/ppermute | solution.py:830
  246.5 220.2 %all-gather.14.cloned.1.call-start = ((), (), s32[]{:S(2)}) async-start(), calls=%async_computation.7 | async-start | bytes 21233664 | tf_op jit(solution)/shard_map/all_gather | solution.py:867
  252.3 80.4 %collective-permute-start.19 = (bf16[192,1536]{1,0:T(8,128)(2,1)}, bf16[192,1536]{1,0:T(8,128)(2,1)S(1)}, u32[]{:S(2)}, u32[]{:S(2)}) collective-permute-start(bf16[192,1536]{1,0:T(8,128)(2,1)} %get-tuple-element.99), channel_id=1, source_target_pairs={{0,1},{1,2},{2,3},{3,0},{4,5},{5,6},{6,7},{7,4},{8,9},{9,10},{10,1... | collective-permute-start | bytes 1769480 | tf_op jit(solution)/shard_map/ppermute | solution.py:830
  263.6 69.1 %collective-permute-start.20 = (bf16[192,1536]{1,0:T(8,128)(2,1)}, bf16[192,1536]{1,0:T(8,128)(2,1)S(1)}, u32[]{:S(2)}, u32[]{:S(2)}) collective-permute-start(bf16[192,1536]{1,0:T(8,128)(2,1)} %get-tuple-element.99), channel_id=1, source_target_pairs={{0,2},{1,3},{2,0},{3,1},{4,6},{5,7},{6,4},{7,5},{8,10},{9,11},{10,... | collective-permute-start | bytes 1769480 | tf_op jit(solution)/shard_map/ppermute | solution.py:830
  264.9 67.9 %collective-permute-start.21 = (bf16[192,1536]{1,0:T(8,128)(2,1)}, bf16[192,1536]{1,0:T(8,128)(2,1)S(1)}, u32[]{:S(2)}, u32[]{:S(2)}) collective-permute-start(bf16[192,1536]{1,0:T(8,128)(2,1)} %get-tuple-element.99), channel_id=1, source_target_pairs={{0,3},{1,0},{2,1},{3,2},{4,7},{5,4},{6,5},{7,6},{8,11},{9,8},{10,9... | collective-permute-start | bytes 1769480 | tf_op jit(solution)/shard_map/ppermute | solution.py:830
  335.4 372.1 %reduce-scatter.5.cloned.1.call-start = ((), (), s32[]{:S(2)}) async-start(), calls=%async_computation.8 | async-start | bytes 11796480 | tf_op jit(solution)/shard_map/reduce_scatter | solution.py:1010
  388.4 75.4 %collective-permute-start.23 = (bf16[384,1536]{1,0:T(8,128)(2,1)}, bf16[384,1536]{1,0:T(8,128)(2,1)}, u32[]{:S(2)}, u32[]{:S(2)}) collective-permute-start(bf16[384,1536]{1,0:T(8,128)(2,1)} %get-tuple-element.206), channel_id=1, source_target_pairs={{0,0},{1,4},{2,5},{3,1},{4,2},{5,6},{6,7},{7,3},{8,8},{9,12},{10,1... | collective-permute-start | bytes 3538952 | tf_op jit(solution)/shard_map/ppermute | solution.py:844
  398.7 65.0 %collective-permute-start.24 = (bf16[384,1536]{1,0:T(8,128)(2,1)}, bf16[384,1536]{1,0:T(8,128)(2,1)}, u32[]{:S(2)}, u32[]{:S(2)}) collective-permute-start(bf16[384,1536]{1,0:T(8,128)(2,1)} %get-tuple-element.205), channel_id=1, source_target_pairs={{0,1},{1,5},{2,4},{3,0},{4,3},{5,7},{6,6},{7,2},{8,9},{9,13},{10,1... | collective-permute-start | bytes 3538952 | tf_op jit(solution)/shard_map/ppermute | solution.py:845
  500.0 33.0 %collective-permute-start.26 = (bf16[768,6144]{1,0:T(8,128)(2,1)}, bf16[768,6144]{1,0:T(8,128)(2,1)}, u32[]{:S(2)}, u32[]{:S(2)}) collective-permute-start(bf16[768,6144]{1,0:T(8,128)(2,1)} %convolution_convert_fusion.2), channel_id=1, source_target_pairs={{0,4},{4,0},{1,5},{5,1},{2,6},{6,2},{3,7},{7,3},{8,12},{12,8},{9,1... | collective-permute-start | bytes 28311560 | tf_op jit(solution)/shard_map/ppermute | solution.py:1005
  501.8 31.2 %collective-permute-start.22 = (bf16[384,1536]{1,0:T(8,128)(2,1)S(1)}, bf16[384,1536]{1,0:T(8,128)(2,1)}, u32[]{:S(2)}, u32[]{:S(2)}) collective-permute-start(bf16[384,1536]{1,0:T(8,128)(2,1)S(1)} %get-tuple-element.207), channel_id=1, source_target_pairs={{0,0},{4,1},{5,2},{1,3},{2,4},{6,5},{7,6},{3,7},{8,8},{12,9},{13,1... | collective-permute-start | bytes 3538952 | tf_op jit(solution)/shard_map/ppermute | solution.py:1033
  547.2 294.5 %reduce-scatter.7.cloned.1.call-start = ((), (), s32[]{:S(2)}) async-start(), calls=%async_computation.9 | async-start | bytes 11796480 | tf_op jit(solution)/shard_map/reduce_scatter | solution.py:1010
  561.0 33.6 %collective-permute-start.27 = (bf16[3072,1536]{1,0:T(8,128)(2,1)}, bf16[3072,1536]{1,0:T(8,128)(2,1)}, u32[]{:S(2)}, u32[]{:S(2)}) collective-permute-start(bf16[3072,1536]{1,0:T(8,128)(2,1)} %convolution_convert_fusion.1), channel_id=1, source_target_pairs={{0,4},{4,0},{1,5},{5,1},{2,6},{6,2},{3,7},{7,3},{8,12},{12,8},{9,1... | collective-permute-start | bytes 28311560 | tf_op jit(solution)/shard_map/ppermute | solution.py:1005
  561.8 32.8 %collective-permute-start.25 = (bf16[384,1536]{1,0:T(8,128)(2,1)S(1)}, bf16[384,1536]{1,0:T(8,128)(2,1)}, u32[]{:S(2)}, u32[]{:S(2)}) collective-permute-start(bf16[384,1536]{1,0:T(8,128)(2,1)S(1)} %get-tuple-element.108), channel_id=1, source_target_pairs={{1,0},{5,1},{4,2},{0,3},{3,4},{7,5},{6,6},{2,7},{9,8},{13,9},{12,1... | collective-permute-start | bytes 3538952 | tf_op jit(solution)/shard_map/ppermute | solution.py:1043
  608.3 283.1 %reduce-scatter.11.cloned.1.call-start = ((), (), s32[]{:S(2)}) async-start(), calls=%async_computation.11 | async-start | bytes 10321920 | tf_op jit(solution)/shard_map/reduce_scatter | solution.py:1010
  628.2 30.1 %collective-permute-start.28 = (bf16[768,1536]{1,0:T(8,128)(2,1)}, bf16[768,1536]{1,0:T(8,128)(2,1)}, u32[]{:S(2)}, u32[]{:S(2)}) collective-permute-start(bf16[768,1536]{1,0:T(8,128)(2,1)} %convolution_convert_fusion.5), channel_id=1, source_target_pairs={{0,4},{4,0},{1,5},{5,1},{2,6},{6,2},{3,7},{7,3},{8,12},{12,8},{9,1... | collective-permute-start | bytes 7077896 | tf_op jit(solution)/shard_map/ppermute | solution.py:1005
  648.5 32.4 %collective-permute-start.33 = (bf16[64,1536]{1,0:T(8,128)(2,1)}, bf16[64,1536]{1,0:T(8,128)(2,1)S(1)}, u32[]{:S(2)}, u32[]{:S(2)}) collective-permute-start(bf16[64,1536]{1,0:T(8,128)(2,1)} %get-tuple-element.177), channel_id=1, source_target_pairs={{0,2},{1,3},{2,0},{3,1},{4,6},{5,7},{6,4},{7,5},{8,10},{9,11},{10,... | collective-permute-start | bytes 589832 | tf_op jit(solution)/shard_map/ppermute | solution.py:830
  651.0 29.9 %collective-permute-start.34 = (bf16[64,1536]{1,0:T(8,128)(2,1)}, bf16[64,1536]{1,0:T(8,128)(2,1)S(1)}, u32[]{:S(2)}, u32[]{:S(2)}) collective-permute-start(bf16[64,1536]{1,0:T(8,128)(2,1)} %get-tuple-element.177), channel_id=1, source_target_pairs={{0,3},{1,0},{2,1},{3,2},{4,7},{5,4},{6,5},{7,6},{8,11},{9,8},{10,9... | collective-permute-start | bytes 589832 | tf_op jit(solution)/shard_map/ppermute | solution.py:830
  666.1 24.4 %collective-permute-start.29 = (bf16[768,1536]{1,0:T(8,128)(2,1)}, bf16[768,1536]{1,0:T(8,128)(2,1)S(1)}, u32[]{:S(2)}, u32[]{:S(2)}) collective-permute-start(bf16[768,1536]{1,0:T(8,128)(2,1)} %convolution_convert_fusion.4), channel_id=1, source_target_pairs={{0,4},{4,0},{1,5},{5,1},{2,6},{6,2},{3,7},{7,3},{8,12},{12,8},{9,1... | collective-permute-start | bytes 7077896 | tf_op jit(solution)/shard_map/ppermute | solution.py:1005
  698.4 271.4 %reduce-scatter.9.cloned.1.call-start = ((), (), s32[]{:S(2)}) async-start(), calls=%async_computation.10 | async-start | bytes 8847360 | tf_op jit(solution)/shard_map/reduce_scatter | solution.py:1010
  703.7 88.2 %collective-permute-start.37 = (bf16[2,64,384]{2,1,0:T(8,128)(2,1)S(1)}, bf16[2,64,384]{2,1,0:T(8,128)(2,1)}, u32[]{:S(2)}, u32[]{:S(2)}) collective-permute-start(bf16[2,64,384]{2,1,0:T(8,128)(2,1)S(1)} %fusion.94), channel_id=1, source_target_pairs={{0,2},{1,3},{2,0},{3,1},{4,6},{5,7},{6,4},{7,5},{8,10},{9,11},{10,... | collective-permute-start | bytes 294920 | tf_op jit(solution)/shard_map/ppermute | solution.py:830
  705.3 86.6 %collective-permute-start.38 = (bf16[2,64,384]{2,1,0:T(8,128)(2,1)S(1)}, bf16[2,64,384]{2,1,0:T(8,128)(2,1)}, u32[]{:S(2)}, u32[]{:S(2)}) collective-permute-start(bf16[2,64,384]{2,1,0:T(8,128)(2,1)S(1)} %fusion.94), channel_id=1, source_target_pairs={{0,3},{1,0},{2,1},{3,2},{4,7},{5,4},{6,5},{7,6},{8,11},{9,8},{10,9... | collective-permute-start | bytes 294920 | tf_op jit(solution)/shard_map/ppermute | solution.py:830
  709.1 82.8 %collective-permute-start.39 = (bf16[192,1536]{1,0:T(8,128)(2,1)S(1)}, bf16[192,1536]{1,0:T(8,128)(2,1)S(1)}, u32[]{:S(2)}, u32[]{:S(2)}) collective-permute-start(bf16[192,1536]{1,0:T(8,128)(2,1)S(1)} %get-tuple-element.200), channel_id=1, source_target_pairs={{0,1},{1,2},{2,3},{3,0},{4,5},{5,6},{6,7},{7,4},{8,9},{9,10},{10,1... | collective-permute-start | bytes 1769480 | tf_op jit(solution)/shard_map/ppermute | solution.py:830
  709.7 82.2 %collective-permute-start.40 = (bf16[192,1536]{1,0:T(8,128)(2,1)S(1)}, bf16[192,1536]{1,0:T(8,128)(2,1)}, u32[]{:S(2)}, u32[]{:S(2)}) collective-permute-start(bf16[192,1536]{1,0:T(8,128)(2,1)S(1)} %get-tuple-element.199), channel_id=1, source_target_pairs={{0,2},{1,3},{2,0},{3,1},{4,6},{5,7},{6,4},{7,5},{8,10},{9,11},{10,... | collective-permute-start | bytes 1769480 | tf_op jit(solution)/shard_map/ppermute | solution.py:830
  711.2 80.7 %collective-permute-start.41 = (bf16[192,1536]{1,0:T(8,128)(2,1)S(1)}, bf16[192,1536]{1,0:T(8,128)(2,1)}, u32[]{:S(2)}, u32[]{:S(2)}) collective-permute-start(bf16[192,1536]{1,0:T(8,128)(2,1)S(1)} %get-tuple-element.198), channel_id=1, source_target_pairs={{0,3},{1,0},{2,1},{3,2},{4,7},{5,4},{6,5},{7,6},{8,11},{9,8},{10,9... | collective-permute-start | bytes 1769480 | tf_op jit(solution)/shard_map/ppermute | solution.py:830
  839.6 209.3 %all-gather.18.cloned.1.call-start = ((), (), s32[]{:S(2)}) async-start(), calls=%async_computation.13 | async-start | bytes 17252352 | tf_op jit(solution)/shard_map/all_gather | solution.py:1175
  844.3 21.2 %collective-permute-start.45 = (bf16[768,384]{1,0:T(8,128)(2,1)}, bf16[768,384]{1,0:T(8,128)(2,1)S(1)}, u32[]{:S(2)}, u32[]{:S(2)}) collective-permute-start(bf16[768,384]{1,0:T(8,128)(2,1)} %get-tuple-element.197), channel_id=1, source_target_pairs={{0,1},{1,2},{2,3},{3,0},{4,5},{5,6},{6,7},{7,4},{8,9},{9,10},{10,1... | collective-permute-start | bytes 1769480 | tf_op jit(solution)/shard_map/ppermute | solution.py:830
  845.2 42.5 %collective-permute-start.46 = (bf16[768,384]{1,0:T(8,128)(2,1)}, bf16[768,384]{1,0:T(8,128)(2,1)S(1)}, u32[]{:S(2)}, u32[]{:S(2)}) collective-permute-start(bf16[768,384]{1,0:T(8,128)(2,1)} %get-tuple-element.196), channel_id=1, source_target_pairs={{0,2},{1,3},{2,0},{3,1},{4,6},{5,7},{6,4},{7,5},{8,10},{9,11},{10,... | collective-permute-start | bytes 1769480 | tf_op jit(solution)/shard_map/ppermute | solution.py:830
  846.2 41.5 %collective-permute-start.47 = (bf16[768,384]{1,0:T(8,128)(2,1)S(1)}, bf16[768,384]{1,0:T(8,128)(2,1)}, u32[]{:S(2)}, u32[]{:S(2)}) collective-permute-start(bf16[768,384]{1,0:T(8,128)(2,1)S(1)} %get-tuple-element.195), channel_id=1, source_target_pairs={{0,3},{1,0},{2,1},{3,2},{4,7},{5,4},{6,5},{7,6},{8,11},{9,8},{10,9... | collective-permute-start | bytes 1769480 | tf_op jit(solution)/shard_map/ppermute | solution.py:830
  895.4 24.8 %collective-permute-start.54 = (bf16[576,384]{1,0:T(8,128)(2,1)}, bf16[576,384]{1,0:T(8,128)(2,1)}, u32[]{:S(2)}, u32[]{:S(2)}) collective-permute-start(bf16[576,384]{1,0:T(8,128)(2,1)} %get-tuple-element.218), channel_id=1, source_target_pairs={{0,1},{1,2},{2,3},{3,0},{4,5},{5,6},{6,7},{7,4},{8,9},{9,10},{10,1... | collective-permute-start | bytes 1327112 | tf_op jit(solution)/shard_map/ppermute | solution.py:830
  908.5 29.6 %collective-permute-start.55 = (bf16[576,384]{1,0:T(8,128)(2,1)}, bf16[576,384]{1,0:T(8,128)(2,1)}, u32[]{:S(2)}, u32[]{:S(2)}) collective-permute-start(bf16[576,384]{1,0:T(8,128)(2,1)} %get-tuple-element.217), channel_id=1, source_target_pairs={{0,2},{1,3},{2,0},{3,1},{4,6},{5,7},{6,4},{7,5},{8,10},{9,11},{10,... | collective-permute-start | bytes 1327112 | tf_op jit(solution)/shard_map/ppermute | solution.py:830
  909.3 28.8 %collective-permute-start.56 = (bf16[576,384]{1,0:T(8,128)(2,1)}, bf16[576,384]{1,0:T(8,128)(2,1)}, u32[]{:S(2)}, u32[]{:S(2)}) collective-permute-start(bf16[576,384]{1,0:T(8,128)(2,1)} %get-tuple-element.216), channel_id=1, source_target_pairs={{0,3},{1,0},{2,1},{3,2},{4,7},{5,4},{6,5},{7,6},{8,11},{9,8},{10,9... | collective-permute-start | bytes 1327112 | tf_op jit(solution)/shard_map/ppermute | solution.py:830
  940.5 160.2 %all-gather.16.cloned.1.call-start = ((), (), s32[]{:S(2)}) async-start(), calls=%async_computation.12 | async-start | bytes 3981312 | tf_op jit(solution)/shard_map/all_gather | solution.py:1189
  973.1 28.5 %collective-permute-start.58 = (bf16[576,384]{1,0:T(8,128)(2,1)S(1)}, bf16[576,384]{1,0:T(8,128)(2,1)S(1)}, u32[]{:S(2)}, u32[]{:S(2)}) collective-permute-start(bf16[576,384]{1,0:T(8,128)(2,1)S(1)} %get-tuple-element.214), channel_id=1, source_target_pairs={{0,2},{1,3},{2,0},{3,1},{4,6},{5,7},{6,4},{7,5},{8,10},{9,11},{10,... | collective-permute-start | bytes 1327112 | tf_op jit(solution)/shard_map/ppermute | solution.py:830
  973.8 27.9 %collective-permute-start.59 = (bf16[576,384]{1,0:T(8,128)(2,1)S(1)}, bf16[576,384]{1,0:T(8,128)(2,1)S(1)}, u32[]{:S(2)}, u32[]{:S(2)}) collective-permute-start(bf16[576,384]{1,0:T(8,128)(2,1)S(1)} %get-tuple-element.213), channel_id=1, source_target_pairs={{0,3},{1,0},{2,1},{3,2},{4,7},{5,4},{6,5},{7,6},{8,11},{9,8},{10,9... | collective-permute-start | bytes 1327112 | tf_op jit(solution)/shard_map/ppermute | solution.py:830
  1004.7 44.2 %collective-permute-start.61 = (bf16[384,1536]{1,0:T(8,128)(2,1)S(1)}, bf16[384,1536]{1,0:T(8,128)(2,1)S(1)}, u32[]{:S(2)}, u32[]{:S(2)}) collective-permute-start(bf16[384,1536]{1,0:T(8,128)(2,1)S(1)} %get-tuple-element.194), channel_id=1, source_target_pairs={{1,0},{5,1},{4,2},{0,3},{3,4},{7,5},{6,6},{2,7},{9,8},{13,9},{12,1... | collective-permute-start | bytes 3538952 | tf_op jit(solution)/shard_map/ppermute | solution.py:857
  (131 other events, 1712.7 us)
Sparse Core Ops, SparseCore 0:
  61.1 90.6 all-gather.7
  154.2 78.7 all-gather.9
  246.6 107.9 all-gather.11
  356.9 98.7 all-gather.13
  547.3 97.0 reduce-scatter.4
  648.0 95.0 reduce-scatter.6
  746.8 85.2 reduce-scatter.10
  839.7 76.6 reduce-scatter.8
  940.6 93.9 all-gather.17
  1049.0 51.5 all-gather.15

commit v10 on v9

--- a/solution.py
+++ b/solution.py
@@ -953,8 +953,9 @@
     )
     kv = project(after(hidden_one, count), qkv_matrix[:, width:]).astype(jnp.bfloat16)
     kv_other = lax.ppermute(kv, "core", swap)
-    queries = project(after(hidden_one, kv), qkv_matrix[:, :width]).astype(jnp.bfloat16)
-    expand_came = held(expand_came, kv_other, queries)
+    expand_came = held(expand_came, kv)
+    queries = project(after(hidden_one, kv, *expand_came), qkv_matrix[:, :width])
+    queries = queries.astype(jnp.bfloat16)
     expand_matrix = from_replicas(line_up(expand_share, expand_came))
     reduce_share = share_of(feed_down_weight)
     reduce_came = hops(after(reduce_share, *expand_came))
@@ -1154,7 +1155,9 @@
     )
     for axis in ("core", "x", "y"):
         small += lax.ppermute(small, axis, swap)
-    late_came = shard_hops(after(qkv_sum, *middle_came, small))
+    middle_came = held(middle_came, small)
+    middle_piece = over_shard(middle_kept, middle_came)
+    late_came = shard_hops(after(qkv_sum, *middle_came))
     small_came = shard_hops(small)
     small_own = lax.dynamic_slice_in_dim(small, shard * block, block, 1)
     for part in small_came:
@@ -1165,7 +1168,6 @@
     )
     frames_grad = by_slot(*frames_came).astype(jnp.float32)
 
-    middle_piece = over_shard(middle_kept, middle_came)
     early = jnp.concatenate(
         [up_piece]
         + [down_piece[:, i * block : (i + 1) * block] for i in range(4)]

time: 1130 us -> 1110 us (0.982)
  waiting for transfers between devices: 266 us -> 244 us
    ppermute x36, waiting for transfers between devices: 179 us -> 165 us  [hop(): return lax.ppermute(values, 'shard', pairs)]
    unnamed x223 -> x249, local copies, waits for them, and re-layouts: 46.5 us -> 37.3 us
  transfers between devices with their start and end apart: 72 -> 72, of which waited for: 27 -> 24; matrix products, arithmetic and copies ran while one was open for 36% -> 38% of each run, Pallas kernels for 15% -> 15%
where the time goes in v10:
time: 1110 us; the launch traced here: 1100 us
  matrix products  303 us (27%)
  waiting for transfers between devices  244 us (22%)
  Pallas kernels  174 us (16%)
  starting transfers between devices  160 us (14%)
  local copies, waits for them, and re-layouts  107 us (10%)
  other arithmetic  85.1 us (8%)
  between operations  21.7 us (2%)
    ppermute x36, waiting for transfers between devices, hop(): return lax.ppermute(values, 'shard', pairs)  165 us
    dot_general x8, matrix products, project(): return jnp.dot(left, right, preferred_element_type=jnp.float32)  121 us
    ppermute x36, starting transfers between devices, hop(): return lax.ppermute(values, 'shard', pairs)  103 us
    dot_general x7, matrix products, back_project(): jnp.einsum('re,de->rd', grads, matrix, preferred_element_type=jnp.float32)  93.9 us
    dot_general x13, matrix products, outer_sum(): jnp.einsum('rd,re->de', left, right, preferred_element_type=jnp.float32)  87.8 us
    pallas_call x1, Pallas kernels, self_attend_back(): pl.pallas_call(self_backward_kernel, out_shape=(jax.ShapeDtypeStruct((row...  70.1 us
    pallas_call x1, Pallas kernels, self_attend(): pl.pallas_call(self_forward_kernel, out_shape=(jax.ShapeDtypeStruct((rows...  58.5 us
    unnamed x249, local copies, waits for them, and re-layouts  37.3 us
  transfers between devices with their start and end apart: 72, of which 24 were waited for; matrix products, arithmetic and copies ran while one was open for 38% of the time, Pallas kernels for 15%

profile of v10, /device:TPU:0, one launch (start us, length us, event | category | flops | bytes accessed | tf_op | source)
XLA Modules:
  0.0 1095.1 jit_solution(15161025484914606149)
XLA Ops:
  20.9 12.3 %collective-permute-done = bf16[64,4608]{1,0:T(8,128)(2,1)} collective-permute-done((bf16[64,4608]{1,0:T(8,128)(2,1)S(1)}, bf16[64,4608]{1,0:T(8,128)(2,1)}, u32[]{:S(2)}, u32[]{:S(2)}) %collective-permute-start) | collective-permute-done | bytes 589856 | tf_op jit(solution)/shard_map/ppermute | solution.py:830
  34.2 23.4 %collective-permute-done.1 = bf16[64,4608]{1,0:T(8,128)(2,1)} collective-permute-done((bf16[64,4608]{1,0:T(8,128)(2,1)S(1)}, bf16[64,4608]{1,0:T(8,128)(2,1)}, u32[]{:S(2)}, u32[]{:S(2)}) %collective-permute-start.1) | collective-permute-done | bytes 589856 | tf_op jit(solution)/shard_map/ppermute | solution.py:830
  63.1 12.1 %collective-permute-start.3 = (bf16[48,4608]{1,0:T(8,128)(2,1)S(1)}, bf16[48,4608]{1,0:T(8,128)(2,1)S(1)}, u32[]{:S(2)}, u32[]{:S(2)}) collective-permute-start(bf16[48,4608]{1,0:T(8,128)(2,1)S(1)} %pad_maximum_fusion.7), channel_id=1, source_target_pairs={{0,1},{1,2},{2,3},{3,0},{4,5},{5,6},{6,7},{7,4},{8,9},{9,10},{10,1... | collective-permute-start | bytes 1327112 | tf_op jit(solution)/shard_map/ppermute | solution.py:830
  78.1 10.4 collective-permute-done.3
  88.5 17.1 %collective-permute-done.4 = bf16[48,4608]{1,0:T(8,128)(2,1)S(1)} collective-permute-done((bf16[48,4608]{1,0:T(8,128)(2,1)S(1)}, bf16[48,4608]{1,0:T(8,128)(2,1)S(1)}, u32[]{:S(2)}, u32[]{:S(2)}) %collective-permute-start.4) | collective-permute-done | bytes 442400 | tf_op jit(solution)/shard_map/ppermute | solution.py:830
  124.2 11.1 %collective-permute-start.7 = (bf16[384,1536]{1,0:T(8,128)(2,1)}, bf16[384,1536]{1,0:T(8,128)(2,1)}, u32[]{:S(2)}, u32[]{:S(2)}) collective-permute-start(bf16[384,1536]{1,0:T(8,128)(2,1)} %get-tuple-element.217), channel_id=1, source_target_pairs={{0,1},{1,5},{2,4},{3,0},{4,3},{5,7},{6,6},{7,2},{8,9},{9,13},{10,1... | collective-permute-start | bytes 3538952 | tf_op jit(solution)/shard_map/ppermute | solution.py:845
  154.6 20.9 %collective-permute-done.7 = bf16[384,1536]{1,0:T(8,128)(2,1)} collective-permute-done((bf16[384,1536]{1,0:T(8,128)(2,1)}, bf16[384,1536]{1,0:T(8,128)(2,1)}, u32[]{:S(2)}, u32[]{:S(2)}) %collective-permute-start.7) | collective-permute-done | bytes 1179680 | tf_op jit(solution)/shard_map/ppermute | solution.py:845
  175.5 16.7 %collective-permute-start.10 = (bf16[48,6144]{1,0:T(8,128)(2,1)}, bf16[48,6144]{1,0:T(8,128)(2,1)}, u32[]{:S(2)}, u32[]{:S(2)}) collective-permute-start(bf16[48,6144]{1,0:T(8,128)(2,1)} %get-tuple-element.91), channel_id=1, source_target_pairs={{0,2},{1,3},{2,0},{3,1},{4,6},{5,7},{6,4},{7,5},{8,10},{9,11},{10,... | collective-permute-start | bytes 1769480 | tf_op jit(solution)/shard_map/ppermute | solution.py:830
  200.3 12.2 %fusion.14.own_k.own_v = bf16[768,3072]{1,0:T(8,128)(2,1)} fusion(bf16[768,1536]{1,0:T(8,128)(2,1)} %fusion.18, bf16[1536,4608]{1,0:T(8,128)(2,1)} %bitcast.204), kind=kOutput, calls=%fused_computation.36 | convolution fusion | flops 7250116608 | bytes 16515072 | tf_op jit(solution)/shard_map/dot_general | solution.py:28
  216.7 16.4 %collective-permute-done.11 = bf16[48,6144]{1,0:T(8,128)(2,1)} collective-permute-done((bf16[48,6144]{1,0:T(8,128)(2,1)}, bf16[48,6144]{1,0:T(8,128)(2,1)}, u32[]{:S(2)}, u32[]{:S(2)}) %collective-permute-start.11) | collective-permute-done | bytes 589856 | tf_op jit(solution)/shard_map/ppermute | solution.py:830
  243.8 5.7 collective-permute-start.19
  253.9 6.9 fusion.64.q_ref
  260.8 58.5 %self_attend.1 = (bf16[768,1536]{1,0:T(8,128)(2,1)S(1)}, f32[96,768]{1,0:T(8,128)S(1)}) custom-call(s32[5]{0:T(128)S(1)} %stack.66.place, bf16[768,1536]{1,0:T(8,128)(2,1)S(1)} %fusion.64.q_ref, bf16[768,3072]{1,0:T(8,128)(2,1)S(1)} %bitcast.172, bf16[768,3072]{1,0:T(8,128)(2,1)S(1)} %bitcast.172, bf16[768,3072]{1,0:T(8,128)(2,1)} %collective-permute-done.14.other_k.other_v, ...), custom_call_target="tpu_custom_call" | custom-call | flops 7247757312 | bytes 18874368 | tf_op jit(solution)/shard_map/self_attend/pallas_call | solution.py:569
  336.1 6.9 collective-permute-done.16
  344.5 7.1 fusion.134
  360.5 10.4 collective-permute-start.23
  373.3 6.8 cross_attend.1
  386.9 63.0 %multiply_convert_fusion = (bf16[768,6144]{1,0:T(8,128)(2,1)}, f32[768,6144]{1,0:T(8,128)}, f32[768,6144]{1,0:T(8,128)}) fusion(bf16[1536,6144]{1,0:T(8,128)(2,1)} %bitcast.200, f32[768,1536]{1,0:T(8,128)} %copy-done.24, f32[1536]{0:T(1024)S(1)} %add.437, f32[1536]{0:T(1024)S(1)} %mul.317, f32[768]{0:T(1024)S(1)} %add_rsqrt_fusion, ...), kind=kOutput, calls=%fused_computation.5 | convolution fusion | flops 14808121344 | bytes 70797312 | tf_op jit(solution)/shard_map/dot_general | solution.py:28
  452.9 23.5 %multiply_convert_fusion.1 = (bf16[768,1536]{1,0:T(8,128)(2,1)S(1)}, bf16[768,1536]{1,0:T(8,128)(2,1)}, f32[768,1536]{1,0:T(8,128)}) fusion(f32[]{:T(128)S(6)} %div.75, f32[768]{0:T(1024)S(1)} %copy-done.89, bf16[384,1536]{1,0:T(8,128)(2,1)} %get-tuple-element.210, bf16[384,1536]{1,0:T(8,128)(2,1)S(1)} %get-tuple-element.209, f32[768,1536]{1,0:T(8,128)} %copy-done.24, ...), kind=kOutput, calls=%fused_computation.66 | convolution fusion | flops 14507311104 | bytes 44829700 | tf_op jit(solution)/shard_map/dot_general | solution.py:28
  476.4 9.8 convolution_convert_fusion.2
  489.7 29.5 %add_convert_fusion.2 = bf16[768,6144]{1,0:T(8,128)(2,1)} fusion(f32[768,6144]{1,0:T(8,128)} %get-tuple-element.191, f32[768,6144]{1,0:T(8,128)} %get-tuple-element.244, bf16[768,1536]{1,0:T(8,128)(2,1)} %copy-done.56, bf16[6144,1536]{1,0:T(8,128)(2,1)} %bitcast.203), kind=kOutput, calls=%fused_computation.4 | convolution fusion | flops 14561574912 | bytes 68419584 | tf_op jit(solution)/shard_map/re,de->rd/dot_general | solution.py:36
  519.2 14.1 %add_convert_fusion.1 = bf16[768,6144]{1,0:T(8,128)(2,1)} fusion(bf16[768,6144]{1,0:T(8,128)(2,1)} %collective-permute-done.26, bf16[768,6144]{1,0:T(8,128)(2,1)} %get-tuple-element.190, bf16[768,1536]{1,0:T(8,128)(2,1)} %copy-done.56, s32[]{:T(128)S(6)} %select_n.335), kind=kOutput, calls=%fused_computation.3 | convolution fusion | flops 7261913088 | bytes 29491204 | tf_op jit(solution)/shard_map/rd,re->de/dot_general | solution.py:32
  533.3 13.5 %convolution_convert_fusion.1 = bf16[3072,1536]{1,0:T(8,128)(2,1)} fusion(bf16[768,6144]{1,0:T(8,128)(2,1)} %add_convert_fusion.2, s32[]{:T(128)S(6)} %select_n.336, f32[768,1536]{1,0:T(8,128)} %copy-done.24, f32[1536]{0:T(1024)S(1)} %add.437, f32[1536]{0:T(1024)S(1)} %mul.317, f32[768]{0:T(1024)S(1)} %add_rsqrt_fusion, f32[768]{0:T(1024)S(1)} %broadcast_multiply_fusion.6), kind=kOutput, calls=%fused_computation.21 | convolution fusion | flops 7258374144 | bytes 18892804 | tf_op jit(solution)/shard_map/rd,re->de/dot_general | solution.py:32
  547.8 6.8 collective-permute-start.25
  554.6 21.6 %fusion.136 = f32[768,1536]{1,0:T(8,128)} fusion(bf16[768,6144]{1,0:T(8,128)(2,1)} %add_convert_fusion.2, bf16[1536,6144]{1,0:T(8,128)(2,1)} %bitcast.201), kind=kOutput, calls=%fused_computation.302 | convolution fusion | flops 14495514624 | bytes 33030144 | tf_op jit(solution)/shard_map/re,de->rd/dot_general | solution.py:36
  581.2 14.0 %add_convert_fusion = bf16[3072,1536]{1,0:T(8,128)(2,1)} fusion(bf16[3072,1536]{1,0:T(8,128)(2,1)} %collective-permute-done.27, bf16[768,6144]{1,0:T(8,128)(2,1)} %add_convert_fusion.2, s32[]{:T(128)S(6)} %select_n.339, f32[768,1536]{1,0:T(8,128)S(1)} %bitcast.176, f32[1536]{0:T(1024)S(1)} %add.437, f32[1536]{0:T(1024)S(1)} %mul.317, ...), kind=kOutput, calls=%fused_computation.2 | convolution fusion | flops 7267811328 | bytes 28329988 | tf_op jit(solution)/shard_map/rd,re->de/dot_general | solution.py:32
  595.3 6.1 multiply_reduce_fusion.1
  601.4 9.6 fusion.131
  614.5 6.6 fusion.61.grad_ref
  621.1 9.5 cross_attend_back.1
  638.0 5.9 collective-permute-done.32
  652.4 9.4 multiply_reduce_fusion.2
  669.5 7.5 fusion.55.grad_ref
  705.7 70.1 %self_attend_back.1 = (bf16[768,1536]{1,0:T(8,128)(2,1)S(1)}, bf16[768,1536]{1,0:T(8,128)(2,1)S(1)}, bf16[768,1536]{1,0:T(8,128)(2,1)S(1)}, bf16[768,1536]{1,0:T(8,128)(2,1)}, bf16[768,1536]{1,0:T(8,128)(2,1)}) custom-call(s32[5]{0:T(128)S(1)} %copy-done.14, bf16[768,1536]{1,0:T(8,128)(2,1)S(1)} %copy-done.21, bf16[768,3072]{1,0:T(8,128)(2,1)} %fusion.14.own_k.own_v, ...), custom_call_target="tpu_custom_call" | custom-call | flops 18119393280 | bytes 37748736 | tf_op jit(solution)/shard_map/self_attend_back/pallas_call | solution.py:598
  790.9 7.8 convolution_convert_fusion
  798.8 18.6 %fusion.137 = f32[768,1536]{1,0:T(8,128)} fusion(bf16[768,4608]{1,0:T(8,128)(2,1)} %copy-done.30, bf16[1536,4608]{1,0:T(8,128)(2,1)} %bitcast.206), kind=kOutput, calls=%fused_computation.303 | convolution fusion | flops 10871635968 | bytes 25952256 | tf_op jit(solution)/shard_map/re,de->rd/dot_general | solution.py:36
  817.4 9.8 add_convert_fusion.3
  856.1 19.6 %collective-permute-done.46 = bf16[768,384]{1,0:T(8,128)(2,1)} collective-permute-done((bf16[768,384]{1,0:T(8,128)(2,1)}, bf16[768,384]{1,0:T(8,128)(2,1)}, u32[]{:S(2)}, u32[]{:S(2)}) %collective-permute-start.46) | collective-permute-done | bytes 589856 | tf_op jit(solution)/shard_map/ppermute | solution.py:830
  891.0 12.7 %collective-permute-start.54 = (bf16[576,384]{1,0:T(8,128)(2,1)}, bf16[576,384]{1,0:T(8,128)(2,1)}, u32[]{:S(2)}, u32[]{:S(2)}) collective-permute-start(bf16[576,384]{1,0:T(8,128)(2,1)} %get-tuple-element.224), channel_id=1, source_target_pairs={{0,1},{1,2},{2,3},{3,0},{4,5},{5,6},{6,7},{7,4},{8,9},{9,10},{10,1... | collective-permute-start | bytes 1327112 | tf_op jit(solution)/shard_map/ppermute | solution.py:830
  915.9 18.6 %collective-permute-done.55 = bf16[576,384]{1,0:T(8,128)(2,1)} collective-permute-done((bf16[576,384]{1,0:T(8,128)(2,1)}, bf16[576,384]{1,0:T(8,128)(2,1)}, u32[]{:S(2)}, u32[]{:S(2)}) %collective-permute-start.55) | collective-permute-done | bytes 442400 | tf_op jit(solution)/shard_map/ppermute | solution.py:830
  937.0 10.0 collective-permute-start.51
  960.2 5.7 collective-permute-done.57
  965.9 17.5 %collective-permute-done.58 = bf16[576,384]{1,0:T(8,128)(2,1)S(1)} collective-permute-done((bf16[576,384]{1,0:T(8,128)(2,1)S(1)}, bf16[576,384]{1,0:T(8,128)(2,1)S(1)}, u32[]{:S(2)}, u32[]{:S(2)}) %collective-permute-start.58) | collective-permute-done | bytes 442400 | tf_op jit(solution)/shard_map/ppermute | solution.py:830
  986.5 11.1 %collective-permute-start.61 = (bf16[384,1536]{1,0:T(8,128)(2,1)S(1)}, bf16[384,1536]{1,0:T(8,128)(2,1)S(1)}, u32[]{:S(2)}, u32[]{:S(2)}) collective-permute-start(bf16[384,1536]{1,0:T(8,128)(2,1)S(1)} %get-tuple-element.200), channel_id=1, source_target_pairs={{1,0},{5,1},{4,2},{0,3},{3,4},{7,5},{6,6},{2,7},{9,8},{13,9},{12,1... | collective-permute-start | bytes 3538952 | tf_op jit(solution)/shard_map/ppermute | solution.py:857
  999.7 29.7 %collective-permute-done.61 = bf16[384,1536]{1,0:T(8,128)(2,1)S(1)} collective-permute-done((bf16[384,1536]{1,0:T(8,128)(2,1)S(1)}, bf16[384,1536]{1,0:T(8,128)(2,1)S(1)}, u32[]{:S(2)}, u32[]{:S(2)}) %collective-permute-start.61) | collective-permute-done | bytes 1179680 | tf_op jit(solution)/shard_map/ppermute | solution.py:857
  1038.7 5.4 copy-done.2
  1049.3 8.1 unpack.19
  1068.2 11.9 %all-gather.16.cloned.1.call-done = bf16[4608,384]{1,0:T(8,128)(2,1)} async-done(((bf16[576,384]{1,0:T(8,128)(2,1)}), bf16[4608,384]{1,0:T(8,128)(2,1)}) %all-gather.16.cloned.1.call-update) | async-done | bytes 3538960 | tf_op jit(solution)/shard_map/all_gather | solution.py:1191
  (567 shorter events, 311.7 us)
Async XLA Ops:
  7.2 193.1 %all-gather.8.cloned.1.call-start = ((), (), s32[]{:S(2)}) async-start(), calls=%async_computation.4 | async-start | bytes 15925248 | tf_op jit(solution)/shard_map/all_gather | solution.py:867
  16.7 40.9 %collective-permute-start.1 = (bf16[64,4608]{1,0:T(8,128)(2,1)S(1)}, bf16[64,4608]{1,0:T(8,128)(2,1)}, u32[]{:S(2)}, u32[]{:S(2)}) collective-permute-start(bf16[64,4608]{1,0:T(8,128)(2,1)S(1)} %pad_maximum_fusion.5), channel_id=1, source_target_pairs={{0,2},{1,3},{2,0},{3,1},{4,6},{5,7},{6,4},{7,5},{8,10},{9,11},{10,... | collective-permute-start | bytes 1769480 | tf_op jit(solution)/shard_map/ppermute | solution.py:830
  19.3 39.3 %collective-permute-start.2 = (bf16[64,4608]{1,0:T(8,128)(2,1)S(1)}, bf16[64,4608]{1,0:T(8,128)(2,1)}, u32[]{:S(2)}, u32[]{:S(2)}) collective-permute-start(bf16[64,4608]{1,0:T(8,128)(2,1)S(1)} %pad_maximum_fusion.5), channel_id=1, source_target_pairs={{0,3},{1,0},{2,1},{3,2},{4,7},{5,4},{6,5},{7,6},{8,11},{9,8},{10,9... | collective-permute-start | bytes 1769480 | tf_op jit(solution)/shard_map/ppermute | solution.py:830
  61.0 283.4 %all-gather.10.cloned.1.call-start = ((), (), s32[]{:S(2)}) async-start(), calls=%async_computation.5 | async-start | bytes 15925248 | tf_op jit(solution)/shard_map/all_gather | solution.py:867
  63.1 25.4 %collective-permute-start.3 = (bf16[48,4608]{1,0:T(8,128)(2,1)S(1)}, bf16[48,4608]{1,0:T(8,128)(2,1)S(1)}, u32[]{:S(2)}, u32[]{:S(2)}) collective-permute-start(bf16[48,4608]{1,0:T(8,128)(2,1)S(1)} %pad_maximum_fusion.7), channel_id=1, source_target_pairs={{0,1},{1,2},{2,3},{3,0},{4,5},{5,6},{6,7},{7,4},{8,9},{9,10},{10,1... | collective-permute-start | bytes 1327112 | tf_op jit(solution)/shard_map/ppermute | solution.py:830
  75.4 30.3 %collective-permute-start.4 = (bf16[48,4608]{1,0:T(8,128)(2,1)S(1)}, bf16[48,4608]{1,0:T(8,128)(2,1)S(1)}, u32[]{:S(2)}, u32[]{:S(2)}) collective-permute-start(bf16[48,4608]{1,0:T(8,128)(2,1)S(1)} %pad_maximum_fusion.7), channel_id=1, source_target_pairs={{0,2},{1,3},{2,0},{3,1},{4,6},{5,7},{6,4},{7,5},{8,10},{9,11},{10,... | collective-permute-start | bytes 1327112 | tf_op jit(solution)/shard_map/ppermute | solution.py:830
  78.1 27.6 %collective-permute-start.5 = (bf16[48,4608]{1,0:T(8,128)(2,1)S(1)}, bf16[48,4608]{1,0:T(8,128)(2,1)S(1)}, u32[]{:S(2)}, u32[]{:S(2)}) collective-permute-start(bf16[48,4608]{1,0:T(8,128)(2,1)S(1)} %pad_maximum_fusion.7), channel_id=1, source_target_pairs={{0,3},{1,0},{2,1},{3,2},{4,7},{5,4},{6,5},{7,6},{8,11},{9,8},{10,9... | collective-permute-start | bytes 1327112 | tf_op jit(solution)/shard_map/ppermute | solution.py:830
  107.0 280.0 %all-gather.12.cloned.1.call-start = ((), (), s32[]{:S(2)}) async-start(), calls=%async_computation.6 | async-start | bytes 21233664 | tf_op jit(solution)/shard_map/all_gather | solution.py:867
  122.3 32.4 %collective-permute-start.6 = (bf16[384,1536]{1,0:T(8,128)(2,1)}, bf16[384,1536]{1,0:T(8,128)(2,1)S(1)}, u32[]{:S(2)}, u32[]{:S(2)}) collective-permute-start(bf16[384,1536]{1,0:T(8,128)(2,1)} %get-tuple-element.218), channel_id=1, source_target_pairs={{0,0},{1,4},{2,5},{3,1},{4,2},{5,6},{6,7},{7,3},{8,8},{9,12},{10,1... | collective-permute-start | bytes 3538952 | tf_op jit(solution)/shard_map/ppermute | solution.py:844
  124.2 51.4 %collective-permute-start.7 = (bf16[384,1536]{1,0:T(8,128)(2,1)}, bf16[384,1536]{1,0:T(8,128)(2,1)}, u32[]{:S(2)}, u32[]{:S(2)}) collective-permute-start(bf16[384,1536]{1,0:T(8,128)(2,1)} %get-tuple-element.217), channel_id=1, source_target_pairs={{0,1},{1,5},{2,4},{3,0},{4,3},{5,7},{6,6},{7,2},{8,9},{9,13},{10,1... | collective-permute-start | bytes 3538952 | tf_op jit(solution)/shard_map/ppermute | solution.py:845
  175.5 41.2 %collective-permute-start.10 = (bf16[48,6144]{1,0:T(8,128)(2,1)}, bf16[48,6144]{1,0:T(8,128)(2,1)}, u32[]{:S(2)}, u32[]{:S(2)}) collective-permute-start(bf16[48,6144]{1,0:T(8,128)(2,1)} %get-tuple-element.91), channel_id=1, source_target_pairs={{0,2},{1,3},{2,0},{3,1},{4,6},{5,7},{6,4},{7,5},{8,10},{9,11},{10,... | collective-permute-start | bytes 1769480 | tf_op jit(solution)/shard_map/ppermute | solution.py:830
  192.3 40.8 %collective-permute-start.11 = (bf16[48,6144]{1,0:T(8,128)(2,1)}, bf16[48,6144]{1,0:T(8,128)(2,1)}, u32[]{:S(2)}, u32[]{:S(2)}) collective-permute-start(bf16[48,6144]{1,0:T(8,128)(2,1)} %get-tuple-element.91), channel_id=1, source_target_pairs={{0,3},{1,0},{2,1},{3,2},{4,7},{5,4},{6,5},{7,6},{8,11},{9,8},{10,9... | collective-permute-start | bytes 1769480 | tf_op jit(solution)/shard_map/ppermute | solution.py:830
  192.3 40.8 %collective-permute-start.9 = (bf16[48,6144]{1,0:T(8,128)(2,1)}, bf16[48,6144]{1,0:T(8,128)(2,1)}, u32[]{:S(2)}, u32[]{:S(2)}) collective-permute-start(bf16[48,6144]{1,0:T(8,128)(2,1)} %get-tuple-element.91), channel_id=1, source_target_pairs={{0,1},{1,2},{2,3},{3,0},{4,5},{5,6},{6,7},{7,4},{8,9},{9,10},{10,1... | collective-permute-start | bytes 1769480 | tf_op jit(solution)/shard_map/ppermute | solution.py:830
  237.9 215.0 %all-gather.14.cloned.1.call-start = ((), (), s32[]{:S(2)}) async-start(), calls=%async_computation.7 | async-start | bytes 21233664 | tf_op jit(solution)/shard_map/all_gather | solution.py:867
  243.8 75.6 %collective-permute-start.19 = (bf16[192,1536]{1,0:T(8,128)(2,1)}, bf16[192,1536]{1,0:T(8,128)(2,1)S(1)}, u32[]{:S(2)}, u32[]{:S(2)}) collective-permute-start(bf16[192,1536]{1,0:T(8,128)(2,1)} %get-tuple-element.102), channel_id=1, source_target_pairs={{0,1},{1,2},{2,3},{3,0},{4,5},{5,6},{6,7},{7,4},{8,9},{9,10},{10,1... | collective-permute-start | bytes 1769480 | tf_op jit(solution)/shard_map/ppermute | solution.py:830
  249.5 69.9 %collective-permute-start.20 = (bf16[192,1536]{1,0:T(8,128)(2,1)}, bf16[192,1536]{1,0:T(8,128)(2,1)S(1)}, u32[]{:S(2)}, u32[]{:S(2)}) collective-permute-start(bf16[192,1536]{1,0:T(8,128)(2,1)} %get-tuple-element.102), channel_id=1, source_target_pairs={{0,2},{1,3},{2,0},{3,1},{4,6},{5,7},{6,4},{7,5},{8,10},{9,11},{10,... | collective-permute-start | bytes 1769480 | tf_op jit(solution)/shard_map/ppermute | solution.py:830
  250.9 68.5 %collective-permute-start.21 = (bf16[192,1536]{1,0:T(8,128)(2,1)}, bf16[192,1536]{1,0:T(8,128)(2,1)S(1)}, u32[]{:S(2)}, u32[]{:S(2)}) collective-permute-start(bf16[192,1536]{1,0:T(8,128)(2,1)} %get-tuple-element.102), channel_id=1, source_target_pairs={{0,3},{1,0},{2,1},{3,2},{4,7},{5,4},{6,5},{7,6},{8,11},{9,8},{10,9... | collective-permute-start | bytes 1769480 | tf_op jit(solution)/shard_map/ppermute | solution.py:830
  322.0 372.0 %reduce-scatter.5.cloned.1.call-start = ((), (), s32[]{:S(2)}) async-start(), calls=%async_computation.8 | async-start | bytes 11796480 | tf_op jit(solution)/shard_map/reduce_scatter | solution.py:1011
  344.3 28.9 %collective-permute-start.18 = (bf16[64,1536]{1,0:T(8,128)(2,1)S(1)}, bf16[64,1536]{1,0:T(8,128)(2,1)S(1)}, u32[]{:S(2)}, u32[]{:S(2)}) collective-permute-start(bf16[64,1536]{1,0:T(8,128)(2,1)S(1)} %fusion.89), channel_id=1, source_target_pairs={{0,4},{4,0},{1,5},{5,1},{2,6},{6,2},{3,7},{7,3},{8,12},{12,8},{9,1... | collective-permute-start | bytes 589832 | tf_op jit(solution)/shard_map/ppermute | solution.py:973
  360.5 89.4 %collective-permute-start.23 = (bf16[384,1536]{1,0:T(8,128)(2,1)}, bf16[384,1536]{1,0:T(8,128)(2,1)}, u32[]{:S(2)}, u32[]{:S(2)}) collective-permute-start(bf16[384,1536]{1,0:T(8,128)(2,1)} %get-tuple-element.212), channel_id=1, source_target_pairs={{0,0},{1,4},{2,5},{3,1},{4,2},{5,6},{6,7},{7,3},{8,8},{9,12},{10,1... | collective-permute-start | bytes 3538952 | tf_op jit(solution)/shard_map/ppermute | solution.py:844
  370.9 79.0 %collective-permute-start.24 = (bf16[384,1536]{1,0:T(8,128)(2,1)}, bf16[384,1536]{1,0:T(8,128)(2,1)}, u32[]{:S(2)}, u32[]{:S(2)}) collective-permute-start(bf16[384,1536]{1,0:T(8,128)(2,1)} %get-tuple-element.211), channel_id=1, source_target_pairs={{0,1},{1,5},{2,4},{3,0},{4,3},{5,7},{6,6},{7,2},{8,9},{9,13},{10,1... | collective-permute-start | bytes 3538952 | tf_op jit(solution)/shard_map/ppermute | solution.py:845
  486.2 33.0 %collective-permute-start.26 = (bf16[768,6144]{1,0:T(8,128)(2,1)}, bf16[768,6144]{1,0:T(8,128)(2,1)}, u32[]{:S(2)}, u32[]{:S(2)}) collective-permute-start(bf16[768,6144]{1,0:T(8,128)(2,1)} %convolution_convert_fusion.2), channel_id=1, source_target_pairs={{0,4},{4,0},{1,5},{5,1},{2,6},{6,2},{3,7},{7,3},{8,12},{12,8},{9,1... | collective-permute-start | bytes 28311560 | tf_op jit(solution)/shard_map/ppermute | solution.py:1006
  487.9 31.2 %collective-permute-start.22 = (bf16[384,1536]{1,0:T(8,128)(2,1)S(1)}, bf16[384,1536]{1,0:T(8,128)(2,1)}, u32[]{:S(2)}, u32[]{:S(2)}) collective-permute-start(bf16[384,1536]{1,0:T(8,128)(2,1)S(1)} %get-tuple-element.213), channel_id=1, source_target_pairs={{0,0},{4,1},{5,2},{1,3},{2,4},{6,5},{7,6},{3,7},{8,8},{12,9},{13,1... | collective-permute-start | bytes 3538952 | tf_op jit(solution)/shard_map/ppermute | solution.py:1034
  533.3 296.9 %reduce-scatter.7.cloned.1.call-start = ((), (), s32[]{:S(2)}) async-start(), calls=%async_computation.9 | async-start | bytes 11796480 | tf_op jit(solution)/shard_map/reduce_scatter | solution.py:1011
  546.8 34.3 %collective-permute-start.27 = (bf16[3072,1536]{1,0:T(8,128)(2,1)}, bf16[3072,1536]{1,0:T(8,128)(2,1)}, u32[]{:S(2)}, u32[]{:S(2)}) collective-permute-start(bf16[3072,1536]{1,0:T(8,128)(2,1)} %convolution_convert_fusion.1), channel_id=1, source_target_pairs={{0,4},{4,0},{1,5},{5,1},{2,6},{6,2},{3,7},{7,3},{8,12},{12,8},{9,1... | collective-permute-start | bytes 28311560 | tf_op jit(solution)/shard_map/ppermute | solution.py:1006
  547.8 33.3 %collective-permute-start.25 = (bf16[384,1536]{1,0:T(8,128)(2,1)S(1)}, bf16[384,1536]{1,0:T(8,128)(2,1)}, u32[]{:S(2)}, u32[]{:S(2)}) collective-permute-start(bf16[384,1536]{1,0:T(8,128)(2,1)S(1)} %get-tuple-element.111), channel_id=1, source_target_pairs={{1,0},{5,1},{4,2},{0,3},{3,4},{7,5},{6,6},{2,7},{9,8},{13,9},{12,1... | collective-permute-start | bytes 3538952 | tf_op jit(solution)/shard_map/ppermute | solution.py:1044
  595.2 291.8 %reduce-scatter.11.cloned.1.call-start = ((), (), s32[]{:S(2)}) async-start(), calls=%async_computation.11 | async-start | bytes 10321920 | tf_op jit(solution)/shard_map/reduce_scatter | solution.py:1011
  614.5 30.1 %collective-permute-start.28 = (bf16[768,1536]{1,0:T(8,128)(2,1)}, bf16[768,1536]{1,0:T(8,128)(2,1)}, u32[]{:S(2)}, u32[]{:S(2)}) collective-permute-start(bf16[768,1536]{1,0:T(8,128)(2,1)} %convolution_convert_fusion.5), channel_id=1, source_target_pairs={{0,4},{4,0},{1,5},{5,1},{2,6},{6,2},{3,7},{7,3},{8,12},{12,8},{9,1... | collective-permute-start | bytes 7077896 | tf_op jit(solution)/shard_map/ppermute | solution.py:1006
  635.2 32.5 %collective-permute-start.33 = (bf16[64,1536]{1,0:T(8,128)(2,1)}, bf16[64,1536]{1,0:T(8,128)(2,1)S(1)}, u32[]{:S(2)}, u32[]{:S(2)}) collective-permute-start(bf16[64,1536]{1,0:T(8,128)(2,1)} %get-tuple-element.183), channel_id=1, source_target_pairs={{0,2},{1,3},{2,0},{3,1},{4,6},{5,7},{6,4},{7,5},{8,10},{9,11},{10,... | collective-permute-start | bytes 589832 | tf_op jit(solution)/shard_map/ppermute | solution.py:830
  637.5 30.3 %collective-permute-start.34 = (bf16[64,1536]{1,0:T(8,128)(2,1)}, bf16[64,1536]{1,0:T(8,128)(2,1)S(1)}, u32[]{:S(2)}, u32[]{:S(2)}) collective-permute-start(bf16[64,1536]{1,0:T(8,128)(2,1)} %get-tuple-element.183), channel_id=1, source_target_pairs={{0,3},{1,0},{2,1},{3,2},{4,7},{5,4},{6,5},{7,6},{8,11},{9,8},{10,9... | collective-permute-start | bytes 589832 | tf_op jit(solution)/shard_map/ppermute | solution.py:830
  652.3 24.7 %collective-permute-start.29 = (bf16[768,1536]{1,0:T(8,128)(2,1)}, bf16[768,1536]{1,0:T(8,128)(2,1)S(1)}, u32[]{:S(2)}, u32[]{:S(2)}) collective-permute-start(bf16[768,1536]{1,0:T(8,128)(2,1)} %convolution_convert_fusion.4), channel_id=1, source_target_pairs={{0,4},{4,0},{1,5},{5,1},{2,6},{6,2},{3,7},{7,3},{8,12},{12,8},{9,1... | collective-permute-start | bytes 7077896 | tf_op jit(solution)/shard_map/ppermute | solution.py:1006
  684.9 264.5 %reduce-scatter.9.cloned.1.call-start = ((), (), s32[]{:S(2)}) async-start(), calls=%async_computation.10 | async-start | bytes 8847360 | tf_op jit(solution)/shard_map/reduce_scatter | solution.py:1011
  690.2 88.4 %collective-permute-start.37 = (bf16[2,64,384]{2,1,0:T(8,128)(2,1)S(1)}, bf16[2,64,384]{2,1,0:T(8,128)(2,1)}, u32[]{:S(2)}, u32[]{:S(2)}) collective-permute-start(bf16[2,64,384]{2,1,0:T(8,128)(2,1)S(1)} %fusion.94), channel_id=1, source_target_pairs={{0,2},{1,3},{2,0},{3,1},{4,6},{5,7},{6,4},{7,5},{8,10},{9,11},{10,... | collective-permute-start | bytes 294920 | tf_op jit(solution)/shard_map/ppermute | solution.py:830
  692.6 86.0 %collective-permute-start.38 = (bf16[2,64,384]{2,1,0:T(8,128)(2,1)S(1)}, bf16[2,64,384]{2,1,0:T(8,128)(2,1)}, u32[]{:S(2)}, u32[]{:S(2)}) collective-permute-start(bf16[2,64,384]{2,1,0:T(8,128)(2,1)S(1)} %fusion.94), channel_id=1, source_target_pairs={{0,3},{1,0},{2,1},{3,2},{4,7},{5,4},{6,5},{7,6},{8,11},{9,8},{10,9... | collective-permute-start | bytes 294920 | tf_op jit(solution)/shard_map/ppermute | solution.py:830
  695.6 83.0 %collective-permute-start.39 = (bf16[192,1536]{1,0:T(8,128)(2,1)S(1)}, bf16[192,1536]{1,0:T(8,128)(2,1)S(1)}, u32[]{:S(2)}, u32[]{:S(2)}) collective-permute-start(bf16[192,1536]{1,0:T(8,128)(2,1)S(1)} %get-tuple-element.206), channel_id=1, source_target_pairs={{0,1},{1,2},{2,3},{3,0},{4,5},{5,6},{6,7},{7,4},{8,9},{9,10},{10,1... | collective-permute-start | bytes 1769480 | tf_op jit(solution)/shard_map/ppermute | solution.py:830
  696.2 82.4 %collective-permute-start.40 = (bf16[192,1536]{1,0:T(8,128)(2,1)S(1)}, bf16[192,1536]{1,0:T(8,128)(2,1)}, u32[]{:S(2)}, u32[]{:S(2)}) collective-permute-start(bf16[192,1536]{1,0:T(8,128)(2,1)S(1)} %get-tuple-element.205), channel_id=1, source_target_pairs={{0,2},{1,3},{2,0},{3,1},{4,6},{5,7},{6,4},{7,5},{8,10},{9,11},{10,... | collective-permute-start | bytes 1769480 | tf_op jit(solution)/shard_map/ppermute | solution.py:830
  697.8 80.8 %collective-permute-start.41 = (bf16[192,1536]{1,0:T(8,128)(2,1)S(1)}, bf16[192,1536]{1,0:T(8,128)(2,1)}, u32[]{:S(2)}, u32[]{:S(2)}) collective-permute-start(bf16[192,1536]{1,0:T(8,128)(2,1)S(1)} %get-tuple-element.204), channel_id=1, source_target_pairs={{0,3},{1,0},{2,1},{3,2},{4,7},{5,4},{6,5},{7,6},{8,11},{9,8},{10,9... | collective-permute-start | bytes 1769480 | tf_op jit(solution)/shard_map/ppermute | solution.py:830
  827.3 202.1 %all-gather.18.cloned.1.call-start = ((), (), s32[]{:S(2)}) async-start(), calls=%async_computation.13 | async-start | bytes 17252352 | tf_op jit(solution)/shard_map/all_gather | solution.py:1177
  833.0 23.1 %collective-permute-start.45 = (bf16[768,384]{1,0:T(8,128)(2,1)}, bf16[768,384]{1,0:T(8,128)(2,1)}, u32[]{:S(2)}, u32[]{:S(2)}) collective-permute-start(bf16[768,384]{1,0:T(8,128)(2,1)} %get-tuple-element.203), channel_id=1, source_target_pairs={{0,1},{1,2},{2,3},{3,0},{4,5},{5,6},{6,7},{7,4},{8,9},{9,10},{10,1... | collective-permute-start | bytes 1769480 | tf_op jit(solution)/shard_map/ppermute | solution.py:830
  833.0 42.7 %collective-permute-start.46 = (bf16[768,384]{1,0:T(8,128)(2,1)}, bf16[768,384]{1,0:T(8,128)(2,1)}, u32[]{:S(2)}, u32[]{:S(2)}) collective-permute-start(bf16[768,384]{1,0:T(8,128)(2,1)} %get-tuple-element.202), channel_id=1, source_target_pairs={{0,2},{1,3},{2,0},{3,1},{4,6},{5,7},{6,4},{7,5},{8,10},{9,11},{10,... | collective-permute-start | bytes 1769480 | tf_op jit(solution)/shard_map/ppermute | solution.py:830
  834.3 41.4 %collective-permute-start.47 = (bf16[768,384]{1,0:T(8,128)(2,1)}, bf16[768,384]{1,0:T(8,128)(2,1)}, u32[]{:S(2)}, u32[]{:S(2)}) collective-permute-start(bf16[768,384]{1,0:T(8,128)(2,1)} %get-tuple-element.201), channel_id=1, source_target_pairs={{0,3},{1,0},{2,1},{3,2},{4,7},{5,4},{6,5},{7,6},{8,11},{9,8},{10,9... | collective-permute-start | bytes 1769480 | tf_op jit(solution)/shard_map/ppermute | solution.py:830
  891.0 24.9 %collective-permute-start.54 = (bf16[576,384]{1,0:T(8,128)(2,1)}, bf16[576,384]{1,0:T(8,128)(2,1)}, u32[]{:S(2)}, u32[]{:S(2)}) collective-permute-start(bf16[576,384]{1,0:T(8,128)(2,1)} %get-tuple-element.224), channel_id=1, source_target_pairs={{0,1},{1,2},{2,3},{3,0},{4,5},{5,6},{6,7},{7,4},{8,9},{9,10},{10,1... | collective-permute-start | bytes 1327112 | tf_op jit(solution)/shard_map/ppermute | solution.py:830
  903.7 30.8 %collective-permute-start.55 = (bf16[576,384]{1,0:T(8,128)(2,1)}, bf16[576,384]{1,0:T(8,128)(2,1)}, u32[]{:S(2)}, u32[]{:S(2)}) collective-permute-start(bf16[576,384]{1,0:T(8,128)(2,1)} %get-tuple-element.223), channel_id=1, source_target_pairs={{0,2},{1,3},{2,0},{3,1},{4,6},{5,7},{6,4},{7,5},{8,10},{9,11},{10,... | collective-permute-start | bytes 1327112 | tf_op jit(solution)/shard_map/ppermute | solution.py:830
  905.0 29.5 %collective-permute-start.56 = (bf16[576,384]{1,0:T(8,128)(2,1)}, bf16[576,384]{1,0:T(8,128)(2,1)}, u32[]{:S(2)}, u32[]{:S(2)}) collective-permute-start(bf16[576,384]{1,0:T(8,128)(2,1)} %get-tuple-element.222), channel_id=1, source_target_pairs={{0,3},{1,0},{2,1},{3,2},{4,7},{5,4},{6,5},{7,6},{8,11},{9,8},{10,9... | collective-permute-start | bytes 1327112 | tf_op jit(solution)/shard_map/ppermute | solution.py:830
  936.9 143.1 %all-gather.16.cloned.1.call-start = ((), (), s32[]{:S(2)}) async-start(), calls=%async_computation.12 | async-start | bytes 3981312 | tf_op jit(solution)/shard_map/all_gather | solution.py:1191
  951.9 31.5 %collective-permute-start.58 = (bf16[576,384]{1,0:T(8,128)(2,1)S(1)}, bf16[576,384]{1,0:T(8,128)(2,1)S(1)}, u32[]{:S(2)}, u32[]{:S(2)}) collective-permute-start(bf16[576,384]{1,0:T(8,128)(2,1)S(1)} %get-tuple-element.220), channel_id=1, source_target_pairs={{0,2},{1,3},{2,0},{3,1},{4,6},{5,7},{6,4},{7,5},{8,10},{9,11},{10,... | collective-permute-start | bytes 1327112 | tf_op jit(solution)/shard_map/ppermute | solution.py:830
  953.4 30.0 %collective-permute-start.59 = (bf16[576,384]{1,0:T(8,128)(2,1)S(1)}, bf16[576,384]{1,0:T(8,128)(2,1)S(1)}, u32[]{:S(2)}, u32[]{:S(2)}) collective-permute-start(bf16[576,384]{1,0:T(8,128)(2,1)S(1)} %get-tuple-element.219), channel_id=1, source_target_pairs={{0,3},{1,0},{2,1},{3,2},{4,7},{5,4},{6,5},{7,6},{8,11},{9,8},{10,9... | collective-permute-start | bytes 1327112 | tf_op jit(solution)/shard_map/ppermute | solution.py:830
  986.5 42.8 %collective-permute-start.61 = (bf16[384,1536]{1,0:T(8,128)(2,1)S(1)}, bf16[384,1536]{1,0:T(8,128)(2,1)S(1)}, u32[]{:S(2)}, u32[]{:S(2)}) collective-permute-start(bf16[384,1536]{1,0:T(8,128)(2,1)S(1)} %get-tuple-element.200), channel_id=1, source_target_pairs={{1,0},{5,1},{4,2},{0,3},{3,4},{7,5},{6,6},{2,7},{9,8},{13,9},{12,1... | collective-permute-start | bytes 3538952 | tf_op jit(solution)/shard_map/ppermute | solution.py:857
  (144 other events, 2140.6 us)
Sparse Core Ops, SparseCore 0:
  61.1 90.6 all-gather.7
  154.2 78.7 all-gather.9
  238.0 101.9 all-gather.11
  342.3 98.7 all-gather.13
  533.4 96.8 reduce-scatter.4
  633.8 95.0 reduce-scatter.6
  732.7 85.3 reduce-scatter.10
  827.3 76.7 reduce-scatter.8
  937.0 91.2 all-gather.17
  1030.6 49.3 all-gather.15

commit v11 on v10

--- a/solution.py
+++ b/solution.py
@@ -1136,11 +1136,22 @@
     text_grad = line_up(text_own, text_came).astype(jnp.float32)
     text_grad = text_grad.transpose(1, 2, 0, 3).reshape(text_states.shape)
     qkv_sum = over_outer(qkv_ours)
+    middle_kept = after(middle_sum[: middle_rows - text_split], qkv_ours)
+    middle_came = shard_hops(middle_kept)
+    middle_piece = over_shard(middle_kept, middle_came)
+    early = jnp.concatenate(
+        [up_piece]
+        + [down_piece[:, i * block : (i + 1) * block] for i in range(4)]
+        + [text_piece, middle_piece],
+        axis=0,
+    )
     grad_norm, gain_self, bias_self = norm_back(
-        after(grad_hidden_one, qkv_ours, *up_came), inputs, parts_one, norms[0]
-    )
-    middle_kept = after(middle_sum[: middle_rows - text_split], qkv_ours, *up_came)
-    middle_came = shard_hops(middle_kept)
+        after(grad_hidden_one, qkv_ours, early), inputs, parts_one, norms[0]
+    )
+    frames_low = (grad_after_self + grad_norm).astype(jnp.bfloat16)
+    late_came = held(shard_hops(after(qkv_sum, *middle_came)), frames_low)
+    frames_came = from_chip(after(frames_low, *late_came))
+    frames_grad = by_slot(*frames_came).astype(jnp.float32)
     small = jnp.stack(
         [
             gain_self,
@@ -1153,27 +1164,14 @@
             jnp.zeros((width,), jnp.float32),
         ]
     )
+    small = after(small, *late_came)
     for axis in ("core", "x", "y"):
         small += lax.ppermute(small, axis, swap)
-    middle_came = held(middle_came, small)
-    middle_piece = over_shard(middle_kept, middle_came)
-    late_came = shard_hops(after(qkv_sum, *middle_came))
     small_came = shard_hops(small)
     small_own = lax.dynamic_slice_in_dim(small, shard * block, block, 1)
     for part in small_came:
         small_own += part
     loss = small_own[6, 0] / (width * count)
-    frames_came = from_chip(
-        after((grad_after_self + grad_norm).astype(jnp.bfloat16), *late_came, *small_came)
-    )
-    frames_grad = by_slot(*frames_came).astype(jnp.float32)
-
-    early = jnp.concatenate(
-        [up_piece]
-        + [down_piece[:, i * block : (i + 1) * block] for i in range(4)]
-        + [text_piece, middle_piece],
-        axis=0,
-    )
     early = lax.all_gather(after(early, text_grad), REPLICAS, axis=0)
     piece = width // replicas
     square = (block, width)
@@ -1188,7 +1186,9 @@
     probe_grad = unpack(early, piece, at + 1, square, 0, 2)
     merge_grad = unpack(early, piece, at + 2, square, 0, 2)
     late = over_shard(qkv_sum, late_came)
-    late = lax.all_gather(after(late, early, *frames_came), REPLICAS, axis=0, tiled=True)
+    late = lax.all_gather(
+        after(late, early, *frames_came, *small_came), REPLICAS, axis=0, tiled=True
+    )
     late = late.reshape(-1, block, block)
     qkv_grad = [unpack(late, block, 0, square, 2 * i, 2) for i in range(3)]
     return (

time: 1110 us -> 1100 us (level)
    ppermute x2, waiting for transfers between devices: 29.7 us -> 0.01 us  [from_chip(): return (lax.ppermute(one, spot, back[0]), lax.ppermute(two, spot, back[1]))]
    ppermute x36, waiting for transfers between devices: 165 us -> 189 us  [hop(): return lax.ppermute(values, 'shard', pairs)]
    all_gather x1, waiting for transfers between devices: 11.9 us -> 0.01 us  [clip_body(): lax.all_gather(after(late, early, *frames_came, *small_came), REPLICAS, a...]
    unnamed x249 -> x229, local copies, waits for them, and re-layouts: 37.3 us -> 37.9 us
  transfers between devices with their start and end apart: 72 -> 72, of which waited for: 24 -> 26; matrix products, arithmetic and copies ran while one was open for 38% -> 38% of each run, Pallas kernels for 15% -> 15%
where the time goes in v11:
time: 1100 us; the launch traced here: 1090 us
  matrix products  303 us (28%)
  waiting for transfers between devices  234 us (21%)
  Pallas kernels  174 us (16%)
  starting transfers between devices  162 us (15%)
  local copies, waits for them, and re-layouts  110 us (10%)
  other arithmetic  85.3 us (8%)
  between operations  21.5 us (2%)
    ppermute x36, waiting for transfers between devices, hop(): return lax.ppermute(values, 'shard', pairs)  189 us
    dot_general x8, matrix products, project(): return jnp.dot(left, right, preferred_element_type=jnp.float32)  121 us
    ppermute x36, starting transfers between devices, hop(): return lax.ppermute(values, 'shard', pairs)  103 us
    dot_general x7, matrix products, back_project(): jnp.einsum('re,de->rd', grads, matrix, preferred_element_type=jnp.float32)  93.9 us
    dot_general x13, matrix products, outer_sum(): jnp.einsum('rd,re->de', left, right, preferred_element_type=jnp.float32)  87.8 us
    pallas_call x1, Pallas kernels, self_attend_back(): pl.pallas_call(self_backward_kernel, out_shape=(jax.ShapeDtypeStruct((row...  70.1 us
    pallas_call x1, Pallas kernels, self_attend(): pl.pallas_call(self_forward_kernel, out_shape=(jax.ShapeDtypeStruct((rows...  58.5 us
    unnamed x229, local copies, waits for them, and re-layouts  37.9 us
  transfers between devices with their start and end apart: 72, of which 26 were waited for; matrix products, arithmetic and copies ran while one was open for 38% of the time, Pallas kernels for 15%

profile of v11, /device:TPU:0, one launch (start us, length us, event | category | flops | bytes accessed | tf_op | source)
XLA Modules:
  0.0 1090.8 jit_solution(8650647035217120920)
XLA Ops:
  20.9 12.3 %collective-permute-done = bf16[64,4608]{1,0:T(8,128)(2,1)} collective-permute-done((bf16[64,4608]{1,0:T(8,128)(2,1)S(1)}, bf16[64,4608]{1,0:T(8,128)(2,1)}, u32[]{:S(2)}, u32[]{:S(2)}) %collective-permute-start) | collective-permute-done | bytes 589856 | tf_op jit(solution)/shard_map/ppermute | solution.py:830
  34.2 23.4 %collective-permute-done.1 = bf16[64,4608]{1,0:T(8,128)(2,1)} collective-permute-done((bf16[64,4608]{1,0:T(8,128)(2,1)S(1)}, bf16[64,4608]{1,0:T(8,128)(2,1)}, u32[]{:S(2)}, u32[]{:S(2)}) %collective-permute-start.1) | collective-permute-done | bytes 589856 | tf_op jit(solution)/shard_map/ppermute | solution.py:830
  63.1 12.1 %collective-permute-start.3 = (bf16[48,4608]{1,0:T(8,128)(2,1)S(1)}, bf16[48,4608]{1,0:T(8,128)(2,1)S(1)}, u32[]{:S(2)}, u32[]{:S(2)}) collective-permute-start(bf16[48,4608]{1,0:T(8,128)(2,1)S(1)} %pad_maximum_fusion.7), channel_id=1, source_target_pairs={{0,1},{1,2},{2,3},{3,0},{4,5},{5,6},{6,7},{7,4},{8,9},{9,10},{10,1... | collective-permute-start | bytes 1327112 | tf_op jit(solution)/shard_map/ppermute | solution.py:830
  78.1 10.4 collective-permute-done.3
  88.5 17.1 %collective-permute-done.4 = bf16[48,4608]{1,0:T(8,128)(2,1)S(1)} collective-permute-done((bf16[48,4608]{1,0:T(8,128)(2,1)S(1)}, bf16[48,4608]{1,0:T(8,128)(2,1)S(1)}, u32[]{:S(2)}, u32[]{:S(2)}) %collective-permute-start.4) | collective-permute-done | bytes 442400 | tf_op jit(solution)/shard_map/ppermute | solution.py:830
  124.2 11.1 %collective-permute-start.7 = (bf16[384,1536]{1,0:T(8,128)(2,1)}, bf16[384,1536]{1,0:T(8,128)(2,1)}, u32[]{:S(2)}, u32[]{:S(2)}) collective-permute-start(bf16[384,1536]{1,0:T(8,128)(2,1)} %get-tuple-element.219), channel_id=1, source_target_pairs={{0,1},{1,5},{2,4},{3,0},{4,3},{5,7},{6,6},{7,2},{8,9},{9,13},{10,1... | collective-permute-start | bytes 3538952 | tf_op jit(solution)/shard_map/ppermute | solution.py:845
  154.6 20.9 %collective-permute-done.7 = bf16[384,1536]{1,0:T(8,128)(2,1)} collective-permute-done((bf16[384,1536]{1,0:T(8,128)(2,1)}, bf16[384,1536]{1,0:T(8,128)(2,1)}, u32[]{:S(2)}, u32[]{:S(2)}) %collective-permute-start.7) | collective-permute-done | bytes 1179680 | tf_op jit(solution)/shard_map/ppermute | solution.py:845
  175.5 16.7 %collective-permute-start.10 = (bf16[48,6144]{1,0:T(8,128)(2,1)}, bf16[48,6144]{1,0:T(8,128)(2,1)}, u32[]{:S(2)}, u32[]{:S(2)}) collective-permute-start(bf16[48,6144]{1,0:T(8,128)(2,1)} %get-tuple-element.92), channel_id=1, source_target_pairs={{0,2},{1,3},{2,0},{3,1},{4,6},{5,7},{6,4},{7,5},{8,10},{9,11},{10,... | collective-permute-start | bytes 1769480 | tf_op jit(solution)/shard_map/ppermute | solution.py:830
  200.3 12.2 %fusion.14.own_k.own_v = bf16[768,3072]{1,0:T(8,128)(2,1)} fusion(bf16[768,1536]{1,0:T(8,128)(2,1)} %fusion.18, bf16[1536,4608]{1,0:T(8,128)(2,1)} %bitcast.204), kind=kOutput, calls=%fused_computation.36 | convolution fusion | flops 7250116608 | bytes 16515072 | tf_op jit(solution)/shard_map/dot_general | solution.py:28
  216.7 16.4 %collective-permute-done.11 = bf16[48,6144]{1,0:T(8,128)(2,1)} collective-permute-done((bf16[48,6144]{1,0:T(8,128)(2,1)}, bf16[48,6144]{1,0:T(8,128)(2,1)}, u32[]{:S(2)}, u32[]{:S(2)}) %collective-permute-start.11) | collective-permute-done | bytes 589856 | tf_op jit(solution)/shard_map/ppermute | solution.py:830
  243.8 5.7 collective-permute-start.19
  253.9 6.9 fusion.64.q_ref
  260.8 58.5 %self_attend.1 = (bf16[768,1536]{1,0:T(8,128)(2,1)S(1)}, f32[96,768]{1,0:T(8,128)S(1)}) custom-call(s32[5]{0:T(128)S(1)} %stack.66.place, bf16[768,1536]{1,0:T(8,128)(2,1)S(1)} %fusion.64.q_ref, bf16[768,3072]{1,0:T(8,128)(2,1)S(1)} %bitcast.172, bf16[768,3072]{1,0:T(8,128)(2,1)S(1)} %bitcast.172, bf16[768,3072]{1,0:T(8,128)(2,1)} %collective-permute-done.14.other_k.other_v, ...), custom_call_target="tpu_custom_call" | custom-call | flops 7247757312 | bytes 18874368 | tf_op jit(solution)/shard_map/self_attend/pallas_call | solution.py:569
  336.1 6.9 collective-permute-done.16
  344.5 7.1 fusion.134
  360.5 10.4 collective-permute-start.23
  373.3 6.8 cross_attend.1
  386.8 63.1 %multiply_convert_fusion = (bf16[768,6144]{1,0:T(8,128)(2,1)}, f32[768,6144]{1,0:T(8,128)}, f32[768,6144]{1,0:T(8,128)}) fusion(bf16[1536,6144]{1,0:T(8,128)(2,1)} %bitcast.200, f32[768,1536]{1,0:T(8,128)} %copy-done.24, f32[1536]{0:T(1024)S(1)} %add.437, f32[1536]{0:T(1024)S(1)} %mul.317, f32[768]{0:T(1024)S(1)} %add_rsqrt_fusion, ...), kind=kOutput, calls=%fused_computation.5 | convolution fusion | flops 14808121344 | bytes 70797312 | tf_op jit(solution)/shard_map/dot_general | solution.py:28
  452.8 23.5 %multiply_convert_fusion.1 = (bf16[768,1536]{1,0:T(8,128)(2,1)S(1)}, bf16[768,1536]{1,0:T(8,128)(2,1)}, f32[768,1536]{1,0:T(8,128)}) fusion(f32[]{:T(128)S(6)} %div.75, f32[768]{0:T(1024)S(1)} %copy-done.85, bf16[384,1536]{1,0:T(8,128)(2,1)} %get-tuple-element.212, bf16[384,1536]{1,0:T(8,128)(2,1)S(1)} %get-tuple-element.211, f32[768,1536]{1,0:T(8,128)} %copy-done.24, ...), kind=kOutput, calls=%fused_computation.66 | convolution fusion | flops 14507311104 | bytes 44829700 | tf_op jit(solution)/shard_map/dot_general | solution.py:28
  476.3 9.7 convolution_convert_fusion.2
  489.6 29.5 %add_convert_fusion.2 = bf16[768,6144]{1,0:T(8,128)(2,1)} fusion(f32[768,6144]{1,0:T(8,128)} %get-tuple-element.193, f32[768,6144]{1,0:T(8,128)} %get-tuple-element.246, bf16[768,1536]{1,0:T(8,128)(2,1)} %copy-done.55, bf16[6144,1536]{1,0:T(8,128)(2,1)} %bitcast.203), kind=kOutput, calls=%fused_computation.4 | convolution fusion | flops 14561574912 | bytes 68419584 | tf_op jit(solution)/shard_map/re,de->rd/dot_general | solution.py:36
  519.1 14.1 %add_convert_fusion.1 = bf16[768,6144]{1,0:T(8,128)(2,1)} fusion(bf16[768,6144]{1,0:T(8,128)(2,1)} %collective-permute-done.26, bf16[768,6144]{1,0:T(8,128)(2,1)} %get-tuple-element.192, bf16[768,1536]{1,0:T(8,128)(2,1)} %copy-done.55, s32[]{:T(128)S(6)} %select_n.335), kind=kOutput, calls=%fused_computation.3 | convolution fusion | flops 7261913088 | bytes 29491204 | tf_op jit(solution)/shard_map/rd,re->de/dot_general | solution.py:32
  533.3 13.5 %convolution_convert_fusion.1 = bf16[3072,1536]{1,0:T(8,128)(2,1)} fusion(bf16[768,6144]{1,0:T(8,128)(2,1)} %add_convert_fusion.2, s32[]{:T(128)S(6)} %select_n.336, f32[768,1536]{1,0:T(8,128)} %copy-done.24, f32[1536]{0:T(1024)S(1)} %add.437, f32[1536]{0:T(1024)S(1)} %mul.317, f32[768]{0:T(1024)S(1)} %add_rsqrt_fusion, f32[768]{0:T(1024)S(1)} %broadcast_multiply_fusion.6), kind=kOutput, calls=%fused_computation.21 | convolution fusion | flops 7258374144 | bytes 18892804 | tf_op jit(solution)/shard_map/rd,re->de/dot_general | solution.py:32
  547.9 6.8 collective-permute-start.25
  554.7 21.6 %fusion.136 = f32[768,1536]{1,0:T(8,128)} fusion(bf16[768,6144]{1,0:T(8,128)(2,1)} %add_convert_fusion.2, bf16[1536,6144]{1,0:T(8,128)(2,1)} %bitcast.201), kind=kOutput, calls=%fused_computation.302 | convolution fusion | flops 14495514624 | bytes 33030144 | tf_op jit(solution)/shard_map/re,de->rd/dot_general | solution.py:36
  581.2 14.0 %add_convert_fusion = bf16[3072,1536]{1,0:T(8,128)(2,1)} fusion(bf16[3072,1536]{1,0:T(8,128)(2,1)} %collective-permute-done.27, bf16[768,6144]{1,0:T(8,128)(2,1)} %add_convert_fusion.2, s32[]{:T(128)S(6)} %select_n.339, f32[768,1536]{1,0:T(8,128)S(1)} %bitcast.176, f32[1536]{0:T(1024)S(1)} %add.437, f32[1536]{0:T(1024)S(1)} %mul.317, ...), kind=kOutput, calls=%fused_computation.2 | convolution fusion | flops 7267811328 | bytes 28329988 | tf_op jit(solution)/shard_map/rd,re->de/dot_general | solution.py:32
  595.3 6.1 multiply_reduce_fusion.1
  601.4 9.6 fusion.131
  614.5 6.6 fusion.61.grad_ref
  621.1 9.5 cross_attend_back.1
  638.0 5.9 collective-permute-done.32
  652.4 9.4 multiply_reduce_fusion.2
  669.5 7.5 fusion.55.grad_ref
  705.7 70.1 %self_attend_back.1 = (bf16[768,1536]{1,0:T(8,128)(2,1)S(1)}, bf16[768,1536]{1,0:T(8,128)(2,1)S(1)}, bf16[768,1536]{1,0:T(8,128)(2,1)S(1)}, bf16[768,1536]{1,0:T(8,128)(2,1)}, bf16[768,1536]{1,0:T(8,128)(2,1)}) custom-call(s32[5]{0:T(128)S(1)} %copy-done.14, bf16[768,1536]{1,0:T(8,128)(2,1)S(1)} %copy-done.21, bf16[768,3072]{1,0:T(8,128)(2,1)} %fusion.14.own_k.own_v, ...), custom_call_target="tpu_custom_call" | custom-call | flops 18119393280 | bytes 37748736 | tf_op jit(solution)/shard_map/self_attend_back/pallas_call | solution.py:598
  790.9 7.8 convolution_convert_fusion
  798.8 18.7 %fusion.137 = f32[768,1536]{1,0:T(8,128)} fusion(bf16[768,4608]{1,0:T(8,128)(2,1)} %copy-done.30, bf16[1536,4608]{1,0:T(8,128)(2,1)} %bitcast.206), kind=kOutput, calls=%fused_computation.303 | convolution fusion | flops 10871635968 | bytes 25952256 | tf_op jit(solution)/shard_map/re,de->rd/dot_general | solution.py:36
  817.5 9.8 add_convert_fusion.3
  852.6 21.9 %collective-permute-done.46 = bf16[768,384]{1,0:T(8,128)(2,1)S(1)} collective-permute-done((bf16[768,384]{1,0:T(8,128)(2,1)}, bf16[768,384]{1,0:T(8,128)(2,1)S(1)}, u32[]{:S(2)}, u32[]{:S(2)}) %collective-permute-start.46) | collective-permute-done | bytes 589856 | tf_op jit(solution)/shard_map/ppermute | solution.py:830
  882.2 12.7 %collective-permute-start.48 = (bf16[576,384]{1,0:T(8,128)(2,1)}, bf16[576,384]{1,0:T(8,128)(2,1)}, u32[]{:S(2)}, u32[]{:S(2)}) collective-permute-start(bf16[576,384]{1,0:T(8,128)(2,1)} %get-tuple-element.224), channel_id=1, source_target_pairs={{0,1},{1,2},{2,3},{3,0},{4,5},{5,6},{6,7},{7,4},{8,9},{9,10},{10,1... | collective-permute-start | bytes 1327112 | tf_op jit(solution)/shard_map/ppermute | solution.py:830
  899.5 7.6 collective-permute-done.48
  907.2 17.9 %collective-permute-done.49 = bf16[576,384]{1,0:T(8,128)(2,1)} collective-permute-done((bf16[576,384]{1,0:T(8,128)(2,1)}, bf16[576,384]{1,0:T(8,128)(2,1)}, u32[]{:S(2)}, u32[]{:S(2)}) %collective-permute-start.49) | collective-permute-done | bytes 442400 | tf_op jit(solution)/shard_map/ppermute | solution.py:830
  933.8 10.0 collective-permute-start.51
  946.3 5.4 fusion.24
  955.9 17.2 %collective-permute-done.52 = bf16[576,384]{1,0:T(8,128)(2,1)S(1)} collective-permute-done((bf16[576,384]{1,0:T(8,128)(2,1)S(1)}, bf16[576,384]{1,0:T(8,128)(2,1)S(1)}, u32[]{:S(2)}, u32[]{:S(2)}) %collective-permute-start.52) | collective-permute-done | bytes 442400 | tf_op jit(solution)/shard_map/ppermute | solution.py:830
  976.7 13.4 %collective-permute-start.61 = (bf16[384,1536]{1,0:T(8,128)(2,1)S(1)}, bf16[384,1536]{1,0:T(8,128)(2,1)S(1)}, u32[]{:S(2)}, u32[]{:S(2)}) collective-permute-start(bf16[384,1536]{1,0:T(8,128)(2,1)S(1)} %get-tuple-element.202), channel_id=1, source_target_pairs={{1,0},{5,1},{4,2},{0,3},{3,4},{7,5},{6,6},{2,7},{9,8},{13,9},{12,1... | collective-permute-start | bytes 3538952 | tf_op jit(solution)/shard_map/ppermute | solution.py:857
  1018.9 17.7 %collective-permute-done.58 = f32[8,384]{1,0:T(8,128)} collective-permute-done((f32[8,384]{1,0:T(8,128)}, f32[8,384]{1,0:T(8,128)}, u32[]{:S(2)}, u32[]{:S(2)}) %collective-permute-start.58) | collective-permute-done | bytes 12320 | tf_op jit(solution)/shard_map/ppermute | solution.py:830
  1046.0 5.6 copy-done.2
  1056.8 8.1 unpack.19
  (547 shorter events, 320.1 us)
Async XLA Ops:
  7.2 193.1 %all-gather.8.cloned.1.call-start = ((), (), s32[]{:S(2)}) async-start(), calls=%async_computation.4 | async-start | bytes 15925248 | tf_op jit(solution)/shard_map/all_gather | solution.py:867
  16.7 40.9 %collective-permute-start.1 = (bf16[64,4608]{1,0:T(8,128)(2,1)S(1)}, bf16[64,4608]{1,0:T(8,128)(2,1)}, u32[]{:S(2)}, u32[]{:S(2)}) collective-permute-start(bf16[64,4608]{1,0:T(8,128)(2,1)S(1)} %pad_maximum_fusion.5), channel_id=1, source_target_pairs={{0,2},{1,3},{2,0},{3,1},{4,6},{5,7},{6,4},{7,5},{8,10},{9,11},{10,... | collective-permute-start | bytes 1769480 | tf_op jit(solution)/shard_map/ppermute | solution.py:830
  19.3 39.3 %collective-permute-start.2 = (bf16[64,4608]{1,0:T(8,128)(2,1)S(1)}, bf16[64,4608]{1,0:T(8,128)(2,1)}, u32[]{:S(2)}, u32[]{:S(2)}) collective-permute-start(bf16[64,4608]{1,0:T(8,128)(2,1)S(1)} %pad_maximum_fusion.5), channel_id=1, source_target_pairs={{0,3},{1,0},{2,1},{3,2},{4,7},{5,4},{6,5},{7,6},{8,11},{9,8},{10,9... | collective-permute-start | bytes 1769480 | tf_op jit(solution)/shard_map/ppermute | solution.py:830
  61.0 283.4 %all-gather.10.cloned.1.call-start = ((), (), s32[]{:S(2)}) async-start(), calls=%async_computation.5 | async-start | bytes 15925248 | tf_op jit(solution)/shard_map/all_gather | solution.py:867
  63.1 25.4 %collective-permute-start.3 = (bf16[48,4608]{1,0:T(8,128)(2,1)S(1)}, bf16[48,4608]{1,0:T(8,128)(2,1)S(1)}, u32[]{:S(2)}, u32[]{:S(2)}) collective-permute-start(bf16[48,4608]{1,0:T(8,128)(2,1)S(1)} %pad_maximum_fusion.7), channel_id=1, source_target_pairs={{0,1},{1,2},{2,3},{3,0},{4,5},{5,6},{6,7},{7,4},{8,9},{9,10},{10,1... | collective-permute-start | bytes 1327112 | tf_op jit(solution)/shard_map/ppermute | solution.py:830
  75.4 30.3 %collective-permute-start.4 = (bf16[48,4608]{1,0:T(8,128)(2,1)S(1)}, bf16[48,4608]{1,0:T(8,128)(2,1)S(1)}, u32[]{:S(2)}, u32[]{:S(2)}) collective-permute-start(bf16[48,4608]{1,0:T(8,128)(2,1)S(1)} %pad_maximum_fusion.7), channel_id=1, source_target_pairs={{0,2},{1,3},{2,0},{3,1},{4,6},{5,7},{6,4},{7,5},{8,10},{9,11},{10,... | collective-permute-start | bytes 1327112 | tf_op jit(solution)/shard_map/ppermute | solution.py:830
  78.1 27.6 %collective-permute-start.5 = (bf16[48,4608]{1,0:T(8,128)(2,1)S(1)}, bf16[48,4608]{1,0:T(8,128)(2,1)S(1)}, u32[]{:S(2)}, u32[]{:S(2)}) collective-permute-start(bf16[48,4608]{1,0:T(8,128)(2,1)S(1)} %pad_maximum_fusion.7), channel_id=1, source_target_pairs={{0,3},{1,0},{2,1},{3,2},{4,7},{5,4},{6,5},{7,6},{8,11},{9,8},{10,9... | collective-permute-start | bytes 1327112 | tf_op jit(solution)/shard_map/ppermute | solution.py:830
  107.0 279.8 %all-gather.12.cloned.1.call-start = ((), (), s32[]{:S(2)}) async-start(), calls=%async_computation.6 | async-start | bytes 21233664 | tf_op jit(solution)/shard_map/all_gather | solution.py:867
  122.3 32.4 %collective-permute-start.6 = (bf16[384,1536]{1,0:T(8,128)(2,1)}, bf16[384,1536]{1,0:T(8,128)(2,1)S(1)}, u32[]{:S(2)}, u32[]{:S(2)}) collective-permute-start(bf16[384,1536]{1,0:T(8,128)(2,1)} %get-tuple-element.220), channel_id=1, source_target_pairs={{0,0},{1,4},{2,5},{3,1},{4,2},{5,6},{6,7},{7,3},{8,8},{9,12},{10,1... | collective-permute-start | bytes 3538952 | tf_op jit(solution)/shard_map/ppermute | solution.py:844
  124.2 51.4 %collective-permute-start.7 = (bf16[384,1536]{1,0:T(8,128)(2,1)}, bf16[384,1536]{1,0:T(8,128)(2,1)}, u32[]{:S(2)}, u32[]{:S(2)}) collective-permute-start(bf16[384,1536]{1,0:T(8,128)(2,1)} %get-tuple-element.219), channel_id=1, source_target_pairs={{0,1},{1,5},{2,4},{3,0},{4,3},{5,7},{6,6},{7,2},{8,9},{9,13},{10,1... | collective-permute-start | bytes 3538952 | tf_op jit(solution)/shard_map/ppermute | solution.py:845
  175.5 41.2 %collective-permute-start.10 = (bf16[48,6144]{1,0:T(8,128)(2,1)}, bf16[48,6144]{1,0:T(8,128)(2,1)}, u32[]{:S(2)}, u32[]{:S(2)}) collective-permute-start(bf16[48,6144]{1,0:T(8,128)(2,1)} %get-tuple-element.92), channel_id=1, source_target_pairs={{0,2},{1,3},{2,0},{3,1},{4,6},{5,7},{6,4},{7,5},{8,10},{9,11},{10,... | collective-permute-start | bytes 1769480 | tf_op jit(solution)/shard_map/ppermute | solution.py:830
  192.3 40.8 %collective-permute-start.11 = (bf16[48,6144]{1,0:T(8,128)(2,1)}, bf16[48,6144]{1,0:T(8,128)(2,1)}, u32[]{:S(2)}, u32[]{:S(2)}) collective-permute-start(bf16[48,6144]{1,0:T(8,128)(2,1)} %get-tuple-element.92), channel_id=1, source_target_pairs={{0,3},{1,0},{2,1},{3,2},{4,7},{5,4},{6,5},{7,6},{8,11},{9,8},{10,9... | collective-permute-start | bytes 1769480 | tf_op jit(solution)/shard_map/ppermute | solution.py:830
  192.3 40.8 %collective-permute-start.9 = (bf16[48,6144]{1,0:T(8,128)(2,1)}, bf16[48,6144]{1,0:T(8,128)(2,1)}, u32[]{:S(2)}, u32[]{:S(2)}) collective-permute-start(bf16[48,6144]{1,0:T(8,128)(2,1)} %get-tuple-element.92), channel_id=1, source_target_pairs={{0,1},{1,2},{2,3},{3,0},{4,5},{5,6},{6,7},{7,4},{8,9},{9,10},{10,1... | collective-permute-start | bytes 1769480 | tf_op jit(solution)/shard_map/ppermute | solution.py:830
  237.9 215.0 %all-gather.14.cloned.1.call-start = ((), (), s32[]{:S(2)}) async-start(), calls=%async_computation.7 | async-start | bytes 21233664 | tf_op jit(solution)/shard_map/all_gather | solution.py:867
  243.8 75.6 %collective-permute-start.19 = (bf16[192,1536]{1,0:T(8,128)(2,1)}, bf16[192,1536]{1,0:T(8,128)(2,1)S(1)}, u32[]{:S(2)}, u32[]{:S(2)}) collective-permute-start(bf16[192,1536]{1,0:T(8,128)(2,1)} %get-tuple-element.103), channel_id=1, source_target_pairs={{0,1},{1,2},{2,3},{3,0},{4,5},{5,6},{6,7},{7,4},{8,9},{9,10},{10,1... | collective-permute-start | bytes 1769480 | tf_op jit(solution)/shard_map/ppermute | solution.py:830
  249.5 69.9 %collective-permute-start.20 = (bf16[192,1536]{1,0:T(8,128)(2,1)}, bf16[192,1536]{1,0:T(8,128)(2,1)S(1)}, u32[]{:S(2)}, u32[]{:S(2)}) collective-permute-start(bf16[192,1536]{1,0:T(8,128)(2,1)} %get-tuple-element.103), channel_id=1, source_target_pairs={{0,2},{1,3},{2,0},{3,1},{4,6},{5,7},{6,4},{7,5},{8,10},{9,11},{10,... | collective-permute-start | bytes 1769480 | tf_op jit(solution)/shard_map/ppermute | solution.py:830
  250.9 68.5 %collective-permute-start.21 = (bf16[192,1536]{1,0:T(8,128)(2,1)}, bf16[192,1536]{1,0:T(8,128)(2,1)S(1)}, u32[]{:S(2)}, u32[]{:S(2)}) collective-permute-start(bf16[192,1536]{1,0:T(8,128)(2,1)} %get-tuple-element.103), channel_id=1, source_target_pairs={{0,3},{1,0},{2,1},{3,2},{4,7},{5,4},{6,5},{7,6},{8,11},{9,8},{10,9... | collective-permute-start | bytes 1769480 | tf_op jit(solution)/shard_map/ppermute | solution.py:830
  322.0 372.0 %reduce-scatter.5.cloned.1.call-start = ((), (), s32[]{:S(2)}) async-start(), calls=%async_computation.8 | async-start | bytes 11796480 | tf_op jit(solution)/shard_map/reduce_scatter | solution.py:1011
  344.3 28.9 %collective-permute-start.18 = (bf16[64,1536]{1,0:T(8,128)(2,1)S(1)}, bf16[64,1536]{1,0:T(8,128)(2,1)S(1)}, u32[]{:S(2)}, u32[]{:S(2)}) collective-permute-start(bf16[64,1536]{1,0:T(8,128)(2,1)S(1)} %fusion.89), channel_id=1, source_target_pairs={{0,4},{4,0},{1,5},{5,1},{2,6},{6,2},{3,7},{7,3},{8,12},{12,8},{9,1... | collective-permute-start | bytes 589832 | tf_op jit(solution)/shard_map/ppermute | solution.py:973
  360.5 89.4 %collective-permute-start.23 = (bf16[384,1536]{1,0:T(8,128)(2,1)}, bf16[384,1536]{1,0:T(8,128)(2,1)}, u32[]{:S(2)}, u32[]{:S(2)}) collective-permute-start(bf16[384,1536]{1,0:T(8,128)(2,1)} %get-tuple-element.214), channel_id=1, source_target_pairs={{0,0},{1,4},{2,5},{3,1},{4,2},{5,6},{6,7},{7,3},{8,8},{9,12},{10,1... | collective-permute-start | bytes 3538952 | tf_op jit(solution)/shard_map/ppermute | solution.py:844
  370.9 79.0 %collective-permute-start.24 = (bf16[384,1536]{1,0:T(8,128)(2,1)}, bf16[384,1536]{1,0:T(8,128)(2,1)}, u32[]{:S(2)}, u32[]{:S(2)}) collective-permute-start(bf16[384,1536]{1,0:T(8,128)(2,1)} %get-tuple-element.213), channel_id=1, source_target_pairs={{0,1},{1,5},{2,4},{3,0},{4,3},{5,7},{6,6},{7,2},{8,9},{9,13},{10,1... | collective-permute-start | bytes 3538952 | tf_op jit(solution)/shard_map/ppermute | solution.py:845
  486.1 33.0 %collective-permute-start.26 = (bf16[768,6144]{1,0:T(8,128)(2,1)}, bf16[768,6144]{1,0:T(8,128)(2,1)}, u32[]{:S(2)}, u32[]{:S(2)}) collective-permute-start(bf16[768,6144]{1,0:T(8,128)(2,1)} %convolution_convert_fusion.2), channel_id=1, source_target_pairs={{0,4},{4,0},{1,5},{5,1},{2,6},{6,2},{3,7},{7,3},{8,12},{12,8},{9,1... | collective-permute-start | bytes 28311560 | tf_op jit(solution)/shard_map/ppermute | solution.py:1006
  487.9 31.2 %collective-permute-start.22 = (bf16[384,1536]{1,0:T(8,128)(2,1)S(1)}, bf16[384,1536]{1,0:T(8,128)(2,1)}, u32[]{:S(2)}, u32[]{:S(2)}) collective-permute-start(bf16[384,1536]{1,0:T(8,128)(2,1)S(1)} %get-tuple-element.215), channel_id=1, source_target_pairs={{0,0},{4,1},{5,2},{1,3},{2,4},{6,5},{7,6},{3,7},{8,8},{12,9},{13,1... | collective-permute-start | bytes 3538952 | tf_op jit(solution)/shard_map/ppermute | solution.py:1034
  533.2 296.0 %reduce-scatter.7.cloned.1.call-start = ((), (), s32[]{:S(2)}) async-start(), calls=%async_computation.9 | async-start | bytes 11796480 | tf_op jit(solution)/shard_map/reduce_scatter | solution.py:1011
  546.8 34.4 %collective-permute-start.27 = (bf16[3072,1536]{1,0:T(8,128)(2,1)}, bf16[3072,1536]{1,0:T(8,128)(2,1)}, u32[]{:S(2)}, u32[]{:S(2)}) collective-permute-start(bf16[3072,1536]{1,0:T(8,128)(2,1)} %convolution_convert_fusion.1), channel_id=1, source_target_pairs={{0,4},{4,0},{1,5},{5,1},{2,6},{6,2},{3,7},{7,3},{8,12},{12,8},{9,1... | collective-permute-start | bytes 28311560 | tf_op jit(solution)/shard_map/ppermute | solution.py:1006
  547.9 33.4 %collective-permute-start.25 = (bf16[384,1536]{1,0:T(8,128)(2,1)S(1)}, bf16[384,1536]{1,0:T(8,128)(2,1)}, u32[]{:S(2)}, u32[]{:S(2)}) collective-permute-start(bf16[384,1536]{1,0:T(8,128)(2,1)S(1)} %get-tuple-element.112), channel_id=1, source_target_pairs={{1,0},{5,1},{4,2},{0,3},{3,4},{7,5},{6,6},{2,7},{9,8},{13,9},{12,1... | collective-permute-start | bytes 3538952 | tf_op jit(solution)/shard_map/ppermute | solution.py:1044
  595.3 283.0 %reduce-scatter.9.cloned.1.call-start = ((), (), s32[]{:S(2)}) async-start(), calls=%async_computation.10 | async-start | bytes 10321920 | tf_op jit(solution)/shard_map/reduce_scatter | solution.py:1011
  614.5 30.1 %collective-permute-start.28 = (bf16[768,1536]{1,0:T(8,128)(2,1)}, bf16[768,1536]{1,0:T(8,128)(2,1)}, u32[]{:S(2)}, u32[]{:S(2)}) collective-permute-start(bf16[768,1536]{1,0:T(8,128)(2,1)} %convolution_convert_fusion.5), channel_id=1, source_target_pairs={{0,4},{4,0},{1,5},{5,1},{2,6},{6,2},{3,7},{7,3},{8,12},{12,8},{9,1... | collective-permute-start | bytes 7077896 | tf_op jit(solution)/shard_map/ppermute | solution.py:1006
  635.3 32.5 %collective-permute-start.33 = (bf16[64,1536]{1,0:T(8,128)(2,1)}, bf16[64,1536]{1,0:T(8,128)(2,1)S(1)}, u32[]{:S(2)}, u32[]{:S(2)}) collective-permute-start(bf16[64,1536]{1,0:T(8,128)(2,1)} %get-tuple-element.185), channel_id=1, source_target_pairs={{0,2},{1,3},{2,0},{3,1},{4,6},{5,7},{6,4},{7,5},{8,10},{9,11},{10,... | collective-permute-start | bytes 589832 | tf_op jit(solution)/shard_map/ppermute | solution.py:830
  637.5 30.3 %collective-permute-start.34 = (bf16[64,1536]{1,0:T(8,128)(2,1)}, bf16[64,1536]{1,0:T(8,128)(2,1)S(1)}, u32[]{:S(2)}, u32[]{:S(2)}) collective-permute-start(bf16[64,1536]{1,0:T(8,128)(2,1)} %get-tuple-element.185), channel_id=1, source_target_pairs={{0,3},{1,0},{2,1},{3,2},{4,7},{5,4},{6,5},{7,6},{8,11},{9,8},{10,9... | collective-permute-start | bytes 589832 | tf_op jit(solution)/shard_map/ppermute | solution.py:830
  685.0 247.4 %reduce-scatter.11.cloned.1.call-start = ((), (), s32[]{:S(2)}) async-start(), calls=%async_computation.11 | async-start | bytes 8847360 | tf_op jit(solution)/shard_map/reduce_scatter | solution.py:1011
  690.2 88.4 %collective-permute-start.37 = (bf16[2,64,384]{2,1,0:T(8,128)(2,1)S(1)}, bf16[2,64,384]{2,1,0:T(8,128)(2,1)}, u32[]{:S(2)}, u32[]{:S(2)}) collective-permute-start(bf16[2,64,384]{2,1,0:T(8,128)(2,1)S(1)} %fusion.94), channel_id=1, source_target_pairs={{0,2},{1,3},{2,0},{3,1},{4,6},{5,7},{6,4},{7,5},{8,10},{9,11},{10,... | collective-permute-start | bytes 294920 | tf_op jit(solution)/shard_map/ppermute | solution.py:830
  692.6 86.0 %collective-permute-start.38 = (bf16[2,64,384]{2,1,0:T(8,128)(2,1)S(1)}, bf16[2,64,384]{2,1,0:T(8,128)(2,1)}, u32[]{:S(2)}, u32[]{:S(2)}) collective-permute-start(bf16[2,64,384]{2,1,0:T(8,128)(2,1)S(1)} %fusion.94), channel_id=1, source_target_pairs={{0,3},{1,0},{2,1},{3,2},{4,7},{5,4},{6,5},{7,6},{8,11},{9,8},{10,9... | collective-permute-start | bytes 294920 | tf_op jit(solution)/shard_map/ppermute | solution.py:830
  695.6 83.0 %collective-permute-start.39 = (bf16[192,1536]{1,0:T(8,128)(2,1)S(1)}, bf16[192,1536]{1,0:T(8,128)(2,1)S(1)}, u32[]{:S(2)}, u32[]{:S(2)}) collective-permute-start(bf16[192,1536]{1,0:T(8,128)(2,1)S(1)} %get-tuple-element.208), channel_id=1, source_target_pairs={{0,1},{1,2},{2,3},{3,0},{4,5},{5,6},{6,7},{7,4},{8,9},{9,10},{10,1... | collective-permute-start | bytes 1769480 | tf_op jit(solution)/shard_map/ppermute | solution.py:830
  696.3 82.3 %collective-permute-start.40 = (bf16[192,1536]{1,0:T(8,128)(2,1)S(1)}, bf16[192,1536]{1,0:T(8,128)(2,1)}, u32[]{:S(2)}, u32[]{:S(2)}) collective-permute-start(bf16[192,1536]{1,0:T(8,128)(2,1)S(1)} %get-tuple-element.207), channel_id=1, source_target_pairs={{0,2},{1,3},{2,0},{3,1},{4,6},{5,7},{6,4},{7,5},{8,10},{9,11},{10,... | collective-permute-start | bytes 1769480 | tf_op jit(solution)/shard_map/ppermute | solution.py:830
  697.8 80.8 %collective-permute-start.41 = (bf16[192,1536]{1,0:T(8,128)(2,1)S(1)}, bf16[192,1536]{1,0:T(8,128)(2,1)}, u32[]{:S(2)}, u32[]{:S(2)}) collective-permute-start(bf16[192,1536]{1,0:T(8,128)(2,1)S(1)} %get-tuple-element.206), channel_id=1, source_target_pairs={{0,3},{1,0},{2,1},{3,2},{4,7},{5,4},{6,5},{7,6},{8,11},{9,8},{10,9... | collective-permute-start | bytes 1769480 | tf_op jit(solution)/shard_map/ppermute | solution.py:830
  827.3 209.4 %all-gather.18.cloned.1.call-start = ((), (), s32[]{:S(2)}) async-start(), calls=%async_computation.13 | async-start | bytes 17252352 | tf_op jit(solution)/shard_map/all_gather | solution.py:1175
  831.9 42.6 %collective-permute-start.46 = (bf16[768,384]{1,0:T(8,128)(2,1)}, bf16[768,384]{1,0:T(8,128)(2,1)S(1)}, u32[]{:S(2)}, u32[]{:S(2)}) collective-permute-start(bf16[768,384]{1,0:T(8,128)(2,1)} %get-tuple-element.204), channel_id=1, source_target_pairs={{0,2},{1,3},{2,0},{3,1},{4,6},{5,7},{6,4},{7,5},{8,10},{9,11},{10,... | collective-permute-start | bytes 1769480 | tf_op jit(solution)/shard_map/ppermute | solution.py:830
  833.2 41.3 %collective-permute-start.47 = (bf16[768,384]{1,0:T(8,128)(2,1)S(1)}, bf16[768,384]{1,0:T(8,128)(2,1)}, u32[]{:S(2)}, u32[]{:S(2)}) collective-permute-start(bf16[768,384]{1,0:T(8,128)(2,1)S(1)} %get-tuple-element.203), channel_id=1, source_target_pairs={{0,3},{1,0},{2,1},{3,2},{4,7},{5,4},{6,5},{7,6},{8,11},{9,8},{10,9... | collective-permute-start | bytes 1769480 | tf_op jit(solution)/shard_map/ppermute | solution.py:830
  882.2 25.0 %collective-permute-start.48 = (bf16[576,384]{1,0:T(8,128)(2,1)}, bf16[576,384]{1,0:T(8,128)(2,1)}, u32[]{:S(2)}, u32[]{:S(2)}) collective-permute-start(bf16[576,384]{1,0:T(8,128)(2,1)} %get-tuple-element.224), channel_id=1, source_target_pairs={{0,1},{1,2},{2,3},{3,0},{4,5},{5,6},{6,7},{7,4},{8,9},{9,10},{10,1... | collective-permute-start | bytes 1327112 | tf_op jit(solution)/shard_map/ppermute | solution.py:830
  894.9 30.2 %collective-permute-start.49 = (bf16[576,384]{1,0:T(8,128)(2,1)}, bf16[576,384]{1,0:T(8,128)(2,1)}, u32[]{:S(2)}, u32[]{:S(2)}) collective-permute-start(bf16[576,384]{1,0:T(8,128)(2,1)} %get-tuple-element.226), channel_id=1, source_target_pairs={{0,2},{1,3},{2,0},{3,1},{4,6},{5,7},{6,4},{7,5},{8,10},{9,11},{10,... | collective-permute-start | bytes 1327112 | tf_op jit(solution)/shard_map/ppermute | solution.py:830
  896.3 28.8 %collective-permute-start.50 = (bf16[576,384]{1,0:T(8,128)(2,1)}, bf16[576,384]{1,0:T(8,128)(2,1)}, u32[]{:S(2)}, u32[]{:S(2)}) collective-permute-start(bf16[576,384]{1,0:T(8,128)(2,1)} %get-tuple-element.225), channel_id=1, source_target_pairs={{0,3},{1,0},{2,1},{3,2},{4,7},{5,4},{6,5},{7,6},{8,11},{9,8},{10,9... | collective-permute-start | bytes 1327112 | tf_op jit(solution)/shard_map/ppermute | solution.py:830
  927.5 148.2 %all-gather.16.cloned.1.call-start = ((), (), s32[]{:S(2)}) async-start(), calls=%async_computation.12 | async-start | bytes 3981312 | tf_op jit(solution)/shard_map/all_gather | solution.py:1189
  943.8 29.3 %collective-permute-start.52 = (bf16[576,384]{1,0:T(8,128)(2,1)S(1)}, bf16[576,384]{1,0:T(8,128)(2,1)S(1)}, u32[]{:S(2)}, u32[]{:S(2)}) collective-permute-start(bf16[576,384]{1,0:T(8,128)(2,1)S(1)} %get-tuple-element.222), channel_id=1, source_target_pairs={{0,2},{1,3},{2,0},{3,1},{4,6},{5,7},{6,4},{7,5},{8,10},{9,11},{10,... | collective-permute-start | bytes 1327112 | tf_op jit(solution)/shard_map/ppermute | solution.py:830
  945.3 27.8 %collective-permute-start.53 = (bf16[576,384]{1,0:T(8,128)(2,1)S(1)}, bf16[576,384]{1,0:T(8,128)(2,1)S(1)}, u32[]{:S(2)}, u32[]{:S(2)}) collective-permute-start(bf16[576,384]{1,0:T(8,128)(2,1)S(1)} %get-tuple-element.221), channel_id=1, source_target_pairs={{0,3},{1,0},{2,1},{3,2},{4,7},{5,4},{6,5},{7,6},{8,11},{9,8},{10,9... | collective-permute-start | bytes 1327112 | tf_op jit(solution)/shard_map/ppermute | solution.py:830
  974.4 62.2 %collective-permute-start.60 = (bf16[384,1536]{1,0:T(8,128)(2,1)}, bf16[384,1536]{1,0:T(8,128)(2,1)S(1)}, u32[]{:S(2)}, u32[]{:S(2)}) collective-permute-start(bf16[384,1536]{1,0:T(8,128)(2,1)} %get-tuple-element.201), channel_id=1, source_target_pairs={{0,0},{4,1},{5,2},{1,3},{2,4},{6,5},{7,6},{3,7},{8,8},{12,9},{13,1... | collective-permute-start | bytes 3538952 | tf_op jit(solution)/shard_map/ppermute | solution.py:857
  976.7 59.9 %collective-permute-start.61 = (bf16[384,1536]{1,0:T(8,128)(2,1)S(1)}, bf16[384,1536]{1,0:T(8,128)(2,1)S(1)}, u32[]{:S(2)}, u32[]{:S(2)}) collective-permute-start(bf16[384,1536]{1,0:T(8,128)(2,1)S(1)} %get-tuple-element.202), channel_id=1, source_target_pairs={{1,0},{5,1},{4,2},{0,3},{3,4},{7,5},{6,6},{2,7},{9,8},{13,9},{12,1... | collective-permute-start | bytes 3538952 | tf_op jit(solution)/shard_map/ppermute | solution.py:857
  1010.7 25.9 %collective-permute-start.58 = (f32[8,384]{1,0:T(8,128)}, f32[8,384]{1,0:T(8,128)}, u32[]{:S(2)}, u32[]{:S(2)}) collective-permute-start(f32[8,384]{1,0:T(8,128)} %get-tuple-element.236), channel_id=1, source_target_pairs={{0,2},{1,3},{2,0},{3,1},{4,6},{5,7},{6,4},{7,5},{8,10},{9,11},{10,... | collective-permute-start | bytes 36872 | tf_op jit(solution)/shard_map/ppermute | solution.py:830
  (134 other events, 1977.1 us)
Sparse Core Ops, SparseCore 0:
  61.1 90.6 all-gather.7
  154.2 78.7 all-gather.9
  238.0 101.9 all-gather.11
  342.3 98.8 all-gather.13
  533.3 96.9 reduce-scatter.4
  633.9 95.0 reduce-scatter.6
  732.7 85.2 reduce-scatter.8
  827.4 75.7 reduce-scatter.10
  927.6 93.2 all-gather.17
  1036.8 36.4 all-gather.15

commit v12 on v11

--- a/solution.py
+++ b/solution.py
@@ -1187,7 +1187,7 @@
     merge_grad = unpack(early, piece, at + 2, square, 0, 2)
     late = over_shard(qkv_sum, late_came)
     late = lax.all_gather(
-        after(late, early, *frames_came, *small_came), REPLICAS, axis=0, tiled=True
+        after(late, early, *frames_came, small), REPLICAS, axis=0, tiled=True
     )
     late = late.reshape(-1, block, block)
     qkv_grad = [unpack(late, block, 0, square, 2 * i, 2) for i in range(3)]

time: 1100 us -> 1110 us (level)
  starting transfers between devices: 162 us -> 177 us
    ppermute x36, waiting for transfers between devices: 189 us -> 171 us  [hop(): return lax.ppermute(values, 'shard', pairs)]
    ppermute x36, starting transfers between devices: 103 us -> 118 us  [hop(): return lax.ppermute(values, 'shard', pairs)]
    ppermute x2, waiting for transfers between devices: 0.01 us -> 11.1 us  [from_chip(): return (lax.ppermute(one, spot, back[0]), lax.ppermute(two, spot, back[1]))]
where the time goes in v12:
time: 1110 us; the launch traced here: 1100 us
  matrix products  303 us (27%)
  waiting for transfers between devices  225 us (20%)
  starting transfers between devices  177 us (16%)
  Pallas kernels  174 us (16%)
  local copies, waits for them, and re-layouts  109 us (10%)
  other arithmetic  86.6 us (8%)
  between operations  21.5 us (2%)
    ppermute x36, waiting for transfers between devices, hop(): return lax.ppermute(values, 'shard', pairs)  171 us
    dot_general x8, matrix products, project(): return jnp.dot(left, right, preferred_element_type=jnp.float32)  121 us
    ppermute x36, starting transfers between devices, hop(): return lax.ppermute(values, 'shard', pairs)  118 us
    dot_general x7, matrix products, back_project(): jnp.einsum('re,de->rd', grads, matrix, preferred_element_type=jnp.float32)  93.9 us
    dot_general x13, matrix products, outer_sum(): jnp.einsum('rd,re->de', left, right, preferred_element_type=jnp.float32)  87.8 us
    pallas_call x1, Pallas kernels, self_attend_back(): pl.pallas_call(self_backward_kernel, out_shape=(jax.ShapeDtypeStruct((row...  70.1 us
    pallas_call x1, Pallas kernels, self_attend(): pl.pallas_call(self_forward_kernel, out_shape=(jax.ShapeDtypeStruct((rows...  58.5 us
    unnamed x229, local copies, waits for them, and re-layouts  37 us
  transfers between devices with their start and end apart: 72, of which 26 were waited for; matrix products, arithmetic and copies ran while one was open for 38% of the time, Pallas kernels for 15%

profile of v12, /device:TPU:0, one launch (start us, length us, event | category | flops | bytes accessed | tf_op | source)
XLA Modules:
  0.0 1096.3 jit_solution(12603288159349205581)
XLA Ops:
  20.9 12.3 %collective-permute-done = bf16[64,4608]{1,0:T(8,128)(2,1)} collective-permute-done((bf16[64,4608]{1,0:T(8,128)(2,1)S(1)}, bf16[64,4608]{1,0:T(8,128)(2,1)}, u32[]{:S(2)}, u32[]{:S(2)}) %collective-permute-start) | collective-permute-done | bytes 589856 | tf_op jit(solution)/shard_map/ppermute | solution.py:830
  34.2 23.4 %collective-permute-done.1 = bf16[64,4608]{1,0:T(8,128)(2,1)} collective-permute-done((bf16[64,4608]{1,0:T(8,128)(2,1)S(1)}, bf16[64,4608]{1,0:T(8,128)(2,1)}, u32[]{:S(2)}, u32[]{:S(2)}) %collective-permute-start.1) | collective-permute-done | bytes 589856 | tf_op jit(solution)/shard_map/ppermute | solution.py:830
  63.1 12.1 %collective-permute-start.3 = (bf16[48,4608]{1,0:T(8,128)(2,1)S(1)}, bf16[48,4608]{1,0:T(8,128)(2,1)S(1)}, u32[]{:S(2)}, u32[]{:S(2)}) collective-permute-start(bf16[48,4608]{1,0:T(8,128)(2,1)S(1)} %pad_maximum_fusion.7), channel_id=1, source_target_pairs={{0,1},{1,2},{2,3},{3,0},{4,5},{5,6},{6,7},{7,4},{8,9},{9,10},{10,1... | collective-permute-start | bytes 1327112 | tf_op jit(solution)/shard_map/ppermute | solution.py:830
  78.1 10.4 collective-permute-done.3
  88.5 17.1 %collective-permute-done.4 = bf16[48,4608]{1,0:T(8,128)(2,1)S(1)} collective-permute-done((bf16[48,4608]{1,0:T(8,128)(2,1)S(1)}, bf16[48,4608]{1,0:T(8,128)(2,1)S(1)}, u32[]{:S(2)}, u32[]{:S(2)}) %collective-permute-start.4) | collective-permute-done | bytes 442400 | tf_op jit(solution)/shard_map/ppermute | solution.py:830
  124.2 11.1 %collective-permute-start.7 = (bf16[384,1536]{1,0:T(8,128)(2,1)}, bf16[384,1536]{1,0:T(8,128)(2,1)}, u32[]{:S(2)}, u32[]{:S(2)}) collective-permute-start(bf16[384,1536]{1,0:T(8,128)(2,1)} %get-tuple-element.219), channel_id=1, source_target_pairs={{0,1},{1,5},{2,4},{3,0},{4,3},{5,7},{6,6},{7,2},{8,9},{9,13},{10,1... | collective-permute-start | bytes 3538952 | tf_op jit(solution)/shard_map/ppermute | solution.py:845
  154.6 20.9 %collective-permute-done.7 = bf16[384,1536]{1,0:T(8,128)(2,1)} collective-permute-done((bf16[384,1536]{1,0:T(8,128)(2,1)}, bf16[384,1536]{1,0:T(8,128)(2,1)}, u32[]{:S(2)}, u32[]{:S(2)}) %collective-permute-start.7) | collective-permute-done | bytes 1179680 | tf_op jit(solution)/shard_map/ppermute | solution.py:845
  175.5 16.7 %collective-permute-start.10 = (bf16[48,6144]{1,0:T(8,128)(2,1)}, bf16[48,6144]{1,0:T(8,128)(2,1)}, u32[]{:S(2)}, u32[]{:S(2)}) collective-permute-start(bf16[48,6144]{1,0:T(8,128)(2,1)} %get-tuple-element.92), channel_id=1, source_target_pairs={{0,2},{1,3},{2,0},{3,1},{4,6},{5,7},{6,4},{7,5},{8,10},{9,11},{10,... | collective-permute-start | bytes 1769480 | tf_op jit(solution)/shard_map/ppermute | solution.py:830
  200.3 12.2 %fusion.14.own_k.own_v = bf16[768,3072]{1,0:T(8,128)(2,1)} fusion(bf16[768,1536]{1,0:T(8,128)(2,1)} %fusion.18, bf16[1536,4608]{1,0:T(8,128)(2,1)} %bitcast.204), kind=kOutput, calls=%fused_computation.36 | convolution fusion | flops 7250116608 | bytes 16515072 | tf_op jit(solution)/shard_map/dot_general | solution.py:28
  216.7 16.4 %collective-permute-done.11 = bf16[48,6144]{1,0:T(8,128)(2,1)} collective-permute-done((bf16[48,6144]{1,0:T(8,128)(2,1)}, bf16[48,6144]{1,0:T(8,128)(2,1)}, u32[]{:S(2)}, u32[]{:S(2)}) %collective-permute-start.11) | collective-permute-done | bytes 589856 | tf_op jit(solution)/shard_map/ppermute | solution.py:830
  243.8 5.7 collective-permute-start.19
  253.9 6.9 fusion.64.q_ref
  260.8 58.5 %self_attend.1 = (bf16[768,1536]{1,0:T(8,128)(2,1)S(1)}, f32[96,768]{1,0:T(8,128)S(1)}) custom-call(s32[5]{0:T(128)S(1)} %stack.66.place, bf16[768,1536]{1,0:T(8,128)(2,1)S(1)} %fusion.64.q_ref, bf16[768,3072]{1,0:T(8,128)(2,1)S(1)} %bitcast.172, bf16[768,3072]{1,0:T(8,128)(2,1)S(1)} %bitcast.172, bf16[768,3072]{1,0:T(8,128)(2,1)} %collective-permute-done.14.other_k.other_v, ...), custom_call_target="tpu_custom_call" | custom-call | flops 7247757312 | bytes 18874368 | tf_op jit(solution)/shard_map/self_attend/pallas_call | solution.py:569
  336.1 6.9 collective-permute-done.16
  344.5 7.1 fusion.134
  360.5 10.4 collective-permute-start.23
  373.3 6.8 cross_attend.1
  386.8 63.1 %multiply_convert_fusion = (bf16[768,6144]{1,0:T(8,128)(2,1)}, f32[768,6144]{1,0:T(8,128)}, f32[768,6144]{1,0:T(8,128)}) fusion(bf16[1536,6144]{1,0:T(8,128)(2,1)} %bitcast.200, f32[768,1536]{1,0:T(8,128)} %copy-done.24, f32[1536]{0:T(1024)S(1)} %add.437, f32[1536]{0:T(1024)S(1)} %mul.317, f32[768]{0:T(1024)S(1)} %add_rsqrt_fusion, ...), kind=kOutput, calls=%fused_computation.5 | convolution fusion | flops 14808121344 | bytes 70797312 | tf_op jit(solution)/shard_map/dot_general | solution.py:28
  452.8 23.5 %multiply_convert_fusion.1 = (bf16[768,1536]{1,0:T(8,128)(2,1)S(1)}, bf16[768,1536]{1,0:T(8,128)(2,1)}, f32[768,1536]{1,0:T(8,128)}) fusion(f32[]{:T(128)S(6)} %div.75, f32[768]{0:T(1024)S(1)} %copy-done.85, bf16[384,1536]{1,0:T(8,128)(2,1)} %get-tuple-element.212, bf16[384,1536]{1,0:T(8,128)(2,1)S(1)} %get-tuple-element.211, f32[768,1536]{1,0:T(8,128)} %copy-done.24, ...), kind=kOutput, calls=%fused_computation.66 | convolution fusion | flops 14507311104 | bytes 44829700 | tf_op jit(solution)/shard_map/dot_general | solution.py:28
  476.3 9.7 convolution_convert_fusion.2
  489.6 29.5 %add_convert_fusion.2 = bf16[768,6144]{1,0:T(8,128)(2,1)} fusion(f32[768,6144]{1,0:T(8,128)} %get-tuple-element.193, f32[768,6144]{1,0:T(8,128)} %get-tuple-element.246, bf16[768,1536]{1,0:T(8,128)(2,1)} %copy-done.55, bf16[6144,1536]{1,0:T(8,128)(2,1)} %bitcast.203), kind=kOutput, calls=%fused_computation.4 | convolution fusion | flops 14561574912 | bytes 68419584 | tf_op jit(solution)/shard_map/re,de->rd/dot_general | solution.py:36
  519.1 14.1 %add_convert_fusion.1 = bf16[768,6144]{1,0:T(8,128)(2,1)} fusion(bf16[768,6144]{1,0:T(8,128)(2,1)} %collective-permute-done.26, bf16[768,6144]{1,0:T(8,128)(2,1)} %get-tuple-element.192, bf16[768,1536]{1,0:T(8,128)(2,1)} %copy-done.55, s32[]{:T(128)S(6)} %select_n.335), kind=kOutput, calls=%fused_computation.3 | convolution fusion | flops 7261913088 | bytes 29491204 | tf_op jit(solution)/shard_map/rd,re->de/dot_general | solution.py:32
  533.3 13.5 %convolution_convert_fusion.1 = bf16[3072,1536]{1,0:T(8,128)(2,1)} fusion(bf16[768,6144]{1,0:T(8,128)(2,1)} %add_convert_fusion.2, s32[]{:T(128)S(6)} %select_n.336, f32[768,1536]{1,0:T(8,128)} %copy-done.24, f32[1536]{0:T(1024)S(1)} %add.437, f32[1536]{0:T(1024)S(1)} %mul.317, f32[768]{0:T(1024)S(1)} %add_rsqrt_fusion, f32[768]{0:T(1024)S(1)} %broadcast_multiply_fusion.6), kind=kOutput, calls=%fused_computation.21 | convolution fusion | flops 7258374144 | bytes 18892804 | tf_op jit(solution)/shard_map/rd,re->de/dot_general | solution.py:32
  547.9 6.8 collective-permute-start.25
  554.7 21.6 %fusion.136 = f32[768,1536]{1,0:T(8,128)} fusion(bf16[768,6144]{1,0:T(8,128)(2,1)} %add_convert_fusion.2, bf16[1536,6144]{1,0:T(8,128)(2,1)} %bitcast.201), kind=kOutput, calls=%fused_computation.302 | convolution fusion | flops 14495514624 | bytes 33030144 | tf_op jit(solution)/shard_map/re,de->rd/dot_general | solution.py:36
  581.2 14.0 %add_convert_fusion = bf16[3072,1536]{1,0:T(8,128)(2,1)} fusion(bf16[3072,1536]{1,0:T(8,128)(2,1)} %collective-permute-done.27, bf16[768,6144]{1,0:T(8,128)(2,1)} %add_convert_fusion.2, s32[]{:T(128)S(6)} %select_n.339, f32[768,1536]{1,0:T(8,128)S(1)} %bitcast.176, f32[1536]{0:T(1024)S(1)} %add.437, f32[1536]{0:T(1024)S(1)} %mul.317, ...), kind=kOutput, calls=%fused_computation.2 | convolution fusion | flops 7267811328 | bytes 28329988 | tf_op jit(solution)/shard_map/rd,re->de/dot_general | solution.py:32
  595.3 6.1 multiply_reduce_fusion.1
  601.4 9.6 fusion.131
  614.5 6.6 fusion.61.grad_ref
  621.1 9.5 cross_attend_back.1
  638.0 5.9 collective-permute-done.32
  652.4 9.4 multiply_reduce_fusion.2
  669.5 7.5 fusion.55.grad_ref
  705.7 70.1 %self_attend_back.1 = (bf16[768,1536]{1,0:T(8,128)(2,1)S(1)}, bf16[768,1536]{1,0:T(8,128)(2,1)S(1)}, bf16[768,1536]{1,0:T(8,128)(2,1)S(1)}, bf16[768,1536]{1,0:T(8,128)(2,1)}, bf16[768,1536]{1,0:T(8,128)(2,1)}) custom-call(s32[5]{0:T(128)S(1)} %copy-done.14, bf16[768,1536]{1,0:T(8,128)(2,1)S(1)} %copy-done.21, bf16[768,3072]{1,0:T(8,128)(2,1)} %fusion.14.own_k.own_v, ...), custom_call_target="tpu_custom_call" | custom-call | flops 18119393280 | bytes 37748736 | tf_op jit(solution)/shard_map/self_attend_back/pallas_call | solution.py:598
  790.9 7.8 convolution_convert_fusion
  798.8 18.7 %fusion.137 = f32[768,1536]{1,0:T(8,128)} fusion(bf16[768,4608]{1,0:T(8,128)(2,1)} %copy-done.30, bf16[1536,4608]{1,0:T(8,128)(2,1)} %bitcast.206), kind=kOutput, calls=%fused_computation.303 | convolution fusion | flops 10871635968 | bytes 25952256 | tf_op jit(solution)/shard_map/re,de->rd/dot_general | solution.py:36
  817.5 9.8 add_convert_fusion.3
  852.6 21.9 %collective-permute-done.46 = bf16[768,384]{1,0:T(8,128)(2,1)S(1)} collective-permute-done((bf16[768,384]{1,0:T(8,128)(2,1)}, bf16[768,384]{1,0:T(8,128)(2,1)S(1)}, u32[]{:S(2)}, u32[]{:S(2)}) %collective-permute-start.46) | collective-permute-done | bytes 589856 | tf_op jit(solution)/shard_map/ppermute | solution.py:830
  882.2 12.7 %collective-permute-start.48 = (bf16[576,384]{1,0:T(8,128)(2,1)}, bf16[576,384]{1,0:T(8,128)(2,1)}, u32[]{:S(2)}, u32[]{:S(2)}) collective-permute-start(bf16[576,384]{1,0:T(8,128)(2,1)} %get-tuple-element.224), channel_id=1, source_target_pairs={{0,1},{1,2},{2,3},{3,0},{4,5},{5,6},{6,7},{7,4},{8,9},{9,10},{10,1... | collective-permute-start | bytes 1327112 | tf_op jit(solution)/shard_map/ppermute | solution.py:830
  899.5 7.6 collective-permute-done.48
  907.2 17.9 %collective-permute-done.49 = bf16[576,384]{1,0:T(8,128)(2,1)} collective-permute-done((bf16[576,384]{1,0:T(8,128)(2,1)}, bf16[576,384]{1,0:T(8,128)(2,1)}, u32[]{:S(2)}, u32[]{:S(2)}) %collective-permute-start.49) | collective-permute-done | bytes 442400 | tf_op jit(solution)/shard_map/ppermute | solution.py:830
  933.8 10.0 collective-permute-start.51
  946.3 5.4 fusion.24
  955.9 17.2 %collective-permute-done.52 = bf16[576,384]{1,0:T(8,128)(2,1)S(1)} collective-permute-done((bf16[576,384]{1,0:T(8,128)(2,1)S(1)}, bf16[576,384]{1,0:T(8,128)(2,1)S(1)}, u32[]{:S(2)}, u32[]{:S(2)}) %collective-permute-start.52) | collective-permute-done | bytes 442400 | tf_op jit(solution)/shard_map/ppermute | solution.py:830
  976.7 13.4 %collective-permute-start.61 = (bf16[384,1536]{1,0:T(8,128)(2,1)S(1)}, bf16[384,1536]{1,0:T(8,128)(2,1)S(1)}, u32[]{:S(2)}, u32[]{:S(2)}) collective-permute-start(bf16[384,1536]{1,0:T(8,128)(2,1)S(1)} %get-tuple-element.202), channel_id=1, source_target_pairs={{1,0},{5,1},{4,2},{0,3},{3,4},{7,5},{6,6},{2,7},{9,8},{13,9},{12,1... | collective-permute-start | bytes 3538952 | tf_op jit(solution)/shard_map/ppermute | solution.py:857
  1011.0 11.1 %collective-permute-done.61 = bf16[384,1536]{1,0:T(8,128)(2,1)S(1)} collective-permute-done((bf16[384,1536]{1,0:T(8,128)(2,1)S(1)}, bf16[384,1536]{1,0:T(8,128)(2,1)S(1)}, u32[]{:S(2)}, u32[]{:S(2)}) %collective-permute-start.61) | collective-permute-done | bytes 1179680 | tf_op jit(solution)/shard_map/ppermute | solution.py:857
  1024.6 15.5 %collective-permute-start.57 = (f32[8,384]{1,0:T(8,128)S(1)}, f32[8,384]{1,0:T(8,128)S(1)}, u32[]{:S(2)}, u32[]{:S(2)}) collective-permute-start(f32[8,384]{1,0:T(8,128)S(1)} %get-tuple-element.234), channel_id=1, source_target_pairs={{0,1},{1,2},{2,3},{3,0},{4,5},{5,6},{6,7},{7,4},{8,9},{9,10},{10,1... | collective-permute-start | bytes 36872 | tf_op jit(solution)/shard_map/ppermute | solution.py:830
  1062.3 8.1 unpack.19
  (547 shorter events, 322.3 us)
Async XLA Ops:
  7.2 193.1 %all-gather.8.cloned.1.call-start = ((), (), s32[]{:S(2)}) async-start(), calls=%async_computation.4 | async-start | bytes 15925248 | tf_op jit(solution)/shard_map/all_gather | solution.py:867
  16.7 40.9 %collective-permute-start.1 = (bf16[64,4608]{1,0:T(8,128)(2,1)S(1)}, bf16[64,4608]{1,0:T(8,128)(2,1)}, u32[]{:S(2)}, u32[]{:S(2)}) collective-permute-start(bf16[64,4608]{1,0:T(8,128)(2,1)S(1)} %pad_maximum_fusion.5), channel_id=1, source_target_pairs={{0,2},{1,3},{2,0},{3,1},{4,6},{5,7},{6,4},{7,5},{8,10},{9,11},{10,... | collective-permute-start | bytes 1769480 | tf_op jit(solution)/shard_map/ppermute | solution.py:830
  19.3 39.3 %collective-permute-start.2 = (bf16[64,4608]{1,0:T(8,128)(2,1)S(1)}, bf16[64,4608]{1,0:T(8,128)(2,1)}, u32[]{:S(2)}, u32[]{:S(2)}) collective-permute-start(bf16[64,4608]{1,0:T(8,128)(2,1)S(1)} %pad_maximum_fusion.5), channel_id=1, source_target_pairs={{0,3},{1,0},{2,1},{3,2},{4,7},{5,4},{6,5},{7,6},{8,11},{9,8},{10,9... | collective-permute-start | bytes 1769480 | tf_op jit(solution)/shard_map/ppermute | solution.py:830
  61.0 283.4 %all-gather.10.cloned.1.call-start = ((), (), s32[]{:S(2)}) async-start(), calls=%async_computation.5 | async-start | bytes 15925248 | tf_op jit(solution)/shard_map/all_gather | solution.py:867
  63.1 25.4 %collective-permute-start.3 = (bf16[48,4608]{1,0:T(8,128)(2,1)S(1)}, bf16[48,4608]{1,0:T(8,128)(2,1)S(1)}, u32[]{:S(2)}, u32[]{:S(2)}) collective-permute-start(bf16[48,4608]{1,0:T(8,128)(2,1)S(1)} %pad_maximum_fusion.7), channel_id=1, source_target_pairs={{0,1},{1,2},{2,3},{3,0},{4,5},{5,6},{6,7},{7,4},{8,9},{9,10},{10,1... | collective-permute-start | bytes 1327112 | tf_op jit(solution)/shard_map/ppermute | solution.py:830
  75.4 30.3 %collective-permute-start.4 = (bf16[48,4608]{1,0:T(8,128)(2,1)S(1)}, bf16[48,4608]{1,0:T(8,128)(2,1)S(1)}, u32[]{:S(2)}, u32[]{:S(2)}) collective-permute-start(bf16[48,4608]{1,0:T(8,128)(2,1)S(1)} %pad_maximum_fusion.7), channel_id=1, source_target_pairs={{0,2},{1,3},{2,0},{3,1},{4,6},{5,7},{6,4},{7,5},{8,10},{9,11},{10,... | collective-permute-start | bytes 1327112 | tf_op jit(solution)/shard_map/ppermute | solution.py:830
  78.1 27.6 %collective-permute-start.5 = (bf16[48,4608]{1,0:T(8,128)(2,1)S(1)}, bf16[48,4608]{1,0:T(8,128)(2,1)S(1)}, u32[]{:S(2)}, u32[]{:S(2)}) collective-permute-start(bf16[48,4608]{1,0:T(8,128)(2,1)S(1)} %pad_maximum_fusion.7), channel_id=1, source_target_pairs={{0,3},{1,0},{2,1},{3,2},{4,7},{5,4},{6,5},{7,6},{8,11},{9,8},{10,9... | collective-permute-start | bytes 1327112 | tf_op jit(solution)/shard_map/ppermute | solution.py:830
  107.0 279.8 %all-gather.12.cloned.1.call-start = ((), (), s32[]{:S(2)}) async-start(), calls=%async_computation.6 | async-start | bytes 21233664 | tf_op jit(solution)/shard_map/all_gather | solution.py:867
  122.3 32.4 %collective-permute-start.6 = (bf16[384,1536]{1,0:T(8,128)(2,1)}, bf16[384,1536]{1,0:T(8,128)(2,1)S(1)}, u32[]{:S(2)}, u32[]{:S(2)}) collective-permute-start(bf16[384,1536]{1,0:T(8,128)(2,1)} %get-tuple-element.220), channel_id=1, source_target_pairs={{0,0},{1,4},{2,5},{3,1},{4,2},{5,6},{6,7},{7,3},{8,8},{9,12},{10,1... | collective-permute-start | bytes 3538952 | tf_op jit(solution)/shard_map/ppermute | solution.py:844
  124.2 51.4 %collective-permute-start.7 = (bf16[384,1536]{1,0:T(8,128)(2,1)}, bf16[384,1536]{1,0:T(8,128)(2,1)}, u32[]{:S(2)}, u32[]{:S(2)}) collective-permute-start(bf16[384,1536]{1,0:T(8,128)(2,1)} %get-tuple-element.219), channel_id=1, source_target_pairs={{0,1},{1,5},{2,4},{3,0},{4,3},{5,7},{6,6},{7,2},{8,9},{9,13},{10,1... | collective-permute-start | bytes 3538952 | tf_op jit(solution)/shard_map/ppermute | solution.py:845
  175.5 41.2 %collective-permute-start.10 = (bf16[48,6144]{1,0:T(8,128)(2,1)}, bf16[48,6144]{1,0:T(8,128)(2,1)}, u32[]{:S(2)}, u32[]{:S(2)}) collective-permute-start(bf16[48,6144]{1,0:T(8,128)(2,1)} %get-tuple-element.92), channel_id=1, source_target_pairs={{0,2},{1,3},{2,0},{3,1},{4,6},{5,7},{6,4},{7,5},{8,10},{9,11},{10,... | collective-permute-start | bytes 1769480 | tf_op jit(solution)/shard_map/ppermute | solution.py:830
  192.3 40.8 %collective-permute-start.11 = (bf16[48,6144]{1,0:T(8,128)(2,1)}, bf16[48,6144]{1,0:T(8,128)(2,1)}, u32[]{:S(2)}, u32[]{:S(2)}) collective-permute-start(bf16[48,6144]{1,0:T(8,128)(2,1)} %get-tuple-element.92), channel_id=1, source_target_pairs={{0,3},{1,0},{2,1},{3,2},{4,7},{5,4},{6,5},{7,6},{8,11},{9,8},{10,9... | collective-permute-start | bytes 1769480 | tf_op jit(solution)/shard_map/ppermute | solution.py:830
  192.3 40.8 %collective-permute-start.9 = (bf16[48,6144]{1,0:T(8,128)(2,1)}, bf16[48,6144]{1,0:T(8,128)(2,1)}, u32[]{:S(2)}, u32[]{:S(2)}) collective-permute-start(bf16[48,6144]{1,0:T(8,128)(2,1)} %get-tuple-element.92), channel_id=1, source_target_pairs={{0,1},{1,2},{2,3},{3,0},{4,5},{5,6},{6,7},{7,4},{8,9},{9,10},{10,1... | collective-permute-start | bytes 1769480 | tf_op jit(solution)/shard_map/ppermute | solution.py:830
  237.9 215.0 %all-gather.14.cloned.1.call-start = ((), (), s32[]{:S(2)}) async-start(), calls=%async_computation.7 | async-start | bytes 21233664 | tf_op jit(solution)/shard_map/all_gather | solution.py:867
  243.8 75.6 %collective-permute-start.19 = (bf16[192,1536]{1,0:T(8,128)(2,1)}, bf16[192,1536]{1,0:T(8,128)(2,1)S(1)}, u32[]{:S(2)}, u32[]{:S(2)}) collective-permute-start(bf16[192,1536]{1,0:T(8,128)(2,1)} %get-tuple-element.103), channel_id=1, source_target_pairs={{0,1},{1,2},{2,3},{3,0},{4,5},{5,6},{6,7},{7,4},{8,9},{9,10},{10,1... | collective-permute-start | bytes 1769480 | tf_op jit(solution)/shard_map/ppermute | solution.py:830
  249.5 69.9 %collective-permute-start.20 = (bf16[192,1536]{1,0:T(8,128)(2,1)}, bf16[192,1536]{1,0:T(8,128)(2,1)S(1)}, u32[]{:S(2)}, u32[]{:S(2)}) collective-permute-start(bf16[192,1536]{1,0:T(8,128)(2,1)} %get-tuple-element.103), channel_id=1, source_target_pairs={{0,2},{1,3},{2,0},{3,1},{4,6},{5,7},{6,4},{7,5},{8,10},{9,11},{10,... | collective-permute-start | bytes 1769480 | tf_op jit(solution)/shard_map/ppermute | solution.py:830
  250.9 68.5 %collective-permute-start.21 = (bf16[192,1536]{1,0:T(8,128)(2,1)}, bf16[192,1536]{1,0:T(8,128)(2,1)S(1)}, u32[]{:S(2)}, u32[]{:S(2)}) collective-permute-start(bf16[192,1536]{1,0:T(8,128)(2,1)} %get-tuple-element.103), channel_id=1, source_target_pairs={{0,3},{1,0},{2,1},{3,2},{4,7},{5,4},{6,5},{7,6},{8,11},{9,8},{10,9... | collective-permute-start | bytes 1769480 | tf_op jit(solution)/shard_map/ppermute | solution.py:830
  322.0 372.0 %reduce-scatter.5.cloned.1.call-start = ((), (), s32[]{:S(2)}) async-start(), calls=%async_computation.8 | async-start | bytes 11796480 | tf_op jit(solution)/shard_map/reduce_scatter | solution.py:1011
  344.3 28.9 %collective-permute-start.18 = (bf16[64,1536]{1,0:T(8,128)(2,1)S(1)}, bf16[64,1536]{1,0:T(8,128)(2,1)S(1)}, u32[]{:S(2)}, u32[]{:S(2)}) collective-permute-start(bf16[64,1536]{1,0:T(8,128)(2,1)S(1)} %fusion.89), channel_id=1, source_target_pairs={{0,4},{4,0},{1,5},{5,1},{2,6},{6,2},{3,7},{7,3},{8,12},{12,8},{9,1... | collective-permute-start | bytes 589832 | tf_op jit(solution)/shard_map/ppermute | solution.py:973
  360.5 89.4 %collective-permute-start.23 = (bf16[384,1536]{1,0:T(8,128)(2,1)}, bf16[384,1536]{1,0:T(8,128)(2,1)}, u32[]{:S(2)}, u32[]{:S(2)}) collective-permute-start(bf16[384,1536]{1,0:T(8,128)(2,1)} %get-tuple-element.214), channel_id=1, source_target_pairs={{0,0},{1,4},{2,5},{3,1},{4,2},{5,6},{6,7},{7,3},{8,8},{9,12},{10,1... | collective-permute-start | bytes 3538952 | tf_op jit(solution)/shard_map/ppermute | solution.py:844
  370.9 79.0 %collective-permute-start.24 = (bf16[384,1536]{1,0:T(8,128)(2,1)}, bf16[384,1536]{1,0:T(8,128)(2,1)}, u32[]{:S(2)}, u32[]{:S(2)}) collective-permute-start(bf16[384,1536]{1,0:T(8,128)(2,1)} %get-tuple-element.213), channel_id=1, source_target_pairs={{0,1},{1,5},{2,4},{3,0},{4,3},{5,7},{6,6},{7,2},{8,9},{9,13},{10,1... | collective-permute-start | bytes 3538952 | tf_op jit(solution)/shard_map/ppermute | solution.py:845
  486.1 33.0 %collective-permute-start.26 = (bf16[768,6144]{1,0:T(8,128)(2,1)}, bf16[768,6144]{1,0:T(8,128)(2,1)}, u32[]{:S(2)}, u32[]{:S(2)}) collective-permute-start(bf16[768,6144]{1,0:T(8,128)(2,1)} %convolution_convert_fusion.2), channel_id=1, source_target_pairs={{0,4},{4,0},{1,5},{5,1},{2,6},{6,2},{3,7},{7,3},{8,12},{12,8},{9,1... | collective-permute-start | bytes 28311560 | tf_op jit(solution)/shard_map/ppermute | solution.py:1006
  487.9 31.2 %collective-permute-start.22 = (bf16[384,1536]{1,0:T(8,128)(2,1)S(1)}, bf16[384,1536]{1,0:T(8,128)(2,1)}, u32[]{:S(2)}, u32[]{:S(2)}) collective-permute-start(bf16[384,1536]{1,0:T(8,128)(2,1)S(1)} %get-tuple-element.215), channel_id=1, source_target_pairs={{0,0},{4,1},{5,2},{1,3},{2,4},{6,5},{7,6},{3,7},{8,8},{12,9},{13,1... | collective-permute-start | bytes 3538952 | tf_op jit(solution)/shard_map/ppermute | solution.py:1034
  533.2 296.0 %reduce-scatter.7.cloned.1.call-start = ((), (), s32[]{:S(2)}) async-start(), calls=%async_computation.9 | async-start | bytes 11796480 | tf_op jit(solution)/shard_map/reduce_scatter | solution.py:1011
  546.8 34.4 %collective-permute-start.27 = (bf16[3072,1536]{1,0:T(8,128)(2,1)}, bf16[3072,1536]{1,0:T(8,128)(2,1)}, u32[]{:S(2)}, u32[]{:S(2)}) collective-permute-start(bf16[3072,1536]{1,0:T(8,128)(2,1)} %convolution_convert_fusion.1), channel_id=1, source_target_pairs={{0,4},{4,0},{1,5},{5,1},{2,6},{6,2},{3,7},{7,3},{8,12},{12,8},{9,1... | collective-permute-start | bytes 28311560 | tf_op jit(solution)/shard_map/ppermute | solution.py:1006
  547.9 33.4 %collective-permute-start.25 = (bf16[384,1536]{1,0:T(8,128)(2,1)S(1)}, bf16[384,1536]{1,0:T(8,128)(2,1)}, u32[]{:S(2)}, u32[]{:S(2)}) collective-permute-start(bf16[384,1536]{1,0:T(8,128)(2,1)S(1)} %get-tuple-element.112), channel_id=1, source_target_pairs={{1,0},{5,1},{4,2},{0,3},{3,4},{7,5},{6,6},{2,7},{9,8},{13,9},{12,1... | collective-permute-start | bytes 3538952 | tf_op jit(solution)/shard_map/ppermute | solution.py:1044
  595.3 283.0 %reduce-scatter.9.cloned.1.call-start = ((), (), s32[]{:S(2)}) async-start(), calls=%async_computation.10 | async-start | bytes 10321920 | tf_op jit(solution)/shard_map/reduce_scatter | solution.py:1011
  614.5 30.1 %collective-permute-start.28 = (bf16[768,1536]{1,0:T(8,128)(2,1)}, bf16[768,1536]{1,0:T(8,128)(2,1)}, u32[]{:S(2)}, u32[]{:S(2)}) collective-permute-start(bf16[768,1536]{1,0:T(8,128)(2,1)} %convolution_convert_fusion.5), channel_id=1, source_target_pairs={{0,4},{4,0},{1,5},{5,1},{2,6},{6,2},{3,7},{7,3},{8,12},{12,8},{9,1... | collective-permute-start | bytes 7077896 | tf_op jit(solution)/shard_map/ppermute | solution.py:1006
  635.3 32.5 %collective-permute-start.33 = (bf16[64,1536]{1,0:T(8,128)(2,1)}, bf16[64,1536]{1,0:T(8,128)(2,1)S(1)}, u32[]{:S(2)}, u32[]{:S(2)}) collective-permute-start(bf16[64,1536]{1,0:T(8,128)(2,1)} %get-tuple-element.185), channel_id=1, source_target_pairs={{0,2},{1,3},{2,0},{3,1},{4,6},{5,7},{6,4},{7,5},{8,10},{9,11},{10,... | collective-permute-start | bytes 589832 | tf_op jit(solution)/shard_map/ppermute | solution.py:830
  637.5 30.3 %collective-permute-start.34 = (bf16[64,1536]{1,0:T(8,128)(2,1)}, bf16[64,1536]{1,0:T(8,128)(2,1)S(1)}, u32[]{:S(2)}, u32[]{:S(2)}) collective-permute-start(bf16[64,1536]{1,0:T(8,128)(2,1)} %get-tuple-element.185), channel_id=1, source_target_pairs={{0,3},{1,0},{2,1},{3,2},{4,7},{5,4},{6,5},{7,6},{8,11},{9,8},{10,9... | collective-permute-start | bytes 589832 | tf_op jit(solution)/shard_map/ppermute | solution.py:830
  652.4 24.7 %collective-permute-start.29 = (bf16[768,1536]{1,0:T(8,128)(2,1)}, bf16[768,1536]{1,0:T(8,128)(2,1)S(1)}, u32[]{:S(2)}, u32[]{:S(2)}) collective-permute-start(bf16[768,1536]{1,0:T(8,128)(2,1)} %convolution_convert_fusion.4), channel_id=1, source_target_pairs={{0,4},{4,0},{1,5},{5,1},{2,6},{6,2},{3,7},{7,3},{8,12},{12,8},{9,1... | collective-permute-start | bytes 7077896 | tf_op jit(solution)/shard_map/ppermute | solution.py:1006
  685.0 247.4 %reduce-scatter.11.cloned.1.call-start = ((), (), s32[]{:S(2)}) async-start(), calls=%async_computation.11 | async-start | bytes 8847360 | tf_op jit(solution)/shard_map/reduce_scatter | solution.py:1011
  690.2 88.4 %collective-permute-start.37 = (bf16[2,64,384]{2,1,0:T(8,128)(2,1)S(1)}, bf16[2,64,384]{2,1,0:T(8,128)(2,1)}, u32[]{:S(2)}, u32[]{:S(2)}) collective-permute-start(bf16[2,64,384]{2,1,0:T(8,128)(2,1)S(1)} %fusion.94), channel_id=1, source_target_pairs={{0,2},{1,3},{2,0},{3,1},{4,6},{5,7},{6,4},{7,5},{8,10},{9,11},{10,... | collective-permute-start | bytes 294920 | tf_op jit(solution)/shard_map/ppermute | solution.py:830
  692.6 86.0 %collective-permute-start.38 = (bf16[2,64,384]{2,1,0:T(8,128)(2,1)S(1)}, bf16[2,64,384]{2,1,0:T(8,128)(2,1)}, u32[]{:S(2)}, u32[]{:S(2)}) collective-permute-start(bf16[2,64,384]{2,1,0:T(8,128)(2,1)S(1)} %fusion.94), channel_id=1, source_target_pairs={{0,3},{1,0},{2,1},{3,2},{4,7},{5,4},{6,5},{7,6},{8,11},{9,8},{10,9... | collective-permute-start | bytes 294920 | tf_op jit(solution)/shard_map/ppermute | solution.py:830
  695.6 83.0 %collective-permute-start.39 = (bf16[192,1536]{1,0:T(8,128)(2,1)S(1)}, bf16[192,1536]{1,0:T(8,128)(2,1)S(1)}, u32[]{:S(2)}, u32[]{:S(2)}) collective-permute-start(bf16[192,1536]{1,0:T(8,128)(2,1)S(1)} %get-tuple-element.208), channel_id=1, source_target_pairs={{0,1},{1,2},{2,3},{3,0},{4,5},{5,6},{6,7},{7,4},{8,9},{9,10},{10,1... | collective-permute-start | bytes 1769480 | tf_op jit(solution)/shard_map/ppermute | solution.py:830
  696.3 82.3 %collective-permute-start.40 = (bf16[192,1536]{1,0:T(8,128)(2,1)S(1)}, bf16[192,1536]{1,0:T(8,128)(2,1)}, u32[]{:S(2)}, u32[]{:S(2)}) collective-permute-start(bf16[192,1536]{1,0:T(8,128)(2,1)S(1)} %get-tuple-element.207), channel_id=1, source_target_pairs={{0,2},{1,3},{2,0},{3,1},{4,6},{5,7},{6,4},{7,5},{8,10},{9,11},{10,... | collective-permute-start | bytes 1769480 | tf_op jit(solution)/shard_map/ppermute | solution.py:830
  697.8 80.8 %collective-permute-start.41 = (bf16[192,1536]{1,0:T(8,128)(2,1)S(1)}, bf16[192,1536]{1,0:T(8,128)(2,1)}, u32[]{:S(2)}, u32[]{:S(2)}) collective-permute-start(bf16[192,1536]{1,0:T(8,128)(2,1)S(1)} %get-tuple-element.206), channel_id=1, source_target_pairs={{0,3},{1,0},{2,1},{3,2},{4,7},{5,4},{6,5},{7,6},{8,11},{9,8},{10,9... | collective-permute-start | bytes 1769480 | tf_op jit(solution)/shard_map/ppermute | solution.py:830
  827.3 194.8 %all-gather.18.cloned.1.call-start = ((), (), s32[]{:S(2)}) async-start(), calls=%async_computation.13 | async-start | bytes 17252352 | tf_op jit(solution)/shard_map/all_gather | solution.py:1175
  831.9 42.6 %collective-permute-start.46 = (bf16[768,384]{1,0:T(8,128)(2,1)}, bf16[768,384]{1,0:T(8,128)(2,1)S(1)}, u32[]{:S(2)}, u32[]{:S(2)}) collective-permute-start(bf16[768,384]{1,0:T(8,128)(2,1)} %get-tuple-element.204), channel_id=1, source_target_pairs={{0,2},{1,3},{2,0},{3,1},{4,6},{5,7},{6,4},{7,5},{8,10},{9,11},{10,... | collective-permute-start | bytes 1769480 | tf_op jit(solution)/shard_map/ppermute | solution.py:830
  833.2 41.3 %collective-permute-start.47 = (bf16[768,384]{1,0:T(8,128)(2,1)S(1)}, bf16[768,384]{1,0:T(8,128)(2,1)}, u32[]{:S(2)}, u32[]{:S(2)}) collective-permute-start(bf16[768,384]{1,0:T(8,128)(2,1)S(1)} %get-tuple-element.203), channel_id=1, source_target_pairs={{0,3},{1,0},{2,1},{3,2},{4,7},{5,4},{6,5},{7,6},{8,11},{9,8},{10,9... | collective-permute-start | bytes 1769480 | tf_op jit(solution)/shard_map/ppermute | solution.py:830
  882.2 25.0 %collective-permute-start.48 = (bf16[576,384]{1,0:T(8,128)(2,1)}, bf16[576,384]{1,0:T(8,128)(2,1)}, u32[]{:S(2)}, u32[]{:S(2)}) collective-permute-start(bf16[576,384]{1,0:T(8,128)(2,1)} %get-tuple-element.224), channel_id=1, source_target_pairs={{0,1},{1,2},{2,3},{3,0},{4,5},{5,6},{6,7},{7,4},{8,9},{9,10},{10,1... | collective-permute-start | bytes 1327112 | tf_op jit(solution)/shard_map/ppermute | solution.py:830
  894.9 30.2 %collective-permute-start.49 = (bf16[576,384]{1,0:T(8,128)(2,1)}, bf16[576,384]{1,0:T(8,128)(2,1)}, u32[]{:S(2)}, u32[]{:S(2)}) collective-permute-start(bf16[576,384]{1,0:T(8,128)(2,1)} %get-tuple-element.226), channel_id=1, source_target_pairs={{0,2},{1,3},{2,0},{3,1},{4,6},{5,7},{6,4},{7,5},{8,10},{9,11},{10,... | collective-permute-start | bytes 1327112 | tf_op jit(solution)/shard_map/ppermute | solution.py:830
  896.3 28.8 %collective-permute-start.50 = (bf16[576,384]{1,0:T(8,128)(2,1)}, bf16[576,384]{1,0:T(8,128)(2,1)}, u32[]{:S(2)}, u32[]{:S(2)}) collective-permute-start(bf16[576,384]{1,0:T(8,128)(2,1)} %get-tuple-element.225), channel_id=1, source_target_pairs={{0,3},{1,0},{2,1},{3,2},{4,7},{5,4},{6,5},{7,6},{8,11},{9,8},{10,9... | collective-permute-start | bytes 1327112 | tf_op jit(solution)/shard_map/ppermute | solution.py:830
  927.5 153.7 %all-gather.16.cloned.1.call-start = ((), (), s32[]{:S(2)}) async-start(), calls=%async_computation.12 | async-start | bytes 3981312 | tf_op jit(solution)/shard_map/all_gather | solution.py:1189
  943.8 29.3 %collective-permute-start.52 = (bf16[576,384]{1,0:T(8,128)(2,1)S(1)}, bf16[576,384]{1,0:T(8,128)(2,1)S(1)}, u32[]{:S(2)}, u32[]{:S(2)}) collective-permute-start(bf16[576,384]{1,0:T(8,128)(2,1)S(1)} %get-tuple-element.222), channel_id=1, source_target_pairs={{0,2},{1,3},{2,0},{3,1},{4,6},{5,7},{6,4},{7,5},{8,10},{9,11},{10,... | collective-permute-start | bytes 1327112 | tf_op jit(solution)/shard_map/ppermute | solution.py:830
  945.3 27.8 %collective-permute-start.53 = (bf16[576,384]{1,0:T(8,128)(2,1)S(1)}, bf16[576,384]{1,0:T(8,128)(2,1)S(1)}, u32[]{:S(2)}, u32[]{:S(2)}) collective-permute-start(bf16[576,384]{1,0:T(8,128)(2,1)S(1)} %get-tuple-element.221), channel_id=1, source_target_pairs={{0,3},{1,0},{2,1},{3,2},{4,7},{5,4},{6,5},{7,6},{8,11},{9,8},{10,9... | collective-permute-start | bytes 1327112 | tf_op jit(solution)/shard_map/ppermute | solution.py:830
  974.4 36.6 %collective-permute-start.60 = (bf16[384,1536]{1,0:T(8,128)(2,1)}, bf16[384,1536]{1,0:T(8,128)(2,1)S(1)}, u32[]{:S(2)}, u32[]{:S(2)}) collective-permute-start(bf16[384,1536]{1,0:T(8,128)(2,1)} %get-tuple-element.201), channel_id=1, source_target_pairs={{0,0},{4,1},{5,2},{1,3},{2,4},{6,5},{7,6},{3,7},{8,8},{12,9},{13,1... | collective-permute-start | bytes 3538952 | tf_op jit(solution)/shard_map/ppermute | solution.py:857
  976.7 45.4 %collective-permute-start.61 = (bf16[384,1536]{1,0:T(8,128)(2,1)S(1)}, bf16[384,1536]{1,0:T(8,128)(2,1)S(1)}, u32[]{:S(2)}, u32[]{:S(2)}) collective-permute-start(bf16[384,1536]{1,0:T(8,128)(2,1)S(1)} %get-tuple-element.202), channel_id=1, source_target_pairs={{1,0},{5,1},{4,2},{0,3},{3,4},{7,5},{6,6},{2,7},{9,8},{13,9},{12,1... | collective-permute-start | bytes 3538952 | tf_op jit(solution)/shard_map/ppermute | solution.py:857
  (134 other events, 1949.4 us)
Sparse Core Ops, SparseCore 0:
  61.1 90.6 all-gather.7
  154.2 78.7 all-gather.9
  238.0 101.9 all-gather.11
  342.3 98.8 all-gather.13
  533.3 96.9 reduce-scatter.4
  633.9 95.0 reduce-scatter.6
  732.7 85.2 reduce-scatter.8
  827.4 75.7 reduce-scatter.10
  927.6 93.2 all-gather.17
  1023.2 48.7 all-gather.15

commit v13 on v11

--- a/solution.py
+++ b/solution.py
@@ -954,6 +954,7 @@
     kv = project(after(hidden_one, count), qkv_matrix[:, width:]).astype(jnp.bfloat16)
     kv_other = lax.ppermute(kv, "core", swap)
     expand_came = held(expand_came, kv)
+    text_came = held(text_came, kv)
     queries = project(after(hidden_one, kv, *expand_came), qkv_matrix[:, :width])
     queries = queries.astype(jnp.bfloat16)
     expand_matrix = from_replicas(line_up(expand_share, expand_came))
@@ -962,10 +963,9 @@
     output_matrix = rest[:, :width]
     probe_matrix = rest[:, width : 2 * width]
     merge_matrix = rest[:, 2 * width :]
-    mixed_self, lse = self_attend(after(places, *expand_came), queries, kv, kv_other)
+    mixed_self, lse = self_attend(after(places, *expand_came, *text_came), queries, kv, kv_other)
     reduce_came = held(reduce_came, mixed_self)
     reduce_matrix = from_replicas(line_up(reduce_share, reduce_came))
-    text_came = held(text_came, mixed_self)
     text_half = lax.dynamic_index_in_dim(text_part, shard, 0, keepdims=False).astype(jnp.float32)
     for values in text_came:
         text_half += values.astype(jnp.float32)

time: 1100 us -> 1120 us (1.018)
  starting transfers between devices: 162 us -> 189 us
    ppermute x2, starting transfers between devices: 13.4 us -> 26.1 us  [to_chip(): two = lax.ppermute(jnp.where(lower, pair[1], pair[0]), spot, there[1])]
    ppermute x36, starting transfers between devices: 103 us -> 116 us  [hop(): return lax.ppermute(values, 'shard', pairs)]
    unnamed x229 -> x223, local copies, waits for them, and re-layouts: 37.9 us -> 37.3 us
  transfers between devices with their start and end apart: 72 -> 72, of which waited for: 26 -> 24; matrix products, arithmetic and copies ran while one was open for 38% -> 38% of each run, Pallas kernels for 15% -> 15%
where the time goes in v13:
time: 1120 us; the launch traced here: 1110 us
  matrix products  303 us (27%)
  waiting for transfers between devices  224 us (20%)
  starting transfers between devices  189 us (17%)
  Pallas kernels  174 us (16%)
  local copies, waits for them, and re-layouts  109 us (10%)
  other arithmetic  87.7 us (8%)
  between operations  21.5 us (2%)
    ppermute x36, waiting for transfers between devices, hop(): return lax.ppermute(values, 'shard', pairs)  179 us
    dot_general x8, matrix products, project(): return jnp.dot(left, right, preferred_element_type=jnp.float32)  121 us
    ppermute x36, starting transfers between devices, hop(): return lax.ppermute(values, 'shard', pairs)  116 us
    dot_general x7, matrix products, back_project(): jnp.einsum('re,de->rd', grads, matrix, preferred_element_type=jnp.float32)  94.1 us
    dot_general x13, matrix products, outer_sum(): jnp.einsum('rd,re->de', left, right, preferred_element_type=jnp.float32)  87.6 us
    pallas_call x1, Pallas kernels, self_attend_back(): pl.pallas_call(self_backward_kernel, out_shape=(jax.ShapeDtypeStruct((row...  70.1 us
    pallas_call x1, Pallas kernels, self_attend(): pl.pallas_call(self_forward_kernel, out_shape=(jax.ShapeDtypeStruct((rows...  58.5 us
    unnamed x223, local copies, waits for them, and re-layouts  37.3 us
  transfers between devices with their start and end apart: 72, of which 24 were waited for; matrix products, arithmetic and copies ran while one was open for 38% of the time, Pallas kernels for 15%

profile of v13, /device:TPU:0, one launch (start us, length us, event | category | flops | bytes accessed | tf_op | source)
XLA Modules:
  0.0 1108.7 jit_solution(16979754872372824435)
XLA Ops:
  20.9 12.3 %collective-permute-done = bf16[64,4608]{1,0:T(8,128)(2,1)} collective-permute-done((bf16[64,4608]{1,0:T(8,128)(2,1)S(1)}, bf16[64,4608]{1,0:T(8,128)(2,1)}, u32[]{:S(2)}, u32[]{:S(2)}) %collective-permute-start) | collective-permute-done | bytes 589856 | tf_op jit(solution)/shard_map/ppermute | solution.py:830
  34.2 23.4 %collective-permute-done.1 = bf16[64,4608]{1,0:T(8,128)(2,1)} collective-permute-done((bf16[64,4608]{1,0:T(8,128)(2,1)S(1)}, bf16[64,4608]{1,0:T(8,128)(2,1)}, u32[]{:S(2)}, u32[]{:S(2)}) %collective-permute-start.1) | collective-permute-done | bytes 589856 | tf_op jit(solution)/shard_map/ppermute | solution.py:830
  63.1 12.1 %collective-permute-start.3 = (bf16[48,4608]{1,0:T(8,128)(2,1)S(1)}, bf16[48,4608]{1,0:T(8,128)(2,1)S(1)}, u32[]{:S(2)}, u32[]{:S(2)}) collective-permute-start(bf16[48,4608]{1,0:T(8,128)(2,1)S(1)} %pad_maximum_fusion.7), channel_id=1, source_target_pairs={{0,1},{1,2},{2,3},{3,0},{4,5},{5,6},{6,7},{7,4},{8,9},{9,10},{10,1... | collective-permute-start | bytes 1327112 | tf_op jit(solution)/shard_map/ppermute | solution.py:830
  78.1 10.4 collective-permute-done.3
  88.5 17.1 %collective-permute-done.4 = bf16[48,4608]{1,0:T(8,128)(2,1)S(1)} collective-permute-done((bf16[48,4608]{1,0:T(8,128)(2,1)S(1)}, bf16[48,4608]{1,0:T(8,128)(2,1)S(1)}, u32[]{:S(2)}, u32[]{:S(2)}) %collective-permute-start.4) | collective-permute-done | bytes 442400 | tf_op jit(solution)/shard_map/ppermute | solution.py:830
  124.2 11.1 %collective-permute-start.7 = (bf16[384,1536]{1,0:T(8,128)(2,1)}, bf16[384,1536]{1,0:T(8,128)(2,1)}, u32[]{:S(2)}, u32[]{:S(2)}) collective-permute-start(bf16[384,1536]{1,0:T(8,128)(2,1)} %get-tuple-element.219), channel_id=1, source_target_pairs={{0,1},{1,5},{2,4},{3,0},{4,3},{5,7},{6,6},{7,2},{8,9},{9,13},{10,1... | collective-permute-start | bytes 3538952 | tf_op jit(solution)/shard_map/ppermute | solution.py:845
  154.6 20.9 %collective-permute-done.7 = bf16[384,1536]{1,0:T(8,128)(2,1)} collective-permute-done((bf16[384,1536]{1,0:T(8,128)(2,1)}, bf16[384,1536]{1,0:T(8,128)(2,1)}, u32[]{:S(2)}, u32[]{:S(2)}) %collective-permute-start.7) | collective-permute-done | bytes 1179680 | tf_op jit(solution)/shard_map/ppermute | solution.py:845
  175.5 16.7 %collective-permute-start.10 = (bf16[48,6144]{1,0:T(8,128)(2,1)}, bf16[48,6144]{1,0:T(8,128)(2,1)}, u32[]{:S(2)}, u32[]{:S(2)}) collective-permute-start(bf16[48,6144]{1,0:T(8,128)(2,1)} %get-tuple-element.92), channel_id=1, source_target_pairs={{0,2},{1,3},{2,0},{3,1},{4,6},{5,7},{6,4},{7,5},{8,10},{9,11},{10,... | collective-permute-start | bytes 1769480 | tf_op jit(solution)/shard_map/ppermute | solution.py:830
  200.3 12.2 %fusion.14.own_k.own_v = bf16[768,3072]{1,0:T(8,128)(2,1)} fusion(bf16[768,1536]{1,0:T(8,128)(2,1)} %fusion.18, bf16[1536,4608]{1,0:T(8,128)(2,1)} %bitcast.204), kind=kOutput, calls=%fused_computation.36 | convolution fusion | flops 7250116608 | bytes 16515072 | tf_op jit(solution)/shard_map/dot_general | solution.py:28
  216.7 16.4 %collective-permute-done.11 = bf16[48,6144]{1,0:T(8,128)(2,1)} collective-permute-done((bf16[48,6144]{1,0:T(8,128)(2,1)}, bf16[48,6144]{1,0:T(8,128)(2,1)}, u32[]{:S(2)}, u32[]{:S(2)}) %collective-permute-start.11) | collective-permute-done | bytes 589856 | tf_op jit(solution)/shard_map/ppermute | solution.py:830
  246.4 5.6 collective-permute-start.14
  258.4 11.4 %collective-permute-start.20 = (bf16[192,1536]{1,0:T(8,128)(2,1)}, bf16[192,1536]{1,0:T(8,128)(2,1)S(1)}, u32[]{:S(2)}, u32[]{:S(2)}) collective-permute-start(bf16[192,1536]{1,0:T(8,128)(2,1)} %get-tuple-element.103), channel_id=1, source_target_pairs={{0,2},{1,3},{2,0},{3,1},{4,6},{5,7},{6,4},{7,5},{8,10},{9,11},{10,... | collective-permute-start | bytes 1769480 | tf_op jit(solution)/shard_map/ppermute | solution.py:830
  275.0 6.3 fusion.64.q_ref
  281.5 58.5 %self_attend.1 = (bf16[768,1536]{1,0:T(8,128)(2,1)S(1)}, f32[96,768]{1,0:T(8,128)S(1)}) custom-call(s32[5]{0:T(128)S(1)} %stack.66.place, bf16[768,1536]{1,0:T(8,128)(2,1)S(1)} %fusion.64.q_ref, bf16[768,3072]{1,0:T(8,128)(2,1)S(1)} %bitcast.172, bf16[768,3072]{1,0:T(8,128)(2,1)S(1)} %bitcast.172, bf16[768,3072]{1,0:T(8,128)(2,1)} %collective-permute-done.17.other_k.other_v, ...), custom_call_target="tpu_custom_call" | custom-call | flops 7247757312 | bytes 18874368 | tf_op jit(solution)/shard_map/self_attend/pallas_call | solution.py:569
  347.9 7.1 fusion.134
  363.4 10.9 collective-permute-start.23
  374.2 15.0 %collective-permute-start.24 = (bf16[384,1536]{1,0:T(8,128)(2,1)}, bf16[384,1536]{1,0:T(8,128)(2,1)}, u32[]{:S(2)}, u32[]{:S(2)}) collective-permute-start(bf16[384,1536]{1,0:T(8,128)(2,1)} %get-tuple-element.213), channel_id=1, source_target_pairs={{0,1},{1,5},{2,4},{3,0},{4,3},{5,7},{6,6},{7,2},{8,9},{9,13},{10,1... | collective-permute-start | bytes 3538952 | tf_op jit(solution)/shard_map/ppermute | solution.py:845
  389.3 6.8 cross_attend.1
  402.7 63.8 %multiply_convert_fusion = (bf16[768,6144]{1,0:T(8,128)(2,1)}, f32[768,6144]{1,0:T(8,128)}, f32[768,6144]{1,0:T(8,128)}) fusion(bf16[1536,6144]{1,0:T(8,128)(2,1)} %bitcast.200, f32[768,1536]{1,0:T(8,128)} %copy-done.24, f32[1536]{0:T(1024)S(1)} %add.437, f32[1536]{0:T(1024)S(1)} %mul.317, f32[768]{0:T(1024)S(1)} %add_rsqrt_fusion, ...), kind=kOutput, calls=%fused_computation.5 | convolution fusion | flops 14808121344 | bytes 70797312 | tf_op jit(solution)/shard_map/dot_general | solution.py:28
  469.5 23.5 %multiply_convert_fusion.1 = (bf16[768,1536]{1,0:T(8,128)(2,1)S(1)}, bf16[768,1536]{1,0:T(8,128)(2,1)}, f32[768,1536]{1,0:T(8,128)}) fusion(f32[]{:T(128)S(6)} %div.75, f32[768]{0:T(1024)S(1)} %copy-done.85, bf16[384,1536]{1,0:T(8,128)(2,1)} %get-tuple-element.212, bf16[384,1536]{1,0:T(8,128)(2,1)S(1)} %get-tuple-element.211, f32[768,1536]{1,0:T(8,128)} %copy-done.24, ...), kind=kOutput, calls=%fused_computation.66 | convolution fusion | flops 14507311104 | bytes 44829700 | tf_op jit(solution)/shard_map/dot_general | solution.py:28
  493.0 9.7 convolution_convert_fusion.2
  508.0 29.5 %add_convert_fusion.2 = bf16[768,6144]{1,0:T(8,128)(2,1)} fusion(f32[768,6144]{1,0:T(8,128)} %get-tuple-element.193, f32[768,6144]{1,0:T(8,128)} %get-tuple-element.246, bf16[768,1536]{1,0:T(8,128)(2,1)} %copy-done.55, bf16[6144,1536]{1,0:T(8,128)(2,1)} %bitcast.203), kind=kOutput, calls=%fused_computation.4 | convolution fusion | flops 14561574912 | bytes 68419584 | tf_op jit(solution)/shard_map/re,de->rd/dot_general | solution.py:36
  537.5 14.0 %add_convert_fusion.1 = bf16[768,6144]{1,0:T(8,128)(2,1)} fusion(bf16[768,6144]{1,0:T(8,128)(2,1)} %collective-permute-done.26, bf16[768,6144]{1,0:T(8,128)(2,1)} %get-tuple-element.192, bf16[768,1536]{1,0:T(8,128)(2,1)} %copy-done.55, s32[]{:T(128)S(6)} %select_n.335), kind=kOutput, calls=%fused_computation.3 | convolution fusion | flops 7261913088 | bytes 29491204 | tf_op jit(solution)/shard_map/rd,re->de/dot_general | solution.py:32
  551.6 13.5 %convolution_convert_fusion.1 = bf16[3072,1536]{1,0:T(8,128)(2,1)} fusion(bf16[768,6144]{1,0:T(8,128)(2,1)} %add_convert_fusion.2, s32[]{:T(128)S(6)} %select_n.336, f32[768,1536]{1,0:T(8,128)} %copy-done.24, f32[1536]{0:T(1024)S(1)} %add.437, f32[1536]{0:T(1024)S(1)} %mul.317, f32[768]{0:T(1024)S(1)} %add_rsqrt_fusion, f32[768]{0:T(1024)S(1)} %broadcast_multiply_fusion.6), kind=kOutput, calls=%fused_computation.21 | convolution fusion | flops 7258374144 | bytes 18892804 | tf_op jit(solution)/shard_map/rd,re->de/dot_general | solution.py:32
  565.5 6.8 collective-permute-start.25
  572.3 21.7 %fusion.136 = f32[768,1536]{1,0:T(8,128)} fusion(bf16[768,6144]{1,0:T(8,128)(2,1)} %add_convert_fusion.2, bf16[1536,6144]{1,0:T(8,128)(2,1)} %bitcast.201), kind=kOutput, calls=%fused_computation.302 | convolution fusion | flops 14495514624 | bytes 33030144 | tf_op jit(solution)/shard_map/re,de->rd/dot_general | solution.py:36
  598.8 14.0 %add_convert_fusion = bf16[3072,1536]{1,0:T(8,128)(2,1)} fusion(bf16[3072,1536]{1,0:T(8,128)(2,1)} %collective-permute-done.27, bf16[768,6144]{1,0:T(8,128)(2,1)} %add_convert_fusion.2, s32[]{:T(128)S(6)} %select_n.339, f32[768,1536]{1,0:T(8,128)S(1)} %bitcast.176, f32[1536]{0:T(1024)S(1)} %add.437, f32[1536]{0:T(1024)S(1)} %mul.317, ...), kind=kOutput, calls=%fused_computation.2 | convolution fusion | flops 7267811328 | bytes 28329988 | tf_op jit(solution)/shard_map/rd,re->de/dot_general | solution.py:32
  612.9 6.1 multiply_reduce_fusion.1
  619.1 9.7 fusion.131
  632.3 6.6 fusion.61.grad_ref
  638.9 9.5 cross_attend_back.1
  655.7 5.9 collective-permute-done.32
  670.1 9.4 multiply_reduce_fusion.2
  687.2 7.6 fusion.55.grad_ref
  723.5 70.1 %self_attend_back.1 = (bf16[768,1536]{1,0:T(8,128)(2,1)S(1)}, bf16[768,1536]{1,0:T(8,128)(2,1)S(1)}, bf16[768,1536]{1,0:T(8,128)(2,1)S(1)}, bf16[768,1536]{1,0:T(8,128)(2,1)}, bf16[768,1536]{1,0:T(8,128)(2,1)}) custom-call(s32[5]{0:T(128)S(1)} %copy-done.14, bf16[768,1536]{1,0:T(8,128)(2,1)S(1)} %copy-done.21, bf16[768,3072]{1,0:T(8,128)(2,1)} %fusion.14.own_k.own_v, ...), custom_call_target="tpu_custom_call" | custom-call | flops 18119393280 | bytes 37748736 | tf_op jit(solution)/shard_map/self_attend_back/pallas_call | solution.py:598
  808.7 7.8 convolution_convert_fusion
  816.6 18.7 %fusion.137 = f32[768,1536]{1,0:T(8,128)} fusion(bf16[768,4608]{1,0:T(8,128)(2,1)} %copy-done.30, bf16[1536,4608]{1,0:T(8,128)(2,1)} %bitcast.206), kind=kOutput, calls=%fused_computation.303 | convolution fusion | flops 10871635968 | bytes 25952256 | tf_op jit(solution)/shard_map/re,de->rd/dot_general | solution.py:36
  835.3 9.8 add_convert_fusion.3
  870.2 22.2 %collective-permute-done.46 = bf16[768,384]{1,0:T(8,128)(2,1)S(1)} collective-permute-done((bf16[768,384]{1,0:T(8,128)(2,1)}, bf16[768,384]{1,0:T(8,128)(2,1)S(1)}, u32[]{:S(2)}, u32[]{:S(2)}) %collective-permute-start.46) | collective-permute-done | bytes 589856 | tf_op jit(solution)/shard_map/ppermute | solution.py:830
  900.1 12.7 %collective-permute-start.48 = (bf16[576,384]{1,0:T(8,128)(2,1)}, bf16[576,384]{1,0:T(8,128)(2,1)}, u32[]{:S(2)}, u32[]{:S(2)}) collective-permute-start(bf16[576,384]{1,0:T(8,128)(2,1)} %get-tuple-element.224), channel_id=1, source_target_pairs={{0,1},{1,2},{2,3},{3,0},{4,5},{5,6},{6,7},{7,4},{8,9},{9,10},{10,1... | collective-permute-start | bytes 1327112 | tf_op jit(solution)/shard_map/ppermute | solution.py:830
  917.4 7.4 collective-permute-done.48
  924.8 17.9 %collective-permute-done.49 = bf16[576,384]{1,0:T(8,128)(2,1)} collective-permute-done((bf16[576,384]{1,0:T(8,128)(2,1)}, bf16[576,384]{1,0:T(8,128)(2,1)}, u32[]{:S(2)}, u32[]{:S(2)}) %collective-permute-start.49) | collective-permute-done | bytes 442400 | tf_op jit(solution)/shard_map/ppermute | solution.py:830
  951.5 10.0 collective-permute-start.51
  973.8 17.2 %collective-permute-done.52 = bf16[576,384]{1,0:T(8,128)(2,1)S(1)} collective-permute-done((bf16[576,384]{1,0:T(8,128)(2,1)S(1)}, bf16[576,384]{1,0:T(8,128)(2,1)S(1)}, u32[]{:S(2)}, u32[]{:S(2)}) %collective-permute-start.52) | collective-permute-done | bytes 442400 | tf_op jit(solution)/shard_map/ppermute | solution.py:830
  994.6 13.2 %collective-permute-start.61 = (bf16[384,1536]{1,0:T(8,128)(2,1)S(1)}, bf16[384,1536]{1,0:T(8,128)(2,1)S(1)}, u32[]{:S(2)}, u32[]{:S(2)}) collective-permute-start(bf16[384,1536]{1,0:T(8,128)(2,1)S(1)} %get-tuple-element.202), channel_id=1, source_target_pairs={{1,0},{5,1},{4,2},{0,3},{3,4},{7,5},{6,6},{2,7},{9,8},{13,9},{12,1... | collective-permute-start | bytes 3538952 | tf_op jit(solution)/shard_map/ppermute | solution.py:857
  1036.8 17.7 %collective-permute-done.58 = f32[8,384]{1,0:T(8,128)} collective-permute-done((f32[8,384]{1,0:T(8,128)}, f32[8,384]{1,0:T(8,128)}, u32[]{:S(2)}, u32[]{:S(2)}) %collective-permute-start.58) | collective-permute-done | bytes 12320 | tf_op jit(solution)/shard_map/ppermute | solution.py:830
  1063.8 5.6 copy-done.2
  1074.7 8.1 unpack.19
  (541 shorter events, 323.2 us)
Async XLA Ops:
  7.2 193.1 %all-gather.8.cloned.1.call-start = ((), (), s32[]{:S(2)}) async-start(), calls=%async_computation.4 | async-start | bytes 15925248 | tf_op jit(solution)/shard_map/all_gather | solution.py:867
  16.7 40.9 %collective-permute-start.1 = (bf16[64,4608]{1,0:T(8,128)(2,1)S(1)}, bf16[64,4608]{1,0:T(8,128)(2,1)}, u32[]{:S(2)}, u32[]{:S(2)}) collective-permute-start(bf16[64,4608]{1,0:T(8,128)(2,1)S(1)} %pad_maximum_fusion.5), channel_id=1, source_target_pairs={{0,2},{1,3},{2,0},{3,1},{4,6},{5,7},{6,4},{7,5},{8,10},{9,11},{10,... | collective-permute-start | bytes 1769480 | tf_op jit(solution)/shard_map/ppermute | solution.py:830
  19.3 39.3 %collective-permute-start.2 = (bf16[64,4608]{1,0:T(8,128)(2,1)S(1)}, bf16[64,4608]{1,0:T(8,128)(2,1)}, u32[]{:S(2)}, u32[]{:S(2)}) collective-permute-start(bf16[64,4608]{1,0:T(8,128)(2,1)S(1)} %pad_maximum_fusion.5), channel_id=1, source_target_pairs={{0,3},{1,0},{2,1},{3,2},{4,7},{5,4},{6,5},{7,6},{8,11},{9,8},{10,9... | collective-permute-start | bytes 1769480 | tf_op jit(solution)/shard_map/ppermute | solution.py:830
  61.0 286.9 %all-gather.10.cloned.1.call-start = ((), (), s32[]{:S(2)}) async-start(), calls=%async_computation.5 | async-start | bytes 15925248 | tf_op jit(solution)/shard_map/all_gather | solution.py:867
  63.1 25.4 %collective-permute-start.3 = (bf16[48,4608]{1,0:T(8,128)(2,1)S(1)}, bf16[48,4608]{1,0:T(8,128)(2,1)S(1)}, u32[]{:S(2)}, u32[]{:S(2)}) collective-permute-start(bf16[48,4608]{1,0:T(8,128)(2,1)S(1)} %pad_maximum_fusion.7), channel_id=1, source_target_pairs={{0,1},{1,2},{2,3},{3,0},{4,5},{5,6},{6,7},{7,4},{8,9},{9,10},{10,1... | collective-permute-start | bytes 1327112 | tf_op jit(solution)/shard_map/ppermute | solution.py:830
  75.4 30.3 %collective-permute-start.4 = (bf16[48,4608]{1,0:T(8,128)(2,1)S(1)}, bf16[48,4608]{1,0:T(8,128)(2,1)S(1)}, u32[]{:S(2)}, u32[]{:S(2)}) collective-permute-start(bf16[48,4608]{1,0:T(8,128)(2,1)S(1)} %pad_maximum_fusion.7), channel_id=1, source_target_pairs={{0,2},{1,3},{2,0},{3,1},{4,6},{5,7},{6,4},{7,5},{8,10},{9,11},{10,... | collective-permute-start | bytes 1327112 | tf_op jit(solution)/shard_map/ppermute | solution.py:830
  78.1 27.6 %collective-permute-start.5 = (bf16[48,4608]{1,0:T(8,128)(2,1)S(1)}, bf16[48,4608]{1,0:T(8,128)(2,1)S(1)}, u32[]{:S(2)}, u32[]{:S(2)}) collective-permute-start(bf16[48,4608]{1,0:T(8,128)(2,1)S(1)} %pad_maximum_fusion.7), channel_id=1, source_target_pairs={{0,3},{1,0},{2,1},{3,2},{4,7},{5,4},{6,5},{7,6},{8,11},{9,8},{10,9... | collective-permute-start | bytes 1327112 | tf_op jit(solution)/shard_map/ppermute | solution.py:830
  107.0 295.8 %all-gather.12.cloned.1.call-start = ((), (), s32[]{:S(2)}) async-start(), calls=%async_computation.6 | async-start | bytes 21233664 | tf_op jit(solution)/shard_map/all_gather | solution.py:867
  122.3 32.4 %collective-permute-start.6 = (bf16[384,1536]{1,0:T(8,128)(2,1)}, bf16[384,1536]{1,0:T(8,128)(2,1)S(1)}, u32[]{:S(2)}, u32[]{:S(2)}) collective-permute-start(bf16[384,1536]{1,0:T(8,128)(2,1)} %get-tuple-element.220), channel_id=1, source_target_pairs={{0,0},{1,4},{2,5},{3,1},{4,2},{5,6},{6,7},{7,3},{8,8},{9,12},{10,1... | collective-permute-start | bytes 3538952 | tf_op jit(solution)/shard_map/ppermute | solution.py:844
  124.2 51.4 %collective-permute-start.7 = (bf16[384,1536]{1,0:T(8,128)(2,1)}, bf16[384,1536]{1,0:T(8,128)(2,1)}, u32[]{:S(2)}, u32[]{:S(2)}) collective-permute-start(bf16[384,1536]{1,0:T(8,128)(2,1)} %get-tuple-element.219), channel_id=1, source_target_pairs={{0,1},{1,5},{2,4},{3,0},{4,3},{5,7},{6,6},{7,2},{8,9},{9,13},{10,1... | collective-permute-start | bytes 3538952 | tf_op jit(solution)/shard_map/ppermute | solution.py:845
  175.5 41.2 %collective-permute-start.10 = (bf16[48,6144]{1,0:T(8,128)(2,1)}, bf16[48,6144]{1,0:T(8,128)(2,1)}, u32[]{:S(2)}, u32[]{:S(2)}) collective-permute-start(bf16[48,6144]{1,0:T(8,128)(2,1)} %get-tuple-element.92), channel_id=1, source_target_pairs={{0,2},{1,3},{2,0},{3,1},{4,6},{5,7},{6,4},{7,5},{8,10},{9,11},{10,... | collective-permute-start | bytes 1769480 | tf_op jit(solution)/shard_map/ppermute | solution.py:830
  192.3 40.8 %collective-permute-start.11 = (bf16[48,6144]{1,0:T(8,128)(2,1)}, bf16[48,6144]{1,0:T(8,128)(2,1)}, u32[]{:S(2)}, u32[]{:S(2)}) collective-permute-start(bf16[48,6144]{1,0:T(8,128)(2,1)} %get-tuple-element.92), channel_id=1, source_target_pairs={{0,3},{1,0},{2,1},{3,2},{4,7},{5,4},{6,5},{7,6},{8,11},{9,8},{10,9... | collective-permute-start | bytes 1769480 | tf_op jit(solution)/shard_map/ppermute | solution.py:830
  192.3 40.8 %collective-permute-start.9 = (bf16[48,6144]{1,0:T(8,128)(2,1)}, bf16[48,6144]{1,0:T(8,128)(2,1)}, u32[]{:S(2)}, u32[]{:S(2)}) collective-permute-start(bf16[48,6144]{1,0:T(8,128)(2,1)} %get-tuple-element.92), channel_id=1, source_target_pairs={{0,1},{1,2},{2,3},{3,0},{4,5},{5,6},{6,7},{7,4},{8,9},{9,10},{10,1... | collective-permute-start | bytes 1769480 | tf_op jit(solution)/shard_map/ppermute | solution.py:830
  237.9 231.5 %all-gather.14.cloned.1.call-start = ((), (), s32[]{:S(2)}) async-start(), calls=%async_computation.7 | async-start | bytes 21233664 | tf_op jit(solution)/shard_map/all_gather | solution.py:867
  238.1 43.3 %collective-permute-start.17 = (bf16[768,3072]{1,0:T(8,128)(2,1)}, bf16[768,3072]{1,0:T(8,128)(2,1)}, u32[]{:S(2)}, u32[]{:S(2)}) collective-permute-start(bf16[768,3072]{1,0:T(8,128)(2,1)} %fusion.14.own_k.own_v), channel_id=1, source_target_pairs={{0,4},{4,0},{1,5},{5,1},{2,6},{6,2},{3,7},{7,3},{8,12},{12,8},{9,1... | collective-permute-start | bytes 14155784 | tf_op jit(solution)/shard_map/ppermute | solution.py:955
  258.3 81.7 %collective-permute-start.19 = (bf16[192,1536]{1,0:T(8,128)(2,1)}, bf16[192,1536]{1,0:T(8,128)(2,1)S(1)}, u32[]{:S(2)}, u32[]{:S(2)}) collective-permute-start(bf16[192,1536]{1,0:T(8,128)(2,1)} %get-tuple-element.103), channel_id=1, source_target_pairs={{0,1},{1,2},{2,3},{3,0},{4,5},{5,6},{6,7},{7,4},{8,9},{9,10},{10,1... | collective-permute-start | bytes 1769480 | tf_op jit(solution)/shard_map/ppermute | solution.py:830
  258.4 81.6 %collective-permute-start.20 = (bf16[192,1536]{1,0:T(8,128)(2,1)}, bf16[192,1536]{1,0:T(8,128)(2,1)S(1)}, u32[]{:S(2)}, u32[]{:S(2)}) collective-permute-start(bf16[192,1536]{1,0:T(8,128)(2,1)} %get-tuple-element.103), channel_id=1, source_target_pairs={{0,2},{1,3},{2,0},{3,1},{4,6},{5,7},{6,4},{7,5},{8,10},{9,11},{10,... | collective-permute-start | bytes 1769480 | tf_op jit(solution)/shard_map/ppermute | solution.py:830
  269.8 70.2 %collective-permute-start.21 = (bf16[192,1536]{1,0:T(8,128)(2,1)}, bf16[192,1536]{1,0:T(8,128)(2,1)S(1)}, u32[]{:S(2)}, u32[]{:S(2)}) collective-permute-start(bf16[192,1536]{1,0:T(8,128)(2,1)} %get-tuple-element.103), channel_id=1, source_target_pairs={{0,3},{1,0},{2,1},{3,2},{4,7},{5,4},{6,5},{7,6},{8,11},{9,8},{10,9... | collective-permute-start | bytes 1769480 | tf_op jit(solution)/shard_map/ppermute | solution.py:830
  342.7 369.2 %reduce-scatter.5.cloned.1.call-start = ((), (), s32[]{:S(2)}) async-start(), calls=%async_computation.8 | async-start | bytes 11796480 | tf_op jit(solution)/shard_map/reduce_scatter | solution.py:1011
  363.4 103.1 %collective-permute-start.23 = (bf16[384,1536]{1,0:T(8,128)(2,1)}, bf16[384,1536]{1,0:T(8,128)(2,1)}, u32[]{:S(2)}, u32[]{:S(2)}) collective-permute-start(bf16[384,1536]{1,0:T(8,128)(2,1)} %get-tuple-element.214), channel_id=1, source_target_pairs={{0,0},{1,4},{2,5},{3,1},{4,2},{5,6},{6,7},{7,3},{8,8},{9,12},{10,1... | collective-permute-start | bytes 3538952 | tf_op jit(solution)/shard_map/ppermute | solution.py:844
  374.2 92.3 %collective-permute-start.24 = (bf16[384,1536]{1,0:T(8,128)(2,1)}, bf16[384,1536]{1,0:T(8,128)(2,1)}, u32[]{:S(2)}, u32[]{:S(2)}) collective-permute-start(bf16[384,1536]{1,0:T(8,128)(2,1)} %get-tuple-element.213), channel_id=1, source_target_pairs={{0,1},{1,5},{2,4},{3,0},{4,3},{5,7},{6,6},{7,2},{8,9},{9,13},{10,1... | collective-permute-start | bytes 3538952 | tf_op jit(solution)/shard_map/ppermute | solution.py:845
  502.6 34.9 %collective-permute-start.26 = (bf16[768,6144]{1,0:T(8,128)(2,1)}, bf16[768,6144]{1,0:T(8,128)(2,1)}, u32[]{:S(2)}, u32[]{:S(2)}) collective-permute-start(bf16[768,6144]{1,0:T(8,128)(2,1)} %convolution_convert_fusion.2), channel_id=1, source_target_pairs={{0,4},{4,0},{1,5},{5,1},{2,6},{6,2},{3,7},{7,3},{8,12},{12,8},{9,1... | collective-permute-start | bytes 28311560 | tf_op jit(solution)/shard_map/ppermute | solution.py:1006
  506.3 31.2 %collective-permute-start.22 = (bf16[384,1536]{1,0:T(8,128)(2,1)S(1)}, bf16[384,1536]{1,0:T(8,128)(2,1)}, u32[]{:S(2)}, u32[]{:S(2)}) collective-permute-start(bf16[384,1536]{1,0:T(8,128)(2,1)S(1)} %get-tuple-element.215), channel_id=1, source_target_pairs={{0,0},{4,1},{5,2},{1,3},{2,4},{6,5},{7,6},{3,7},{8,8},{12,9},{13,1... | collective-permute-start | bytes 3538952 | tf_op jit(solution)/shard_map/ppermute | solution.py:1034
  551.6 295.5 %reduce-scatter.7.cloned.1.call-start = ((), (), s32[]{:S(2)}) async-start(), calls=%async_computation.9 | async-start | bytes 11796480 | tf_op jit(solution)/shard_map/reduce_scatter | solution.py:1011
  565.1 33.7 %collective-permute-start.27 = (bf16[3072,1536]{1,0:T(8,128)(2,1)}, bf16[3072,1536]{1,0:T(8,128)(2,1)}, u32[]{:S(2)}, u32[]{:S(2)}) collective-permute-start(bf16[3072,1536]{1,0:T(8,128)(2,1)} %convolution_convert_fusion.1), channel_id=1, source_target_pairs={{0,4},{4,0},{1,5},{5,1},{2,6},{6,2},{3,7},{7,3},{8,12},{12,8},{9,1... | collective-permute-start | bytes 28311560 | tf_op jit(solution)/shard_map/ppermute | solution.py:1006
  565.5 33.3 %collective-permute-start.25 = (bf16[384,1536]{1,0:T(8,128)(2,1)S(1)}, bf16[384,1536]{1,0:T(8,128)(2,1)}, u32[]{:S(2)}, u32[]{:S(2)}) collective-permute-start(bf16[384,1536]{1,0:T(8,128)(2,1)S(1)} %get-tuple-element.112), channel_id=1, source_target_pairs={{1,0},{5,1},{4,2},{0,3},{3,4},{7,5},{6,6},{2,7},{9,8},{13,9},{12,1... | collective-permute-start | bytes 3538952 | tf_op jit(solution)/shard_map/ppermute | solution.py:1044
  612.8 283.2 %reduce-scatter.9.cloned.1.call-start = ((), (), s32[]{:S(2)}) async-start(), calls=%async_computation.10 | async-start | bytes 10321920 | tf_op jit(solution)/shard_map/reduce_scatter | solution.py:1011
  632.2 30.1 %collective-permute-start.28 = (bf16[768,1536]{1,0:T(8,128)(2,1)}, bf16[768,1536]{1,0:T(8,128)(2,1)}, u32[]{:S(2)}, u32[]{:S(2)}) collective-permute-start(bf16[768,1536]{1,0:T(8,128)(2,1)} %convolution_convert_fusion.5), channel_id=1, source_target_pairs={{0,4},{4,0},{1,5},{5,1},{2,6},{6,2},{3,7},{7,3},{8,12},{12,8},{9,1... | collective-permute-start | bytes 7077896 | tf_op jit(solution)/shard_map/ppermute | solution.py:1006
  652.9 32.6 %collective-permute-start.33 = (bf16[64,1536]{1,0:T(8,128)(2,1)}, bf16[64,1536]{1,0:T(8,128)(2,1)S(1)}, u32[]{:S(2)}, u32[]{:S(2)}) collective-permute-start(bf16[64,1536]{1,0:T(8,128)(2,1)} %get-tuple-element.185), channel_id=1, source_target_pairs={{0,2},{1,3},{2,0},{3,1},{4,6},{5,7},{6,4},{7,5},{8,10},{9,11},{10,... | collective-permute-start | bytes 589832 | tf_op jit(solution)/shard_map/ppermute | solution.py:830
  655.3 30.2 %collective-permute-start.34 = (bf16[64,1536]{1,0:T(8,128)(2,1)}, bf16[64,1536]{1,0:T(8,128)(2,1)S(1)}, u32[]{:S(2)}, u32[]{:S(2)}) collective-permute-start(bf16[64,1536]{1,0:T(8,128)(2,1)} %get-tuple-element.185), channel_id=1, source_target_pairs={{0,3},{1,0},{2,1},{3,2},{4,7},{5,4},{6,5},{7,6},{8,11},{9,8},{10,9... | collective-permute-start | bytes 589832 | tf_op jit(solution)/shard_map/ppermute | solution.py:830
  702.7 247.3 %reduce-scatter.11.cloned.1.call-start = ((), (), s32[]{:S(2)}) async-start(), calls=%async_computation.11 | async-start | bytes 8847360 | tf_op jit(solution)/shard_map/reduce_scatter | solution.py:1011
  708.0 88.4 %collective-permute-start.37 = (bf16[2,64,384]{2,1,0:T(8,128)(2,1)S(1)}, bf16[2,64,384]{2,1,0:T(8,128)(2,1)}, u32[]{:S(2)}, u32[]{:S(2)}) collective-permute-start(bf16[2,64,384]{2,1,0:T(8,128)(2,1)S(1)} %fusion.94), channel_id=1, source_target_pairs={{0,2},{1,3},{2,0},{3,1},{4,6},{5,7},{6,4},{7,5},{8,10},{9,11},{10,... | collective-permute-start | bytes 294920 | tf_op jit(solution)/shard_map/ppermute | solution.py:830
  710.3 86.1 %collective-permute-start.38 = (bf16[2,64,384]{2,1,0:T(8,128)(2,1)S(1)}, bf16[2,64,384]{2,1,0:T(8,128)(2,1)}, u32[]{:S(2)}, u32[]{:S(2)}) collective-permute-start(bf16[2,64,384]{2,1,0:T(8,128)(2,1)S(1)} %fusion.94), channel_id=1, source_target_pairs={{0,3},{1,0},{2,1},{3,2},{4,7},{5,4},{6,5},{7,6},{8,11},{9,8},{10,9... | collective-permute-start | bytes 294920 | tf_op jit(solution)/shard_map/ppermute | solution.py:830
  713.4 83.0 %collective-permute-start.39 = (bf16[192,1536]{1,0:T(8,128)(2,1)S(1)}, bf16[192,1536]{1,0:T(8,128)(2,1)S(1)}, u32[]{:S(2)}, u32[]{:S(2)}) collective-permute-start(bf16[192,1536]{1,0:T(8,128)(2,1)S(1)} %get-tuple-element.208), channel_id=1, source_target_pairs={{0,1},{1,2},{2,3},{3,0},{4,5},{5,6},{6,7},{7,4},{8,9},{9,10},{10,1... | collective-permute-start | bytes 1769480 | tf_op jit(solution)/shard_map/ppermute | solution.py:830
  714.0 82.5 %collective-permute-start.40 = (bf16[192,1536]{1,0:T(8,128)(2,1)S(1)}, bf16[192,1536]{1,0:T(8,128)(2,1)}, u32[]{:S(2)}, u32[]{:S(2)}) collective-permute-start(bf16[192,1536]{1,0:T(8,128)(2,1)S(1)} %get-tuple-element.207), channel_id=1, source_target_pairs={{0,2},{1,3},{2,0},{3,1},{4,6},{5,7},{6,4},{7,5},{8,10},{9,11},{10,... | collective-permute-start | bytes 1769480 | tf_op jit(solution)/shard_map/ppermute | solution.py:830
  715.6 80.9 %collective-permute-start.41 = (bf16[192,1536]{1,0:T(8,128)(2,1)S(1)}, bf16[192,1536]{1,0:T(8,128)(2,1)}, u32[]{:S(2)}, u32[]{:S(2)}) collective-permute-start(bf16[192,1536]{1,0:T(8,128)(2,1)S(1)} %get-tuple-element.206), channel_id=1, source_target_pairs={{0,3},{1,0},{2,1},{3,2},{4,7},{5,4},{6,5},{7,6},{8,11},{9,8},{10,9... | collective-permute-start | bytes 1769480 | tf_op jit(solution)/shard_map/ppermute | solution.py:830
  845.1 209.4 %all-gather.18.cloned.1.call-start = ((), (), s32[]{:S(2)}) async-start(), calls=%async_computation.13 | async-start | bytes 17252352 | tf_op jit(solution)/shard_map/all_gather | solution.py:1175
  849.7 42.6 %collective-permute-start.46 = (bf16[768,384]{1,0:T(8,128)(2,1)}, bf16[768,384]{1,0:T(8,128)(2,1)S(1)}, u32[]{:S(2)}, u32[]{:S(2)}) collective-permute-start(bf16[768,384]{1,0:T(8,128)(2,1)} %get-tuple-element.204), channel_id=1, source_target_pairs={{0,2},{1,3},{2,0},{3,1},{4,6},{5,7},{6,4},{7,5},{8,10},{9,11},{10,... | collective-permute-start | bytes 1769480 | tf_op jit(solution)/shard_map/ppermute | solution.py:830
  850.8 41.5 %collective-permute-start.47 = (bf16[768,384]{1,0:T(8,128)(2,1)S(1)}, bf16[768,384]{1,0:T(8,128)(2,1)}, u32[]{:S(2)}, u32[]{:S(2)}) collective-permute-start(bf16[768,384]{1,0:T(8,128)(2,1)S(1)} %get-tuple-element.203), channel_id=1, source_target_pairs={{0,3},{1,0},{2,1},{3,2},{4,7},{5,4},{6,5},{7,6},{8,11},{9,8},{10,9... | collective-permute-start | bytes 1769480 | tf_op jit(solution)/shard_map/ppermute | solution.py:830
  900.1 24.8 %collective-permute-start.48 = (bf16[576,384]{1,0:T(8,128)(2,1)}, bf16[576,384]{1,0:T(8,128)(2,1)}, u32[]{:S(2)}, u32[]{:S(2)}) collective-permute-start(bf16[576,384]{1,0:T(8,128)(2,1)} %get-tuple-element.224), channel_id=1, source_target_pairs={{0,1},{1,2},{2,3},{3,0},{4,5},{5,6},{6,7},{7,4},{8,9},{9,10},{10,1... | collective-permute-start | bytes 1327112 | tf_op jit(solution)/shard_map/ppermute | solution.py:830
  912.8 30.0 %collective-permute-start.49 = (bf16[576,384]{1,0:T(8,128)(2,1)}, bf16[576,384]{1,0:T(8,128)(2,1)}, u32[]{:S(2)}, u32[]{:S(2)}) collective-permute-start(bf16[576,384]{1,0:T(8,128)(2,1)} %get-tuple-element.226), channel_id=1, source_target_pairs={{0,2},{1,3},{2,0},{3,1},{4,6},{5,7},{6,4},{7,5},{8,10},{9,11},{10,... | collective-permute-start | bytes 1327112 | tf_op jit(solution)/shard_map/ppermute | solution.py:830
  913.9 28.9 %collective-permute-start.50 = (bf16[576,384]{1,0:T(8,128)(2,1)}, bf16[576,384]{1,0:T(8,128)(2,1)}, u32[]{:S(2)}, u32[]{:S(2)}) collective-permute-start(bf16[576,384]{1,0:T(8,128)(2,1)} %get-tuple-element.225), channel_id=1, source_target_pairs={{0,3},{1,0},{2,1},{3,2},{4,7},{5,4},{6,5},{7,6},{8,11},{9,8},{10,9... | collective-permute-start | bytes 1327112 | tf_op jit(solution)/shard_map/ppermute | solution.py:830
  945.2 148.5 %all-gather.16.cloned.1.call-start = ((), (), s32[]{:S(2)}) async-start(), calls=%async_computation.12 | async-start | bytes 3981312 | tf_op jit(solution)/shard_map/all_gather | solution.py:1189
  961.5 29.5 %collective-permute-start.52 = (bf16[576,384]{1,0:T(8,128)(2,1)S(1)}, bf16[576,384]{1,0:T(8,128)(2,1)S(1)}, u32[]{:S(2)}, u32[]{:S(2)}) collective-permute-start(bf16[576,384]{1,0:T(8,128)(2,1)S(1)} %get-tuple-element.222), channel_id=1, source_target_pairs={{0,2},{1,3},{2,0},{3,1},{4,6},{5,7},{6,4},{7,5},{8,10},{9,11},{10,... | collective-permute-start | bytes 1327112 | tf_op jit(solution)/shard_map/ppermute | solution.py:830
  963.2 27.9 %collective-permute-start.53 = (bf16[576,384]{1,0:T(8,128)(2,1)S(1)}, bf16[576,384]{1,0:T(8,128)(2,1)S(1)}, u32[]{:S(2)}, u32[]{:S(2)}) collective-permute-start(bf16[576,384]{1,0:T(8,128)(2,1)S(1)} %get-tuple-element.221), channel_id=1, source_target_pairs={{0,3},{1,0},{2,1},{3,2},{4,7},{5,4},{6,5},{7,6},{8,11},{9,8},{10,9... | collective-permute-start | bytes 1327112 | tf_op jit(solution)/shard_map/ppermute | solution.py:830
  992.3 62.2 %collective-permute-start.60 = (bf16[384,1536]{1,0:T(8,128)(2,1)}, bf16[384,1536]{1,0:T(8,128)(2,1)S(1)}, u32[]{:S(2)}, u32[]{:S(2)}) collective-permute-start(bf16[384,1536]{1,0:T(8,128)(2,1)} %get-tuple-element.201), channel_id=1, source_target_pairs={{0,0},{4,1},{5,2},{1,3},{2,4},{6,5},{7,6},{3,7},{8,8},{12,9},{13,1... | collective-permute-start | bytes 3538952 | tf_op jit(solution)/shard_map/ppermute | solution.py:857
  994.6 59.9 %collective-permute-start.61 = (bf16[384,1536]{1,0:T(8,128)(2,1)S(1)}, bf16[384,1536]{1,0:T(8,128)(2,1)S(1)}, u32[]{:S(2)}, u32[]{:S(2)}) collective-permute-start(bf16[384,1536]{1,0:T(8,128)(2,1)S(1)} %get-tuple-element.202), channel_id=1, source_target_pairs={{1,0},{5,1},{4,2},{0,3},{3,4},{7,5},{6,6},{2,7},{9,8},{13,9},{12,1... | collective-permute-start | bytes 3538952 | tf_op jit(solution)/shard_map/ppermute | solution.py:857
  1028.4 26.1 %collective-permute-start.58 = (f32[8,384]{1,0:T(8,128)}, f32[8,384]{1,0:T(8,128)}, u32[]{:S(2)}, u32[]{:S(2)}) collective-permute-start(f32[8,384]{1,0:T(8,128)} %get-tuple-element.236), channel_id=1, source_target_pairs={{0,2},{1,3},{2,0},{3,1},{4,6},{5,7},{6,4},{7,5},{8,10},{9,11},{10,... | collective-permute-start | bytes 36872 | tf_op jit(solution)/shard_map/ppermute | solution.py:830
  (131 other events, 2009.1 us)
Sparse Core Ops, SparseCore 0:
  61.1 90.6 all-gather.7
  154.2 78.7 all-gather.9
  238.0 101.9 all-gather.11
  342.8 115.5 all-gather.13
  551.7 96.5 reduce-scatter.4
  651.8 95.0 reduce-scatter.6
  750.6 85.3 reduce-scatter.8
  845.2 75.8 reduce-scatter.10
  945.3 93.5 all-gather.17
  1054.7 36.4 all-gather.15
